TPU v7x, 32 devices: a whole 2x2x4 slice. The times are simulated.
32 devices in a mesh: dp: 4 (over y, x), fsdp: 8 (over z, core).
Axes of the slice: x: 2, y: 2, z: 4, core: 2. Of those that a mesh axis runs over, the one named last changes fastest.
Arguments:
- tokens: bfloat16 [2, 5120, 960], P(None, ('dp', 'fsdp')), may hold values from -6 to 6
- cotangent: bfloat16 [2, 5120, 960], P(None, ('dp', 'fsdp')), may hold values from -6 to 6
- counts: int32 [2, 32], P(None, ('dp', 'fsdp')), may hold values from 128 to 160, as said below
- w_query: bfloat16 [960, 960], P('dp', 'fsdp'), may hold values from -0.25 to 0.25
- key_weight: bfloat16 [960, 320], P('dp', 'fsdp'), may hold values from -0.25 to 0.25
- value_weight: bfloat16 [960, 320], P('dp', 'fsdp'), may hold values from -0.1875 to 0.1875
- w_out: bfloat16 [960, 960], P('dp', 'fsdp'), may hold values from -0.75 to 0.75
- w_gate: bfloat16 [960, 2560], P('dp', 'fsdp'), may hold values from -0.1875 to 0.1875
- w_up: bfloat16 [960, 2560], P('dp', 'fsdp'), may hold values from -0.1875 to 0.1875
- w_down: bfloat16 [2560, 960], P('dp', 'fsdp'), may hold values from -0.125 to 0.125
- gains: bfloat16 [2, 960], P(None, 'fsdp'), may hold values from 0.5 to 1.5
Outputs:
- output: bfloat16 [2, 5120, 960], P(None, ('dp', 'fsdp'))
- grad_tokens: float32 [2, 5120, 960], P(None, ('dp', 'fsdp'))
- grad_query: float32 [960, 960], P('dp', 'fsdp')
- grad_key: float32 [960, 320], P('dp', 'fsdp')
- grad_value: float32 [960, 320], P('dp', 'fsdp')
- grad_out: float32 [960, 960], P('dp', 'fsdp')
- grad_gate: float32 [960, 2560], P('dp', 'fsdp')
- grad_up: float32 [960, 2560], P('dp', 'fsdp')
- grad_down: float32 [2560, 960], P('dp', 'fsdp')
- grad_gains: float32 [2, 960], P(None, 'fsdp')
Inputs may be any that keep to these rules, and one draw needn't show every extreme that they name: `counts`: the used slots of the 8 devices that share a dp index form one sequence per micro-batch, in device order; in every such group and micro-batch some device uses all 160 slots.
All inputs are finite; a program needn't handle non-finite values.
Results may differ from a plain program's by a relative error of at most 0.02.
Values may be sent and summed in bfloat16 or wider, within the bound.
No kernel may reach another device: no remote copies, remote signals or barrier semaphores. Data moves between devices by JAX's collectives and lax.ppermute only.
A program may use at most 192 MiB of HBM per device.

v0:
```python
import jax
import jax.numpy as jnp
from jax import lax
from jax.sharding import PartitionSpec as P

MODEL_WIDTH = 960
QUERY_HEADS = 15
KEY_HEADS = 5
HEAD_WIDTH = 64


EPSILON = 1e-05
ROPE_BASE = 100000.0
SCORE_SCALE = 0.125


def rope_tables(position, head_size):
    half_size = head_size // 2
    frequency = ROPE_BASE ** (-(jnp.arange(half_size, dtype=jnp.float32) * 2.0) / head_size)
    angles = position.astype(jnp.float32)[:, None] * frequency[None, :]
    return (jnp.cos(angles)[:, None, :], jnp.sin(angles)[:, None, :])


def apply_rotation(values, cosine_table, sine_values):
    half_size = values.shape[-1] // 2
    front_half = values[..., :half_size]
    back_half = values[..., half_size:]
    return jnp.concatenate(
        [
            front_half * cosine_table - back_half * sine_values,
            back_half * cosine_table + front_half * sine_values,
        ],
        -1,
    )


def normalize(values, gain_row):
    inv_rms = lax.rsqrt(jnp.mean(values * values, -1, keepdims=True) + EPSILON)
    return (values * inv_rms * gain_row, inv_rms)


def norm_back(values, inv_rms, gain_row, incoming):
    weighted = incoming * gain_row
    return inv_rms * weighted - values * inv_rms * inv_rms * inv_rms * jnp.mean(
        weighted * values, -1, keepdims=True
    )


def build_mask(count_row, device, slot_capacity):
    group_width = count_row.shape[0]
    local_slot = jnp.arange(slot_capacity, dtype=jnp.int32)
    offsets = jnp.cumsum(count_row) - count_row
    is_mine = jnp.arange(group_width, dtype=jnp.int32) == device
    own_offset = jnp.sum(jnp.where(is_mine, offsets, 0))
    own_count = jnp.sum(jnp.where(is_mine, count_row, 0))
    query_pos = own_offset + local_slot
    query_valid = local_slot < own_count
    key_pos = (offsets[:, None] + local_slot[None, :]).reshape(-1)
    key_valid = (local_slot[None, :] < count_row[:, None]).reshape(-1)
    slot_ids = jnp.arange(group_width * slot_capacity, dtype=jnp.int32)
    own_slots = device * slot_capacity + local_slot
    allowed = query_valid[:, None] & key_valid[None, :] & (
        key_pos[None, :] <= query_pos[:, None]
    ) | (slot_ids[None, :] == own_slots[:, None])
    return (allowed, query_pos)


def kept_fetch(w_query, key_weight, value_weight, w_out, w_gate, w_up, w_down, gains):
    columns = (
        lax.all_gather(w_query, "fsdp", axis=1, tiled=True),
        lax.all_gather(key_weight, "fsdp", axis=1, tiled=True),
        lax.all_gather(value_weight, "fsdp", axis=1, tiled=True),
        lax.all_gather(w_out, "fsdp", axis=1, tiled=True),
        lax.all_gather(w_gate, "fsdp", axis=1, tiled=True),
        lax.all_gather(w_up, "fsdp", axis=1, tiled=True),
        lax.all_gather(w_down, "fsdp", axis=1, tiled=True),
        lax.all_gather(gains, "fsdp", axis=1, tiled=True),
    )
    matrices = (
        lax.all_gather(columns[0], "dp", axis=0, tiled=True),
        lax.all_gather(columns[1], "dp", axis=0, tiled=True),
        lax.all_gather(columns[2], "dp", axis=0, tiled=True),
        lax.all_gather(columns[3], "dp", axis=0, tiled=True),
        lax.all_gather(columns[4], "dp", axis=0, tiled=True),
        lax.all_gather(columns[5], "dp", axis=0, tiled=True),
        lax.all_gather(columns[6], "dp", axis=0, tiled=True),
    )
    return (matrices, columns[7].astype(jnp.float32))


def times_transpose(left, right):
    return jnp.einsum("rk,jk->rj", left, right, preferred_element_type=jnp.float32)


def rows_product(left, right):
    return jnp.einsum("rd,rk->dk", left, right, preferred_element_type=jnp.float32)


def local(
    tokens, cotangent, counts, w_query, key_weight, value_weight, w_out, w_gate, w_up, w_down, gains
):
    group_counts = lax.all_gather(counts, "fsdp", axis=1, tiled=True)
    device = lax.axis_index("fsdp")
    slot_capacity = tokens.shape[1]
    key_value_width = KEY_HEADS * HEAD_WIDTH
    device_share = QUERY_HEADS // KEY_HEADS
    kept_weights, kept_gain = kept_fetch(
        w_query, key_weight, value_weight, w_out, w_gate, w_up, w_down, gains
    )
    outputs = []
    grad_inputs = []
    saved = [[] for index_unused in range(11)]
    gain_one_total = jnp.zeros((MODEL_WIDTH,), jnp.float32)
    gain_two_total = jnp.zeros((MODEL_WIDTH,), jnp.float32)
    for micro_idx in range(tokens.shape[0]):
        matrices, gain_pair = (kept_weights, kept_gain)
        full_query, full_key, full_value, full_out, full_gate, full_up, full_down = matrices
        inputs = tokens[micro_idx].astype(jnp.float32)
        allowed, query_pos = build_mask(group_counts[micro_idx], device, slot_capacity)
        cosine_table, sine_values = rope_tables(query_pos, HEAD_WIDTH)
        first_normed, scale_one = normalize(inputs, gain_pair[0])
        normed_low = first_normed.astype(jnp.bfloat16)
        reduced_query = apply_rotation(
            jnp.dot(normed_low, full_query, preferred_element_type=jnp.float32).reshape(
                slot_capacity, QUERY_HEADS, HEAD_WIDTH
            ),
            cosine_table,
            sine_values,
        ).astype(jnp.bfloat16)
        key_low = (
            apply_rotation(
                jnp.dot(normed_low, full_key, preferred_element_type=jnp.float32).reshape(
                    slot_capacity, KEY_HEADS, HEAD_WIDTH
                ),
                cosine_table,
                sine_values,
            )
            .astype(jnp.bfloat16)
            .reshape(slot_capacity, key_value_width)
        )
        value_low = jnp.dot(normed_low, full_value, preferred_element_type=jnp.float32).astype(
            jnp.bfloat16
        )
        grouped_keys, grouped_values = (
            lax.all_gather(key_low, "fsdp", axis=0, tiled=True),
            lax.all_gather(value_low, "fsdp", axis=0, tiled=True),
        )
        heads_of_key = grouped_keys.reshape(-1, KEY_HEADS, HEAD_WIDTH)
        heads_of_value = grouped_values.reshape(-1, KEY_HEADS, HEAD_WIDTH)
        heads_of_query = reduced_query.reshape(slot_capacity, KEY_HEADS, device_share, HEAD_WIDTH)
        scores = (
            jnp.einsum(
                "qngd,knd->ngqk", heads_of_query, heads_of_key, preferred_element_type=jnp.float32
            )
            * SCORE_SCALE
        )
        masked = jnp.where(allowed, scores, -1e30)
        row_top = jnp.max(masked, -1, keepdims=True)
        exponent = jnp.where(allowed, jnp.exp(masked - row_top), 0.0)
        row_total = jnp.sum(exponent, -1, keepdims=True)
        prob_low = (exponent / row_total).astype(jnp.bfloat16)
        log_total = row_top + jnp.log(row_total)
        mixed_heads = jnp.einsum(
            "ngqk,knd->qngd", prob_low, heads_of_value, preferred_element_type=jnp.float32
        ).reshape(slot_capacity, MODEL_WIDTH)
        attended = mixed_heads.astype(jnp.bfloat16)
        hidden_state = inputs + jnp.dot(attended, full_out, preferred_element_type=jnp.float32)
        normed_two, scale_two = normalize(hidden_state, gain_pair[1])
        normed_two_low = normed_two.astype(jnp.bfloat16)
        gate_act = jnp.dot(normed_two_low, full_gate, preferred_element_type=jnp.float32)
        upward = jnp.dot(normed_two_low, full_up, preferred_element_type=jnp.float32)
        sigmoid_gate = jax.nn.sigmoid(gate_act)
        product = (gate_act * sigmoid_gate * upward).astype(jnp.bfloat16)
        outputs.append(
            (hidden_state + jnp.dot(product, full_down, preferred_element_type=jnp.float32)).astype(
                jnp.bfloat16
            )
        )
        matrices, gain_pair = (kept_weights, kept_gain)
        full_query, full_key, full_value, full_out, full_gate, full_up, full_down = matrices
        grad_low = cotangent[micro_idx]
        grad_product = times_transpose(grad_low, full_down)
        grad_gate = (
            grad_product * upward * sigmoid_gate * (1.0 + gate_act * (1.0 - sigmoid_gate))
        ).astype(jnp.bfloat16)
        grad_upward = (grad_product * gate_act * sigmoid_gate).astype(jnp.bfloat16)
        grad_normed_two = times_transpose(grad_gate, full_gate) + times_transpose(
            grad_upward, full_up
        )
        gain_two_total = gain_two_total + jnp.sum(grad_normed_two * hidden_state * scale_two, 0)
        grad_hidden = grad_low.astype(jnp.float32) + norm_back(
            hidden_state, scale_two, gain_pair[1], grad_normed_two
        )
        grad_branch = grad_hidden.astype(jnp.bfloat16)
        mixed_gradient = times_transpose(grad_branch, full_out).astype(jnp.bfloat16)
        head_gradient = mixed_gradient.reshape(slot_capacity, KEY_HEADS, device_share, HEAD_WIDTH)
        again_scores = (
            jnp.einsum(
                "qngd,knd->ngqk", heads_of_query, heads_of_key, preferred_element_type=jnp.float32
            )
            * SCORE_SCALE
        )
        probability = jnp.where(allowed, jnp.exp(again_scores - log_total), 0.0)
        grad_prob = jnp.einsum(
            "qngd,knd->ngqk", head_gradient, heads_of_value, preferred_element_type=jnp.float32
        )
        row_delta = jnp.sum(probability * grad_prob, -1, keepdims=True)
        grad_scores = (probability * (grad_prob - row_delta)).astype(jnp.bfloat16)
        grad_query_rot = (
            jnp.einsum(
                "ngqk,knd->qngd", grad_scores, heads_of_key, preferred_element_type=jnp.float32
            ).reshape(slot_capacity, QUERY_HEADS, HEAD_WIDTH)
            * SCORE_SCALE
        )
        key_part = (
            jnp.einsum(
                "ngqk,qngd->knd", grad_scores, heads_of_query, preferred_element_type=jnp.float32
            ).reshape(-1, key_value_width)
            * SCORE_SCALE
        )
        value_part = jnp.einsum(
            "ngqk,qngd->knd",
            probability.astype(jnp.bfloat16),
            head_gradient,
            preferred_element_type=jnp.float32,
        ).reshape(-1, key_value_width)
        key_gradient, value_grad = (
            lax.psum_scatter(
                key_part.astype(jnp.bfloat16), "fsdp", scatter_dimension=0, tiled=True
            ).astype(jnp.float32),
            lax.psum_scatter(
                value_part.astype(jnp.bfloat16), "fsdp", scatter_dimension=0, tiled=True
            ).astype(jnp.float32),
        )
        grad_query = (
            apply_rotation(grad_query_rot, cosine_table, -sine_values)
            .astype(jnp.bfloat16)
            .reshape(slot_capacity, MODEL_WIDTH)
        )
        grad_key = (
            apply_rotation(
                key_gradient.reshape(slot_capacity, KEY_HEADS, HEAD_WIDTH),
                cosine_table,
                -sine_values,
            )
            .astype(jnp.bfloat16)
            .reshape(slot_capacity, key_value_width)
        )
        grad_value = value_grad.astype(jnp.bfloat16)
        grad_normed_one = (
            times_transpose(grad_query, full_query)
            + times_transpose(grad_key, full_key)
            + times_transpose(grad_value, full_value)
        )
        gain_one_total = gain_one_total + jnp.sum(grad_normed_one * inputs * scale_one, 0)
        grad_inputs.append(
            grad_hidden + norm_back(inputs, scale_one, gain_pair[0], grad_normed_one)
        )
        kept_rows = (
            normed_low,
            grad_query,
            grad_key,
            grad_value,
            attended,
            grad_branch,
            normed_two_low,
            grad_gate,
            grad_upward,
            product,
            grad_low,
        )
        for slot_index in range(11):
            saved[slot_index].append(kept_rows[slot_index])
    joined = [jnp.concatenate(column_list, 0) for column_list in saved]
    gain_terms = jnp.stack([gain_one_total, gain_two_total], 0)
    slices = (
        lax.all_to_all(joined[1], "fsdp", split_axis=1, concat_axis=0, tiled=True),
        lax.all_to_all(joined[2], "fsdp", split_axis=1, concat_axis=0, tiled=True),
        lax.all_to_all(joined[3], "fsdp", split_axis=1, concat_axis=0, tiled=True),
        lax.all_to_all(joined[5], "fsdp", split_axis=1, concat_axis=0, tiled=True),
        lax.all_to_all(joined[7], "fsdp", split_axis=1, concat_axis=0, tiled=True),
        lax.all_to_all(joined[8], "fsdp", split_axis=1, concat_axis=0, tiled=True),
        lax.all_to_all(joined[10], "fsdp", split_axis=1, concat_axis=0, tiled=True),
    )
    pieces = (
        lax.all_gather(joined[0], "fsdp", axis=0, tiled=True),
        lax.all_gather(joined[4], "fsdp", axis=0, tiled=True),
        lax.all_gather(joined[6], "fsdp", axis=0, tiled=True),
        lax.all_gather(joined[9], "fsdp", axis=0, tiled=True),
    )
    picked = [member for member in slices]
    gain_part = lax.psum_scatter(gain_terms, "fsdp", scatter_dimension=1, tiled=True)
    summed_rows = (
        lax.psum_scatter(
            rows_product(pieces[0], picked[0]).astype(jnp.bfloat16),
            "dp",
            scatter_dimension=0,
            tiled=True,
        ).astype(jnp.float32),
        lax.psum_scatter(
            rows_product(pieces[0], picked[1]).astype(jnp.bfloat16),
            "dp",
            scatter_dimension=0,
            tiled=True,
        ).astype(jnp.float32),
        lax.psum_scatter(
            rows_product(pieces[0], picked[2]).astype(jnp.bfloat16),
            "dp",
            scatter_dimension=0,
            tiled=True,
        ).astype(jnp.float32),
        lax.psum_scatter(
            rows_product(pieces[1], picked[3]).astype(jnp.bfloat16),
            "dp",
            scatter_dimension=0,
            tiled=True,
        ).astype(jnp.float32),
        lax.psum_scatter(
            rows_product(pieces[2], picked[4]).astype(jnp.bfloat16),
            "dp",
            scatter_dimension=0,
            tiled=True,
        ).astype(jnp.float32),
        lax.psum_scatter(
            rows_product(pieces[2], picked[5]).astype(jnp.bfloat16),
            "dp",
            scatter_dimension=0,
            tiled=True,
        ).astype(jnp.float32),
        lax.psum_scatter(
            rows_product(pieces[3], picked[6]).astype(jnp.bfloat16),
            "dp",
            scatter_dimension=0,
            tiled=True,
        ).astype(jnp.float32),
    )
    gain_grad = lax.psum(gain_part, "dp")
    return (
        jnp.stack(outputs, 0),
        jnp.stack(grad_inputs, 0),
        summed_rows[0],
        summed_rows[1],
        summed_rows[2],
        summed_rows[3],
        summed_rows[4],
        summed_rows[5],
        summed_rows[6],
        gain_grad,
    )


def solution(mesh):
    in_specs = (
        P(None, ("dp", "fsdp"), None),
        P(None, ("dp", "fsdp"), None),
        P(None, ("dp", "fsdp")),
        P("dp", "fsdp"),
        P("dp", "fsdp"),
        P("dp", "fsdp"),
        P("dp", "fsdp"),
        P("dp", "fsdp"),
        P("dp", "fsdp"),
        P("dp", "fsdp"),
        P(None, "fsdp"),
    )
    out_specs = (
        P(None, ("dp", "fsdp"), None),
        P(None, ("dp", "fsdp"), None),
        P("dp", "fsdp"),
        P("dp", "fsdp"),
        P("dp", "fsdp"),
        P("dp", "fsdp"),
        P("dp", "fsdp"),
        P("dp", "fsdp"),
        P("dp", "fsdp"),
        P(None, "fsdp"),
    )
    return jax.shard_map(local, mesh=mesh, in_specs=in_specs, out_specs=out_specs, check_vma=False)
```

profile of v0, /device:TPU:0, one launch (start us, length us, event | category | flops | bytes accessed | tf_op | source)
XLA Modules:
  0.0 993.7 jit_solution(5394020222352563223)
XLA Ops:
  10.4 16.9 %all_gather.80 = bf16[240,960]{0,1:T(8,128)(2,1)S(1)} all-gather(bf16[240,120]{0,1:T(8,128)(2,1)S(1)} %copy.136), channel_id=1, replica_groups=mesh['dp'=4,'fsdp'=8] {'fsdp'}, dimensions={1}, use_global_device_ids=true | all-gather | bytes 518400 | tf_op jit(solution)/shard_map/all_gather | solution.py:70
  29.3 15.5 %all_gather.82 = bf16[240,960]{0,1:T(8,128)(2,1)S(1)} all-gather(bf16[240,120]{0,1:T(8,128)(2,1)S(1)} %copy.139), channel_id=1, replica_groups=mesh['dp'=4,'fsdp'=8] {'fsdp'}, dimensions={1}, use_global_device_ids=true | all-gather | bytes 518400 | tf_op jit(solution)/shard_map/all_gather | solution.py:73
  48.5 13.5 %all-gather.25.cloned.1.call-done = bf16[240,2560]{0,1:T(8,128)(2,1)} async-done(((bf16[240,320]{0,1:T(8,128)(2,1)}), bf16[240,2560]{0,1:T(8,128)(2,1)}) %all-gather.25.cloned.1.call-update) | async-done | bytes 1228816 | tf_op jit(solution)/shard_map/all_gather | solution.py:75
  64.5 21.8 %all-gather.29.cloned.1.call-done = bf16[640,960]{0,1:T(8,128)(2,1)} async-done(((bf16[640,120]{0,1:T(8,128)(2,1)}), bf16[640,960]{0,1:T(8,128)(2,1)}) %all-gather.29.cloned.1.call-update) | async-done | bytes 1228816 | tf_op jit(solution)/shard_map/all_gather | solution.py:76
  111.2 14.0 %all_gather.73 = bf16[240,320]{0,1:T(8,128)(2,1)S(1)} all-gather(bf16[240,40]{0,1:T(8,128)(2,1)S(1)} %copy-done.78), channel_id=1, replica_groups=mesh['dp'=4,'fsdp'=8] {'fsdp'}, dimensions={1}, use_global_device_ids=true | all-gather | bytes 172800 | tf_op jit(solution)/shard_map/all_gather | solution.py:72
  125.2 14.9 %all-gather.1 = bf16[4,240,320]{1,2,0:T(8,128)(2,1)S(1)} all-gather(bf16[1,240,320]{1,2,0:T(8,128)(2,1)S(1)} %bitcast.503), channel_id=1, replica_groups=mesh['dp'=4,'fsdp'=8] {'dp'}, dimensions={0}, use_global_device_ids=true | all-gather | bytes 768000 | tf_op jit(solution)/shard_map/all_gather | solution.py:82
  142.1 14.0 %all_gather.77 = bf16[240,320]{0,1:T(8,128)(2,1)S(1)} all-gather(bf16[240,40]{0,1:T(8,128)(2,1)S(1)} %copy-done.79), channel_id=1, replica_groups=mesh['dp'=4,'fsdp'=8] {'fsdp'}, dimensions={1}, use_global_device_ids=true | all-gather | bytes 172800 | tf_op jit(solution)/shard_map/all_gather | solution.py:71
  171.4 16.4 %all_gather.90 = bf16[1280,320]{1,0:T(8,128)(2,1)S(1)} all-gather(bf16[160,320]{1,0:T(8,128)(2,1)S(1)} %convolution_convert_fusion.7), channel_id=1, replica_groups=mesh['dp'=4,'fsdp'=8] {'fsdp'}, dimensions={0}, use_global_device_ids=true | all-gather | bytes 921600 | tf_op jit(solution)/shard_map/all_gather | solution.py:146
  194.6 17.0 %all_gather.91 = bf16[1280,320]{1,0:T(8,128)(2,1)S(1)} all-gather(bf16[160,320]{1,0:T(8,128)(2,1)S(1)} %copy.144), channel_id=1, replica_groups=mesh['dp'=4,'fsdp'=8] {'fsdp'}, dimensions={0}, use_global_device_ids=true | all-gather | bytes 921600 | tf_op jit(solution)/shard_map/all_gather | solution.py:145
  212.1 17.0 %all_gather.75 = bf16[1280,320]{1,0:T(8,128)(2,1)S(1)} all-gather(bf16[160,320]{1,0:T(8,128)(2,1)S(1)} %convolution_convert_fusion.8), channel_id=1, replica_groups=mesh['dp'=4,'fsdp'=8] {'fsdp'}, dimensions={0}, use_global_device_ids=true | all-gather | bytes 921600 | tf_op jit(solution)/shard_map/all_gather | solution.py:146
  230.6 17.2 %all_gather.79 = bf16[1280,320]{1,0:T(8,128)(2,1)S(1)} all-gather(bf16[160,320]{1,0:T(8,128)(2,1)S(1)} %copy.134), channel_id=1, replica_groups=mesh['dp'=4,'fsdp'=8] {'fsdp'}, dimensions={0}, use_global_device_ids=true | all-gather | bytes 921600 | tf_op jit(solution)/shard_map/all_gather | solution.py:145
  278.1 13.9 %fusion.41 = bf16[5,64,3,160]{3,1,2,0:T(8,128)(2,1)S(1)} fusion(bf16[1280,5,64,1]{0,2,3,1:T(8,128)(2,1)S(1)} %bitcast.469, f32[5,1280,160,3]{1,2,3,0:T(8,128)S(1)} %get-tuple-element.91, f32[5,3,160]{2,1,0:T(4,128)S(1)} %fusion.12, f32[5,3,160]{2,1,0:T(4,128)S(1)} %get-tuple-element.90, pred[160,1280]{1,0:T(8,128)(4,1)S(1)} %get-tuple-element.75), kind=kOutput, calls=%fused_computation.62 | convolution fusion | flops 411801600 | bytes 13638400 | tf_op jit(solution)/shard_map/ngqk,knd->qngd/dot_general | solution.py:163
  306.2 35.2 %all-gather.31.cloned.1.call-done = bf16[2560,960]{0,1:T(8,128)(2,1)} async-done(((bf16[640,960]{0,1:T(8,128)(2,1)}), bf16[2560,960]{0,1:T(8,128)(2,1)}) %all-gather.31.cloned.1.call-update) | async-done | bytes 4915216 | tf_op jit(solution)/shard_map/all_gather | solution.py:86
  368.1 13.6 %fusion = (f32[5,3,160]{2,1,0:T(4,128)S(1)}, f32[5,1280,160,3]{1,2,3,0:T(8,128)}) fusion(f32[5,1280,160,3]{1,2,3,0:T(8,128)} %copy-done.1, f32[5,3,160]{2,1,0:T(4,128)} %log_add_fusion, pred[160,1280]{1,0:T(8,128)(4,1)} %copy-done.14, bf16[1280,5,64,1]{0,2,3,1:T(8,128)(2,1)} %bitcast.466, bf16[160,5,3,64]{0,3,2,1:T(8,128)(2,1)} %bitcast.484), kind=kOutput, calls=%fused_computation.2 | convolution fusion | flops 408573600 | bytes 25926400 | tf_op jit(solution)/shard_map/qngd,knd->ngqk/dot_general | solution.py:204
  399.3 13.6 %fusion.3 = (f32[5,3,160]{2,1,0:T(4,128)S(1)}, f32[5,1280,160,3]{1,2,3,0:T(8,128)}) fusion(f32[5,1280,160,3]{1,2,3,0:T(8,128)} %copy-done, f32[5,3,160]{2,1,0:T(4,128)} %log_add_fusion.1, pred[160,1280]{1,0:T(8,128)(4,1)S(1)} %get-tuple-element.75, bf16[1280,5,64,1]{0,2,3,1:T(8,128)(2,1)} %bitcast.468, bf16[160,5,3,64]{0,3,2,1:T(8,128)(2,1)S(1)} %bitcast.486), kind=kOutput, calls=%fused_computation.7 | convolution fusion | flops 408573600 | bytes 25926400 | tf_op jit(solution)/shard_map/qngd,knd->ngqk/dot_general | solution.py:204
  460.7 21.0 %all-to-all-done = bf16[320,8,120]{2,0,1:T(8,128)(2,1)S(1)} async-done(((bf16[320,8,120]{2,0,1:T(8,128)(2,1)}), bf16[320,8,120]{2,0,1:T(8,128)(2,1)S(1)}, u32[]{:S(2)}, u32[]{:S(2)}) %all-to-all-start) | async-done | bytes 614432 | tf_op jit(solution)/shard_map/all_to_all | solution.py:277
  506.5 20.0 %all-to-all-done.3 = bf16[320,8,120]{2,0,1:T(8,128)(2,1)S(1)} async-done(((bf16[320,8,120]{2,0,1:T(8,128)(2,1)}), bf16[320,8,120]{2,0,1:T(8,128)(2,1)S(1)}, u32[]{:S(2)}, u32[]{:S(2)}) %all-to-all-start.3) | async-done | bytes 614432 | tf_op jit(solution)/shard_map/all_to_all | solution.py:280
  579.8 58.3 %all-to-all-done.4 = bf16[320,8,320]{0,2,1:T(8,128)(2,1)} async-done(((bf16[320,8,320]{0,2,1:T(8,128)(2,1)}), bf16[320,8,320]{0,2,1:T(8,128)(2,1)}, u32[]{:S(2)}, u32[]{:S(2)}) %all-to-all-start.4) | async-done | bytes 1638432 | tf_op jit(solution)/shard_map/all_to_all | solution.py:281
  654.9 53.0 %all-reduce.6 = f32[2,960]{1,0:T(2,128)S(1)} all-reduce(f32[2,960]{1,0:T(2,128)S(1)} %pad_maximum_fusion.21), channel_id=13, replica_groups=mesh['dp'=4,'fsdp'=8] {'fsdp'}, use_global_device_ids=true, to_apply=%region_35.36.clone | all-reduce | flops 1920 | bytes 15360
  726.5 27.6 %all-to-all-start.6 = ((bf16[320,8,120]{2,0,1:T(8,128)(2,1)}), bf16[320,8,120]{2,0,1:T(8,128)(2,1)S(1)}, u32[]{:S(2)}, u32[]{:S(2)}) async-start(bf16[320,8,120]{2,0,1:T(8,128)(2,1)} %pad_maximum_fusion.10), calls=%async_computation.6 | async-start | bytes 1310720 | tf_op jit(solution)/shard_map/all_to_all | solution.py:283
  768.0 21.3 %all-to-all-done.6 = bf16[320,8,120]{2,0,1:T(8,128)(2,1)S(1)} async-done(((bf16[320,8,120]{2,0,1:T(8,128)(2,1)}), bf16[320,8,120]{2,0,1:T(8,128)(2,1)S(1)}, u32[]{:S(2)}, u32[]{:S(2)}) %all-to-all-start.6) | async-done | bytes 614432 | tf_op jit(solution)/shard_map/all_to_all | solution.py:283
  789.3 78.2 %all-gather.39.cloned.1.call-done = bf16[2560,2560]{1,0:T(8,128)(2,1)} async-done(((bf16[320,2560]{1,0:T(8,128)(2,1)}), bf16[2560,2560]{1,0:T(8,128)(2,1)}) %all-gather.39.cloned.1.call-update) | async-done | bytes 13107216 | tf_op jit(solution)/shard_map/all_gather | solution.py:289
  894.1 62.5 %all-reduce.10.cloned.1.call-done = (bf16[960,40]{0,1:T(8,128)(2,1)}, bf16[960,40]{0,1:T(8,128)(2,1)}, bf16[960,320]{0,1:T(8,128)(2,1)}, bf16[960,320]{0,1:T(8,128)(2,1)}) async-done(((bf16[960,40]{0,1:T(8,128)(2,1)}, bf16[960,40]{0,1:T(8,128)(2,1)}, bf16[960,320]{0,1:T(8,128)(2,1)}, bf16[960,320]{0,1:T(8,128)(2,1)}), (bf16[960,40]{0,1:T(8,128)(2,1)}, bf16[960,40]{0,1:T(8,128)(2,1)}, ...) | async-done | bytes 1382416
  963.1 21.7 %reduce-scatter.35.cloned.1.call-done = bf16[640,120]{1,0:T(8,128)(2,1)} async-done(((bf16[2560,120]{1,0:T(8,128)(2,1)}), bf16[640,120]{1,0:T(8,128)(2,1)}) %reduce-scatter.35.cloned.1.call-update) | async-done | bytes 153616
  (466 shorter events, 357.8 us)
Async XLA Ops:
  7.2 38.7 %all-gather.21.cloned.1.call-start = ((), (), s32[]{:S(2)}) async-start(), calls=%async_computation.16 | async-start | bytes 1474560 | tf_op jit(solution)/shard_map/all_gather | solution.py:74
  7.9 54.1 %all-gather.25.cloned.1.call-start = ((), (), s32[]{:S(2)}) async-start(), calls=%async_computation.18 | async-start | bytes 1474560 | tf_op jit(solution)/shard_map/all_gather | solution.py:75
  8.7 77.6 %all-gather.29.cloned.1.call-start = ((), (), s32[]{:S(2)}) async-start(), calls=%async_computation.20 | async-start | bytes 1382400 | tf_op jit(solution)/shard_map/all_gather | solution.py:76
  9.4 241.6 %all-gather.17.cloned.1.call-start = ((), (), s32[]{:S(2)}) async-start(), calls=%async_computation.14 | async-start | bytes 2457600 | tf_op jit(solution)/shard_map/all_gather | solution.py:80
  28.3 263.7 %all-gather.19.cloned.1.call-start = ((), (), s32[]{:S(2)}) async-start(), calls=%async_computation.15 | async-start | bytes 2457600 | tf_op jit(solution)/shard_map/all_gather | solution.py:83
  45.8 251.0 %all-gather.23.cloned.1.call-start = ((), (), s32[]{:S(2)}) async-start(), calls=%async_computation.17 | async-start | bytes 6144000 | tf_op jit(solution)/shard_map/all_gather | solution.py:84
  48.4 253.1 %all-gather.27.cloned.1.call-start = ((), (), s32[]{:S(2)}) async-start(), calls=%async_computation.19 | async-start | bytes 6144000 | tf_op jit(solution)/shard_map/all_gather | solution.py:85
  64.5 277.0 %all-gather.31.cloned.1.call-start = ((), (), s32[]{:S(2)}) async-start(), calls=%async_computation.21 | async-start | bytes 6144000 | tf_op jit(solution)/shard_map/all_gather | solution.py:86
  86.3 374.4 %all-gather.33.cloned.1.call-start = ((), (), s32[]{:S(2)}) async-start(), calls=%async_computation.22 | async-start | bytes 5898240 | tf_op jit(solution)/shard_map/all_gather | solution.py:286
  98.1 404.6 %reduce-scatter.31.cloned.1.call-start = ((), (), s32[]{:S(2)}) async-start(), calls=%async_computation.28 | async-start | bytes 1105920
  399.2 104.5 %reduce-scatter.27.cloned.1.call-start = ((), (), s32[]{:S(2)}) async-start(), calls=%async_computation.26 | async-start | bytes 1105920
  425.0 105.0 %reduce-scatter.33.cloned.1.call-start = ((), (), s32[]{:S(2)}) async-start(), calls=%async_computation.29 | async-start | bytes 1105920
  434.1 100.7 %reduce-scatter.29.cloned.1.call-start = ((), (), s32[]{:S(2)}) async-start(), calls=%async_computation.27 | async-start | bytes 1105920
  460.6 185.6 %reduce-scatter.37.cloned.1.call-start = ((), (), s32[]{:S(2)}) async-start(), calls=%async_computation.31 | async-start | bytes 307200
  487.7 220.2 %all-gather.35.cloned.1.call-start = ((), (), s32[]{:S(2)}) async-start(), calls=%async_computation.23 | async-start | bytes 5898240 | tf_op jit(solution)/shard_map/all_gather | solution.py:287
  492.6 266.5 %all-gather.37.cloned.1.call-start = ((), (), s32[]{:S(2)}) async-start(), calls=%async_computation.24 | async-start | bytes 5898240 | tf_op jit(solution)/shard_map/all_gather | solution.py:288
  493.6 373.9 %all-gather.39.cloned.1.call-start = ((), (), s32[]{:S(2)}) async-start(), calls=%async_computation.25 | async-start | bytes 14745600 | tf_op jit(solution)/shard_map/all_gather | solution.py:289
  498.9 27.6 %all-to-all-start.3 = ((bf16[320,8,120]{2,0,1:T(8,128)(2,1)}), bf16[320,8,120]{2,0,1:T(8,128)(2,1)S(1)}, u32[]{:S(2)}, u32[]{:S(2)}) async-start(bf16[320,8,120]{2,0,1:T(8,128)(2,1)} %copy.154), calls=%async_computation.3 | async-start | bytes 1310720 | tf_op jit(solution)/shard_map/all_to_all | solution.py:280
  552.8 85.2 %all-to-all-start.4 = ((bf16[320,8,320]{0,2,1:T(8,128)(2,1)}), bf16[320,8,320]{0,2,1:T(8,128)(2,1)}, u32[]{:S(2)}, u32[]{:S(2)}) async-start(bf16[320,8,320]{0,2,1:T(8,128)(2,1)} %bitcast.113), calls=%async_computation.4 | async-start | bytes 3932160 | tf_op jit(solution)/shard_map/all_to_all | solution.py:281
  638.0 88.5 %all-to-all-start.5 = ((bf16[320,8,320]{0,2,1:T(8,128)(2,1)}), bf16[320,8,320]{0,2,1:T(8,128)(2,1)}, u32[]{:S(2)}, u32[]{:S(2)}) async-start(bf16[320,8,320]{0,2,1:T(8,128)(2,1)} %bitcast.455), calls=%async_computation.5 | async-start | bytes 3932160 | tf_op jit(solution)/shard_map/all_to_all | solution.py:282
  642.5 250.1 %reduce-scatter.39.cloned.1.call-start = ((), (), s32[]{:S(2)}) async-start(), calls=%async_computation.32 | async-start | bytes 307200
  726.5 62.9 %all-to-all-start.6 = ((bf16[320,8,120]{2,0,1:T(8,128)(2,1)}), bf16[320,8,120]{2,0,1:T(8,128)(2,1)S(1)}, u32[]{:S(2)}, u32[]{:S(2)}) async-start(bf16[320,8,120]{2,0,1:T(8,128)(2,1)} %pad_maximum_fusion.10), calls=%async_computation.6 | async-start | bytes 1310720 | tf_op jit(solution)/shard_map/all_to_all | solution.py:283
  754.1 202.5 %all-reduce.10.cloned.1.call-start = ((), (), s32[]{:S(2)}) async-start(), calls=%async_computation.33 | async-start | bytes 2949120
  767.7 217.1 %reduce-scatter.35.cloned.1.call-start = ((), (), s32[]{:S(2)}) async-start(), calls=%async_computation.30 | async-start | bytes 819200
  (112 other events, 2123.9 us)
Sparse Core Ops, SparseCore 0:
  9.7 27.8 all-gather.20
  39.2 22.7 all-gather.24
  63.7 22.5 all-gather.28
  88.0 33.6 all-gather.16
  123.4 35.3 all-gather.18
  161.1 59.1 all-gather.22
  222.1 58.6 all-gather.26
  282.7 58.6 all-gather.30
  343.7 56.0 all-gather.32
  402.5 30.8 reduce-scatter.30
  435.7 30.2 reduce-scatter.26
  468.2 31.0 reduce-scatter.32
  501.7 33.0 reduce-scatter.28
  538.0 25.1 reduce-scatter.36
  564.7 82.3 all-gather.34
  648.6 84.3 all-gather.36
  734.5 133.0 all-gather.38
  870.8 21.7 reduce-scatter.38
  896.6 59.9 all-reduce.9
  959.3 25.3 reduce-scatter.34
where the time goes:
time: 1000 us; the launch traced here: 994 us
  waiting for transfers between devices  372 us (37%)
  blocking collectives  237 us (24%)
  matrix products  176 us (18%)
  local copies, waits for them, and re-layouts  73.1 us (7%)
  other arithmetic  65.3 us (7%)
  starting transfers between devices  53 us (5%)
  between operations  17.6 us (2%)
    unnamed x28, waiting for transfers between devices  94.3 us
    all_gather x1, waiting for transfers between devices, local(): lax.all_gather(joined[9], 'fsdp', axis=0, tiled=True)  78.2 us
    all_to_all x1, waiting for transfers between devices, local(): lax.all_to_all(joined[7], 'fsdp', split_axis=1, concat_axis=0, tiled=True)  58.3 us
    unnamed x1, blocking collectives  53 us
    dot_general x14, matrix products, times_transpose(): jnp.einsum('rk,jk->rj', left, right, preferred_element_type=jnp.float32)  35.5 us
    all_gather x1, waiting for transfers between devices, kept_fetch(): lax.all_gather(columns[6], 'dp', axis=0, tiled=True)  35.2 us
    all_gather x2, blocking collectives, local(): lax.all_gather(key_low, 'fsdp', axis=0, tiled=True)  34.2 us
    dot_general x7, matrix products, rows_product(): jnp.einsum('rd,rk->dk', left, right, preferred_element_type=jnp.float32)  33.7 us
  transfers between devices with their start and end apart: 27, of which 14 were waited for; matrix products, arithmetic and copies ran while one was open for 30% of the time, Pallas kernels for 0%

commit v1 on v0

--- a/solution.py
+++ b/solution.py
@@ -1,6 +1,8 @@
 import jax
 import jax.numpy as jnp
 from jax import lax
+from jax.experimental import pallas as pl
+from jax.experimental.pallas import tpu as pltpu
 from jax.sharding import PartitionSpec as P
 
 MODEL_WIDTH = 960
@@ -349,6 +351,816 @@
     )
 
 
+def swap_core(value):
+    return lax.ppermute(value, "fsdp", [(j, j ^ 1) for j in range(8)])
+
+
+def swap_dp(value, mask):
+    return lax.ppermute(value, "dp", [(j, j ^ mask) for j in range(4)])
+
+
+def shift_z(value, step):
+    return lax.ppermute(value, "fsdp", [(j, (j + 2 * step) % 8) for j in range(8)])
+
+
+def shift_z_up(value, step):
+    return lax.ppermute(value, "fsdp", [(j, j + 2 * step) for j in range(8) if j + 2 * step < 8])
+
+
+def shift_z_down(value, step):
+    return lax.ppermute(value, "fsdp", [(j, j - 2 * step) for j in range(8) if j - 2 * step >= 0])
+
+
+def add_low(*terms):
+    total = terms[0].astype(jnp.float32)
+    for term in terms[1:]:
+        total = total + term.astype(jnp.float32)
+    return total.astype(jnp.bfloat16)
+
+
+def product_nn(left, right):
+    return lax.dot_general(
+        left, right, (((1,), (0,)), ((), ())), preferred_element_type=jnp.float32
+    )
+
+
+def product_nt(left, right):
+    return lax.dot_general(
+        left, right, (((1,), (1,)), ((), ())), preferred_element_type=jnp.float32
+    )
+
+
+def product_tn(left, right):
+    return lax.dot_general(
+        left, right, (((0,), (0,)), ((), ())), preferred_element_type=jnp.float32
+    )
+
+
+VMEM = pl.BlockSpec(memory_space=pltpu.VMEM)
+SMEM = pl.BlockSpec(memory_space=pltpu.SMEM)
+ANY = pl.BlockSpec(memory_space=pl.ANY)
+
+
+def run(body, name, ins, in_specs, outs, out_specs, scratch, flops, megabytes):
+    moved = sum(v.size * v.dtype.itemsize for v in ins)
+    moved += sum(v.size * v.dtype.itemsize for v in outs)
+    return pl.pallas_call(
+        body,
+        out_shape=tuple(outs),
+        in_specs=in_specs,
+        out_specs=tuple(out_specs),
+        scratch_shapes=scratch,
+        compiler_params=pltpu.CompilerParams(vmem_limit_bytes=megabytes * 1024 * 1024),
+        cost_estimate=pl.CostEstimate(flops=flops, bytes_accessed=moved, transcendentals=0),
+        name=name,
+    )(*ins)
+
+
+def struct(shape, dtype=jnp.bfloat16):
+    return jax.ShapeDtypeStruct(shape, dtype)
+
+
+def column_index(ids_ref, core_rel, s):
+    return 2 * lax.rem(ids_ref[1] - s + 4, 4) + (ids_ref[2] ^ core_rel)
+
+
+def start_row(index, size):
+    return pl.ds(pl.multiple_of(index * size, 8), size)
+
+
+def project_kernel(
+    ids_ref, own_ref, other_ref, n1_ref, cos_ref, sin_ref, q_ref, kv_ref, proj_ref, turned_ref
+):
+    width = n1_ref.shape[0] * n1_ref.shape[1]
+    kv_width = KEY_HEADS * HEAD_WIDTH
+    q_cols, k_cols = width // 8, kv_width // 8
+    for core_rel, w_ref in ((0, own_ref), (1, other_ref)):
+
+        def body(s, carry, core_rel=core_rel, w_ref=w_ref):
+            f = column_index(ids_ref, core_rel, s)
+            total = product_nn(w_ref[s], n1_ref[ids_ref[0]])
+            for k in range(1, 4):
+                total += product_nn(w_ref[k * 4 + s], n1_ref[ids_ref[0] ^ k])
+            proj_ref[start_row(f, q_cols), :] = total[:q_cols]
+            proj_ref[pl.ds(pl.multiple_of(width + f * k_cols, 8), k_cols), :] = total[
+                q_cols : q_cols + k_cols
+            ]
+            proj_ref[pl.ds(pl.multiple_of(width + kv_width + f * k_cols, 8), k_cols), :] = total[
+                q_cols + k_cols : q_cols + 2 * k_cols
+            ]
+            return carry
+
+        lax.fori_loop(0, 4, body, 0)
+    cosine, sine = cos_ref[...], sin_ref[...]
+    half = HEAD_WIDTH // 2
+
+    def heads(head, carry):
+        front = proj_ref[pl.ds(pl.multiple_of(head * HEAD_WIDTH, 8), half), :]
+        back = proj_ref[pl.ds(pl.multiple_of(head * HEAD_WIDTH + half, 8), half), :]
+        q_ref[head, :half, :] = (
+            (front * cosine - back * sine).astype(jnp.bfloat16) * SCORE_SCALE
+        ).astype(jnp.bfloat16)
+        q_ref[head, half:, :] = (
+            (back * cosine + front * sine).astype(jnp.bfloat16) * SCORE_SCALE
+        ).astype(jnp.bfloat16)
+        return carry
+
+    lax.fori_loop(0, QUERY_HEADS, heads, 0)
+    for head in range(KEY_HEADS):
+        base = width + head * HEAD_WIDTH
+        front = proj_ref[base : base + half, :]
+        back = proj_ref[base + half : base + 2 * half, :]
+        turned_ref[head * HEAD_WIDTH : head * HEAD_WIDTH + half, :] = front * cosine - back * sine
+        turned_ref[head * HEAD_WIDTH + half : (head + 1) * HEAD_WIDTH, :] = (
+            back * cosine + front * sine
+        )
+    turned_ref[kv_width:, :] = proj_ref[width + kv_width :, :]
+    kv_ref[...] = turned_ref[...].T.astype(jnp.bfloat16)
+
+
+def stage_heads(mb, cap, own_ref, other_ref, k_ref, v_ref):
+    kv_width = KEY_HEADS * HEAD_WIDTH
+    for core_rel, source in ((0, own_ref), (1, other_ref)):
+        for s in range(4):
+            block = core_rel * 4 + s
+            rows = source[s, mb * cap : (mb + 1) * cap, :]
+            for n in range(KEY_HEADS):
+                lanes = n * HEAD_WIDTH
+                k_ref[n, block * cap : (block + 1) * cap, :] = rows[:, lanes : lanes + HEAD_WIDTH]
+                lanes += kv_width
+                v_ref[n, block * cap : (block + 1) * cap, :] = rows[:, lanes : lanes + HEAD_WIDTH]
+
+
+def stage_bias(ids_ref, counts_ref, mb, cap, share, bias_ref):
+    slot = ids_ref[3]
+    own_count = counts_ref[mb * 8 + slot]
+    key = lax.broadcasted_iota(jnp.int32, (cap, cap), 0)
+    query = lax.broadcasted_iota(jnp.int32, (cap, cap), 1)
+    query_used = query < own_count
+    for core_rel in range(2):
+        for s in range(4):
+            block = core_rel * 4 + s
+            f = column_index(ids_ref, core_rel, s)
+            count = counts_ref[mb * 8 + f]
+            reach = jnp.where(f < slot, cap, jnp.where(f == slot, 0, -2 * cap))
+            self_off = jnp.where(f == slot, 0, 2 * cap)
+            allowed = (query_used & (key < count) & (key <= query + reach)) | (
+                key == query + self_off
+            )
+            tile = jnp.where(allowed, 0.0, -1e30)
+            for g in range(share):
+                bias_ref[block * cap : (block + 1) * cap, g * cap : (g + 1) * cap] = tile
+
+
+def join_heads(ref, n, share, mb, cap):
+    return jnp.concatenate(
+        [ref[share * n + g, :, mb * cap : (mb + 1) * cap] for g in range(share)], 1
+    )
+
+
+def attend_kernel(
+    ids_ref, counts_ref, q_ref, own_ref, other_ref, att_ref, lse_ref, k_ref, v_ref, bias_ref
+):
+    cap = q_ref.shape[2] // 2
+    share = QUERY_HEADS // KEY_HEADS
+    for mb in range(2):
+        stage_heads(mb, cap, own_ref, other_ref, k_ref, v_ref)
+        stage_bias(ids_ref, counts_ref, mb, cap, share, bias_ref)
+
+        def body(n, carry, mb=mb):
+            scores = product_nn(k_ref[n], join_heads(q_ref, n, share, mb, cap)) + bias_ref[...]
+            top = jnp.max(scores, 0, keepdims=True)
+            exponent = jnp.exp(scores - top)
+            total = jnp.sum(exponent, 0, keepdims=True)
+            mixed = product_tn(v_ref[n], exponent.astype(jnp.bfloat16)) / total
+            mixed = mixed.astype(jnp.bfloat16)
+            for g in range(share):
+                att_ref[share * n + g, :, mb * cap : (mb + 1) * cap] = mixed[
+                    :, g * cap : (g + 1) * cap
+                ]
+            lse_ref[mb * KEY_HEADS + n] = top + jnp.log(total)
+            return carry
+
+        lax.fori_loop(0, KEY_HEADS, body, 0)
+
+
+def attend_back_kernel(
+    ids_ref,
+    counts_ref,
+    q_ref,
+    do_ref,
+    own_ref,
+    other_ref,
+    lse_ref,
+    cos_ref,
+    sin_ref,
+    dq_ref,
+    dkv_own_ref,
+    dkv_other_ref,
+    k_ref,
+    v_ref,
+    bias_ref,
+    dk_ref,
+    dv_ref,
+):
+    cap = q_ref.shape[2] // 2
+    share = QUERY_HEADS // KEY_HEADS
+    half = HEAD_WIDTH // 2
+    kv_width = KEY_HEADS * HEAD_WIDTH
+    for mb in range(2):
+        stage_heads(mb, cap, own_ref, other_ref, k_ref, v_ref)
+        stage_bias(ids_ref, counts_ref, mb, cap, share, bias_ref)
+        cosine = jnp.concatenate([cos_ref[:, mb * cap : (mb + 1) * cap]] * share, 1)
+        sine = jnp.concatenate([sin_ref[:, mb * cap : (mb + 1) * cap]] * share, 1)
+
+        def body(n, carry, mb=mb, cosine=cosine, sine=sine):
+            query = join_heads(q_ref, n, share, mb, cap)
+            grad = join_heads(do_ref, n, share, mb, cap)
+            keys = k_ref[n]
+            prob = jnp.exp(
+                product_nn(keys, query) + bias_ref[...] - lse_ref[mb * KEY_HEADS + n]
+            )
+            dprob = product_nn(v_ref[n], grad)
+            delta = jnp.sum(prob * dprob, 0, keepdims=True)
+            dscore = (prob * (dprob - delta)).astype(jnp.bfloat16)
+            dq = product_tn(keys, dscore) * SCORE_SCALE
+            front, back = dq[:half], dq[half:]
+            turned = jnp.concatenate(
+                [front * cosine + back * sine, back * cosine - front * sine], 0
+            ).astype(jnp.bfloat16)
+            for g in range(share):
+                dq_ref[share * n + g, :, mb * cap : (mb + 1) * cap] = turned[
+                    :, g * cap : (g + 1) * cap
+                ]
+            dk_ref[n] = product_nt(dscore, query).astype(jnp.bfloat16)
+            dv_ref[n] = product_nt(prob.astype(jnp.bfloat16), grad).astype(jnp.bfloat16)
+            return carry
+
+        lax.fori_loop(0, KEY_HEADS, body, 0)
+        for core_rel, target in ((0, dkv_own_ref), (1, dkv_other_ref)):
+            for s in range(4):
+                block = core_rel * 4 + s
+                for n in range(KEY_HEADS):
+                    lanes = n * HEAD_WIDTH
+                    target[s, mb * cap : (mb + 1) * cap, lanes : lanes + HEAD_WIDTH] = dk_ref[
+                        n, block * cap : (block + 1) * cap, :
+                    ]
+                    lanes += kv_width
+                    target[s, mb * cap : (mb + 1) * cap, lanes : lanes + HEAD_WIDTH] = dv_ref[
+                        n, block * cap : (block + 1) * cap, :
+                    ]
+
+
+def hidden_kernel(ids_ref, own_ref, other_ref, att_ref, x_ref, gain_ref, h_ref, n2_ref):
+    q_cols = h_ref.shape[0] // 8
+    for core_rel, w_ref in ((0, own_ref), (1, other_ref)):
+
+        def body(s, carry, core_rel=core_rel, w_ref=w_ref):
+            f = column_index(ids_ref, core_rel, s)
+            total = product_nn(w_ref[s], att_ref[ids_ref[0]])
+            for k in range(1, 4):
+                total += product_nn(w_ref[k * 4 + s], att_ref[ids_ref[0] ^ k])
+            h_ref[start_row(f, q_cols), :] = total[:q_cols]
+            return carry
+
+        lax.fori_loop(0, 4, body, 0)
+    h = h_ref[...] + x_ref[...].astype(jnp.float32)
+    h_ref[...] = h
+    n2_ref[...] = (h * mean_square(h) * gain_ref[...]).astype(jnp.bfloat16)
+
+
+def turn_point_kernel(
+    ids_ref,
+    parts_ref,
+    arrived_ref,
+    h_ref,
+    dy_ref,
+    gain_ref,
+    own_ref,
+    other_ref,
+    att_ref,
+    out_ref,
+    dh_ref,
+    grad_own_ref,
+    grad_other_ref,
+    do_ref,
+    gain_grad_ref,
+    da_ref,
+    mixed_ref,
+):
+    rows = h_ref.shape[1]
+    q_cols = h_ref.shape[0] // 8
+    h = h_ref[...]
+    out_ref[...] = (
+        h + parts_ref[0, :, :rows] + arrived_ref[0].astype(jnp.float32)
+    ).astype(jnp.bfloat16)
+    dn = parts_ref[1, :, :rows] + arrived_ref[1].astype(jnp.float32)
+    rms = mean_square(h)
+    gain_grad_ref[...] = jnp.sum(dn * h * rms, 1, keepdims=True)
+    weighted = dn * gain_ref[...]
+    dh = (
+        dy_ref[...].astype(jnp.float32)
+        + rms * weighted
+        - h * (rms * rms * rms * jnp.mean(weighted * h, 0, keepdims=True))
+    )
+    dh_ref[...] = dh
+    da_ref[...] = dh
+    mixed_ref[...] = jnp.zeros_like(mixed_ref)
+    for core_rel, w_ref, grad_ref in ((0, own_ref, grad_own_ref), (1, other_ref, grad_other_ref)):
+
+        def body(s, carry, core_rel=core_rel, w_ref=w_ref, grad_ref=grad_ref):
+            f = column_index(ids_ref, core_rel, s)
+            piece = jnp.concatenate(
+                [da_ref[start_row(f, q_cols), :], jnp.zeros((8, rows), jnp.float32)], 0
+            ).astype(jnp.bfloat16)
+            for k in range(4):
+                i = ids_ref[0] ^ k
+                mixed_ref[i] += product_tn(w_ref[k * 4 + s], piece)
+                grad_ref[k * 4 + s] = product_nt(piece, att_ref[i]).astype(jnp.bfloat16)
+            return carry
+
+        lax.fori_loop(0, 4, body, 0)
+    do_ref[...] = mixed_ref[...].astype(jnp.bfloat16)
+
+
+def finish_kernel(
+    ids_ref,
+    own_ref,
+    other_ref,
+    n1_ref,
+    dq_ref,
+    dkv_ref,
+    cos_ref,
+    sin_ref,
+    dh_ref,
+    x_ref,
+    gain_ref,
+    tokens_ref,
+    grad_own_ref,
+    grad_other_ref,
+    gain_grad_ref,
+    d_ref,
+    dn_ref,
+):
+    width, rows = dh_ref.shape
+    kv_width = KEY_HEADS * HEAD_WIDTH
+    q_cols, k_cols = width // 8, kv_width // 8
+    half = HEAD_WIDTH // 2
+    cosine, sine = cos_ref[...], sin_ref[...]
+    d_ref[:width, :] = dq_ref[...].astype(jnp.float32)
+    d_ref[width:, :] = dkv_ref[...].T
+    for head in range(KEY_HEADS):
+        base = width + head * HEAD_WIDTH
+        front = d_ref[base : base + half, :]
+        back = d_ref[base + half : base + 2 * half, :]
+        d_ref[base : base + half, :] = front * cosine + back * sine
+        d_ref[base + half : base + 2 * half, :] = back * cosine - front * sine
+    dn_ref[...] = jnp.zeros_like(dn_ref)
+    for core_rel, w_ref, grad_ref in ((0, own_ref, grad_own_ref), (1, other_ref, grad_other_ref)):
+
+        def body(s, carry, core_rel=core_rel, w_ref=w_ref, grad_ref=grad_ref):
+            f = column_index(ids_ref, core_rel, s)
+            piece = jnp.concatenate(
+                [
+                    d_ref[start_row(f, q_cols), :],
+                    d_ref[pl.ds(pl.multiple_of(width + f * k_cols, 8), k_cols), :],
+                    d_ref[pl.ds(pl.multiple_of(width + kv_width + f * k_cols, 8), k_cols), :],
+                    jnp.zeros((8, rows), jnp.float32),
+                ],
+                0,
+            ).astype(jnp.bfloat16)
+            for k in range(4):
+                i = ids_ref[0] ^ k
+                dn_ref[i] += product_tn(w_ref[k * 4 + s], piece)
+                grad_ref[k * 4 + s] = product_nt(piece, n1_ref[i]).astype(jnp.bfloat16)
+            return carry
+
+        lax.fori_loop(0, 4, body, 0)
+    x = x_ref[...].astype(jnp.float32)
+    rms = mean_square(x)
+    dn = dn_ref[...].reshape(width, rows)
+    gain_grad_ref[...] = jnp.sum(dn * x * rms, 1, keepdims=True)
+    weighted = dn * gain_ref[...]
+    tokens_ref[...] = (
+        dh_ref[...]
+        + rms * weighted
+        - x * (rms * rms * rms * jnp.mean(weighted * x, 0, keepdims=True))
+    )
+
+
+def mlp_kernel(*refs):
+    ids_ref, normed_ref, dy_ref = refs[:3]
+    pieces = refs[3:13]
+    parts_ref = refs[13]
+    grads = refs[14:24]
+    w_ref, grad_ref, gu_ref, prod_ref, dgu_ref, sem_in, sem_out = refs[24:]
+    dp_id = ids_ref[0]
+    z_id = ids_ref[1]
+    half = prod_ref.shape[1]
+    block = normed_ref.shape[1]
+
+    def views(ref, group):
+        low = 2 * group
+        return [
+            ref.at[pl.ds(low, 2)],
+            ref.at[pl.ds(4 + low, 2)],
+            ref.at[pl.ds(8 + low, 2)],
+            ref.at[12 + low],
+            ref.at[13 + low],
+        ]
+
+    loads = []
+    for group in range(2):
+        for j, target in enumerate(views(w_ref, group)):
+            index = group * 5 + j
+            loads.append(pltpu.make_async_copy(pieces[index], target, sem_in.at[index]))
+    for load in loads:
+        load.start()
+    for group in range(2):
+        for load in loads[group * 5 : group * 5 + 5]:
+            load.wait()
+
+        def forward(s, carry):
+            m = lax.rem(z_id - s + 4, 4)
+            total = product_nn(w_ref[s, : 2 * half, :], normed_ref[dp_id])
+            for k in range(1, 4):
+                total += product_nn(w_ref[k * 4 + s, : 2 * half, :], normed_ref[dp_id ^ k])
+            gu_ref[m] = total
+            gate = total[:half]
+            prod_ref[m] = (gate * jax.nn.sigmoid(gate) * total[half:]).astype(jnp.bfloat16)
+            return carry
+
+        lax.fori_loop(2 * group, 2 * group + 2, forward, 0)
+    parts_ref[...] = jnp.zeros_like(parts_ref)
+
+    def middle(k, carry):
+        m = dp_id ^ k
+        product = prod_ref[m]
+        dprod = jnp.zeros(product.shape, jnp.float32)
+        for s in range(4):
+            zz = lax.rem(z_id - s + 4, 4)
+            weight = w_ref[k * 4 + s, 2 * half : 3 * half, :]
+            dy = dy_ref[zz]
+            dprod += product_nn(weight, dy)
+            parts_ref[0, pl.ds(pl.multiple_of(zz * block, 16), block), :] += product_tn(
+                weight, product
+            )
+            grad_ref[k * 4 + s, 2 * half :, :] = product_nt(product, dy).astype(jnp.bfloat16)
+        gate = gu_ref[m, :half, :]
+        up = gu_ref[m, half:, :]
+        sig = jax.nn.sigmoid(gate)
+        dgu_ref[m, :half, :] = (dprod * up * sig * (1.0 + gate * (1.0 - sig))).astype(jnp.bfloat16)
+        dgu_ref[m, half:, :] = (dprod * gate * sig).astype(jnp.bfloat16)
+        return carry
+
+    lax.fori_loop(0, 4, middle, 0)
+
+    def backward(s, carry):
+        m = lax.rem(z_id - s + 4, 4)
+        dgu = dgu_ref[m]
+        for k in range(4):
+            i = dp_id ^ k
+            parts_ref[1, pl.ds(pl.multiple_of(i * block, 16), block), :] += product_tn(
+                w_ref[k * 4 + s, : 2 * half, :], dgu
+            )
+            grad_ref[k * 4 + s, : 2 * half, :] = product_nt(dgu, normed_ref[i]).astype(
+                jnp.bfloat16
+            )
+        return carry
+
+    stores = []
+    for group in range(2):
+        lax.fori_loop(2 * group, 2 * group + 2, backward, 0)
+        for j, source in enumerate(views(grad_ref, group)):
+            index = group * 5 + j
+            store = pltpu.make_async_copy(source, grads[index], sem_out.at[index])
+            store.start()
+            stores.append(store)
+    for store in stores:
+        store.wait()
+
+
+def mean_square(values):
+    return lax.rsqrt(jnp.mean(values * values, 0, keepdims=True) + EPSILON)
+
+
+def fast(
+    tokens, cotangent, counts, w_query, key_weight, value_weight, w_out, w_gate, w_up, w_down, gains
+):
+    dp_id = lax.axis_index("dp")
+    slot = lax.axis_index("fsdp")
+    z_id = slot // 2
+    core_id = slot % 2
+    ids = jnp.stack([dp_id, z_id, core_id, slot]).astype(jnp.int32)
+    batches, cap, width = tokens.shape
+    rows = batches * cap
+    block = w_query.shape[0]
+    q_cols, k_cols = w_query.shape[1], key_weight.shape[1]
+    half = w_gate.shape[1]
+    kv_width = KEY_HEADS * HEAD_WIDTH
+    share = QUERY_HEADS // KEY_HEADS
+    depth = 3 * half
+    o1, o2, o3 = q_cols, q_cols + k_cols, q_cols + 2 * k_cols
+
+    extra = jnp.zeros((8, block), jnp.bfloat16)
+    extra = extra.at[0].set(gains.reshape(-1))
+    extra = extra.at[1, :batches].set(counts[:, 0].astype(jnp.bfloat16))
+    first_piece = jnp.concatenate([w_query.T, key_weight.T, value_weight.T, extra], 0)
+    chain = [first_piece]
+    for _ in range(3):
+        chain.append(shift_z(chain[-1], 1))
+    along = jnp.stack(chain, 0)
+
+    down_halves = w_down.reshape(2, half, -1)
+    own_down = lax.dynamic_index_in_dim(down_halves, core_id, 0, keepdims=False)
+    other_down = swap_core(
+        lax.dynamic_index_in_dim(down_halves, 1 - core_id, 0, keepdims=False)
+    )
+    down = jnp.where(
+        core_id == 0,
+        jnp.concatenate([own_down, other_down], 1),
+        jnp.concatenate([other_down, own_down], 1),
+    )
+    out_rows = jnp.concatenate([w_out.T, jnp.zeros((8, block), jnp.bfloat16)], 0)
+    mlp_piece = jnp.concatenate([w_gate.T, w_up.T, down, out_rows], 0)
+    mlp_piece, along = lax.optimization_barrier((mlp_piece, along))
+
+    extras = along[:, o3 : o3 + 2, :]
+    other_extras = swap_core(extras)
+    from_x = swap_dp(along, 1)
+    from_y = swap_dp(along, 2)
+    first_own = jnp.concatenate(
+        [along, from_x, from_y, swap_dp(from_x[:2], 2), swap_dp(from_y[2:], 1)], 0
+    )
+    first_other = swap_core(first_own)
+
+    mlp_chain = [mlp_piece]
+    for _ in range(3):
+        mlp_chain.append(shift_z(mlp_chain[-1], 1))
+    pieces, out_pieces = [], [[], [], [], []]
+    for group in range(2):
+        own = jnp.stack(mlp_chain[2 * group : 2 * group + 2], 0)
+        if group == 0:
+            own, first_other = lax.optimization_barrier((own, first_other))
+        by_x = swap_dp(own, 1)
+        by_y = swap_dp(own, 2)
+        far_a = swap_dp(by_x[0], 2)
+        far_b = swap_dp(by_y[1], 1)
+        pieces += [own, by_x, by_y, far_a, far_b]
+        for k, part in enumerate((own, by_x, by_y, jnp.stack([far_a, far_b], 0))):
+            out_pieces[k].append(part[:, depth:])
+    out_own = jnp.concatenate([part for pair in out_pieces for part in pair], 0)
+    out_other = swap_core(out_own)
+
+    by_core = jnp.where(
+        core_id == 0, jnp.stack([extras, other_extras], 1), jnp.stack([other_extras, extras], 1)
+    )
+    by_core = by_core[::-1]
+    by_core = lax.dynamic_slice_in_dim(jnp.concatenate([by_core, by_core], 0), 3 - z_id, 4, 0)
+    gain = by_core[:, :, 0, :].reshape(8, 2, q_cols).transpose(0, 2, 1).reshape(width, 2)
+    gain = gain.astype(jnp.float32)
+    gain_one, gain_two = gain[:, :1], gain[:, 1:]
+    group_counts = by_core[:, :, 1, :batches].reshape(8, batches).astype(jnp.int32)
+    flat_counts = group_counts.T.reshape(-1)
+    before = jnp.sum(
+        jnp.where(jnp.arange(8, dtype=jnp.int32)[:, None] < slot, group_counts, 0), 0
+    )
+    position = (before[:, None] + jnp.arange(cap, dtype=jnp.int32)[None, :]).reshape(-1)
+    cosine, sine = rope_tables(position, HEAD_WIDTH)
+    cosine, sine = cosine[:, 0, :].T, sine[:, 0, :].T
+
+    dy = cotangent.reshape(rows, width).T
+    dy_pair = jnp.concatenate([dy, swap_core(dy)], 1).reshape(4, block, 2 * rows)
+    x = tokens.reshape(rows, width).T
+    x_wide = x.astype(jnp.float32)
+    n1 = (x_wide * mean_square(x_wide) * gain_one).astype(jnp.bfloat16).reshape(4, block, rows)
+
+    query, kv = run(
+        project_kernel,
+        "project",
+        (ids, first_own, first_other, n1, cosine, sine),
+        [SMEM] + [VMEM] * 5,
+        (struct((QUERY_HEADS, HEAD_WIDTH, rows)), struct((rows, 2 * kv_width))),
+        [VMEM] * 2,
+        [
+            pltpu.VMEM((width + 2 * kv_width, rows), jnp.float32),
+            pltpu.VMEM((2 * kv_width, rows), jnp.float32),
+        ],
+        2 * (width + 2 * kv_width) * width * rows,
+        32,
+    )
+    kv_chain = [kv]
+    for _ in range(3):
+        kv_chain.append(shift_z_up(kv_chain[-1], 1))
+    kv_own = jnp.stack(kv_chain, 0)
+    kv_other = swap_core(kv_own)
+    pair_flops = 2 * QUERY_HEADS * HEAD_WIDTH * rows * 8 * cap
+    head_scratch = [
+        pltpu.VMEM((KEY_HEADS, 8 * cap, HEAD_WIDTH), jnp.bfloat16),
+        pltpu.VMEM((KEY_HEADS, 8 * cap, HEAD_WIDTH), jnp.bfloat16),
+        pltpu.VMEM((8 * cap, share * cap), jnp.float32),
+    ]
+    attended, lse = run(
+        attend_kernel,
+        "attend",
+        (ids, flat_counts, query, kv_own, kv_other),
+        [SMEM, SMEM] + [VMEM] * 3,
+        (
+            struct((QUERY_HEADS, HEAD_WIDTH, rows)),
+            struct((2 * KEY_HEADS, 1, share * cap), jnp.float32),
+        ),
+        [VMEM] * 2,
+        head_scratch,
+        8 * pair_flops,
+        40,
+    )
+    attended = attended.reshape(4, block, rows)
+    h, n2 = run(
+        hidden_kernel,
+        "hidden",
+        (ids, out_own, out_other, attended, x, gain_two),
+        [SMEM] + [VMEM] * 5,
+        (struct((width, rows), jnp.float32), struct((width, rows))),
+        [VMEM] * 2,
+        [],
+        2 * width * width * rows,
+        32,
+    )
+    n2_pair = jnp.concatenate([n2, swap_core(n2)], 1).reshape(4, block, 2 * rows)
+    one, two = struct((depth, block)), struct((2, depth, block))
+    results = run(
+        mlp_kernel,
+        "mlp",
+        (ids, n2_pair, dy_pair, *pieces),
+        [SMEM, VMEM, VMEM] + [ANY] * 10,
+        [struct((2, width, 2 * rows), jnp.float32)] + [two, two, two, one, one] * 2,
+        [VMEM] + [ANY] * 10,
+        [
+            pltpu.VMEM((16, mlp_piece.shape[0], block), jnp.bfloat16),
+            pltpu.VMEM((16, depth, block), jnp.bfloat16),
+            pltpu.VMEM((4, 2 * half, 2 * rows), jnp.float32),
+            pltpu.VMEM((4, half, 2 * rows), jnp.bfloat16),
+            pltpu.VMEM((4, 2 * half, 2 * rows), jnp.bfloat16),
+            pltpu.SemaphoreType.DMA((10,)),
+            pltpu.SemaphoreType.DMA((10,)),
+        ],
+        18 * 16 * half * block * 2 * rows,
+        56,
+    )
+    parts, mlp_grads = results[0], results[1:]
+    arrived = swap_core(parts[:, :, rows:].astype(jnp.bfloat16))
+    output, dh, out_grad_own, out_grad_other, mixed_gradient, gain_two_grad = run(
+        turn_point_kernel,
+        "turn_point",
+        (ids, parts, arrived, h, dy, gain_two, out_own, out_other, attended),
+        [SMEM] + [VMEM] * 8,
+        (
+            struct((width, rows)),
+            struct((width, rows), jnp.float32),
+            struct(out_own.shape),
+            struct(out_own.shape),
+            struct((4, block, rows)),
+            struct((width, 1), jnp.float32),
+        ),
+        [VMEM] * 6,
+        [
+            pltpu.VMEM((width, rows), jnp.float32),
+            pltpu.VMEM((4, block, rows), jnp.float32),
+        ],
+        4 * width * width * rows,
+        40,
+    )
+    output = output.T.reshape(batches, cap, width)
+
+    mlp_total = None
+    for group in range(2):
+        home, to_x, to_y, far_a, far_b = mlp_grads[group * 5 : group * 5 + 5]
+        via_y = swap_dp(far_a, 2)
+        via_x = swap_dp(far_b, 1)
+        to_x = jnp.stack([add_low(to_x[0], via_y), to_x[1]], 0)
+        to_y = jnp.stack([to_y[0], add_low(to_y[1], via_x)], 0)
+        summed = add_low(home, swap_dp(to_x, 1), swap_dp(to_y, 2))
+        for j in range(2):
+            s = 2 * group + j
+            part = summed[j] if s == 0 else shift_z(summed[j], -s)
+            part = part.astype(jnp.float32)
+            mlp_total = part if mlp_total is None else mlp_total + part
+    grad_gate = mlp_total[:half].T
+    grad_up = mlp_total[half : 2 * half].T
+    down_total = mlp_total[2 * half :]
+    left, right = down_total[:, :q_cols], down_total[:, q_cols:]
+    keep = jnp.where(core_id == 0, left, right)
+    give = jnp.where(core_id == 0, right, left).astype(jnp.bfloat16)
+    taken = swap_core(give).astype(jnp.float32)
+    grad_down = jnp.where(
+        core_id == 0, jnp.concatenate([keep, taken], 0), jnp.concatenate([taken, keep], 0)
+    )
+
+    def reduce_all(own, other):
+        mine = add_low(own, swap_core(other))
+        home, to_x, to_y, far = mine[:4], mine[4:8], mine[8:12], mine[12:]
+        via_y = swap_dp(far[:2], 2)
+        via_x = swap_dp(far[2:], 1)
+        to_x = jnp.concatenate([add_low(to_x[:2], via_y), to_x[2:]], 0)
+        to_y = jnp.concatenate([to_y[:2], add_low(to_y[2:], via_x)], 0)
+        summed = add_low(home, swap_dp(to_x, 1), swap_dp(to_y, 2))
+        total = summed[0].astype(jnp.float32)
+        for s in (1, 2, 3):
+            total = total + shift_z(summed[s], -s).astype(jnp.float32)
+        return total
+
+    grad_out = reduce_all(out_grad_own, out_grad_other)[:q_cols].T
+
+    dq, dkv_own, dkv_other = run(
+        attend_back_kernel,
+        "attend_back",
+        (
+            ids,
+            flat_counts,
+            query,
+            mixed_gradient.reshape(QUERY_HEADS, HEAD_WIDTH, rows),
+            kv_own,
+            kv_other,
+            lse,
+            cosine,
+            sine,
+        ),
+        [SMEM, SMEM] + [VMEM] * 7,
+        (
+            struct((QUERY_HEADS, HEAD_WIDTH, rows)),
+            struct((4, rows, 2 * kv_width)),
+            struct((4, rows, 2 * kv_width)),
+        ),
+        [VMEM] * 3,
+        head_scratch
+        + [
+            pltpu.VMEM((KEY_HEADS, 8 * cap, HEAD_WIDTH), jnp.bfloat16),
+            pltpu.VMEM((KEY_HEADS, 8 * cap, HEAD_WIDTH), jnp.bfloat16),
+        ],
+        20 * pair_flops,
+        48,
+    )
+    dkv = add_low(dkv_own, swap_core(dkv_other))
+    dkv_total = dkv[0].astype(jnp.float32)
+    for s in (1, 2, 3):
+        dkv_total = dkv_total + shift_z_down(dkv[s], s).astype(jnp.float32)
+
+    grad_tokens, first_grad_own, first_grad_other, gain_one_grad = run(
+        finish_kernel,
+        "finish",
+        (
+            ids,
+            first_own,
+            first_other,
+            n1,
+            dq.reshape(width, rows),
+            dkv_total,
+            cosine,
+            sine,
+            dh,
+            x,
+            gain_one,
+        ),
+        [SMEM] + [VMEM] * 10,
+        (
+            struct((width, rows), jnp.float32),
+            struct(first_own.shape),
+            struct(first_own.shape),
+            struct((width, 1), jnp.float32),
+        ),
+        [VMEM] * 4,
+        [
+            pltpu.VMEM((width + 2 * kv_width, rows), jnp.float32),
+            pltpu.VMEM((4, block, rows), jnp.float32),
+        ],
+        4 * (width + 2 * kv_width) * width * rows,
+        48,
+    )
+    grad_tokens = grad_tokens.T.reshape(batches, cap, width)
+    first_total = reduce_all(first_grad_own, first_grad_other)
+    gain_total = jnp.concatenate([gain_one_grad, gain_two_grad], 1).T
+    gain_total = gain_total + swap_core(gain_total)
+    gain_total = gain_total + swap_dp(gain_total, 1)
+    gain_total = gain_total + swap_dp(gain_total, 2)
+    for mask in (2, 4):
+        gain_total = gain_total + lax.ppermute(
+            gain_total, "fsdp", [(j, j ^ mask) for j in range(8)]
+        )
+    gain_grad = lax.dynamic_slice_in_dim(gain_total, slot * q_cols, q_cols, 1)
+    return (
+        output,
+        grad_tokens,
+        first_total[:o1].T,
+        first_total[o1:o2].T,
+        first_total[o2:o3].T,
+        grad_out,
+        grad_gate,
+        grad_up,
+        grad_down,
+        gain_grad,
+    )
+
+
 def solution(mesh):
     in_specs = (
         P(None, ("dp", "fsdp"), None),
@@ -375,4 +1187,6 @@
         P("dp", "fsdp"),
         P(None, "fsdp"),
     )
-    return jax.shard_map(local, mesh=mesh, in_specs=in_specs, out_specs=out_specs, check_vma=False)
+    square = mesh.shape["dp"] == 4 and mesh.shape["fsdp"] == 8
+    return jax.shard_map(
+        fast if square else local, mesh=mesh, in_specs=in_specs, out_specs=out_specs, check_vma=False)

time: 1000 us -> 484 us (0.48)
  blocking collectives: 237 us -> 0 us
  waiting for transfers between devices: 372 us -> 152 us
  matrix products: 176 us -> 0 us
  Pallas kernels: 0 us -> 108 us
  local copies, waits for them, and re-layouts: 73.1 us -> 104 us
  other arithmetic: 65.3 us -> 43.6 us
  between operations: 17.6 us -> 2.28 us
  starting transfers between devices: 53 us -> 65.1 us
    dot_general x47 -> x0, matrix products: 176 us -> none  [the longest x14 35.5 us: times_transpose(): jnp.einsum('rk,jk->rj', left, right, preferred_element_type=jnp.float32)]
    all_gather x12 -> x0, blocking collectives: 174 us -> none  [the longest x2 34.2 us: local(): lax.all_gather(key_low, 'fsdp', axis=0, tiled=True)]
    ppermute x0 -> x66, waiting for transfers between devices: none -> 152 us  [the longest x15 72 us: shift_z(): lax.ppermute(value, 'fsdp', [(j, (j + 2 * step) % 8) for j in range(8)])]
    all_gather x12 -> x0, waiting for transfers between devices: 149 us -> none  [the longest x1 78.2 us: local(): lax.all_gather(joined[9], 'fsdp', axis=0, tiled=True)]
    all_to_all x7 -> x0, waiting for transfers between devices: 129 us -> none  [the longest x1 58.3 us: local(): lax.all_to_all(joined[7], 'fsdp', split_axis=1, concat_axis=0, tiled=True)]
    pallas_call x0 -> x7, Pallas kernels: none -> 108 us  [run(): pl.pallas_call(body, out_shape=tuple(outs), in_specs=in_specs, out_specs=...]
    unnamed x28 -> x0, waiting for transfers between devices: 94.3 us -> none
    ppermute x0 -> x66, starting transfers between devices: none -> 65.1 us  [the longest x30 35.1 us: swap_dp(): return lax.ppermute(value, 'dp', [(j, j ^ mask) for j in range(4)])]
  transfers between devices with their start and end apart: 27 -> 66, of which waited for: 14 -> 29; matrix products, arithmetic and copies ran while one was open for 30% -> 26% of each run, Pallas kernels for 0% -> 14%
where the time goes in v1:
time: 484 us; the launch traced here: 475 us
  waiting for transfers between devices  152 us (31%)
  Pallas kernels  108 us (22%)
  local copies, waits for them, and re-layouts  104 us (21%)
  starting transfers between devices  65.1 us (13%)
  other arithmetic  43.6 us (9%)
    pallas_call x7, Pallas kernels, run(): pl.pallas_call(body, out_shape=tuple(outs), in_specs=in_specs, out_specs=...  108 us
    ppermute x15, waiting for transfers between devices, shift_z(): lax.ppermute(value, 'fsdp', [(j, (j + 2 * step) % 8) for j in range(8)])  72 us
    ppermute x3, waiting for transfers between devices, shift_z_down(): lax.ppermute(value, 'fsdp', [(j, j - 2 * step) for j in range(8) if j - 2...  38 us
    ppermute x30, waiting for transfers between devices, swap_dp(): return lax.ppermute(value, 'dp', [(j, j ^ mask) for j in range(4)])  37.3 us
    ppermute x30, starting transfers between devices, swap_dp(): return lax.ppermute(value, 'dp', [(j, j ^ mask) for j in range(4)])  35.1 us
    unnamed x128, local copies, waits for them, and re-layouts  25.9 us
    ppermute x8, local copies, waits for them, and re-layouts, swap_dp(): return lax.ppermute(value, 'dp', [(j, j ^ mask) for j in range(4)])  16.7 us
    ppermute x15, starting transfers between devices, shift_z(): lax.ppermute(value, 'fsdp', [(j, (j + 2 * step) % 8) for j in range(8)])  14.2 us
  transfers between devices with their start and end apart: 66, of which 29 were waited for; matrix products, arithmetic and copies ran while one was open for 26% of the time, Pallas kernels for 14%

profile of v1, /device:TPU:0, one launch (start us, length us, event | category | flops | bytes accessed | tf_op | source)
XLA Modules:
  0.0 474.8 jit_solution(17343808886008497435)
XLA Ops:
  12.7 5.9 %collective-permute-done.2 = bf16[208,240]{1,0:T(8,128)(2,1)S(1)} collective-permute-done((bf16[208,240]{1,0:T(8,128)(2,1)S(1)}, bf16[208,240]{1,0:T(8,128)(2,1)S(1)}, u32[]{:S(2)}, u32[]{:S(2)}) %collective-permute-start.2) | collective-permute-done | bytes 99872 | tf_op jit(solution)/shard_map/ppermute | solution.py:363
  18.6 6.5 %collective-permute-done.3 = bf16[208,240]{1,0:T(8,128)(2,1)S(1)} collective-permute-done((bf16[208,240]{1,0:T(8,128)(2,1)S(1)}, bf16[208,240]{1,0:T(8,128)(2,1)S(1)}, u32[]{:S(2)}, u32[]{:S(2)}) %collective-permute-start.3) | collective-permute-done | bytes 99872 | tf_op jit(solution)/shard_map/ppermute | solution.py:363
  30.6 9.4 %collective-permute-done.4 = bf16[1088,240]{0,1:T(8,128)(2,1)} collective-permute-done((bf16[1088,240]{0,1:T(8,128)(2,1)}, bf16[1088,240]{0,1:T(8,128)(2,1)}, u32[]{:S(2)}, u32[]{:S(2)}) %collective-permute-start.4) | collective-permute-done | bytes 522272 | tf_op jit(solution)/shard_map/ppermute | solution.py:363
  48.6 4.2 collective-permute-done.10
  54.8 10.0 %collective-permute-done.11 = bf16[1088,240]{0,1:T(8,128)(2,1)} collective-permute-done((bf16[1088,240]{0,1:T(8,128)(2,1)}, bf16[1088,240]{0,1:T(8,128)(2,1)}, u32[]{:S(2)}, u32[]{:S(2)}) %collective-permute-start.11) | collective-permute-done | bytes 522272 | tf_op jit(solution)/shard_map/ppermute | solution.py:363
  84.1 5.1 %project.1 = (bf16[15,64,320]{2,1,0:T(8,128)(2,1)S(1)}, bf16[320,640]{1,0:T(8,128)(2,1)S(1)}) custom-call(s32[4]{0:T(128)S(1)} %pad_add_fusion.ids_ref.refs_0_, bf16[16,208,240]{2,1,0:T(8,128)(2,1)S(1)} %constant_dynamic-update-slice_fusion.1.own_ref, bf16[16,208,240]{2,1,0:T(8,128)(2,1)} %collective-permute-done.9.other_ref, ...), custom_call_target="tpu_custom_call" | custom-call | flops 983040000 | bytes 4915216 | tf_op jit(solution)/shard_map/project/pallas_call | solution.py:407
  90.7 8.4 %collective-permute-done.15 = bf16[2,1088,240]{1,2,0:T(8,128)(2,1)} collective-permute-done((bf16[2,1088,240]{1,2,0:T(8,128)(2,1)}, bf16[2,1088,240]{1,2,0:T(8,128)(2,1)}, u32[]{:S(2)}, u32[]{:S(2)}) %collective-permute-start.15) | collective-permute-done | bytes 1044512 | tf_op jit(solution)/shard_map/ppermute | solution.py:359
  114.3 5.3 %collective-permute-start.24 = (bf16[320,640]{1,0:T(8,128)(2,1)}, bf16[320,640]{1,0:T(8,128)(2,1)}, u32[]{:S(2)}, u32[]{:S(2)}) collective-permute-start(bf16[320,640]{1,0:T(8,128)(2,1)} %collective-permute-done.23), channel_id=1, source_target_pairs={{0,2},{1,3},{2,4},{3,5},{4,6},{5,7},{8,10},{9,11},{10,12},{11,13},... | collective-permute-start | bytes 1228808 | tf_op jit(solution)/shard_map/ppermute | solution.py:367
  119.5 11.3 %collective-permute-done.19 = bf16[1088,240]{0,1:T(8,128)(2,1)} collective-permute-done((bf16[1088,240]{0,1:T(8,128)(2,1)}, bf16[1088,240]{0,1:T(8,128)(2,1)}, u32[]{:S(2)}, u32[]{:S(2)}) %collective-permute-start.19) | collective-permute-done | bytes 522272 | tf_op jit(solution)/shard_map/ppermute | solution.py:359
  163.0 18.3 %attend.1 = (bf16[15,64,320]{2,1,0:T(8,128)(2,1)S(1)}, f32[10,1,480]{2,1,0:T(1,128)S(1)}) custom-call(s32[4]{0:T(128)S(1)} %pad_add_fusion.ids_ref.refs_0_, s32[16]{0:T(128)S(1)} %reshape.205.counts_ref, bf16[15,64,320]{2,1,0:T(8,128)(2,1)S(1)} %copy-done.26, bf16[4,320,640]{2,1,0:T(8,128)(2,1)} %pad_maximum_fusion.own_ref, ...), custom_call_target="tpu_custom_call" | custom-call | flops 6291456000 | bytes 4524880 | tf_op jit(solution)/shard_map/attend/pallas_call | solution.py:407
  181.3 3.4 hidden.1
  201.7 31.7 %mlp.1 = (f32[2,960,640]{2,1,0:T(8,128)}, bf16[2,960,240]{2,1,0:T(8,128)(2,1)}, bf16[2,960,240]{2,1,0:T(8,128)(2,1)}, bf16[2,960,240]{2,1,0:T(8,128)(2,1)}, bf16...) custom-call(s32[4]{0:T(128)} %copy-done.23, ...), custom_call_target="tpu_custom_call" | custom-call | flops 14155776000 | bytes 23101456 | tf_op jit(solution)/shard_map/mlp/pallas_call | solution.py:407
  242.9 3.5 slice.448
  272.2 9.7 %turn_point.1 = (bf16[960,320]{1,0:T(8,128)(2,1)S(1)}, f32[960,320]{1,0:T(8,128)S(1)}, bf16[16,128,240]{2,1,0:T(8,128)(2,1)S(1)}, bf16[16,128,240]{2,1,0:T(8,128...) custom-call(s32[4]{0:T(128)S(1)} %copy-done.24, f32[2,960,640]{2,1,0:T(8,128)} %get-tuple-element.76.parts_ref, ...), custom_call_target="tpu_custom_call" | custom-call | flops 1179648000 | bytes 14999056 | tf_op jit(solution)/shard_map/turn_point/pallas_call | solution.py:407
  286.6 29.4 %attend_back.1 = (bf16[15,64,320]{2,1,0:T(8,128)(2,1)S(1)}, bf16[4,320,640]{2,1,0:T(8,128)(2,1)S(1)}, bf16[4,320,640]{2,1,0:T(8,128)(2,1)}) custom-call(s32[4]{0:T(128)S(1)} %copy-done.24, s32[16]{0:T(128)S(1)} %reshape.205.counts_ref, bf16[15,64,320]{2,1,0:T(8,128)(2,1)S(1)} %copy-done.27, bf16[15,64,320]{2,1,0:T(8,128)(2,1)S(1)} %bitcast.165, ...), custom_call_target="tpu_custom_call" | custom-call | flops 15728640000 | bytes 8498000 | tf_op jit(solution)/shard_map/attend_back/pallas_call | solution.py:407
  323.5 3.3 collective-permute-start.53
  332.1 21.0 %collective-permute-done.58 = bf16[960,240]{1,0:T(8,128)(2,1)} collective-permute-done((bf16[960,240]{1,0:T(8,128)(2,1)}, bf16[960,240]{1,0:T(8,128)(2,1)}, u32[]{:S(2)}, u32[]{:S(2)}) %collective-permute-start.58) | collective-permute-done | bytes 460832 | tf_op jit(solution)/shard_map/ppermute | solution.py:363
  353.1 5.7 %collective-permute-done.53 = bf16[960,240]{1,0:T(8,128)(2,1)} collective-permute-done((bf16[960,240]{1,0:T(8,128)(2,1)}, bf16[960,240]{1,0:T(8,128)(2,1)}, u32[]{:S(2)}, u32[]{:S(2)}) %collective-permute-start.53) | collective-permute-done | bytes 460832 | tf_op jit(solution)/shard_map/ppermute | solution.py:363
  370.6 11.1 %collective-permute-done.30 = bf16[320,640]{1,0:T(8,128)(2,1)} collective-permute-done((bf16[320,640]{1,0:T(8,128)(2,1)}, bf16[320,640]{1,0:T(8,128)(2,1)}, u32[]{:S(2)}, u32[]{:S(2)}) %collective-permute-start.30) | collective-permute-done | bytes 409632 | tf_op jit(solution)/shard_map/ppermute | solution.py:371
  381.7 10.8 %collective-permute-done.32 = bf16[320,640]{1,0:T(8,128)(2,1)} collective-permute-done((bf16[320,640]{1,0:T(8,128)(2,1)}, bf16[320,640]{1,0:T(8,128)(2,1)}, u32[]{:S(2)}, u32[]{:S(2)}) %collective-permute-start.32) | collective-permute-done | bytes 409632 | tf_op jit(solution)/shard_map/ppermute | solution.py:371
  392.5 16.1 %collective-permute-done.31 = bf16[320,640]{1,0:T(8,128)(2,1)} collective-permute-done((bf16[320,640]{1,0:T(8,128)(2,1)}, bf16[320,640]{1,0:T(8,128)(2,1)}, u32[]{:S(2)}, u32[]{:S(2)}) %collective-permute-start.31) | collective-permute-done | bytes 409632 | tf_op jit(solution)/shard_map/ppermute | solution.py:371
  410.2 10.5 %finish.1 = (f32[960,320]{1,0:T(8,128)S(1)}, bf16[16,208,240]{2,1,0:T(8,128)(2,1)}, bf16[16,208,240]{2,1,0:T(8,128)(2,1)}, f32[960,1]{1,0:T(8,128)S(1)}) custom-call(s32[4]{0:T(128)S(1)} %copy-done.24, bf16[16,208,240]{2,1,0:T(8,128)(2,1)} %copy-done, bf16[16,208,240]{2,1,0:T(8,128)(2,1)} %collective-permute-done.9.other_ref, ...), custom_call_target="tpu_custom_call" | custom-call | flops 1966080000 | bytes 11599376 | tf_op jit(solution)/shard_map/finish/pallas_call | solution.py:407
  422.8 3.9 collective-permute-done.42
  431.4 3.4 collective-permute-done.45
  (369 shorter events, 224.7 us)
Async XLA Ops:
  52.9 27.9 %collective-permute-start.9 = (bf16[16,208,240]{2,1,0:T(8,128)(2,1)S(1)}, bf16[16,208,240]{2,1,0:T(8,128)(2,1)}, u32[]{:S(2)}, u32[]{:S(2)}) collective-permute-start(bf16[16,208,240]{2,1,0:T(8,128)(2,1)S(1)} %constant_dynamic-update-slice_fusion.1.own_ref), channel_id=1, source_target_pairs={{0,1},{1,0},{2,3},{3,2},{4,5},{5,4},{6,7},{7,6},{8,9},{9,8},{10,11... | collective-permute-start | bytes 4792328 | tf_op jit(solution)/shard_map/ppermute | solution.py:355
  71.5 27.6 %collective-permute-start.15 = (bf16[2,1088,240]{1,2,0:T(8,128)(2,1)}, bf16[2,1088,240]{1,2,0:T(8,128)(2,1)}, u32[]{:S(2)}, u32[]{:S(2)}) collective-permute-start(bf16[2,1088,240]{1,2,0:T(8,128)(2,1)} %copy.107), channel_id=1, source_target_pairs={{0,16},{8,24},{16,0},{24,8},{1,17},{9,25},{17,1},{25,9},{2,18},{10... | collective-permute-start | bytes 3133448 | tf_op jit(solution)/shard_map/ppermute | solution.py:359
  74.4 28.1 %collective-permute-start.13 = (bf16[2,1088,240]{1,2,0:T(8,128)(2,1)}, bf16[2,1088,240]{1,2,0:T(8,128)(2,1)}, u32[]{:S(2)}, u32[]{:S(2)}) collective-permute-start(bf16[2,1088,240]{1,2,0:T(8,128)(2,1)} %copy.107), channel_id=1, source_target_pairs={{0,8},{8,0},{16,24},{24,16},{1,9},{9,1},{17,25},{25,17},{2,10},{10... | collective-permute-start | bytes 3133448 | tf_op jit(solution)/shard_map/ppermute | solution.py:359
  83.1 50.5 %collective-permute-start.14 = (bf16[2,1088,240]{1,2,0:T(8,128)(2,1)}, bf16[2,1088,240]{1,2,0:T(8,128)(2,1)}, u32[]{:S(2)}, u32[]{:S(2)}) collective-permute-start(bf16[2,1088,240]{1,2,0:T(8,128)(2,1)} %copy.105), channel_id=1, source_target_pairs={{0,16},{8,24},{16,0},{24,8},{1,17},{9,25},{17,1},{25,9},{2,18},{10... | collective-permute-start | bytes 3133448 | tf_op jit(solution)/shard_map/ppermute | solution.py:359
  83.6 53.6 %collective-permute-start.12 = (bf16[2,1088,240]{1,2,0:T(8,128)(2,1)}, bf16[2,1088,240]{1,2,0:T(8,128)(2,1)}, u32[]{:S(2)}, u32[]{:S(2)}) collective-permute-start(bf16[2,1088,240]{1,2,0:T(8,128)(2,1)} %copy.105), channel_id=1, source_target_pairs={{0,8},{8,0},{16,24},{24,16},{1,9},{9,1},{17,25},{25,17},{2,10},{10... | collective-permute-start | bytes 3133448 | tf_op jit(solution)/shard_map/ppermute | solution.py:359
  101.0 29.8 %collective-permute-start.19 = (bf16[1088,240]{0,1:T(8,128)(2,1)}, bf16[1088,240]{0,1:T(8,128)(2,1)}, u32[]{:S(2)}, u32[]{:S(2)}) collective-permute-start(bf16[1088,240]{0,1:T(8,128)(2,1)} %slice_bitcast_fusion), channel_id=1, source_target_pairs={{0,8},{8,0},{16,24},{24,16},{1,9},{9,1},{17,25},{25,17},{2,10},{10... | collective-permute-start | bytes 1566728 | tf_op jit(solution)/shard_map/ppermute | solution.py:359
  104.4 27.7 %collective-permute-start.18 = (bf16[1088,240]{0,1:T(8,128)(2,1)}, bf16[1088,240]{0,1:T(8,128)(2,1)}, u32[]{:S(2)}, u32[]{:S(2)}) collective-permute-start(bf16[1088,240]{0,1:T(8,128)(2,1)} %slice_bitcast_fusion.1), channel_id=1, source_target_pairs={{0,16},{8,24},{16,0},{24,8},{1,17},{9,25},{17,1},{25,9},{2,18},{10... | collective-permute-start | bytes 1566728 | tf_op jit(solution)/shard_map/ppermute | solution.py:359
  114.3 32.3 %collective-permute-start.24 = (bf16[320,640]{1,0:T(8,128)(2,1)}, bf16[320,640]{1,0:T(8,128)(2,1)}, u32[]{:S(2)}, u32[]{:S(2)}) collective-permute-start(bf16[320,640]{1,0:T(8,128)(2,1)} %collective-permute-done.23), channel_id=1, source_target_pairs={{0,2},{1,3},{2,4},{3,5},{4,6},{5,7},{8,10},{9,11},{10,12},{11,13},... | collective-permute-start | bytes 1228808 | tf_op jit(solution)/shard_map/ppermute | solution.py:367
  157.4 34.2 %collective-permute-start.27 = (bf16[960,320]{0,1:T(8,128)(2,1)}, bf16[960,320]{0,1:T(8,128)(2,1)}, u32[]{:S(2)}, u32[]{:S(2)}) collective-permute-start(bf16[960,320]{0,1:T(8,128)(2,1)} %bitcast.46), channel_id=1, source_target_pairs={{0,1},{1,0},{2,3},{3,2},{4,5},{5,4},{6,7},{7,6},{8,9},{9,8},{10,11... | collective-permute-start | bytes 1843208 | tf_op jit(solution)/shard_map/ppermute | solution.py:355
  234.1 19.0 %collective-permute-start.54 = (bf16[960,240]{1,0:T(8,128)(2,1)}, bf16[960,240]{1,0:T(8,128)(2,1)}, u32[]{:S(2)}, u32[]{:S(2)}) collective-permute-start(bf16[960,240]{1,0:T(8,128)(2,1)} %get-tuple-element.97), channel_id=1, source_target_pairs={{0,16},{8,24},{16,0},{24,8},{1,17},{9,25},{17,1},{25,9},{2,18},{10... | collective-permute-start | bytes 1382408 | tf_op jit(solution)/shard_map/ppermute | solution.py:359
  240.9 20.7 %collective-permute-start.49 = (bf16[960,240]{1,0:T(8,128)(2,1)}, bf16[960,240]{1,0:T(8,128)(2,1)}, u32[]{:S(2)}, u32[]{:S(2)}) collective-permute-start(bf16[960,240]{1,0:T(8,128)(2,1)} %get-tuple-element.92), channel_id=1, source_target_pairs={{0,16},{8,24},{16,0},{24,8},{1,17},{9,25},{17,1},{25,9},{2,18},{10... | collective-permute-start | bytes 1382408 | tf_op jit(solution)/shard_map/ppermute | solution.py:359
  251.5 64.5 %collective-permute-start.57 = (bf16[2,960,240]{2,1,0:T(8,128)(2,1)}, bf16[2,960,240]{2,1,0:T(8,128)(2,1)}, u32[]{:S(2)}, u32[]{:S(2)}) collective-permute-start(bf16[2,960,240]{2,1,0:T(8,128)(2,1)} %pad_maximum_fusion.8), channel_id=1, source_target_pairs={{0,16},{8,24},{16,0},{24,8},{1,17},{9,25},{17,1},{25,9},{2,18},{10... | collective-permute-start | bytes 2764808 | tf_op jit(solution)/shard_map/ppermute | solution.py:359
  255.4 60.6 %collective-permute-start.55 = (bf16[2,960,240]{2,1,0:T(8,128)(2,1)}, bf16[2,960,240]{2,1,0:T(8,128)(2,1)}, u32[]{:S(2)}, u32[]{:S(2)}) collective-permute-start(bf16[2,960,240]{2,1,0:T(8,128)(2,1)} %pad_maximum_fusion.7), channel_id=1, source_target_pairs={{0,8},{8,0},{16,24},{24,16},{1,9},{9,1},{17,25},{25,17},{2,10},{10... | collective-permute-start | bytes 2764808 | tf_op jit(solution)/shard_map/ppermute | solution.py:359
  259.9 59.9 %collective-permute-start.52 = (bf16[2,960,240]{2,1,0:T(8,128)(2,1)}, bf16[2,960,240]{2,1,0:T(8,128)(2,1)}, u32[]{:S(2)}, u32[]{:S(2)}) collective-permute-start(bf16[2,960,240]{2,1,0:T(8,128)(2,1)} %pad_maximum_fusion.6), channel_id=1, source_target_pairs={{0,16},{8,24},{16,0},{24,8},{1,17},{9,25},{17,1},{25,9},{2,18},{10... | collective-permute-start | bytes 2764808 | tf_op jit(solution)/shard_map/ppermute | solution.py:359
  263.9 55.9 %collective-permute-start.50 = (bf16[2,960,240]{2,1,0:T(8,128)(2,1)}, bf16[2,960,240]{2,1,0:T(8,128)(2,1)}, u32[]{:S(2)}, u32[]{:S(2)}) collective-permute-start(bf16[2,960,240]{2,1,0:T(8,128)(2,1)} %pad_maximum_fusion.5), channel_id=1, source_target_pairs={{0,8},{8,0},{16,24},{24,16},{1,9},{9,1},{17,25},{25,17},{2,10},{10... | collective-permute-start | bytes 2764808 | tf_op jit(solution)/shard_map/ppermute | solution.py:359
  316.0 44.5 %collective-permute-start.29 = (bf16[4,320,640]{2,1,0:T(8,128)(2,1)}, bf16[4,320,640]{2,1,0:T(8,128)(2,1)}, u32[]{:S(2)}, u32[]{:S(2)}) collective-permute-start(bf16[4,320,640]{2,1,0:T(8,128)(2,1)} %get-tuple-element.83), channel_id=1, source_target_pairs={{0,1},{1,0},{2,3},{3,2},{4,5},{5,4},{6,7},{7,6},{8,9},{9,8},{10,11... | collective-permute-start | bytes 4915208 | tf_op jit(solution)/shard_map/ppermute | solution.py:355
  319.2 33.9 %collective-permute-start.58 = (bf16[960,240]{1,0:T(8,128)(2,1)}, bf16[960,240]{1,0:T(8,128)(2,1)}, u32[]{:S(2)}, u32[]{:S(2)}) collective-permute-start(bf16[960,240]{1,0:T(8,128)(2,1)} %get-tuple-element.159), channel_id=1, source_target_pairs={{0,4},{1,5},{2,6},{3,7},{4,0},{5,1},{6,2},{7,3},{8,12},{9,13},{10,... | collective-permute-start | bytes 1382408 | tf_op jit(solution)/shard_map/ppermute | solution.py:363
  319.2 33.9 %collective-permute-start.59 = (bf16[960,240]{1,0:T(8,128)(2,1)}, bf16[960,240]{1,0:T(8,128)(2,1)}, u32[]{:S(2)}, u32[]{:S(2)}) collective-permute-start(bf16[960,240]{1,0:T(8,128)(2,1)} %get-tuple-element.160), channel_id=1, source_target_pairs={{0,2},{1,3},{2,4},{3,5},{4,6},{5,7},{6,0},{7,1},{8,10},{9,11},{10,... | collective-permute-start | bytes 1382408 | tf_op jit(solution)/shard_map/ppermute | solution.py:363
  323.5 35.3 %collective-permute-start.53 = (bf16[960,240]{1,0:T(8,128)(2,1)}, bf16[960,240]{1,0:T(8,128)(2,1)}, u32[]{:S(2)}, u32[]{:S(2)}) collective-permute-start(bf16[960,240]{1,0:T(8,128)(2,1)} %slice_bitcast_fusion.6), channel_id=1, source_target_pairs={{0,6},{1,7},{2,0},{3,1},{4,2},{5,3},{6,4},{7,5},{8,14},{9,15},{10,... | collective-permute-start | bytes 1382408 | tf_op jit(solution)/shard_map/ppermute | solution.py:363
  332.1 36.7 %collective-permute-start.41 = (bf16[16,128,240]{1,2,0:T(8,128)(2,1)}, bf16[16,128,240]{1,2,0:T(8,128)(2,1)}, u32[]{:S(2)}, u32[]{:S(2)}) collective-permute-start(bf16[16,128,240]{1,2,0:T(8,128)(2,1)} %copy.141), channel_id=1, source_target_pairs={{0,1},{1,0},{2,3},{3,2},{4,5},{5,4},{6,7},{7,6},{8,9},{9,8},{10,11... | collective-permute-start | bytes 2949128 | tf_op jit(solution)/shard_map/ppermute | solution.py:355
  363.8 17.9 %collective-permute-start.30 = (bf16[320,640]{1,0:T(8,128)(2,1)}, bf16[320,640]{1,0:T(8,128)(2,1)}, u32[]{:S(2)}, u32[]{:S(2)}) collective-permute-start(bf16[320,640]{1,0:T(8,128)(2,1)} %get-tuple-element.148), channel_id=1, source_target_pairs={{2,0},{3,1},{4,2},{5,3},{6,4},{7,5},{10,8},{11,9},{12,10},{13,11},... | collective-permute-start | bytes 1228808 | tf_op jit(solution)/shard_map/ppermute | solution.py:371
  365.1 27.4 %collective-permute-start.32 = (bf16[320,640]{1,0:T(8,128)(2,1)}, bf16[320,640]{1,0:T(8,128)(2,1)}, u32[]{:S(2)}, u32[]{:S(2)}) collective-permute-start(bf16[320,640]{1,0:T(8,128)(2,1)} %get-tuple-element.149), channel_id=1, source_target_pairs={{6,0},{7,1},{14,8},{15,9},{22,16},{23,17},{30,24},{31,25}} | collective-permute-start | bytes 1228808 | tf_op jit(solution)/shard_map/ppermute | solution.py:371
  366.4 42.2 %collective-permute-start.31 = (bf16[320,640]{1,0:T(8,128)(2,1)}, bf16[320,640]{1,0:T(8,128)(2,1)}, u32[]{:S(2)}, u32[]{:S(2)}) collective-permute-start(bf16[320,640]{1,0:T(8,128)(2,1)} %get-tuple-element.150), channel_id=1, source_target_pairs={{4,0},{5,1},{6,2},{7,3},{12,8},{13,9},{14,10},{15,11},{20,16},{21,... | collective-permute-start | bytes 1228808 | tf_op jit(solution)/shard_map/ppermute | solution.py:371
  420.7 18.9 %collective-permute-start.33 = (bf16[16,208,240]{2,1,0:T(8,128)(2,1)}, bf16[16,208,240]{2,1,0:T(8,128)(2,1)}, u32[]{:S(2)}, u32[]{:S(2)}) collective-permute-start(bf16[16,208,240]{2,1,0:T(8,128)(2,1)} %get-tuple-element.87), channel_id=1, source_target_pairs={{0,1},{1,0},{2,3},{3,2},{4,5},{5,4},{6,7},{7,6},{8,9},{9,8},{10,11... | collective-permute-start | bytes 4792328 | tf_op jit(solution)/shard_map/ppermute | solution.py:355
  (97 other events, 1092.9 us)

commit v2 on v0

--- a/solution.py
+++ b/solution.py
@@ -1,6 +1,10 @@
+import functools
+
 import jax
 import jax.numpy as jnp
 from jax import lax
+from jax.experimental import pallas as pl
+from jax.experimental.pallas import tpu as pltpu
 from jax.sharding import PartitionSpec as P
 
 MODEL_WIDTH = 960
@@ -349,6 +353,1014 @@
     )
 
 
+def swap_core(value):
+    return lax.ppermute(value, "fsdp", [(j, j ^ 1) for j in range(8)])
+
+
+def swap_dp(value, mask):
+    return lax.ppermute(value, "dp", [(j, j ^ mask) for j in range(4)])
+
+
+def shift_z(value, step):
+    return lax.ppermute(value, "fsdp", [(j, (j + 2 * step) % 8) for j in range(8)])
+
+
+def shift_z_up(value, step):
+    return lax.ppermute(value, "fsdp", [(j, j + 2 * step) for j in range(8) if j + 2 * step < 8])
+
+
+def shift_z_down(value, step):
+    return lax.ppermute(value, "fsdp", [(j, j - 2 * step) for j in range(8) if j - 2 * step >= 0])
+
+
+def add_low(*terms):
+    total = terms[0].astype(jnp.float32)
+    for term in terms[1:]:
+        total = total + term.astype(jnp.float32)
+    return total.astype(jnp.bfloat16)
+
+
+def product_nn(left, right):
+    return lax.dot_general(
+        left, right, (((1,), (0,)), ((), ())), preferred_element_type=jnp.float32
+    )
+
+
+def product_nt(left, right):
+    return lax.dot_general(
+        left, right, (((1,), (1,)), ((), ())), preferred_element_type=jnp.float32
+    )
+
+
+def product_tn(left, right):
+    return lax.dot_general(
+        left, right, (((0,), (0,)), ((), ())), preferred_element_type=jnp.float32
+    )
+
+
+VMEM = pl.BlockSpec(memory_space=pltpu.VMEM)
+SMEM = pl.BlockSpec(memory_space=pltpu.SMEM)
+ANY = pl.BlockSpec(memory_space=pl.ANY)
+
+
+def run(body, name, ins, in_specs, outs, out_specs, scratch, flops, megabytes):
+    moved = sum(v.size * v.dtype.itemsize for v in ins)
+    moved += sum(v.size * v.dtype.itemsize for v in outs)
+    return pl.pallas_call(
+        body,
+        out_shape=tuple(outs),
+        in_specs=in_specs,
+        out_specs=tuple(out_specs),
+        scratch_shapes=scratch,
+        compiler_params=pltpu.CompilerParams(vmem_limit_bytes=megabytes * 1024 * 1024),
+        cost_estimate=pl.CostEstimate(flops=flops, bytes_accessed=moved, transcendentals=0),
+        name=name,
+    )(*ins)
+
+
+def struct(shape, dtype=jnp.bfloat16):
+    return jax.ShapeDtypeStruct(shape, dtype)
+
+
+def column_index(ids_ref, core_rel, s):
+    return 2 * lax.rem(ids_ref[1] - s + 4, 4) + (ids_ref[2] ^ core_rel)
+
+
+def start_row(index, size):
+    return pl.ds(pl.multiple_of(index * size, 8), size)
+
+
+def after(value, *others):
+    return lax.optimization_barrier((value,) + others)[0]
+
+
+def pack_first_kernel(counts_ref, wq_ref, wk_ref, wv_ref, gains_ref, out_ref):
+    block = wq_ref.shape[0]
+    gains = gains_ref[...].astype(jnp.float32)
+    row = lax.broadcasted_iota(jnp.int32, (8, block), 0)
+    lane = lax.broadcasted_iota(jnp.int32, (8, block), 1)
+    first = jnp.concatenate([gains[:1], gains[1:]], 1)
+    used = jnp.where(
+        lane == 0,
+        counts_ref[0, 0].astype(jnp.float32),
+        jnp.where(lane == 1, counts_ref[1, 0].astype(jnp.float32), 0.0),
+    )
+    extra = jnp.where(row == 0, first, jnp.where(row == 1, used, 0.0))
+    full = jnp.concatenate(
+        [
+            wq_ref[...].astype(jnp.float32).T,
+            extra,
+            wk_ref[...].astype(jnp.float32).T,
+            wv_ref[...].astype(jnp.float32).T,
+        ],
+        0,
+    )
+    out_ref[...] = jnp.zeros_like(out_ref)
+    out_ref[:, :block] = full.astype(jnp.bfloat16)
+
+
+def pack_mlp_kernel(ids_ref, wg_ref, wu_ref, wd_ref, other_ref, wo_ref, out_ref):
+    block, half = wg_ref.shape
+    core = ids_ref[2]
+    out_ref[...] = jnp.zeros_like(out_ref)
+    out_ref[:half, :block] = wg_ref[...].astype(jnp.float32).T.astype(jnp.bfloat16)
+    out_ref[half : 2 * half, :block] = wu_ref[...].astype(jnp.float32).T.astype(jnp.bfloat16)
+    own = wd_ref[pl.ds(pl.multiple_of(core * half, 16), half), :]
+    other = other_ref[...]
+    low = jnp.where(core == 0, own, other)
+    high = jnp.where(core == 0, other, own)
+    out_ref[2 * half : 3 * half, :block] = jnp.concatenate([low, high], 1)
+    out_ref[3 * half :, :block] = jnp.concatenate(
+        [wo_ref[...].astype(jnp.float32).T, jnp.zeros((8, block), jnp.float32)], 0
+    ).astype(jnp.bfloat16)
+
+
+def turn_in_kernel(x_ref, dy_ref, xt_ref, dyt_ref):
+    xt_ref[...] = x_ref[...].astype(jnp.float32).T.astype(jnp.bfloat16)
+    dyt_ref[...] = dy_ref[...].astype(jnp.float32).T.astype(jnp.bfloat16)
+
+
+def fill_relative(ids_ref, source_ref, target_ref):
+    block, lanes = source_ref.shape[1:]
+    wide = target_ref.shape[0] // 4
+    for k in range(4):
+        target_ref[k * wide : k * wide + block, :] = source_ref[ids_ref[0] ^ k]
+        target_ref[k * wide + block : (k + 1) * wide, :] = jnp.zeros(
+            (wide - block, lanes), target_ref.dtype
+        )
+
+
+def wide_rows(refs, s, low, high):
+    along, by_x, by_y, far_a, far_b = refs
+    far = far_a if s < 2 else far_b
+    return jnp.concatenate(
+        [along[s, low:high], by_x[s, low:high], by_y[s, low:high], far[s % 2, low:high]], 1
+    )
+
+
+def project_kernel(*refs):
+    ids_ref, own, other = refs[0], refs[1:6], refs[6:11]
+    n1_ref, cos_ref, sin_ref, q_ref, kv_ref, proj_ref, turned_ref, rel_ref = refs[11:]
+    width = n1_ref.shape[0] * n1_ref.shape[1]
+    kv_width = KEY_HEADS * HEAD_WIDTH
+    q_cols, k_cols = width // 8, kv_width // 8
+    depth = own[0].shape[1]
+    fill_relative(ids_ref, n1_ref, rel_ref)
+    for core_rel, weights in ((0, own), (1, other)):
+        for s in range(4):
+            f = column_index(ids_ref, core_rel, s)
+            total = product_nn(wide_rows(weights, s, 0, depth), rel_ref[...])
+            proj_ref[start_row(f, q_cols), :] = total[:q_cols]
+            proj_ref[pl.ds(pl.multiple_of(width + f * k_cols, 8), k_cols), :] = total[
+                q_cols + 8 : q_cols + 8 + k_cols
+            ]
+            proj_ref[pl.ds(pl.multiple_of(width + kv_width + f * k_cols, 8), k_cols), :] = total[
+                q_cols + 8 + k_cols :
+            ]
+    cosine, sine = cos_ref[...], sin_ref[...]
+    half = HEAD_WIDTH // 2
+
+    def heads(head, carry):
+        front = proj_ref[pl.ds(pl.multiple_of(head * HEAD_WIDTH, 8), half), :]
+        back = proj_ref[pl.ds(pl.multiple_of(head * HEAD_WIDTH + half, 8), half), :]
+        q_ref[head, :half, :] = (
+            (front * cosine - back * sine).astype(jnp.bfloat16) * SCORE_SCALE
+        ).astype(jnp.bfloat16)
+        q_ref[head, half:, :] = (
+            (back * cosine + front * sine).astype(jnp.bfloat16) * SCORE_SCALE
+        ).astype(jnp.bfloat16)
+        return carry
+
+    lax.fori_loop(0, QUERY_HEADS, heads, 0)
+    for head in range(KEY_HEADS):
+        base = width + head * HEAD_WIDTH
+        front = proj_ref[base : base + half, :]
+        back = proj_ref[base + half : base + 2 * half, :]
+        turned_ref[head * HEAD_WIDTH : head * HEAD_WIDTH + half, :] = front * cosine - back * sine
+        turned_ref[head * HEAD_WIDTH + half : (head + 1) * HEAD_WIDTH, :] = (
+            back * cosine + front * sine
+        )
+    turned_ref[kv_width:, :] = proj_ref[width + kv_width :, :]
+    kv_ref[...] = turned_ref[...].T.astype(jnp.bfloat16)
+
+
+def stage_heads(mb, cap, blocks, k_ref, v_ref):
+    kv_width = KEY_HEADS * HEAD_WIDTH
+    for block, source in enumerate(blocks):
+        rows = source[mb * cap : (mb + 1) * cap, :]
+        for n in range(KEY_HEADS):
+            lanes = n * HEAD_WIDTH
+            k_ref[n, block * cap : (block + 1) * cap, :] = rows[:, lanes : lanes + HEAD_WIDTH]
+            lanes += kv_width
+            v_ref[n, block * cap : (block + 1) * cap, :] = rows[:, lanes : lanes + HEAD_WIDTH]
+
+
+def stage_bias(ids_ref, counts_ref, mb, cap, share, bias_ref):
+    slot = ids_ref[3]
+    own_count = counts_ref[mb * 8 + slot]
+    key = lax.broadcasted_iota(jnp.int32, (cap, cap), 0)
+    query = lax.broadcasted_iota(jnp.int32, (cap, cap), 1)
+    query_used = query < own_count
+    for core_rel in range(2):
+        for s in range(4):
+            block = core_rel * 4 + s
+            f = column_index(ids_ref, core_rel, s)
+            count = counts_ref[mb * 8 + f]
+            reach = jnp.where(f < slot, cap, jnp.where(f == slot, 0, -2 * cap))
+            self_off = jnp.where(f == slot, 0, 2 * cap)
+            allowed = (query_used & (key < count) & (key <= query + reach)) | (
+                key == query + self_off
+            )
+            tile = jnp.where(allowed, 0.0, -1e30)
+            for g in range(share):
+                bias_ref[block * cap : (block + 1) * cap, g * cap : (g + 1) * cap] = tile
+
+
+def join_heads(ref, n, share, mb, cap):
+    return jnp.concatenate(
+        [ref[share * n + g, :, mb * cap : (mb + 1) * cap] for g in range(share)], 1
+    )
+
+
+def attend_kernel(*refs):
+    ids_ref, counts_ref, q_ref = refs[:3]
+    blocks = refs[3:11]
+    att_ref, lse_ref, k_ref, v_ref, bias_ref = refs[11:]
+    cap = q_ref.shape[2] // 2
+    share = QUERY_HEADS // KEY_HEADS
+    for mb in range(2):
+        stage_heads(mb, cap, blocks, k_ref, v_ref)
+        stage_bias(ids_ref, counts_ref, mb, cap, share, bias_ref)
+
+        def body(n, carry, mb=mb):
+            scores = product_nn(k_ref[n], join_heads(q_ref, n, share, mb, cap)) + bias_ref[...]
+            top = jnp.max(scores, 0, keepdims=True)
+            exponent = jnp.exp(scores - top)
+            total = jnp.sum(exponent, 0, keepdims=True)
+            mixed = product_tn(v_ref[n], exponent.astype(jnp.bfloat16)) / total
+            mixed = mixed.astype(jnp.bfloat16)
+            for g in range(share):
+                att_ref[share * n + g, :, mb * cap : (mb + 1) * cap] = mixed[
+                    :, g * cap : (g + 1) * cap
+                ]
+            lse_ref[mb * KEY_HEADS + n] = top + jnp.log(total)
+            return carry
+
+        lax.fori_loop(0, KEY_HEADS, body, 0)
+
+
+def attend_back_kernel(mb, *refs):
+    ids_ref, counts_ref, q_ref, do_ref = refs[:4]
+    blocks = refs[4:12]
+    lse_ref, cos_ref, sin_ref, dq_ref = refs[12:16]
+    targets = refs[16:24]
+    k_ref, v_ref, bias_ref, dk_ref, dv_ref = refs[24:]
+    cap = q_ref.shape[2] // 2
+    share = QUERY_HEADS // KEY_HEADS
+    half = HEAD_WIDTH // 2
+    kv_width = KEY_HEADS * HEAD_WIDTH
+    stage_heads(mb, cap, blocks, k_ref, v_ref)
+    stage_bias(ids_ref, counts_ref, mb, cap, share, bias_ref)
+    cosine = jnp.concatenate([cos_ref[:, mb * cap : (mb + 1) * cap]] * share, 1)
+    sine = jnp.concatenate([sin_ref[:, mb * cap : (mb + 1) * cap]] * share, 1)
+
+    def body(n, carry):
+        query = join_heads(q_ref, n, share, mb, cap)
+        grad = join_heads(do_ref, n, share, mb, cap)
+        keys = k_ref[n]
+        prob = jnp.exp(product_nn(keys, query) + bias_ref[...] - lse_ref[mb * KEY_HEADS + n])
+        dprob = product_nn(v_ref[n], grad)
+        delta = jnp.sum(prob * dprob, 0, keepdims=True)
+        dscore = (prob * (dprob - delta)).astype(jnp.bfloat16)
+        dq = product_tn(keys, dscore) * SCORE_SCALE
+        front, back = dq[:half], dq[half:]
+        turned = jnp.concatenate(
+            [front * cosine + back * sine, back * cosine - front * sine], 0
+        ).astype(jnp.bfloat16)
+        for g in range(share):
+            dq_ref[share * n + g] = turned[:, g * cap : (g + 1) * cap]
+        dk_ref[n] = product_nt(dscore, query).astype(jnp.bfloat16)
+        dv_ref[n] = product_nt(prob.astype(jnp.bfloat16), grad).astype(jnp.bfloat16)
+        return carry
+
+    lax.fori_loop(0, KEY_HEADS, body, 0)
+    for block, target in enumerate(targets):
+        for n in range(KEY_HEADS):
+            lanes = n * HEAD_WIDTH
+            target[:, lanes : lanes + HEAD_WIDTH] = dk_ref[n, block * cap : (block + 1) * cap, :]
+            lanes += kv_width
+            target[:, lanes : lanes + HEAD_WIDTH] = dv_ref[n, block * cap : (block + 1) * cap, :]
+
+
+def collect_kernel(*refs):
+    pieces, out_ref, sem = refs[:16], refs[16], refs[17]
+    rows, wide = out_ref.shape[1], pieces[0].shape[1]
+    copies = []
+    for k in range(4):
+        for s in range(4):
+            copies.append(
+                pltpu.make_async_copy(
+                    pieces[k * 4 + s].at[pl.ds(pieces[0].shape[0] - rows, rows)],
+                    out_ref.at[s, :, pl.ds(k * wide, wide)],
+                    sem.at[k * 4 + s],
+                )
+            )
+    for copy in copies:
+        copy.start()
+    for copy in copies:
+        copy.wait()
+
+
+def hidden_kernel(ids_ref, own_ref, other_ref, att_ref, x_ref, gain_ref, h_ref, n2_ref, rel_ref):
+    q_cols = h_ref.shape[0] // 8
+    fill_relative(ids_ref, att_ref, rel_ref)
+    for core_rel, w_ref in ((0, own_ref), (1, other_ref)):
+        for s in range(4):
+            f = column_index(ids_ref, core_rel, s)
+            h_ref[start_row(f, q_cols), :] = product_nn(w_ref[s], rel_ref[...])[:q_cols]
+    h = h_ref[...] + x_ref[...].astype(jnp.float32)
+    h_ref[...] = h
+    n2_ref[...] = (h * mean_square(h) * gain_ref[...]).astype(jnp.bfloat16)
+
+
+def turn_point_kernel(
+    ids_ref,
+    parts_ref,
+    arrived_ref,
+    h_ref,
+    dy_ref,
+    gain_ref,
+    own_ref,
+    other_ref,
+    out_ref,
+    dh_ref,
+    do_ref,
+    gain_grad_ref,
+    pieces_ref,
+    da_ref,
+):
+    width, rows = h_ref.shape
+    q_cols = width // 8
+    block = do_ref.shape[1]
+    wide = own_ref.shape[2] // 4
+    h = h_ref[...]
+    out_ref[...] = (h + parts_ref[0] + arrived_ref[0].astype(jnp.float32)).astype(jnp.bfloat16)
+    dn = parts_ref[1] + arrived_ref[1].astype(jnp.float32)
+    rms = mean_square(h)
+    gain_grad_ref[...] = jnp.sum(dn * h * rms, 1, keepdims=True)
+    weighted = dn * gain_ref[...]
+    dh = (
+        dy_ref[...].astype(jnp.float32)
+        + rms * weighted
+        - h * (rms * rms * rms * jnp.mean(weighted * h, 0, keepdims=True))
+    )
+    dh_ref[...] = dh
+    da_ref[...] = dh
+    spread(ids_ref, da_ref, pieces_ref, q_cols)
+    half = pieces_ref.shape[0] // 2
+    mixed = product_tn(own_ref[...].reshape(half, 4 * wide), pieces_ref[:half, :])
+    mixed += product_tn(other_ref[...].reshape(half, 4 * wide), pieces_ref[half:, :])
+    mixed = mixed.astype(jnp.bfloat16)
+    for k in range(4):
+        do_ref[ids_ref[0] ^ k] = mixed[k * wide : k * wide + block]
+
+
+def spread(ids_ref, source_ref, target_ref, cols):
+    rows = source_ref.shape[1]
+    for core_rel in range(2):
+        for s in range(4):
+            f = column_index(ids_ref, core_rel, s)
+            low = (core_rel * 4 + s) * (cols + 8)
+            target_ref[low : low + cols + 8, :] = jnp.concatenate(
+                [source_ref[start_row(f, cols), :], jnp.zeros((8, rows), jnp.float32)], 0
+            ).astype(jnp.bfloat16)
+
+
+def finish_q_kernel(*refs):
+    ids_ref, own, other = refs[0], refs[1:6], refs[6:11]
+    n1_ref, att_ref, dq_a_ref, dq_b_ref, pieces_ref, dn_ref = refs[11:17]
+    grads = refs[17:25]
+    n1_rel, att_rel, d_ref, dq_ref = refs[25:]
+    cap = dq_a_ref.shape[1]
+    width = dq_a_ref.shape[0]
+    q_cols = width // 8
+    depth = q_cols + 8
+    block = n1_ref.shape[1]
+    wide = n1_rel.shape[0] // 4
+    d_ref[:, :cap] = dq_a_ref[...].astype(jnp.float32)
+    d_ref[:, cap:] = dq_b_ref[...].astype(jnp.float32)
+    spread(ids_ref, d_ref, dq_ref, q_cols)
+    fill_relative(ids_ref, n1_ref, n1_rel)
+    fill_relative(ids_ref, att_ref, att_rel)
+    weights = jnp.concatenate(
+        [wide_rows(w, s, 0, depth) for w in (own, other) for s in range(4)], 0
+    )
+    dn = product_tn(weights, dq_ref[...])
+    for k in range(4):
+        dn_ref[ids_ref[0] ^ k] = dn[k * wide : k * wide + block]
+    for core_rel in range(2):
+        for s in range(4):
+            low = (core_rel * 4 + s) * depth
+            gq = product_nt(dq_ref[low : low + depth, :], n1_rel[...]).astype(jnp.bfloat16)
+            go = product_nt(pieces_ref[low : low + depth, :], att_rel[...]).astype(jnp.bfloat16)
+            for k in range(4):
+                target = grads[core_rel * 4 + k]
+                target[s, :depth, :] = gq[:, k * wide : (k + 1) * wide]
+                target[s, depth:, :] = go[:, k * wide : (k + 1) * wide]
+
+
+def finish_kv_kernel(*refs):
+    ids_ref, own, other = refs[0], refs[1:6], refs[6:11]
+    n1_ref, dkv_a_ref, dkv_b_ref, cos_ref, sin_ref, dn_ref, dh_ref, x_ref, gain_ref = refs[11:20]
+    tokens_ref, gain_grad_ref = refs[20:22]
+    grads = refs[22:30]
+    n1_rel, d_ref, dkv_ref = refs[30:]
+    width, rows = dh_ref.shape
+    cap = rows // 2
+    kv_width = KEY_HEADS * HEAD_WIDTH
+    q_cols, k_cols = width // 8, kv_width // 8
+    half = HEAD_WIDTH // 2
+    block = n1_ref.shape[1]
+    wide = n1_rel.shape[0] // 4
+    cosine, sine = cos_ref[...], sin_ref[...]
+    d_ref[:, :cap] = dkv_a_ref[...].T
+    d_ref[:, cap:] = dkv_b_ref[...].T
+    for head in range(KEY_HEADS):
+        base = head * HEAD_WIDTH
+        front = d_ref[base : base + half, :]
+        back = d_ref[base + half : base + 2 * half, :]
+        d_ref[base : base + half, :] = front * cosine + back * sine
+        d_ref[base + half : base + 2 * half, :] = back * cosine - front * sine
+    for core_rel in range(2):
+        for s in range(4):
+            f = column_index(ids_ref, core_rel, s)
+            low = (core_rel * 4 + s) * 2 * k_cols
+            dkv_ref[low : low + 2 * k_cols, :] = jnp.concatenate(
+                [
+                    d_ref[start_row(f, k_cols), :],
+                    d_ref[pl.ds(pl.multiple_of(kv_width + f * k_cols, 8), k_cols), :],
+                ],
+                0,
+            ).astype(jnp.bfloat16)
+    fill_relative(ids_ref, n1_ref, n1_rel)
+    low = q_cols + 8
+    weights = jnp.concatenate(
+        [wide_rows(w, s, low, low + 2 * k_cols) for w in (own, other) for s in range(4)], 0
+    )
+    dn = product_tn(weights, dkv_ref[...])
+    for k in range(4):
+        i = ids_ref[0] ^ k
+        tokens_ref[pl.ds(pl.multiple_of(i * block, 16), block), :] = (
+            dn[k * wide : k * wide + block] + dn_ref[i]
+        )
+    for core_rel in range(2):
+        for s in range(4):
+            low = (core_rel * 4 + s) * 2 * k_cols
+            got = product_nt(dkv_ref[low : low + 2 * k_cols, :], n1_rel[...]).astype(jnp.bfloat16)
+            for k in range(4):
+                grads[core_rel * 4 + k][s] = got[:, k * wide : (k + 1) * wide]
+    x = x_ref[...].astype(jnp.float32)
+    rms = mean_square(x)
+    dn = tokens_ref[...]
+    gain_grad_ref[...] = jnp.sum(dn * x * rms, 1, keepdims=True)
+    weighted = dn * gain_ref[...]
+    tokens_ref[...] = (
+        dh_ref[...]
+        + rms * weighted
+        - x * (rms * rms * rms * jnp.mean(weighted * x, 0, keepdims=True))
+    )
+
+
+def mlp_kernel(*refs):
+    ids_ref, n2_own, n2_other, dy_own, dy_other = refs[:5]
+    pieces = refs[5:21]
+    keep_ref, send_ref = refs[21:23]
+    grads = refs[23:39]
+    wgu, wdn, ggu, gdn, gu_ref, prod_ref, dgu_ref, n2_rel, dy_rel, sem_in, sem_out = refs[39:]
+    dp_id = ids_ref[0]
+    z_id = ids_ref[1]
+    block, rows = n2_own.shape[1:]
+    pair = 2 * rows
+    wide = pieces[0].shape[1]
+    half = prod_ref.shape[0] // 4
+    loads = []
+    for s in range(4):
+        for k in range(4):
+            piece = pieces[k * 4 + s]
+            lanes = pl.ds(k * wide, wide)
+            loads.append(
+                pltpu.make_async_copy(
+                    piece.at[pl.ds(0, 2 * half)],
+                    wgu.at[pl.ds(s * 2 * half, 2 * half), lanes],
+                    sem_in.at[0, k * 4 + s],
+                )
+            )
+    for k in range(4):
+        for s in range(4):
+            loads.append(
+                pltpu.make_async_copy(
+                    pieces[k * 4 + s].at[pl.ds(2 * half, half)],
+                    wdn.at[pl.ds(k * half, half), pl.ds(s * wide, wide)],
+                    sem_in.at[1, k * 4 + s],
+                )
+            )
+    for load in loads:
+        load.start()
+    pad = jnp.zeros((wide - block, pair), jnp.bfloat16)
+    for j in range(4):
+        i = dp_id ^ j
+        zz = lax.rem(z_id - j + 4, 4)
+        n2_rel[j * wide : j * wide + block, :] = jnp.concatenate([n2_own[i], n2_other[i]], 1)
+        dy_rel[j * wide : j * wide + block, :] = jnp.concatenate([dy_own[zz], dy_other[zz]], 1)
+        n2_rel[j * wide + block : (j + 1) * wide, :] = pad
+        dy_rel[j * wide + block : (j + 1) * wide, :] = pad
+    for load in loads[:16]:
+        load.wait()
+
+    def rows_of(index, size):
+        return pl.ds(pl.multiple_of(index * size, 16), size)
+
+    def forward(s, carry):
+        m = lax.rem(z_id - s + 4, 4)
+        k = m ^ dp_id
+        total = product_nn(wgu[rows_of(s, 2 * half), :], n2_rel[...])
+        gu_ref[rows_of(k, 2 * half), :] = total
+        gate = total[:half]
+        prod_ref[rows_of(k, half), :] = (gate * jax.nn.sigmoid(gate) * total[half:]).astype(
+            jnp.bfloat16
+        )
+        return carry
+
+    lax.fori_loop(0, 4, forward, 0)
+    for load in loads[16:]:
+        load.wait()
+
+    def middle(k, carry):
+        s = lax.rem(z_id - (dp_id ^ k) + 4, 4)
+        dprod = product_nn(wdn[rows_of(k, half), :], dy_rel[...])
+        gdn[rows_of(k, half), :] = product_nt(prod_ref[rows_of(k, half), :], dy_rel[...]).astype(
+            jnp.bfloat16
+        )
+        total = gu_ref[rows_of(k, 2 * half), :]
+        gate, up = total[:half], total[half:]
+        sig = jax.nn.sigmoid(gate)
+        dgu_ref[rows_of(s, 2 * half), :] = jnp.concatenate(
+            [dprod * up * sig * (1.0 + gate * (1.0 - sig)), dprod * gate * sig], 0
+        ).astype(jnp.bfloat16)
+        return carry
+
+    lax.fori_loop(0, 4, middle, 0)
+
+    def backward(s, carry):
+        ggu[rows_of(s, 2 * half), :] = product_nt(
+            dgu_ref[rows_of(s, 2 * half), :], n2_rel[...]
+        ).astype(jnp.bfloat16)
+        return carry
+
+    stores = []
+    for k in range(4):
+        for s in range(4):
+            stores.append(
+                pltpu.make_async_copy(
+                    gdn.at[pl.ds(k * half, half), pl.ds(s * wide, wide)],
+                    grads[k * 4 + s].at[pl.ds(2 * half, half)],
+                    sem_out.at[1, k * 4 + s],
+                )
+            )
+    for store in stores:
+        store.start()
+    lax.fori_loop(0, 4, backward, 0)
+    late = []
+    for k in range(4):
+        for s in range(4):
+            late.append(
+                pltpu.make_async_copy(
+                    ggu.at[pl.ds(s * 2 * half, 2 * half), pl.ds(k * wide, wide)],
+                    grads[k * 4 + s].at[pl.ds(0, 2 * half)],
+                    sem_out.at[0, k * 4 + s],
+                )
+            )
+    for store in late:
+        store.start()
+    for j in range(4):
+        lanes = slice(j * wide, (j + 1) * wide)
+        out = product_tn(wdn[:, lanes], prod_ref[...])[:block]
+        zz = rows_of(lax.rem(z_id - j + 4, 4), block)
+        keep_ref[0, zz, :] = out[:, :rows]
+        send_ref[0, zz, :] = out[:, rows:].astype(jnp.bfloat16)
+        dn = product_tn(wgu[:, lanes], dgu_ref[...])[:block]
+        i = rows_of(dp_id ^ j, block)
+        keep_ref[1, i, :] = dn[:, :rows]
+        send_ref[1, i, :] = dn[:, rows:].astype(jnp.bfloat16)
+    for store in stores + late:
+        store.wait()
+
+
+def mean_square(values):
+    return lax.rsqrt(jnp.mean(values * values, 0, keepdims=True) + EPSILON)
+
+
+def fast(
+    tokens, cotangent, counts, w_query, key_weight, value_weight, w_out, w_gate, w_up, w_down, gains
+):
+    dp_id = lax.axis_index("dp")
+    slot = lax.axis_index("fsdp")
+    z_id = slot // 2
+    core_id = slot % 2
+    ids = jnp.stack([dp_id, z_id, core_id, slot]).astype(jnp.int32)
+    batches, cap, width = tokens.shape
+    rows = batches * cap
+    block = w_query.shape[0]
+    wide = -(-block // 128) * 128
+    q_cols, k_cols = w_query.shape[1], key_weight.shape[1]
+    half = w_gate.shape[1]
+    kv_width = KEY_HEADS * HEAD_WIDTH
+    share = QUERY_HEADS // KEY_HEADS
+    q_rows = q_cols + 8
+    depth = q_rows + 2 * k_cols
+    mlp_rows = 3 * half + q_rows
+
+    (first_piece,) = run(
+        pack_first_kernel,
+        "pack_first",
+        (counts, w_query, key_weight, value_weight, gains),
+        [SMEM] + [VMEM] * 4,
+        [struct((depth, wide))],
+        [VMEM],
+        [],
+        0,
+        16,
+    )
+    chain = [first_piece]
+    for _ in range(3):
+        chain.append(shift_z(chain[-1], 1))
+    down_halves = w_down.reshape(2, half, -1)
+    other_down = swap_core(
+        lax.dynamic_index_in_dim(down_halves, 1 - core_id, 0, keepdims=False)
+    )
+    (mlp_piece,) = run(
+        pack_mlp_kernel,
+        "pack_mlp",
+        (ids, w_gate, w_up, w_down, other_down, w_out),
+        [SMEM] + [VMEM] * 5,
+        [struct((mlp_rows, wide))],
+        [VMEM],
+        [],
+        0,
+        16,
+    )
+    x, dy = run(
+        turn_in_kernel,
+        "turn_in",
+        (tokens.reshape(rows, width), cotangent.reshape(rows, width)),
+        [VMEM] * 2,
+        [struct((width, rows))] * 2,
+        [VMEM] * 2,
+        [],
+        0,
+        16,
+    )
+    dy_other = swap_core(dy)
+
+    along = jnp.stack(chain, 0)
+    extras = along[:, q_cols : q_cols + 2, :block]
+    other_extras = swap_core(extras)
+    from_x = swap_dp(along, 1)
+    from_y = swap_dp(along, 2)
+    first_own = [along, from_x, from_y, swap_dp(from_x[:2], 2), swap_dp(from_y[2:], 1)]
+    first_other = [swap_core(piece) for piece in first_own]
+
+    def spread_square(piece):
+        return swap_dp(piece, 1), swap_dp(piece, 2)
+
+    mlp_chain = [mlp_piece, shift_z(after(mlp_piece, along), 1)]
+    for _ in range(2):
+        mlp_chain.append(shift_z(mlp_chain[-1], 1))
+    by_square = [spread_square(mlp_piece)]
+    by_square.append(spread_square(after(mlp_chain[1], first_own[3], first_own[4])))
+
+    by_core = jnp.where(
+        core_id == 0, jnp.stack([extras, other_extras], 1), jnp.stack([other_extras, extras], 1)
+    )
+    by_core = by_core[::-1]
+    by_core = lax.dynamic_slice_in_dim(jnp.concatenate([by_core, by_core], 0), 3 - z_id, 4, 0)
+    gain = by_core[:, :, 0, :].reshape(8, 2, q_cols).transpose(0, 2, 1).reshape(width, 2)
+    gain = gain.astype(jnp.float32)
+    gain_one, gain_two = gain[:, :1], gain[:, 1:]
+    group_counts = by_core[:, :, 1, :batches].reshape(8, batches).astype(jnp.int32)
+    flat_counts = group_counts.T.reshape(-1)
+    before = jnp.sum(
+        jnp.where(jnp.arange(8, dtype=jnp.int32)[:, None] < slot, group_counts, 0), 0
+    )
+    position = (before[:, None] + jnp.arange(cap, dtype=jnp.int32)[None, :]).reshape(-1)
+    cosine, sine = rope_tables(position, HEAD_WIDTH)
+    cosine, sine = cosine[:, 0, :].T, sine[:, 0, :].T
+    x_wide = x.astype(jnp.float32)
+    n1 = (x_wide * mean_square(x_wide) * gain_one).astype(jnp.bfloat16).reshape(4, block, rows)
+
+    query, kv = run(
+        project_kernel,
+        "project",
+        (ids, *first_own, *first_other, n1, cosine, sine),
+        [SMEM] + [VMEM] * 13,
+        (struct((QUERY_HEADS, HEAD_WIDTH, rows)), struct((rows, 2 * kv_width))),
+        [VMEM] * 2,
+        [
+            pltpu.VMEM((width + 2 * kv_width, rows), jnp.float32),
+            pltpu.VMEM((2 * kv_width, rows), jnp.float32),
+            pltpu.VMEM((4 * wide, rows), jnp.bfloat16),
+        ],
+        2 * (width + 2 * kv_width) * width * rows,
+        24,
+    )
+    kv_own, kv_other = [kv], [swap_core(kv)]
+    for _ in range(3):
+        kv_own.append(shift_z_up(kv_own[-1], 1))
+        kv_other.append(swap_core(kv_own[-1]))
+
+    by_square.append(spread_square(after(mlp_chain[2], kv)))
+    far_zero = swap_dp(after(by_square[0][0], kv), 2)
+    far_one = swap_dp(after(by_square[1][1], kv), 1)
+    by_square.append(spread_square(after(mlp_chain[3], kv_own[1])))
+    far_two = swap_dp(after(by_square[2][0], kv_own[2]), 2)
+    far_three = swap_dp(after(by_square[3][1], kv_own[3]), 1)
+    pieces = mlp_chain + [p[0] for p in by_square] + [p[1] for p in by_square]
+    pieces += [far_zero, far_one, far_two, far_three]
+
+    pair_flops = 2 * QUERY_HEADS * HEAD_WIDTH * rows * 8 * cap
+    head_scratch = [
+        pltpu.VMEM((KEY_HEADS, 8 * cap, HEAD_WIDTH), jnp.bfloat16),
+        pltpu.VMEM((KEY_HEADS, 8 * cap, HEAD_WIDTH), jnp.bfloat16),
+        pltpu.VMEM((8 * cap, share * cap), jnp.float32),
+    ]
+    attended, lse = run(
+        attend_kernel,
+        "attend",
+        (ids, flat_counts, query, *kv_own, *kv_other),
+        [SMEM, SMEM] + [VMEM] * 9,
+        (
+            struct((QUERY_HEADS, HEAD_WIDTH, rows)),
+            struct((2 * KEY_HEADS, 1, share * cap), jnp.float32),
+        ),
+        [VMEM] * 2,
+        head_scratch,
+        8 * pair_flops,
+        28,
+    )
+    attended = attended.reshape(4, block, rows)
+    (out_own,) = run(
+        collect_kernel,
+        "collect",
+        tuple(pieces),
+        [ANY] * 16,
+        [struct((4, q_rows, 4 * wide))],
+        [VMEM],
+        [pltpu.SemaphoreType.DMA((16,))],
+        0,
+        8,
+    )
+    out_other = swap_core(out_own)
+    h, n2 = run(
+        hidden_kernel,
+        "hidden",
+        (ids, out_own, out_other, attended, x, gain_two),
+        [SMEM] + [VMEM] * 5,
+        (struct((width, rows), jnp.float32), struct((width, rows))),
+        [VMEM] * 2,
+        [pltpu.VMEM((4 * wide, rows), jnp.bfloat16)],
+        2 * width * width * rows,
+        24,
+    )
+    n2_other = swap_core(n2)
+    blocks = (4, block, rows)
+    results = run(
+        mlp_kernel,
+        "mlp",
+        (
+            ids,
+            n2.reshape(blocks),
+            n2_other.reshape(blocks),
+            dy.reshape(blocks),
+            dy_other.reshape(blocks),
+            *pieces,
+        ),
+        [SMEM] + [VMEM] * 4 + [ANY] * 16,
+        [struct((2, width, rows), jnp.float32), struct((2, width, rows))]
+        + [struct((3 * half, wide))] * 16,
+        [VMEM] * 2 + [ANY] * 16,
+        [
+            pltpu.VMEM((8 * half, 4 * wide), jnp.bfloat16),
+            pltpu.VMEM((4 * half, 4 * wide), jnp.bfloat16),
+            pltpu.VMEM((8 * half, 4 * wide), jnp.bfloat16),
+            pltpu.VMEM((4 * half, 4 * wide), jnp.bfloat16),
+            pltpu.VMEM((8 * half, 2 * rows), jnp.float32),
+            pltpu.VMEM((4 * half, 2 * rows), jnp.bfloat16),
+            pltpu.VMEM((8 * half, 2 * rows), jnp.bfloat16),
+            pltpu.VMEM((4 * wide, 2 * rows), jnp.bfloat16),
+            pltpu.VMEM((4 * wide, 2 * rows), jnp.bfloat16),
+            pltpu.SemaphoreType.DMA((2, 16)),
+            pltpu.SemaphoreType.DMA((2, 16)),
+        ],
+        18 * 16 * half * block * 2 * rows,
+        56,
+    )
+    keep, send, grads = results[0], results[1], results[2:]
+    arrived = swap_core(send)
+    home, to_x, to_y, far = grads[:4], grads[4:8], grads[8:12], grads[12:]
+
+    def first_leg(group, *deps):
+        a, b = 2 * group, 2 * group + 1
+        return (
+            swap_dp(after(far[a], *deps), 2),
+            swap_dp(after(far[b], *deps), 1),
+            swap_dp(after(to_x[b], *deps), 1),
+            swap_dp(after(to_y[a], *deps), 2),
+        )
+
+    def second_leg(group, legs, *deps):
+        a, b = 2 * group, 2 * group + 1
+        via_y, via_x = after(legs[0], *deps), after(legs[1], *deps)
+        x_a = swap_dp(add_low(to_x[a], via_y), 1)
+        y_b = swap_dp(add_low(to_y[b], via_x), 2)
+        return x_a, y_b
+
+    legs_one = first_leg(1)
+    output, dh, mixed_gradient, gain_two_grad, da_pieces = run(
+        turn_point_kernel,
+        "turn_point",
+        (ids, keep, arrived, h, dy, gain_two, out_own, out_other),
+        [SMEM] + [VMEM] * 7,
+        (
+            struct((width, rows)),
+            struct((width, rows), jnp.float32),
+            struct(blocks),
+            struct((width, 1), jnp.float32),
+            struct((8 * q_rows, rows)),
+        ),
+        [VMEM] * 5,
+        [pltpu.VMEM((width, rows), jnp.float32)],
+        2 * width * width * rows,
+        24,
+    )
+    output = output.T.reshape(batches, cap, width)
+    legs_zero = first_leg(0, mixed_gradient)
+    turned_one = second_leg(1, legs_one, mixed_gradient)
+
+    def attend_back(mb):
+        return run(
+            functools.partial(attend_back_kernel, mb),
+            "attend_back",
+            (
+                ids,
+                flat_counts,
+                query,
+                mixed_gradient.reshape(QUERY_HEADS, HEAD_WIDTH, rows),
+                *kv_own,
+                *kv_other,
+                lse,
+                cosine,
+                sine,
+            ),
+            [SMEM, SMEM] + [VMEM] * 13,
+            [struct((QUERY_HEADS, HEAD_WIDTH, cap))] + [struct((cap, 2 * kv_width))] * 8,
+            [VMEM] * 9,
+            head_scratch
+            + [
+                pltpu.VMEM((KEY_HEADS, 8 * cap, HEAD_WIDTH), jnp.bfloat16),
+                pltpu.VMEM((KEY_HEADS, 8 * cap, HEAD_WIDTH), jnp.bfloat16),
+            ],
+            10 * pair_flops,
+            28,
+        )
+
+    def reduce_kv(own, other):
+        summed = [add_low(own[s], swap_core(other[s])) for s in (3, 2, 1, 0)][::-1]
+        total = summed[0].astype(jnp.float32)
+        for s in (3, 2, 1):
+            total = total + shift_z_down(summed[s], s).astype(jnp.float32)
+        return total
+
+    back_a = attend_back(0)
+    dkv_a = reduce_kv(back_a[1:5], back_a[5:9])
+    summed_three = add_low(home[3], legs_one[2], after(turned_one[1], back_a[0]))
+    summed_two = add_low(home[2], turned_one[0], legs_one[3])
+    turned_zero = second_leg(0, legs_zero, back_a[0])
+    hop = shift_z(summed_three, -1)
+    back_b = attend_back(1)
+    dkv_b = reduce_kv(back_b[1:5], back_b[5:9])
+    hop = shift_z(add_low(summed_two, after(hop, back_b[0])), -1)
+    summed_one = add_low(home[1], legs_zero[2], after(turned_zero[1], back_b[0]))
+    hop = shift_z(add_low(summed_one, hop), -1)
+    mlp_total = (
+        home[0].astype(jnp.float32)
+        + turned_zero[0].astype(jnp.float32)
+        + legs_zero[3].astype(jnp.float32)
+        + hop.astype(jnp.float32)
+    )
+    grad_gate = mlp_total[:half, :block].T
+    grad_up = mlp_total[half : 2 * half, :block].T
+    down_total = mlp_total[2 * half :, :block]
+    left, right = down_total[:, :q_cols], down_total[:, q_cols:]
+    stay = jnp.where(core_id == 0, left, right)
+    give = jnp.where(core_id == 0, right, left).astype(jnp.bfloat16)
+    taken = swap_core(give).astype(jnp.float32)
+    grad_down = jnp.where(
+        core_id == 0, jnp.concatenate([stay, taken], 0), jnp.concatenate([taken, stay], 0)
+    )
+
+    def reduce_all(parts):
+        mine = [add_low(parts[k], swap_core(parts[4 + k])) for k in range(4)]
+        summed = [mine[0]] + [swap_dp(mine[k], k) for k in (1, 2, 3)]
+        out = [add_low(*[piece[s] for piece in summed]) for s in range(4)]
+        total = out[0].astype(jnp.float32)
+        for s in (1, 2, 3):
+            total = total + shift_z(out[s], -s).astype(jnp.float32)
+        return total
+
+    q_results = run(
+        finish_q_kernel,
+        "finish_q",
+        (
+            ids,
+            *first_own,
+            *first_other,
+            n1,
+            attended,
+            back_a[0].reshape(width, cap),
+            back_b[0].reshape(width, cap),
+            da_pieces,
+        ),
+        [SMEM] + [VMEM] * 15,
+        [struct(blocks, jnp.float32)] + [struct((4, 2 * q_rows, wide))] * 8,
+        [VMEM] * 9,
+        [
+            pltpu.VMEM((4 * wide, rows), jnp.bfloat16),
+            pltpu.VMEM((4 * wide, rows), jnp.bfloat16),
+            pltpu.VMEM((width, rows), jnp.float32),
+            pltpu.VMEM((8 * q_rows, rows), jnp.bfloat16),
+        ],
+        6 * width * width * rows,
+        32,
+    )
+    dn_q = q_results[0]
+    q_out_total = reduce_all(q_results[1:])
+    grad_query = q_out_total[:q_cols, :block].T
+    grad_out = q_out_total[q_rows : q_rows + q_cols, :block].T
+
+    kv_results = run(
+        finish_kv_kernel,
+        "finish_kv",
+        (
+            ids,
+            *first_own,
+            *first_other,
+            n1,
+            dkv_a,
+            dkv_b,
+            cosine,
+            sine,
+            dn_q,
+            dh,
+            x,
+            gain_one,
+        ),
+        [SMEM] + [VMEM] * 19,
+        [struct((width, rows), jnp.float32), struct((width, 1), jnp.float32)]
+        + [struct((4, 2 * k_cols, wide))] * 8,
+        [VMEM] * 10,
+        [
+            pltpu.VMEM((4 * wide, rows), jnp.bfloat16),
+            pltpu.VMEM((2 * kv_width, rows), jnp.float32),
+            pltpu.VMEM((16 * k_cols, rows), jnp.bfloat16),
+        ],
+        8 * kv_width * width * rows,
+        32,
+    )
+    grad_tokens = kv_results[0].T.reshape(batches, cap, width)
+    kv_total = reduce_all(kv_results[2:])
+    gain_total = jnp.concatenate([kv_results[1], gain_two_grad], 1).T
+    gain_total = gain_total + swap_core(gain_total)
+    gain_total = (gain_total + swap_dp(gain_total, 1)) + (
+        swap_dp(gain_total, 2) + swap_dp(gain_total, 3)
+    )
+    gain_total = (gain_total + shift_z(gain_total, 2)) + (
+        shift_z(gain_total, 1) + shift_z(gain_total, -1)
+    )
+    gain_grad = lax.dynamic_slice_in_dim(gain_total, slot * q_cols, q_cols, 1)
+    return (
+        output,
+        grad_tokens,
+        grad_query,
+        kv_total[:k_cols, :block].T,
+        kv_total[k_cols:, :block].T,
+        grad_out,
+        grad_gate,
+        grad_up,
+        grad_down,
+        gain_grad,
+    )
+
+
 def solution(mesh):
     in_specs = (
         P(None, ("dp", "fsdp"), None),
@@ -375,4 +1387,6 @@
         P("dp", "fsdp"),
         P(None, "fsdp"),
     )
-    return jax.shard_map(local, mesh=mesh, in_specs=in_specs, out_specs=out_specs, check_vma=False)
+    square = mesh.shape["dp"] == 4 and mesh.shape["fsdp"] == 8
+    return jax.shard_map(
+        fast if square else local, mesh=mesh, in_specs=in_specs, out_specs=out_specs, check_vma=False)

time: 1000 us -> 466 us (0.47)
  blocking collectives: 237 us -> 0 us
  matrix products: 176 us -> 0 us
  waiting for transfers between devices: 372 us -> 199 us
  Pallas kernels: 0 us -> 104 us
  other arithmetic: 65.3 us -> 12.6 us
  starting transfers between devices: 53 us -> 80.3 us
  between operations: 17.6 us -> 2.25 us
  local copies, waits for them, and re-layouts: 73.1 us -> 58.6 us
    ppermute x0 -> x97, waiting for transfers between devices: none -> 199 us  [the longest x37 103 us: swap_dp(): return lax.ppermute(value, 'dp', [(j, j ^ mask) for j in range(4)])]
    dot_general x47 -> x0, matrix products: 176 us -> none  [the longest x14 35.5 us: times_transpose(): jnp.einsum('rk,jk->rj', left, right, preferred_element_type=jnp.float32)]
    all_gather x12 -> x0, blocking collectives: 174 us -> none  [the longest x2 34.2 us: local(): lax.all_gather(key_low, 'fsdp', axis=0, tiled=True)]
    all_gather x12 -> x0, waiting for transfers between devices: 149 us -> none  [the longest x1 78.2 us: local(): lax.all_gather(joined[9], 'fsdp', axis=0, tiled=True)]
    all_to_all x7 -> x0, waiting for transfers between devices: 129 us -> none  [the longest x1 58.3 us: local(): lax.all_to_all(joined[7], 'fsdp', split_axis=1, concat_axis=0, tiled=True)]
    pallas_call x0 -> x13, Pallas kernels: none -> 104 us  [run(): pl.pallas_call(body, out_shape=tuple(outs), in_specs=in_specs, out_specs=...]
    unnamed x28 -> x0, waiting for transfers between devices: 94.3 us -> none
    ppermute x0 -> x97, starting transfers between devices: none -> 80.3 us  [the longest x37 35 us: swap_dp(): return lax.ppermute(value, 'dp', [(j, j ^ mask) for j in range(4)])]
  transfers between devices with their start and end apart: 27 -> 97, of which waited for: 14 -> 48; matrix products, arithmetic and copies ran while one was open for 30% -> 7% of each run, Pallas kernels for 0% -> 16%
where the time goes in v2:
time: 466 us; the launch traced here: 457 us
  waiting for transfers between devices  199 us (43%)
  Pallas kernels  104 us (22%)
  starting transfers between devices  80.3 us (17%)
  local copies, waits for them, and re-layouts  58.6 us (13%)
  other arithmetic  12.6 us (3%)
    pallas_call x13, Pallas kernels, run(): pl.pallas_call(body, out_shape=tuple(outs), in_specs=in_specs, out_specs=...  104 us
    ppermute x37, waiting for transfers between devices, swap_dp(): return lax.ppermute(value, 'dp', [(j, j ^ mask) for j in range(4)])  103 us
    ppermute x18, waiting for transfers between devices, shift_z(): lax.ppermute(value, 'fsdp', [(j, (j + 2 * step) % 8) for j in range(8)])  41.3 us
    unnamed x213, local copies, waits for them, and re-layouts  35.6 us
    ppermute x37, starting transfers between devices, swap_dp(): return lax.ppermute(value, 'dp', [(j, j ^ mask) for j in range(4)])  35 us
    ppermute x6, waiting for transfers between devices, shift_z_down(): lax.ppermute(value, 'fsdp', [(j, j - 2 * step) for j in range(8) if j - 2...  33.6 us
    ppermute x18, starting transfers between devices, shift_z(): lax.ppermute(value, 'fsdp', [(j, (j + 2 * step) % 8) for j in range(8)])  19.4 us
    ppermute x3, waiting for transfers between devices, shift_z_up(): lax.ppermute(value, 'fsdp', [(j, j + 2 * step) for j in range(8) if j + 2...  14 us
  transfers between devices with their start and end apart: 97, of which 48 were waited for; matrix products, arithmetic and copies ran while one was open for 7% of the time, Pallas kernels for 16%

profile of v2, /device:TPU:0, one launch (start us, length us, event | category | flops | bytes accessed | tf_op | source)
XLA Modules:
  0.0 457.3 jit_solution(8937630183039902361)
XLA Ops:
  14.9 5.6 %collective-permute-done.2 = bf16[208,256]{1,0:T(8,128)(2,1)S(1)} collective-permute-done((bf16[208,256]{1,0:T(8,128)(2,1)S(1)}, bf16[208,256]{1,0:T(8,128)(2,1)S(1)}, u32[]{:S(2)}, u32[]{:S(2)}) %collective-permute-start.2) | collective-permute-done | bytes 106528 | tf_op jit(solution)/shard_map/ppermute | solution.py:365
  20.5 6.5 %collective-permute-done.3 = bf16[208,256]{1,0:T(8,128)(2,1)S(1)} collective-permute-done((bf16[208,256]{1,0:T(8,128)(2,1)S(1)}, bf16[208,256]{1,0:T(8,128)(2,1)S(1)}, u32[]{:S(2)}, u32[]{:S(2)}) %collective-permute-start.3) | collective-permute-done | bytes 106528 | tf_op jit(solution)/shard_map/ppermute | solution.py:365
  34.6 6.8 %collective-permute-done.10.refs_3_ = bf16[4,208,256]{2,1,0:T(8,128)(2,1)S(1)} collective-permute-done((bf16[4,208,256]{2,1,0:T(8,128)(2,1)S(1)}, bf16[4,208,256]{2,1,0:T(8,128)(2,1)S(1)}, u32[]{:S(2)}, u32[]{:S(2)}) %collective-permute-start.10) | collective-permute-done | bytes 426016 | tf_op jit(solution)/shard_map/ppermute | solution.py:361
  56.7 7.2 %collective-permute-done.5.refs_2_.refs_7_ = bf16[1088,256]{1,0:T(8,128)(2,1)S(1)} collective-permute-done((bf16[1088,256]{1,0:T(8,128)(2,1)}, bf16[1088,256]{1,0:T(8,128)(2,1)S(1)}, u32[]{:S(2)}, u32[]{:S(2)}) %collective-permute-start.5) | collective-permute-done | bytes 557088 | tf_op jit(solution)/shard_map/ppermute | solution.py:365
  76.2 6.7 %collective-permute-done.6.refs_3_.refs_8_ = bf16[1088,256]{1,0:T(8,128)(2,1)S(1)} collective-permute-done((bf16[1088,256]{1,0:T(8,128)(2,1)S(1)}, bf16[1088,256]{1,0:T(8,128)(2,1)S(1)}, u32[]{:S(2)}, u32[]{:S(2)}) %collective-permute-start.6) | collective-permute-done | bytes 557088 | tf_op jit(solution)/shard_map/ppermute | solution.py:365
  95.3 5.9 %collective-permute-done.30.refs_6_.refs_7_ = bf16[320,640]{1,0:T(8,128)(2,1)} collective-permute-done((bf16[320,640]{1,0:T(8,128)(2,1)}, bf16[320,640]{1,0:T(8,128)(2,1)}, u32[]{:S(2)}, u32[]{:S(2)}) %collective-permute-start.30) | collective-permute-done | bytes 409632 | tf_op jit(solution)/shard_map/ppermute | solution.py:369
  103.3 7.1 %collective-permute-done.22.refs_8_.refs_13_ = bf16[1088,256]{1,0:T(8,128)(2,1)S(1)} collective-permute-done((bf16[1088,256]{1,0:T(8,128)(2,1)}, bf16[1088,256]{1,0:T(8,128)(2,1)S(1)}, u32[]{:S(2)}, u32[]{:S(2)}) %collective-permute-start.22) | collective-permute-done | bytes 557088 | tf_op jit(solution)/shard_map/ppermute | solution.py:361
  111.3 11.0 %collective-permute-done.26.refs_12_.refs_17_ = bf16[1088,256]{1,0:T(8,128)(2,1)S(1)} collective-permute-done((bf16[1088,256]{1,0:T(8,128)(2,1)S(1)}, bf16[1088,256]{1,0:T(8,128)(2,1)S(1)}, u32[]{:S(2)}, u32[]{:S(2)}) %collective-permute-start.26) | collective-permute-done | bytes 557088 | tf_op jit(solution)/shard_map/ppermute | solution.py:361
  122.8 11.4 %collective-permute-done.24.refs_10_.refs_15_ = bf16[1088,256]{1,0:T(8,128)(2,1)S(1)} collective-permute-done((bf16[1088,256]{1,0:T(8,128)(2,1)S(1)}, bf16[1088,256]{1,0:T(8,128)(2,1)S(1)}, u32[]{:S(2)}, u32[]{:S(2)}) %collective-permute-start.24) | collective-permute-done | bytes 557088 | tf_op jit(solution)/shard_map/ppermute | solution.py:361
  134.3 6.6 %collective-permute-done.29.refs_14_.refs_19_ = bf16[1088,256]{1,0:T(8,128)(2,1)S(1)} collective-permute-done((bf16[1088,256]{1,0:T(8,128)(2,1)S(1)}, bf16[1088,256]{1,0:T(8,128)(2,1)S(1)}, u32[]{:S(2)}, u32[]{:S(2)}) %collective-permute-start.29) | collective-permute-done | bytes 557088 | tf_op jit(solution)/shard_map/ppermute | solution.py:361
  148.7 18.3 %attend.1 = (bf16[15,64,320]{2,1,0:T(8,128)(2,1)S(1)}, f32[10,1,480]{2,1,0:T(1,128)S(1)}) custom-call(s32[4]{0:T(128)S(1)} %pad_add_fusion.ids_ref.refs_0_, s32[16]{0:T(128)S(1)} %reshape.200.refs_1_, bf16[15,64,320]{2,1,0:T(8,128)(2,1)S(1)} %copy-done.72, bf16[320,640]{1,0:T(8,128)(2,1)} %get-tuple-element.100.refs_3_.refs_4_, ...), custom_call_target="tpu_custom_call" | custom-call | flops 6291456000 | bytes 4524880 | tf_op jit(solution)/shard_map/attend/pallas_call | solution.py:409
  179.3 30.4 %mlp.1 = (f32[2,960,320]{2,1,0:T(8,128)}, bf16[2,960,320]{2,1,0:T(8,128)(2,1)}, bf16[960,256]{1,0:T(8,128)(2,1)}, bf16[960,256]{1,0:T(8,128)(2,1)}, bf16[960,256...) custom-call(s32[4]{0:T(128)} %copy-done.68, ...), custom_call_target="tpu_custom_call" | custom-call | flops 14155776000 | bytes 22921232 | tf_op jit(solution)/shard_map/mlp/pallas_call | solution.py:409
  237.0 14.9 %attend_back.3 = (bf16[15,64,160]{2,1,0:T(8,128)(2,1)S(1)}, bf16[160,640]{1,0:T(8,128)(2,1)S(1)}, bf16[160,640]{1,0:T(8,128)(2,1)S(1)}, bf16[160,640]{1,0:T(8,12...) custom-call(s32[4]{0:T(128)S(1)} %copy-done.69, ...), custom_call_target="tpu_custom_call" | custom-call | flops 7864320000 | bytes 6552400 | tf_op jit(solution)/shard_map/attend_back/pallas_call | solution.py:409
  253.1 15.1 %attend_back.2 = (bf16[15,64,160]{2,1,0:T(8,128)(2,1)S(1)}, bf16[160,640]{1,0:T(8,128)(2,1)S(1)}, bf16[160,640]{1,0:T(8,128)(2,1)S(1)}, bf16[160,640]{1,0:T(8,12...) custom-call(s32[4]{0:T(128)S(1)} %copy-done.69, ...), custom_call_target="tpu_custom_call" | custom-call | flops 7864320000 | bytes 6552400 | tf_op jit(solution)/shard_map/attend_back/pallas_call | solution.py:409
  268.2 6.0 %finish_q.1 = (f32[4,240,320]{2,1,0:T(8,128)S(1)}, bf16[4,256,256]{2,1,0:T(8,128)(2,1)S(1)}, bf16[4,256,256]{2,1,0:T(8,128)(2,1)S(1)}, bf16[4,256,256]{2,1,0:T(8...) custom-call(s32[4]{0:T(128)S(1)} %copy-done.69, ...), custom_call_target="tpu_custom_call" | custom-call | flops 1769472000 | bytes 11329552 | tf_op jit(solution)/shard_map/finish_q/pallas_call | solution.py:409
  281.3 7.6 %collective-permute-done.49 = bf16[160,640]{1,0:T(8,128)(2,1)S(1)} collective-permute-done((bf16[160,640]{1,0:T(8,128)(2,1)S(1)}, bf16[160,640]{1,0:T(8,128)(2,1)S(1)}, u32[]{:S(2)}, u32[]{:S(2)}) %collective-permute-start.49) | collective-permute-done | bytes 204832 | tf_op jit(solution)/shard_map/ppermute | solution.py:373
  290.2 7.5 %collective-permute-done.51 = bf16[160,640]{1,0:T(8,128)(2,1)S(1)} collective-permute-done((bf16[160,640]{1,0:T(8,128)(2,1)S(1)}, bf16[160,640]{1,0:T(8,128)(2,1)S(1)}, u32[]{:S(2)}, u32[]{:S(2)}) %collective-permute-start.51) | collective-permute-done | bytes 204832 | tf_op jit(solution)/shard_map/ppermute | solution.py:373
  302.1 12.6 %collective-permute-done.44 = bf16[160,640]{1,0:T(8,128)(2,1)S(1)} collective-permute-done((bf16[160,640]{1,0:T(8,128)(2,1)S(1)}, bf16[160,640]{1,0:T(8,128)(2,1)S(1)}, u32[]{:S(2)}, u32[]{:S(2)}) %collective-permute-start.44) | collective-permute-done | bytes 204832 | tf_op jit(solution)/shard_map/ppermute | solution.py:373
  339.4 7.1 %collective-permute-done.92 = f32[2,960]{1,0:T(2,128)S(1)} collective-permute-done((f32[2,960]{1,0:T(2,128)S(1)}, f32[2,960]{1,0:T(2,128)S(1)}, u32[]{:S(2)}, u32[]{:S(2)}) %collective-permute-start.92) | collective-permute-done | bytes 7712 | tf_op jit(solution)/shard_map/ppermute | solution.py:361
  363.2 8.3 %collective-permute-done.74 = bf16[960,256]{1,0:T(8,128)(2,1)} collective-permute-done((bf16[960,256]{1,0:T(8,128)(2,1)}, bf16[960,256]{1,0:T(8,128)(2,1)}, u32[]{:S(2)}, u32[]{:S(2)}) %collective-permute-start.74) | collective-permute-done | bytes 491552 | tf_op jit(solution)/shard_map/ppermute | solution.py:361
  384.8 5.9 %collective-permute-done.70 = bf16[4,80,256]{2,1,0:T(8,128)(2,1)S(1)} collective-permute-done((bf16[4,80,256]{2,1,0:T(8,128)(2,1)S(1)}, bf16[4,80,256]{2,1,0:T(8,128)(2,1)S(1)}, u32[]{:S(2)}, u32[]{:S(2)}) %collective-permute-start.70) | collective-permute-done | bytes 163872 | tf_op jit(solution)/shard_map/ppermute | solution.py:361
  394.0 8.3 %collective-permute-done.81 = bf16[960,256]{1,0:T(8,128)(2,1)S(1)} collective-permute-done((bf16[960,256]{1,0:T(8,128)(2,1)S(1)}, bf16[960,256]{1,0:T(8,128)(2,1)S(1)}, u32[]{:S(2)}, u32[]{:S(2)}) %collective-permute-start.81) | collective-permute-done | bytes 491552 | tf_op jit(solution)/shard_map/ppermute | solution.py:361
  417.8 7.6 %collective-permute-done.58 = bf16[4,256,256]{2,1,0:T(8,128)(2,1)S(1)} collective-permute-done((bf16[4,256,256]{2,1,0:T(8,128)(2,1)S(1)}, bf16[4,256,256]{2,1,0:T(8,128)(2,1)S(1)}, u32[]{:S(2)}, u32[]{:S(2)}) %collective-permute-start.58) | collective-permute-done | bytes 524320 | tf_op jit(solution)/shard_map/ppermute | solution.py:361
  431.5 7.5 %collective-permute-done.77 = bf16[960,256]{1,0:T(8,128)(2,1)S(1)} collective-permute-done((bf16[960,256]{1,0:T(8,128)(2,1)S(1)}, bf16[960,256]{1,0:T(8,128)(2,1)S(1)}, u32[]{:S(2)}, u32[]{:S(2)}) %collective-permute-start.77) | collective-permute-done | bytes 491552 | tf_op jit(solution)/shard_map/ppermute | solution.py:361
  (472 shorter events, 223.3 us)
Async XLA Ops:
  65.6 26.8 %collective-permute-start.19 = (bf16[1088,256]{1,0:T(8,128)(2,1)S(1)}, bf16[1088,256]{1,0:T(8,128)(2,1)S(1)}, u32[]{:S(2)}, u32[]{:S(2)}) collective-permute-start(bf16[1088,256]{1,0:T(8,128)(2,1)S(1)} %collective-permute-done.5.refs_2_.refs_7_), channel_id=1, source_target_pairs={{0,8},{8,0},{16,24},{24,16},{1,9},{9,1},{17,25},{25,17},{2,10},{10... | collective-permute-start | bytes 1671176 | tf_op jit(solution)/shard_map/ppermute | solution.py:361
  83.3 27.1 %collective-permute-start.22 = (bf16[1088,256]{1,0:T(8,128)(2,1)}, bf16[1088,256]{1,0:T(8,128)(2,1)S(1)}, u32[]{:S(2)}, u32[]{:S(2)}) collective-permute-start(bf16[1088,256]{1,0:T(8,128)(2,1)} %pack_mlp.1.refs_0_.refs_5_), channel_id=1, source_target_pairs={{0,16},{8,24},{16,0},{24,8},{1,17},{9,25},{17,1},{25,9},{2,18},{10... | collective-permute-start | bytes 1671176 | tf_op jit(solution)/shard_map/ppermute | solution.py:361
  84.9 26.0 %collective-permute-start.12 = (bf16[1088,256]{1,0:T(8,128)(2,1)}, bf16[1088,256]{1,0:T(8,128)(2,1)S(1)}, u32[]{:S(2)}, u32[]{:S(2)}) collective-permute-start(bf16[1088,256]{1,0:T(8,128)(2,1)} %collective-permute-done.4.refs_1_.refs_6_), channel_id=1, source_target_pairs={{0,8},{8,0},{16,24},{24,16},{1,9},{9,1},{17,25},{25,17},{2,10},{10... | collective-permute-start | bytes 1671176 | tf_op jit(solution)/shard_map/ppermute | solution.py:361
  89.5 32.8 %collective-permute-start.26 = (bf16[1088,256]{1,0:T(8,128)(2,1)S(1)}, bf16[1088,256]{1,0:T(8,128)(2,1)S(1)}, u32[]{:S(2)}, u32[]{:S(2)}) collective-permute-start(bf16[1088,256]{1,0:T(8,128)(2,1)S(1)} %collective-permute-done.7.refs_4_.refs_9_), channel_id=1, source_target_pairs={{0,16},{8,24},{16,0},{24,8},{1,17},{9,25},{17,1},{25,9},{2,18},{10... | collective-permute-start | bytes 1671176 | tf_op jit(solution)/shard_map/ppermute | solution.py:361
  101.3 32.9 %collective-permute-start.24 = (bf16[1088,256]{1,0:T(8,128)(2,1)S(1)}, bf16[1088,256]{1,0:T(8,128)(2,1)S(1)}, u32[]{:S(2)}, u32[]{:S(2)}) collective-permute-start(bf16[1088,256]{1,0:T(8,128)(2,1)S(1)} %collective-permute-done.5.refs_2_.refs_7_), channel_id=1, source_target_pairs={{0,16},{8,24},{16,0},{24,8},{1,17},{9,25},{17,1},{25,9},{2,18},{10... | collective-permute-start | bytes 1671176 | tf_op jit(solution)/shard_map/ppermute | solution.py:361
  102.7 31.5 %collective-permute-start.27 = (bf16[1088,256]{1,0:T(8,128)(2,1)S(1)}, bf16[1088,256]{1,0:T(8,128)(2,1)S(1)}, u32[]{:S(2)}, u32[]{:S(2)}) collective-permute-start(bf16[1088,256]{1,0:T(8,128)(2,1)S(1)} %collective-permute-done.23.refs_9_.refs_14_), channel_id=1, source_target_pairs={{0,8},{8,0},{16,24},{24,16},{1,9},{9,1},{17,25},{25,17},{2,10},{10... | collective-permute-start | bytes 1671176 | tf_op jit(solution)/shard_map/ppermute | solution.py:361
  110.4 23.9 %collective-permute-start.21 = (bf16[1088,256]{1,0:T(8,128)(2,1)S(1)}, bf16[1088,256]{1,0:T(8,128)(2,1)S(1)}, u32[]{:S(2)}, u32[]{:S(2)}) collective-permute-start(bf16[1088,256]{1,0:T(8,128)(2,1)S(1)} %collective-permute-done.6.refs_3_.refs_8_), channel_id=1, source_target_pairs={{0,8},{8,0},{16,24},{24,16},{1,9},{9,1},{17,25},{25,17},{2,10},{10... | collective-permute-start | bytes 1671176 | tf_op jit(solution)/shard_map/ppermute | solution.py:361
  110.9 29.9 %collective-permute-start.29 = (bf16[1088,256]{1,0:T(8,128)(2,1)S(1)}, bf16[1088,256]{1,0:T(8,128)(2,1)S(1)}, u32[]{:S(2)}, u32[]{:S(2)}) collective-permute-start(bf16[1088,256]{1,0:T(8,128)(2,1)S(1)} %collective-permute-done.19.refs_6_.refs_11_), channel_id=1, source_target_pairs={{0,16},{8,24},{16,0},{24,8},{1,17},{9,25},{17,1},{25,9},{2,18},{10... | collective-permute-start | bytes 1671176 | tf_op jit(solution)/shard_map/ppermute | solution.py:361
  142.2 24.8 %collective-permute-start.32 = (bf16[4,128,1024]{2,1,0:T(8,128)(2,1)S(1)}, bf16[4,128,1024]{2,1,0:T(8,128)(2,1)}, u32[]{:S(2)}, u32[]{:S(2)}) collective-permute-start(bf16[4,128,1024]{2,1,0:T(8,128)(2,1)S(1)} %collect.1.own_ref), channel_id=1, source_target_pairs={{0,1},{1,0},{2,3},{3,2},{4,5},{5,4},{6,7},{7,6},{8,9},{9,8},{10,11... | collective-permute-start | bytes 3145736 | tf_op jit(solution)/shard_map/ppermute | solution.py:357
  145.9 28.8 %collective-permute-start.38 = (bf16[960,320]{0,1:T(8,128)(2,1)}, bf16[960,320]{0,1:T(8,128)(2,1)}, u32[]{:S(2)}, u32[]{:S(2)}) collective-permute-start(bf16[960,320]{0,1:T(8,128)(2,1)} %copy.86), channel_id=1, source_target_pairs={{0,1},{1,0},{2,3},{3,2},{4,5},{5,4},{6,7},{7,6},{8,9},{9,8},{10,11... | collective-permute-start | bytes 1843208 | tf_op jit(solution)/shard_map/ppermute | solution.py:357
  212.5 121.2 %collective-permute-start.84 = (bf16[960,256]{1,0:T(8,128)(2,1)}, bf16[960,256]{1,0:T(8,128)(2,1)}, u32[]{:S(2)}, u32[]{:S(2)}) collective-permute-start(bf16[960,256]{1,0:T(8,128)(2,1)} %get-tuple-element.178), channel_id=1, source_target_pairs={{0,8},{8,0},{16,24},{24,16},{1,9},{9,1},{17,25},{25,17},{2,10},{10... | collective-permute-start | bytes 1474568 | tf_op jit(solution)/shard_map/ppermute | solution.py:361
  251.8 29.0 %collective-permute-start.47 = (bf16[160,640]{1,0:T(8,128)(2,1)S(1)}, bf16[160,640]{1,0:T(8,128)(2,1)S(1)}, u32[]{:S(2)}, u32[]{:S(2)}) collective-permute-start(bf16[160,640]{1,0:T(8,128)(2,1)S(1)} %get-tuple-element.126), channel_id=1, source_target_pairs={{0,1},{1,0},{2,3},{3,2},{4,5},{5,4},{6,7},{7,6},{8,9},{9,8},{10,11... | collective-permute-start | bytes 614408 | tf_op jit(solution)/shard_map/ppermute | solution.py:357
  252.2 22.9 %collective-permute-start.48 = (bf16[160,640]{1,0:T(8,128)(2,1)S(1)}, bf16[160,640]{1,0:T(8,128)(2,1)S(1)}, u32[]{:S(2)}, u32[]{:S(2)}) collective-permute-start(bf16[160,640]{1,0:T(8,128)(2,1)S(1)} %get-tuple-element.128), channel_id=1, source_target_pairs={{0,1},{1,0},{2,3},{3,2},{4,5},{5,4},{6,7},{7,6},{8,9},{9,8},{10,11... | collective-permute-start | bytes 614408 | tf_op jit(solution)/shard_map/ppermute | solution.py:357
  252.4 23.3 %collective-permute-start.50 = (bf16[160,640]{1,0:T(8,128)(2,1)S(1)}, bf16[160,640]{1,0:T(8,128)(2,1)S(1)}, u32[]{:S(2)}, u32[]{:S(2)}) collective-permute-start(bf16[160,640]{1,0:T(8,128)(2,1)S(1)} %get-tuple-element.130), channel_id=1, source_target_pairs={{0,1},{1,0},{2,3},{3,2},{4,5},{5,4},{6,7},{7,6},{8,9},{9,8},{10,11... | collective-permute-start | bytes 614408 | tf_op jit(solution)/shard_map/ppermute | solution.py:357
  252.8 23.1 %collective-permute-start.52 = (bf16[160,640]{1,0:T(8,128)(2,1)S(1)}, bf16[160,640]{1,0:T(8,128)(2,1)S(1)}, u32[]{:S(2)}, u32[]{:S(2)}) collective-permute-start(bf16[160,640]{1,0:T(8,128)(2,1)S(1)} %get-tuple-element.132), channel_id=1, source_target_pairs={{0,1},{1,0},{2,3},{3,2},{4,5},{5,4},{6,7},{7,6},{8,9},{9,8},{10,11... | collective-permute-start | bytes 614408 | tf_op jit(solution)/shard_map/ppermute | solution.py:357
  333.1 27.8 %collective-permute-start.83 = (bf16[960,256]{1,0:T(8,128)(2,1)}, bf16[960,256]{1,0:T(8,128)(2,1)}, u32[]{:S(2)}, u32[]{:S(2)}) collective-permute-start(bf16[960,256]{1,0:T(8,128)(2,1)} %get-tuple-element.176), channel_id=1, source_target_pairs={{0,8},{8,0},{16,24},{24,16},{1,9},{9,1},{17,25},{25,17},{2,10},{10... | collective-permute-start | bytes 1474568 | tf_op jit(solution)/shard_map/ppermute | solution.py:361
  358.4 32.7 %collective-permute-start.82 = (bf16[960,256]{1,0:T(8,128)(2,1)}, bf16[960,256]{1,0:T(8,128)(2,1)S(1)}, u32[]{:S(2)}, u32[]{:S(2)}) collective-permute-start(bf16[960,256]{1,0:T(8,128)(2,1)} %get-tuple-element.174), channel_id=1, source_target_pairs={{0,16},{8,24},{16,0},{24,8},{1,17},{9,25},{17,1},{25,9},{2,18},{10... | collective-permute-start | bytes 1474568 | tf_op jit(solution)/shard_map/ppermute | solution.py:361
  363.1 28.8 %collective-permute-start.59 = (bf16[4,256,256]{2,1,0:T(8,128)(2,1)S(1)}, bf16[4,256,256]{2,1,0:T(8,128)(2,1)S(1)}, u32[]{:S(2)}, u32[]{:S(2)}) collective-permute-start(bf16[4,256,256]{2,1,0:T(8,128)(2,1)S(1)} %copy-done.81), channel_id=1, source_target_pairs={{0,1},{1,0},{2,3},{3,2},{4,5},{5,4},{6,7},{7,6},{8,9},{9,8},{10,11... | collective-permute-start | bytes 1572872 | tf_op jit(solution)/shard_map/ppermute | solution.py:357
  402.6 22.7 %collective-permute-start.58 = (bf16[4,256,256]{2,1,0:T(8,128)(2,1)S(1)}, bf16[4,256,256]{2,1,0:T(8,128)(2,1)S(1)}, u32[]{:S(2)}, u32[]{:S(2)}) collective-permute-start(bf16[4,256,256]{2,1,0:T(8,128)(2,1)S(1)} %add_convert_fusion.1), channel_id=1, source_target_pairs={{0,16},{8,24},{16,0},{24,8},{1,17},{9,25},{17,1},{25,9},{2,18},{10... | collective-permute-start | bytes 1572872 | tf_op jit(solution)/shard_map/ppermute | solution.py:361
  403.2 26.9 %collective-permute-start.60 = (bf16[4,256,256]{2,1,0:T(8,128)(2,1)S(1)}, bf16[4,256,256]{2,1,0:T(8,128)(2,1)S(1)}, u32[]{:S(2)}, u32[]{:S(2)}) collective-permute-start(bf16[4,256,256]{2,1,0:T(8,128)(2,1)S(1)} %add_convert_fusion), channel_id=1, source_target_pairs={{0,24},{8,16},{16,8},{24,0},{1,25},{9,17},{17,9},{25,1},{2,26},{10... | collective-permute-start | bytes 1572872 | tf_op jit(solution)/shard_map/ppermute | solution.py:361
  410.8 28.2 %collective-permute-start.77 = (bf16[960,256]{1,0:T(8,128)(2,1)S(1)}, bf16[960,256]{1,0:T(8,128)(2,1)S(1)}, u32[]{:S(2)}, u32[]{:S(2)}) collective-permute-start(bf16[960,256]{1,0:T(8,128)(2,1)S(1)} %copy-done.101), channel_id=1, source_target_pairs={{0,8},{8,0},{16,24},{24,16},{1,9},{9,1},{17,25},{25,17},{2,10},{10... | collective-permute-start | bytes 1474568 | tf_op jit(solution)/shard_map/ppermute | solution.py:361
  411.1 29.9 %collective-permute-start.87 = (bf16[960,256]{1,0:T(8,128)(2,1)S(1)}, bf16[960,256]{1,0:T(8,128)(2,1)S(1)}, u32[]{:S(2)}, u32[]{:S(2)}) collective-permute-start(bf16[960,256]{1,0:T(8,128)(2,1)S(1)} %add_convert_fusion.5), channel_id=1, source_target_pairs={{0,6},{1,7},{2,0},{3,1},{4,2},{5,3},{6,4},{7,5},{8,14},{9,15},{10,... | collective-permute-start | bytes 1474568 | tf_op jit(solution)/shard_map/ppermute | solution.py:365
  417.2 35.0 %collective-permute-start.76 = (bf16[960,256]{1,0:T(8,128)(2,1)}, bf16[960,256]{1,0:T(8,128)(2,1)S(1)}, u32[]{:S(2)}, u32[]{:S(2)}) collective-permute-start(bf16[960,256]{1,0:T(8,128)(2,1)} %get-tuple-element.161), channel_id=1, source_target_pairs={{0,16},{8,24},{16,0},{24,8},{1,17},{9,25},{17,1},{25,9},{2,18},{10... | collective-permute-start | bytes 1474568 | tf_op jit(solution)/shard_map/ppermute | solution.py:361
  425.3 26.9 %collective-permute-start.75 = (bf16[960,256]{1,0:T(8,128)(2,1)S(1)}, bf16[960,256]{1,0:T(8,128)(2,1)S(1)}, u32[]{:S(2)}, u32[]{:S(2)}) collective-permute-start(bf16[960,256]{1,0:T(8,128)(2,1)S(1)} %add_convert_fusion.12), channel_id=1, source_target_pairs={{0,8},{8,0},{16,24},{24,16},{1,9},{9,1},{17,25},{25,17},{2,10},{10... | collective-permute-start | bytes 1474568 | tf_op jit(solution)/shard_map/ppermute | solution.py:361
  (175 other events, 2097.0 us)

commit v3 on v2

--- a/solution.py
+++ b/solution.py
@@ -477,14 +477,18 @@
 
 def turn_in_kernel(x_ref, dy_ref, xt_ref, dyt_ref):
     xt_ref[...] = x_ref[...].astype(jnp.float32).T.astype(jnp.bfloat16)
-    dyt_ref[...] = dy_ref[...].astype(jnp.float32).T.astype(jnp.bfloat16)
-
-
-def fill_relative(ids_ref, source_ref, target_ref):
-    block, lanes = source_ref.shape[1:]
+    dyt_ref[...] = jnp.zeros_like(dyt_ref)
+    dyt_ref[:, : dy_ref.shape[0]] = dy_ref[...].astype(jnp.float32).T.astype(jnp.bfloat16)
+
+
+def fill_relative(ids_ref, target_ref, *sources):
+    block, lanes = sources[0].shape[1], target_ref.shape[1]
     wide = target_ref.shape[0] // 4
     for k in range(4):
-        target_ref[k * wide : k * wide + block, :] = source_ref[ids_ref[0] ^ k]
+        parts = [source[ids_ref[0] ^ k] for source in sources]
+        target_ref[k * wide : k * wide + block, :] = (
+            parts[0] if len(parts) == 1 else jnp.concatenate(parts, 1)
+        )
         target_ref[k * wide + block : (k + 1) * wide, :] = jnp.zeros(
             (wide - block, lanes), target_ref.dtype
         )
@@ -505,7 +509,7 @@
     kv_width = KEY_HEADS * HEAD_WIDTH
     q_cols, k_cols = width // 8, kv_width // 8
     depth = own[0].shape[1]
-    fill_relative(ids_ref, n1_ref, rel_ref)
+    fill_relative(ids_ref, rel_ref, n1_ref)
     for core_rel, weights in ((0, own), (1, other)):
         for s in range(4):
             f = column_index(ids_ref, core_rel, s)
@@ -582,31 +586,28 @@
     )
 
 
-def attend_kernel(*refs):
+def attend_kernel(mb, *refs):
     ids_ref, counts_ref, q_ref = refs[:3]
     blocks = refs[3:11]
     att_ref, lse_ref, k_ref, v_ref, bias_ref = refs[11:]
     cap = q_ref.shape[2] // 2
     share = QUERY_HEADS // KEY_HEADS
-    for mb in range(2):
-        stage_heads(mb, cap, blocks, k_ref, v_ref)
-        stage_bias(ids_ref, counts_ref, mb, cap, share, bias_ref)
-
-        def body(n, carry, mb=mb):
-            scores = product_nn(k_ref[n], join_heads(q_ref, n, share, mb, cap)) + bias_ref[...]
-            top = jnp.max(scores, 0, keepdims=True)
-            exponent = jnp.exp(scores - top)
-            total = jnp.sum(exponent, 0, keepdims=True)
-            mixed = product_tn(v_ref[n], exponent.astype(jnp.bfloat16)) / total
-            mixed = mixed.astype(jnp.bfloat16)
-            for g in range(share):
-                att_ref[share * n + g, :, mb * cap : (mb + 1) * cap] = mixed[
-                    :, g * cap : (g + 1) * cap
-                ]
-            lse_ref[mb * KEY_HEADS + n] = top + jnp.log(total)
-            return carry
-
-        lax.fori_loop(0, KEY_HEADS, body, 0)
+    stage_heads(mb, cap, blocks, k_ref, v_ref)
+    stage_bias(ids_ref, counts_ref, mb, cap, share, bias_ref)
+
+    def body(n, carry):
+        scores = product_nn(k_ref[n], join_heads(q_ref, n, share, mb, cap)) + bias_ref[...]
+        top = jnp.max(scores, 0, keepdims=True)
+        exponent = jnp.exp(scores - top)
+        total = jnp.sum(exponent, 0, keepdims=True)
+        mixed = product_tn(v_ref[n], exponent.astype(jnp.bfloat16)) / total
+        mixed = mixed.astype(jnp.bfloat16)
+        for g in range(share):
+            att_ref[share * n + g] = mixed[:, g * cap : (g + 1) * cap]
+        lse_ref[n] = top + jnp.log(total)
+        return carry
+
+    lax.fori_loop(0, KEY_HEADS, body, 0)
 
 
 def attend_back_kernel(mb, *refs):
@@ -628,7 +629,7 @@
         query = join_heads(q_ref, n, share, mb, cap)
         grad = join_heads(do_ref, n, share, mb, cap)
         keys = k_ref[n]
-        prob = jnp.exp(product_nn(keys, query) + bias_ref[...] - lse_ref[mb * KEY_HEADS + n])
+        prob = jnp.exp(product_nn(keys, query) + bias_ref[...] - lse_ref[n])
         dprob = product_nn(v_ref[n], grad)
         delta = jnp.sum(prob * dprob, 0, keepdims=True)
         dscore = (prob * (dprob - delta)).astype(jnp.bfloat16)
@@ -671,16 +672,19 @@
         copy.wait()
 
 
-def hidden_kernel(ids_ref, own_ref, other_ref, att_ref, x_ref, gain_ref, h_ref, n2_ref, rel_ref):
-    q_cols = h_ref.shape[0] // 8
-    fill_relative(ids_ref, att_ref, rel_ref)
+def hidden_kernel(
+    ids_ref, own_ref, other_ref, att_a_ref, att_b_ref, x_ref, gain_ref, h_ref, n2_ref, rel_ref
+):
+    q_cols, rows = h_ref.shape[0] // 8, h_ref.shape[1]
+    fill_relative(ids_ref, rel_ref, att_a_ref, att_b_ref)
     for core_rel, w_ref in ((0, own_ref), (1, other_ref)):
         for s in range(4):
             f = column_index(ids_ref, core_rel, s)
             h_ref[start_row(f, q_cols), :] = product_nn(w_ref[s], rel_ref[...])[:q_cols]
     h = h_ref[...] + x_ref[...].astype(jnp.float32)
     h_ref[...] = h
-    n2_ref[...] = (h * mean_square(h) * gain_ref[...]).astype(jnp.bfloat16)
+    n2_ref[...] = jnp.zeros_like(n2_ref)
+    n2_ref[:, :rows] = (h * mean_square(h) * gain_ref[...]).astype(jnp.bfloat16)
 
 
 def turn_point_kernel(
@@ -704,13 +708,15 @@
     block = do_ref.shape[1]
     wide = own_ref.shape[2] // 4
     h = h_ref[...]
-    out_ref[...] = (h + parts_ref[0] + arrived_ref[0].astype(jnp.float32)).astype(jnp.bfloat16)
-    dn = parts_ref[1] + arrived_ref[1].astype(jnp.float32)
+    out_ref[...] = (h + parts_ref[0] + arrived_ref[0, :, :rows].astype(jnp.float32)).astype(
+        jnp.bfloat16
+    )
+    dn = parts_ref[1] + arrived_ref[1, :, :rows].astype(jnp.float32)
     rms = mean_square(h)
     gain_grad_ref[...] = jnp.sum(dn * h * rms, 1, keepdims=True)
     weighted = dn * gain_ref[...]
     dh = (
-        dy_ref[...].astype(jnp.float32)
+        dy_ref[:, :rows].astype(jnp.float32)
         + rms * weighted
         - h * (rms * rms * rms * jnp.mean(weighted * h, 0, keepdims=True))
     )
@@ -736,11 +742,25 @@
             ).astype(jnp.bfloat16)
 
 
+def out_grad_kernel(ids_ref, att_a_ref, att_b_ref, pieces_ref, *refs):
+    grads, att_rel = refs[:8], refs[8]
+    depth = pieces_ref.shape[0] // 8
+    wide = att_rel.shape[0] // 4
+    fill_relative(ids_ref, att_rel, att_a_ref, att_b_ref)
+    for core_rel in range(2):
+        for s in range(4):
+            low = (core_rel * 4 + s) * depth
+            got = product_nt(pieces_ref[low : low + depth, :], att_rel[...]).astype(jnp.bfloat16)
+            for k in range(4):
+                grads[core_rel * 4 + k][s] = got[:, k * wide : (k + 1) * wide]
+
+
 def finish_q_kernel(*refs):
     ids_ref, own, other = refs[0], refs[1:6], refs[6:11]
-    n1_ref, att_ref, dq_a_ref, dq_b_ref, pieces_ref, dn_ref = refs[11:17]
-    grads = refs[17:25]
-    n1_rel, att_rel, d_ref, dq_ref = refs[25:]
+    n1_ref, dq_a_ref, dq_b_ref = refs[11:14]
+    out_grads = refs[14:22]
+    dn_ref, grads = refs[22], refs[23:31]
+    n1_rel, d_ref, dq_ref = refs[31:]
     cap = dq_a_ref.shape[1]
     width = dq_a_ref.shape[0]
     q_cols = width // 8
@@ -750,8 +770,7 @@
     d_ref[:, :cap] = dq_a_ref[...].astype(jnp.float32)
     d_ref[:, cap:] = dq_b_ref[...].astype(jnp.float32)
     spread(ids_ref, d_ref, dq_ref, q_cols)
-    fill_relative(ids_ref, n1_ref, n1_rel)
-    fill_relative(ids_ref, att_ref, att_rel)
+    fill_relative(ids_ref, n1_rel, n1_ref)
     weights = jnp.concatenate(
         [wide_rows(w, s, 0, depth) for w in (own, other) for s in range(4)], 0
     )
@@ -762,11 +781,10 @@
         for s in range(4):
             low = (core_rel * 4 + s) * depth
             gq = product_nt(dq_ref[low : low + depth, :], n1_rel[...]).astype(jnp.bfloat16)
-            go = product_nt(pieces_ref[low : low + depth, :], att_rel[...]).astype(jnp.bfloat16)
             for k in range(4):
                 target = grads[core_rel * 4 + k]
                 target[s, :depth, :] = gq[:, k * wide : (k + 1) * wide]
-                target[s, depth:, :] = go[:, k * wide : (k + 1) * wide]
+                target[s, depth:, :] = out_grads[core_rel * 4 + k][s]
 
 
 def finish_kv_kernel(*refs):
@@ -802,7 +820,7 @@
                 ],
                 0,
             ).astype(jnp.bfloat16)
-    fill_relative(ids_ref, n1_ref, n1_rel)
+    fill_relative(ids_ref, n1_rel, n1_ref)
     low = q_cols + 8
     weights = jnp.concatenate(
         [wide_rows(w, s, low, low + 2 * k_cols) for w in (own, other) for s in range(4)], 0
@@ -836,123 +854,102 @@
     pieces = refs[5:21]
     keep_ref, send_ref = refs[21:23]
     grads = refs[23:39]
-    wgu, wdn, ggu, gdn, gu_ref, prod_ref, dgu_ref, n2_rel, dy_rel, sem_in, sem_out = refs[39:]
+    wgu, wdn, gu_ref, prod_ref, dgu_ref, n2_rel, dy_rel, sem_in, sem_out = refs[39:]
     dp_id = ids_ref[0]
     z_id = ids_ref[1]
-    block, rows = n2_own.shape[1:]
+    block, rows = keep_ref.shape[1] // 4, keep_ref.shape[2]
     pair = 2 * rows
     wide = pieces[0].shape[1]
     half = prod_ref.shape[0] // 4
-    loads = []
+
+    def gate_up_part(ref, piece, k, s):
+        return piece.at[pl.ds(0, 2 * half)], ref.at[
+            pl.ds(s * 2 * half, 2 * half), pl.ds(k * wide, wide)
+        ]
+
+    def down_part(ref, piece, k, s):
+        return piece.at[pl.ds(2 * half, half)], ref.at[
+            pl.ds(k * half, half), pl.ds(s * wide, wide)
+        ]
+
+    loads, more_loads = [], []
     for s in range(4):
         for k in range(4):
-            piece = pieces[k * 4 + s]
-            lanes = pl.ds(k * wide, wide)
-            loads.append(
-                pltpu.make_async_copy(
-                    piece.at[pl.ds(0, 2 * half)],
-                    wgu.at[pl.ds(s * 2 * half, 2 * half), lanes],
-                    sem_in.at[0, k * 4 + s],
-                )
-            )
-    for k in range(4):
-        for s in range(4):
-            loads.append(
-                pltpu.make_async_copy(
-                    pieces[k * 4 + s].at[pl.ds(2 * half, half)],
-                    wdn.at[pl.ds(k * half, half), pl.ds(s * wide, wide)],
-                    sem_in.at[1, k * 4 + s],
-                )
-            )
-    for load in loads:
+            source, target = gate_up_part(wgu, pieces[k * 4 + s], k, s)
+            loads.append(pltpu.make_async_copy(source, target, sem_in.at[0, k * 4 + s]))
+            source, target = down_part(wdn, pieces[k * 4 + s], k, s)
+            more_loads.append(pltpu.make_async_copy(source, target, sem_in.at[1, k * 4 + s]))
+    for load in loads + more_loads:
         load.start()
     pad = jnp.zeros((wide - block, pair), jnp.bfloat16)
     for j in range(4):
         i = dp_id ^ j
         zz = lax.rem(z_id - j + 4, 4)
-        n2_rel[j * wide : j * wide + block, :] = jnp.concatenate([n2_own[i], n2_other[i]], 1)
-        dy_rel[j * wide : j * wide + block, :] = jnp.concatenate([dy_own[zz], dy_other[zz]], 1)
+        n2_rel[j * wide : j * wide + block, :] = jnp.concatenate(
+            [n2_own[i][:, :rows], n2_other[i][:, :rows]], 1
+        )
+        dy_rel[j * wide : j * wide + block, :] = jnp.concatenate(
+            [dy_own[zz][:, :rows], dy_other[zz][:, :rows]], 1
+        )
         n2_rel[j * wide + block : (j + 1) * wide, :] = pad
         dy_rel[j * wide + block : (j + 1) * wide, :] = pad
-    for load in loads[:16]:
-        load.wait()
 
     def rows_of(index, size):
         return pl.ds(pl.multiple_of(index * size, 16), size)
 
-    def forward(s, carry):
-        m = lax.rem(z_id - s + 4, 4)
-        k = m ^ dp_id
-        total = product_nn(wgu[rows_of(s, 2 * half), :], n2_rel[...])
+    for s in range(4):
+        for load in loads[4 * s : 4 * s + 4]:
+            load.wait()
+        k = lax.rem(z_id - s + 4, 4) ^ dp_id
+        total = product_nn(wgu[s * 2 * half : (s + 1) * 2 * half, :], n2_rel[...])
         gu_ref[rows_of(k, 2 * half), :] = total
         gate = total[:half]
         prod_ref[rows_of(k, half), :] = (gate * jax.nn.sigmoid(gate) * total[half:]).astype(
             jnp.bfloat16
         )
-        return carry
-
-    lax.fori_loop(0, 4, forward, 0)
-    for load in loads[16:]:
+    for load in more_loads:
         load.wait()
-
-    def middle(k, carry):
+    for k in range(4):
         s = lax.rem(z_id - (dp_id ^ k) + 4, 4)
-        dprod = product_nn(wdn[rows_of(k, half), :], dy_rel[...])
-        gdn[rows_of(k, half), :] = product_nt(prod_ref[rows_of(k, half), :], dy_rel[...]).astype(
-            jnp.bfloat16
-        )
-        total = gu_ref[rows_of(k, 2 * half), :]
-        gate, up = total[:half], total[half:]
+        dprod = product_nn(wdn[k * half : (k + 1) * half, :], dy_rel[...])
+        gate = gu_ref[k * 2 * half : k * 2 * half + half, :]
+        up = gu_ref[k * 2 * half + half : (k + 1) * 2 * half, :]
         sig = jax.nn.sigmoid(gate)
         dgu_ref[rows_of(s, 2 * half), :] = jnp.concatenate(
             [dprod * up * sig * (1.0 + gate * (1.0 - sig)), dprod * gate * sig], 0
         ).astype(jnp.bfloat16)
-        return carry
-
-    lax.fori_loop(0, 4, middle, 0)
-
-    def backward(s, carry):
-        ggu[rows_of(s, 2 * half), :] = product_nt(
-            dgu_ref[rows_of(s, 2 * half), :], n2_rel[...]
-        ).astype(jnp.bfloat16)
-        return carry
-
-    stores = []
-    for k in range(4):
-        for s in range(4):
-            stores.append(
-                pltpu.make_async_copy(
-                    gdn.at[pl.ds(k * half, half), pl.ds(s * wide, wide)],
-                    grads[k * 4 + s].at[pl.ds(2 * half, half)],
-                    sem_out.at[1, k * 4 + s],
-                )
-            )
-    for store in stores:
-        store.start()
-    lax.fori_loop(0, 4, backward, 0)
-    late = []
-    for k in range(4):
-        for s in range(4):
-            late.append(
-                pltpu.make_async_copy(
-                    ggu.at[pl.ds(s * 2 * half, 2 * half), pl.ds(k * wide, wide)],
-                    grads[k * 4 + s].at[pl.ds(0, 2 * half)],
-                    sem_out.at[0, k * 4 + s],
-                )
-            )
-    for store in late:
-        store.start()
     for j in range(4):
         lanes = slice(j * wide, (j + 1) * wide)
         out = product_tn(wdn[:, lanes], prod_ref[...])[:block]
         zz = rows_of(lax.rem(z_id - j + 4, 4), block)
         keep_ref[0, zz, :] = out[:, :rows]
-        send_ref[0, zz, :] = out[:, rows:].astype(jnp.bfloat16)
+        send_ref[0, zz, :rows] = out[:, rows:].astype(jnp.bfloat16)
+    for k in range(4):
+        here = slice(k * half, (k + 1) * half)
+        wdn[here, :] = product_nt(prod_ref[here, :], dy_rel[...]).astype(jnp.bfloat16)
+    stores = []
+    for k in range(4):
+        for s in range(4):
+            target, source = down_part(wdn, grads[k * 4 + s], k, s)
+            stores.append(pltpu.make_async_copy(source, target, sem_out.at[1, k * 4 + s]))
+    for store in stores:
+        store.start()
+    for j in range(4):
+        lanes = slice(j * wide, (j + 1) * wide)
         dn = product_tn(wgu[:, lanes], dgu_ref[...])[:block]
         i = rows_of(dp_id ^ j, block)
         keep_ref[1, i, :] = dn[:, :rows]
-        send_ref[1, i, :] = dn[:, rows:].astype(jnp.bfloat16)
-    for store in stores + late:
+        send_ref[1, i, :rows] = dn[:, rows:].astype(jnp.bfloat16)
+    send_ref[:, :, rows:] = jnp.zeros((2, 4 * block, send_ref.shape[2] - rows), jnp.bfloat16)
+    for s in range(4):
+        here = slice(s * 2 * half, (s + 1) * 2 * half)
+        wgu[here, :] = product_nt(dgu_ref[here, :], n2_rel[...]).astype(jnp.bfloat16)
+        for k in range(4):
+            target, source = gate_up_part(wgu, grads[k * 4 + s], k, s)
+            store = pltpu.make_async_copy(source, target, sem_out.at[0, k * 4 + s])
+            store.start()
+            stores.append(store)
+    for store in stores:
         store.wait()
 
 
@@ -979,6 +976,7 @@
     q_rows = q_cols + 8
     depth = q_rows + 2 * k_cols
     mlp_rows = 3 * half + q_rows
+    padded = -(-rows // 128) * 128
 
     (first_piece,) = run(
         pack_first_kernel,
@@ -991,9 +989,7 @@
         0,
         16,
     )
-    chain = [first_piece]
-    for _ in range(3):
-        chain.append(shift_z(chain[-1], 1))
+    chain = [first_piece] + [shift_z(first_piece, step) for step in (1, 2, 3)]
     down_halves = w_down.reshape(2, half, -1)
     other_down = swap_core(
         lax.dynamic_index_in_dim(down_halves, 1 - core_id, 0, keepdims=False)
@@ -1014,7 +1010,7 @@
         "turn_in",
         (tokens.reshape(rows, width), cotangent.reshape(rows, width)),
         [VMEM] * 2,
-        [struct((width, rows))] * 2,
+        [struct((width, rows)), struct((width, padded))],
         [VMEM] * 2,
         [],
         0,
@@ -1025,19 +1021,19 @@
     along = jnp.stack(chain, 0)
     extras = along[:, q_cols : q_cols + 2, :block]
     other_extras = swap_core(extras)
-    from_x = swap_dp(along, 1)
-    from_y = swap_dp(along, 2)
+    x_zero, y_zero = swap_dp(mlp_piece, 1), swap_dp(mlp_piece, 2)
+    along_next = after(along, x_zero, y_zero)
+    from_x = swap_dp(along_next, 1)
+    from_y = swap_dp(along_next, 2)
     first_own = [along, from_x, from_y, swap_dp(from_x[:2], 2), swap_dp(from_y[2:], 1)]
     first_other = [swap_core(piece) for piece in first_own]
 
-    def spread_square(piece):
-        return swap_dp(piece, 1), swap_dp(piece, 2)
-
-    mlp_chain = [mlp_piece, shift_z(after(mlp_piece, along), 1)]
-    for _ in range(2):
-        mlp_chain.append(shift_z(mlp_chain[-1], 1))
-    by_square = [spread_square(mlp_piece)]
-    by_square.append(spread_square(after(mlp_chain[1], first_own[3], first_own[4])))
+    z_one = shift_z(after(mlp_piece, along), 1)
+    z_two = shift_z(z_one, 1)
+    z_three = shift_z(z_two, 1)
+    far_zero = swap_dp(after(x_zero, *first_own[3:]), 2)
+    z_one_next = after(z_one, *first_own[3:])
+    x_one, y_one = swap_dp(z_one_next, 1), swap_dp(z_one_next, 2)
 
     by_core = jnp.where(
         core_id == 0, jnp.stack([extras, other_extras], 1), jnp.stack([other_extras, extras], 1)
@@ -1057,11 +1053,12 @@
     cosine, sine = cosine[:, 0, :].T, sine[:, 0, :].T
     x_wide = x.astype(jnp.float32)
     n1 = (x_wide * mean_square(x_wide) * gain_one).astype(jnp.bfloat16).reshape(4, block, rows)
+    n1_next = after(n1, z_one)
 
     query, kv = run(
         project_kernel,
         "project",
-        (ids, *first_own, *first_other, n1, cosine, sine),
+        (ids, *first_own, *first_other, n1_next, cosine, sine),
         [SMEM] + [VMEM] * 13,
         (struct((QUERY_HEADS, HEAD_WIDTH, rows)), struct((rows, 2 * kv_width))),
         [VMEM] * 2,
@@ -1073,18 +1070,18 @@
         2 * (width + 2 * kv_width) * width * rows,
         24,
     )
-    kv_own, kv_other = [kv], [swap_core(kv)]
-    for _ in range(3):
-        kv_own.append(shift_z_up(kv_own[-1], 1))
-        kv_other.append(swap_core(kv_own[-1]))
-
-    by_square.append(spread_square(after(mlp_chain[2], kv)))
-    far_zero = swap_dp(after(by_square[0][0], kv), 2)
-    far_one = swap_dp(after(by_square[1][1], kv), 1)
-    by_square.append(spread_square(after(mlp_chain[3], kv_own[1])))
-    far_two = swap_dp(after(by_square[2][0], kv_own[2]), 2)
-    far_three = swap_dp(after(by_square[3][1], kv_own[3]), 1)
-    pieces = mlp_chain + [p[0] for p in by_square] + [p[1] for p in by_square]
+    kv_next = after(kv, z_two)
+    kv_own = [kv] + [shift_z_up(kv_next, step) for step in (1, 2, 3)]
+    kv_other = [swap_core(piece) for piece in kv_own]
+    z_two_next, x_zero_next = after(z_two, kv), after(y_one, kv)
+    x_two, y_two = swap_dp(z_two_next, 1), swap_dp(z_two_next, 2)
+    far_one = swap_dp(x_zero_next, 1)
+    x_three, y_three = swap_dp(z_three, 1), swap_dp(z_three, 2)
+    far_two = swap_dp(x_two, 2)
+    far_three = swap_dp(y_three, 1)
+    pieces = [mlp_piece, z_one, z_two, z_three]
+    pieces += [x_zero, x_one, x_two, x_three]
+    pieces += [y_zero, y_one, y_two, y_three]
     pieces += [far_zero, far_one, far_two, far_three]
 
     pair_flops = 2 * QUERY_HEADS * HEAD_WIDTH * rows * 8 * cap
@@ -1093,21 +1090,29 @@
         pltpu.VMEM((KEY_HEADS, 8 * cap, HEAD_WIDTH), jnp.bfloat16),
         pltpu.VMEM((8 * cap, share * cap), jnp.float32),
     ]
-    attended, lse = run(
-        attend_kernel,
-        "attend",
-        (ids, flat_counts, query, *kv_own, *kv_other),
-        [SMEM, SMEM] + [VMEM] * 9,
-        (
-            struct((QUERY_HEADS, HEAD_WIDTH, rows)),
-            struct((2 * KEY_HEADS, 1, share * cap), jnp.float32),
-        ),
-        [VMEM] * 2,
-        head_scratch,
-        8 * pair_flops,
-        28,
-    )
-    attended = attended.reshape(4, block, rows)
+    def attend(mb, queries):
+        return run(
+            functools.partial(attend_kernel, mb),
+            "attend",
+            (ids, flat_counts, queries, *kv_own, *kv_other),
+            [SMEM, SMEM] + [VMEM] * 9,
+            (
+                struct((QUERY_HEADS, HEAD_WIDTH, cap)),
+                struct((KEY_HEADS, 1, share * cap), jnp.float32),
+            ),
+            [VMEM] * 2,
+            head_scratch,
+            4 * pair_flops,
+            24,
+        )
+
+    att_a, lse_a = attend(0, after(query, x_one, y_one, far_zero, x_two, y_two, z_three))
+    att_b, lse_b = attend(1, after(query, x_three, y_three, far_one, far_two, att_a))
+    att_a = att_a.reshape(4, block, cap)
+    att_b = att_b.reshape(4, block, cap)
+    lse = (lse_a, lse_b)
+    blocks = (4, block, rows)
+    wide_blocks = (4, block, padded)
     (out_own,) = run(
         collect_kernel,
         "collect",
@@ -1123,34 +1128,31 @@
     h, n2 = run(
         hidden_kernel,
         "hidden",
-        (ids, out_own, out_other, attended, x, gain_two),
-        [SMEM] + [VMEM] * 5,
-        (struct((width, rows), jnp.float32), struct((width, rows))),
+        (ids, out_own, out_other, att_a, att_b, x, gain_two),
+        [SMEM] + [VMEM] * 6,
+        (struct((width, rows), jnp.float32), struct((width, padded))),
         [VMEM] * 2,
         [pltpu.VMEM((4 * wide, rows), jnp.bfloat16)],
         2 * width * width * rows,
         24,
     )
     n2_other = swap_core(n2)
-    blocks = (4, block, rows)
     results = run(
         mlp_kernel,
         "mlp",
         (
             ids,
-            n2.reshape(blocks),
-            n2_other.reshape(blocks),
-            dy.reshape(blocks),
-            dy_other.reshape(blocks),
+            n2.reshape(wide_blocks),
+            n2_other.reshape(wide_blocks),
+            dy.reshape(wide_blocks),
+            dy_other.reshape(wide_blocks),
             *pieces,
         ),
         [SMEM] + [VMEM] * 4 + [ANY] * 16,
-        [struct((2, width, rows), jnp.float32), struct((2, width, rows))]
+        [struct((2, width, rows), jnp.float32), struct((2, width, padded))]
         + [struct((3 * half, wide))] * 16,
         [VMEM] * 2 + [ANY] * 16,
         [
-            pltpu.VMEM((8 * half, 4 * wide), jnp.bfloat16),
-            pltpu.VMEM((4 * half, 4 * wide), jnp.bfloat16),
             pltpu.VMEM((8 * half, 4 * wide), jnp.bfloat16),
             pltpu.VMEM((4 * half, 4 * wide), jnp.bfloat16),
             pltpu.VMEM((8 * half, 2 * rows), jnp.float32),
@@ -1162,7 +1164,7 @@
             pltpu.SemaphoreType.DMA((2, 16)),
         ],
         18 * 16 * half * block * 2 * rows,
-        56,
+        44,
     )
     keep, send, grads = results[0], results[1], results[2:]
     arrived = swap_core(send)
@@ -1206,7 +1208,7 @@
     legs_zero = first_leg(0, mixed_gradient)
     turned_one = second_leg(1, legs_one, mixed_gradient)
 
-    def attend_back(mb):
+    def attend_back(mb, mixed):
         return run(
             functools.partial(attend_back_kernel, mb),
             "attend_back",
@@ -1214,10 +1216,10 @@
                 ids,
                 flat_counts,
                 query,
-                mixed_gradient.reshape(QUERY_HEADS, HEAD_WIDTH, rows),
+                mixed.reshape(QUERY_HEADS, HEAD_WIDTH, rows),
                 *kv_own,
                 *kv_other,
-                lse,
+                lse[mb],
                 cosine,
                 sine,
             ),
@@ -1230,26 +1232,40 @@
                 pltpu.VMEM((KEY_HEADS, 8 * cap, HEAD_WIDTH), jnp.bfloat16),
             ],
             10 * pair_flops,
-            28,
-        )
-
-    def reduce_kv(own, other):
-        summed = [add_low(own[s], swap_core(other[s])) for s in (3, 2, 1, 0)][::-1]
+            24,
+        )
+
+    def sum_cores(own, other):
+        return [add_low(own[s], swap_core(other[s])) for s in (3, 2, 1, 0)][::-1]
+
+    def sum_z(summed):
         total = summed[0].astype(jnp.float32)
         for s in (3, 2, 1):
             total = total + shift_z_down(summed[s], s).astype(jnp.float32)
         return total
 
-    back_a = attend_back(0)
-    dkv_a = reduce_kv(back_a[1:5], back_a[5:9])
-    summed_three = add_low(home[3], legs_one[2], after(turned_one[1], back_a[0]))
-    summed_two = add_low(home[2], turned_one[0], legs_one[3])
-    turned_zero = second_leg(0, legs_zero, back_a[0])
+    back_a = attend_back(0, after(mixed_gradient, *legs_one))
+    out_grads = run(
+        out_grad_kernel,
+        "out_grad",
+        (ids, att_a, att_b, after(da_pieces, back_a[0])),
+        [SMEM] + [VMEM] * 3,
+        [struct((4, q_rows, wide))] * 8,
+        [VMEM] * 8,
+        [pltpu.VMEM((4 * wide, rows), jnp.bfloat16)],
+        2 * width * width * rows,
+        16,
+    )
+    summed_a = sum_cores(back_a[1:5], back_a[5:9])
+    dkv_a = sum_z(summed_a)
+    back_b = attend_back(1, after(mixed_gradient, *summed_a, *turned_one, out_grads[0]))
+    dkv_b = sum_z(sum_cores(back_b[1:5], back_b[5:9]))
+    turned_zero = second_leg(0, legs_zero, back_b[0])
+    summed_three = add_low(home[3], legs_one[2], after(turned_one[1], back_b[0]))
+    summed_two = add_low(home[2], after(turned_one[0], back_b[0]), legs_one[3])
     hop = shift_z(summed_three, -1)
-    back_b = attend_back(1)
-    dkv_b = reduce_kv(back_b[1:5], back_b[5:9])
-    hop = shift_z(add_low(summed_two, after(hop, back_b[0])), -1)
-    summed_one = add_low(home[1], legs_zero[2], after(turned_zero[1], back_b[0]))
+    hop = shift_z(add_low(summed_two, hop), -1)
+    summed_one = add_low(home[1], legs_zero[2], turned_zero[1])
     hop = shift_z(add_low(summed_one, hop), -1)
     mlp_total = (
         home[0].astype(jnp.float32)
@@ -1284,23 +1300,21 @@
             ids,
             *first_own,
             *first_other,
-            n1,
-            attended,
+            after(n1, dkv_a, *legs_zero),
             back_a[0].reshape(width, cap),
             back_b[0].reshape(width, cap),
-            da_pieces,
+            *out_grads,
         ),
-        [SMEM] + [VMEM] * 15,
+        [SMEM] + [VMEM] * 21,
         [struct(blocks, jnp.float32)] + [struct((4, 2 * q_rows, wide))] * 8,
         [VMEM] * 9,
         [
             pltpu.VMEM((4 * wide, rows), jnp.bfloat16),
-            pltpu.VMEM((4 * wide, rows), jnp.bfloat16),
             pltpu.VMEM((width, rows), jnp.float32),
             pltpu.VMEM((8 * q_rows, rows), jnp.bfloat16),
         ],
-        6 * width * width * rows,
-        32,
+        4 * width * width * rows,
+        24,
     )
     dn_q = q_results[0]
     q_out_total = reduce_all(q_results[1:])
@@ -1314,7 +1328,7 @@
             ids,
             *first_own,
             *first_other,
-            n1,
+            after(n1, *turned_zero),
             dkv_a,
             dkv_b,
             cosine,
@@ -1334,7 +1348,7 @@
             pltpu.VMEM((16 * k_cols, rows), jnp.bfloat16),
         ],
         8 * kv_width * width * rows,
-        32,
+        24,
     )
     grad_tokens = kv_results[0].T.reshape(batches, cap, width)
     kv_total = reduce_all(kv_results[2:])

time: 466 us -> 448 us (0.961)
  waiting for transfers between devices: 199 us -> 165 us
  starting transfers between devices: 80.3 us -> 101 us
  local copies, waits for them, and re-layouts: 58.6 us -> 43.5 us
  other arithmetic: 12.6 us -> 19.8 us
    ppermute x37, waiting for transfers between devices: 103 us -> 80.7 us  [swap_dp(): return lax.ppermute(value, 'dp', [(j, j ^ mask) for j in range(4)])]
    ppermute x18, waiting for transfers between devices: 41.3 us -> 20.3 us  [shift_z(): lax.ppermute(value, 'fsdp', [(j, (j + 2 * step) % 8) for j in range(8)])]
    ppermute x18, starting transfers between devices: 19.4 us -> 35.4 us  [shift_z(): lax.ppermute(value, 'fsdp', [(j, (j + 2 * step) % 8) for j in range(8)])]
    ppermute x6, waiting for transfers between devices: 33.6 us -> 44.7 us  [shift_z_down(): lax.ppermute(value, 'fsdp', [(j, j - 2 * step) for j in range(8) if j - 2...]
    ppermute x3 -> x0, local copies, waits for them, and re-layouts: 7.55 us -> none  [swap_core(): return lax.ppermute(value, 'fsdp', [(j, j ^ 1) for j in range(8)])]
    pallas_call x5 -> x2, local copies, waits for them, and re-layouts: 9.35 us -> 1.99 us  [run(): pl.pallas_call(body, out_shape=tuple(outs), in_specs=in_specs, out_specs=...]
    ppermute x37, starting transfers between devices: 35 us -> 41.8 us  [swap_dp(): return lax.ppermute(value, 'dp', [(j, j ^ mask) for j in range(4)])]
    pallas_call x13 -> x15, Pallas kernels: 104 us -> 108 us  [run(): pl.pallas_call(body, out_shape=tuple(outs), in_specs=in_specs, out_specs=...]
  transfers between devices with their start and end apart: 97 -> 97, of which waited for: 48 -> 44; matrix products, arithmetic and copies ran while one was open for 7% -> 7% of each run, Pallas kernels for 16% -> 14%
where the time goes in v3:
time: 448 us; the launch traced here: 441 us
  waiting for transfers between devices  165 us (37%)
  Pallas kernels  108 us (24%)
  starting transfers between devices  101 us (23%)
  local copies, waits for them, and re-layouts  43.5 us (10%)
  other arithmetic  19.8 us (4%)
    pallas_call x15, Pallas kernels, run(): pl.pallas_call(body, out_shape=tuple(outs), in_specs=in_specs, out_specs=...  108 us
    ppermute x37, waiting for transfers between devices, swap_dp(): return lax.ppermute(value, 'dp', [(j, j ^ mask) for j in range(4)])  80.7 us
    ppermute x6, waiting for transfers between devices, shift_z_down(): lax.ppermute(value, 'fsdp', [(j, j - 2 * step) for j in range(8) if j - 2...  44.7 us
    ppermute x37, starting transfers between devices, swap_dp(): return lax.ppermute(value, 'dp', [(j, j ^ mask) for j in range(4)])  41.8 us
    ppermute x18, starting transfers between devices, shift_z(): lax.ppermute(value, 'fsdp', [(j, (j + 2 * step) % 8) for j in range(8)])  35.4 us
    unnamed x261, local copies, waits for them, and re-layouts  32.8 us
    ppermute x18, waiting for transfers between devices, shift_z(): lax.ppermute(value, 'fsdp', [(j, (j + 2 * step) % 8) for j in range(8)])  20.3 us
    ppermute x3, waiting for transfers between devices, shift_z_up(): lax.ppermute(value, 'fsdp', [(j, j + 2 * step) for j in range(8) if j + 2...  13 us
  transfers between devices with their start and end apart: 97, of which 44 were waited for; matrix products, arithmetic and copies ran while one was open for 7% of the time, Pallas kernels for 14%

profile of v3, /device:TPU:0, one launch (start us, length us, event | category | flops | bytes accessed | tf_op | source)
XLA Modules:
  0.0 441.0 jit_solution(11820667496971908422)
XLA Ops:
  5.4 5.1 %collective-permute-start.3 = (bf16[208,256]{1,0:T(8,128)(2,1)S(1)}, bf16[208,256]{1,0:T(8,128)(2,1)S(1)}, u32[]{:S(2)}, u32[]{:S(2)}) collective-permute-start(bf16[208,256]{1,0:T(8,128)(2,1)S(1)} %pack_first.1), channel_id=1, source_target_pairs={{0,6},{1,7},{2,0},{3,1},{4,2},{5,3},{6,4},{7,5},{8,14},{9,15},{10,... | collective-permute-start | bytes 319496 | tf_op jit(solution)/shard_map/ppermute | solution.py:365
  25.3 7.2 %collective-permute-done.8.refs_8_.refs_13_ = bf16[1088,256]{1,0:T(8,128)(2,1)S(1)} collective-permute-done((bf16[1088,256]{1,0:T(8,128)(2,1)S(1)}, bf16[1088,256]{1,0:T(8,128)(2,1)S(1)}, u32[]{:S(2)}, u32[]{:S(2)}) %collective-permute-start.8) | collective-permute-done | bytes 557088 | tf_op jit(solution)/shard_map/ppermute | solution.py:361
  39.1 5.8 %collective-permute-done.11.refs_3_ = bf16[4,208,256]{2,1,0:T(8,128)(2,1)S(1)} collective-permute-done((bf16[4,208,256]{2,1,0:T(8,128)(2,1)S(1)}, bf16[4,208,256]{2,1,0:T(8,128)(2,1)S(1)}, u32[]{:S(2)}, u32[]{:S(2)}) %collective-permute-start.11) | collective-permute-done | bytes 426016 | tf_op jit(solution)/shard_map/ppermute | solution.py:361
  63.2 4.5 %project.1 = (bf16[15,64,320]{2,1,0:T(8,128)(2,1)S(1)}, bf16[320,640]{1,0:T(8,128)(2,1)}) custom-call(s32[4]{0:T(128)S(1)} %pad_add_fusion.ids_ref.refs_0_, bf16[4,208,256]{2,1,0:T(8,128)(2,1)S(1)} %pad_maximum_fusion.refs_1_, bf16[4,208,256]{2,1,0:T(8,128)(2,1)S(1)} %collective-permute-done.9.refs_2_, ...), custom_call_target="tpu_custom_call" | custom-call | flops 983040000 | bytes 5128208 | tf_op jit(solution)/shard_map/project/pallas_call | solution.py:409
  77.3 9.1 %collective-permute-done.25.refs_12_.refs_17_ = bf16[1088,256]{1,0:T(8,128)(2,1)S(1)} collective-permute-done((bf16[1088,256]{1,0:T(8,128)(2,1)}, bf16[1088,256]{1,0:T(8,128)(2,1)S(1)}, u32[]{:S(2)}, u32[]{:S(2)}) %collective-permute-start.25) | collective-permute-done | bytes 557088 | tf_op jit(solution)/shard_map/ppermute | solution.py:361
  89.3 9.1 %collective-permute-done.24.refs_11_.refs_16_ = bf16[1088,256]{1,0:T(8,128)(2,1)S(1)} collective-permute-done((bf16[1088,256]{1,0:T(8,128)(2,1)S(1)}, bf16[1088,256]{1,0:T(8,128)(2,1)S(1)}, u32[]{:S(2)}, u32[]{:S(2)}) %collective-permute-start.24) | collective-permute-done | bytes 557088 | tf_op jit(solution)/shard_map/ppermute | solution.py:361
  99.4 10.9 %collective-permute-done.23.refs_10_.refs_15_ = bf16[1088,256]{1,0:T(8,128)(2,1)S(1)} collective-permute-done((bf16[1088,256]{1,0:T(8,128)(2,1)}, bf16[1088,256]{1,0:T(8,128)(2,1)S(1)}, u32[]{:S(2)}, u32[]{:S(2)}) %collective-permute-start.23) | collective-permute-done | bytes 557088 | tf_op jit(solution)/shard_map/ppermute | solution.py:361
  125.1 7.5 %collective-permute-done.31.refs_5_.refs_6_ = bf16[320,640]{1,0:T(8,128)(2,1)} collective-permute-done((bf16[320,640]{1,0:T(8,128)(2,1)}, bf16[320,640]{1,0:T(8,128)(2,1)}, u32[]{:S(2)}, u32[]{:S(2)}) %collective-permute-start.31) | collective-permute-done | bytes 409632 | tf_op jit(solution)/shard_map/ppermute | solution.py:369
  132.6 5.5 %collective-permute-done.30.refs_4_.refs_5_ = bf16[320,640]{1,0:T(8,128)(2,1)} collective-permute-done((bf16[320,640]{1,0:T(8,128)(2,1)}, bf16[320,640]{1,0:T(8,128)(2,1)}, u32[]{:S(2)}, u32[]{:S(2)}) %collective-permute-start.30) | collective-permute-done | bytes 409632 | tf_op jit(solution)/shard_map/ppermute | solution.py:369
  141.3 9.8 %attend.2 = (bf16[15,64,160]{2,1,0:T(8,128)(2,1)S(1)}, f32[5,1,480]{2,1,0:T(1,128)S(1)}) custom-call(s32[4]{0:T(128)S(1)} %pad_add_fusion.ids_ref.refs_0_, s32[16]{0:T(128)S(1)} %reshape.207.refs_1_, bf16[15,64,320]{2,1,0:T(8,128)(2,1)S(1)} %copy-done.90, bf16[320,640]{1,0:T(8,128)(2,1)} %get-tuple-element.124.refs_3_.refs_4_, ...), custom_call_target="tpu_custom_call" | custom-call | flops 3145728000 | bytes 4208080 | tf_op jit(solution)/shard_map/attend/pallas_call | solution.py:409
  151.2 10.3 %attend.3 = (bf16[15,64,160]{2,1,0:T(8,128)(2,1)S(1)}, f32[5,1,480]{2,1,0:T(1,128)S(1)}) custom-call(s32[4]{0:T(128)S(1)} %pad_add_fusion.ids_ref.refs_0_, s32[16]{0:T(128)S(1)} %reshape.207.refs_1_, bf16[15,64,320]{2,1,0:T(8,128)(2,1)S(1)} %copy-done.91, bf16[320,640]{1,0:T(8,128)(2,1)} %get-tuple-element.124.refs_3_.refs_4_, ...), custom_call_target="tpu_custom_call" | custom-call | flops 3145728000 | bytes 4208080 | tf_op jit(solution)/shard_map/attend/pallas_call | solution.py:409
  168.1 30.2 %mlp.1 = (f32[2,960,320]{2,1,0:T(8,128)}, bf16[2,960,384]{2,1,0:T(8,128)(2,1)}, bf16[960,256]{1,0:T(8,128)(2,1)S(1)}, bf16[960,256]{1,0:T(8,128)(2,1)S(1)}, bf16...) custom-call(s32[4]{0:T(128)S(1)} %pad_add_fusion.ids_ref.refs_0_, ...), custom_call_target="tpu_custom_call" | custom-call | flops 14155776000 | bytes 23658512 | tf_op jit(solution)/shard_map/mlp/pallas_call | solution.py:409
  218.4 9.1 %collective-permute-done.43 = bf16[960,256]{1,0:T(8,128)(2,1)S(1)} collective-permute-done((bf16[960,256]{1,0:T(8,128)(2,1)S(1)}, bf16[960,256]{1,0:T(8,128)(2,1)S(1)}, u32[]{:S(2)}, u32[]{:S(2)}) %collective-permute-start.43) | collective-permute-done | bytes 491552 | tf_op jit(solution)/shard_map/ppermute | solution.py:361
  230.4 14.7 %attend_back.2 = (bf16[15,64,160]{2,1,0:T(8,128)(2,1)S(1)}, bf16[160,640]{1,0:T(8,128)(2,1)S(1)}, bf16[160,640]{1,0:T(8,128)(2,1)S(1)}, bf16[160,640]{1,0:T(8,12...) custom-call(s32[4]{0:T(128)S(1)} %pad_add_fusion.ids_ref.refs_0_, ...), custom_call_target="tpu_custom_call" | custom-call | flops 7864320000 | bytes 6542800 | tf_op jit(solution)/shard_map/attend_back/pallas_call | solution.py:409
  250.9 14.1 %collective-permute-done.56 = bf16[160,640]{1,0:T(8,128)(2,1)S(1)} collective-permute-done((bf16[160,640]{1,0:T(8,128)(2,1)S(1)}, bf16[160,640]{1,0:T(8,128)(2,1)S(1)}, u32[]{:S(2)}, u32[]{:S(2)}) %collective-permute-start.56) | collective-permute-done | bytes 204832 | tf_op jit(solution)/shard_map/ppermute | solution.py:373
  265.5 10.1 %collective-permute-done.55 = bf16[160,640]{1,0:T(8,128)(2,1)S(1)} collective-permute-done((bf16[160,640]{1,0:T(8,128)(2,1)S(1)}, bf16[160,640]{1,0:T(8,128)(2,1)S(1)}, u32[]{:S(2)}, u32[]{:S(2)}) %collective-permute-start.55) | collective-permute-done | bytes 204832 | tf_op jit(solution)/shard_map/ppermute | solution.py:373
  278.1 8.0 %collective-permute-done.54 = bf16[160,640]{1,0:T(8,128)(2,1)S(1)} collective-permute-done((bf16[160,640]{1,0:T(8,128)(2,1)S(1)}, bf16[160,640]{1,0:T(8,128)(2,1)S(1)}, u32[]{:S(2)}, u32[]{:S(2)}) %collective-permute-start.54) | collective-permute-done | bytes 204832 | tf_op jit(solution)/shard_map/ppermute | solution.py:373
  299.6 14.9 %attend_back.3 = (bf16[15,64,160]{2,1,0:T(8,128)(2,1)S(1)}, bf16[160,640]{1,0:T(8,128)(2,1)S(1)}, bf16[160,640]{1,0:T(8,128)(2,1)S(1)}, bf16[160,640]{1,0:T(8,12...) custom-call(s32[4]{0:T(128)S(1)} %pad_add_fusion.ids_ref.refs_0_, ...), custom_call_target="tpu_custom_call" | custom-call | flops 7864320000 | bytes 6542800 | tf_op jit(solution)/shard_map/attend_back/pallas_call | solution.py:409
  317.4 5.6 %finish_q.1 = (f32[4,240,320]{2,1,0:T(8,128)S(1)}, bf16[4,256,256]{2,1,0:T(8,128)(2,1)S(1)}, bf16[4,256,256]{2,1,0:T(8,128)(2,1)S(1)}, bf16[4,256,256]{2,1,0:T(8...) custom-call(s32[4]{0:T(128)S(1)} %pad_add_fusion.ids_ref.refs_0_, ...), custom_call_target="tpu_custom_call" | custom-call | flops 1179648000 | bytes 12156944 | tf_op jit(solution)/shard_map/finish_q/pallas_call | solution.py:409
  331.7 5.5 %collective-permute-done.59 = bf16[160,640]{1,0:T(8,128)(2,1)S(1)} collective-permute-done((bf16[160,640]{1,0:T(8,128)(2,1)S(1)}, bf16[160,640]{1,0:T(8,128)(2,1)S(1)}, u32[]{:S(2)}, u32[]{:S(2)}) %collective-permute-start.59) | collective-permute-done | bytes 204832 | tf_op jit(solution)/shard_map/ppermute | solution.py:373
  337.6 6.9 %collective-permute-done.61 = bf16[160,640]{1,0:T(8,128)(2,1)S(1)} collective-permute-done((bf16[160,640]{1,0:T(8,128)(2,1)S(1)}, bf16[160,640]{1,0:T(8,128)(2,1)S(1)}, u32[]{:S(2)}, u32[]{:S(2)}) %collective-permute-start.61) | collective-permute-done | bytes 204832 | tf_op jit(solution)/shard_map/ppermute | solution.py:373
  345.5 5.3 %finish_kv.1 = (f32[960,320]{1,0:T(8,128)S(1)}, f32[960,1]{1,0:T(8,128)S(1)}, bf16[4,80,256]{2,1,0:T(8,128)(2,1)S(1)}, bf16[4,80,256]{2,1,0:T(8,128)(2,1)S(1)}, ...) custom-call(s32[4]{0:T(128)S(1)} %copy-done.85, ...), custom_call_target="tpu_custom_call" | custom-call | flops 786432000 | bytes 10542608 | tf_op jit(solution)/shard_map/finish_kv/pallas_call | solution.py:409
  410.2 4.4 %collective-permute-start.88 = (bf16[960,256]{1,0:T(8,128)(2,1)S(1)}, bf16[960,256]{1,0:T(8,128)(2,1)S(1)}, u32[]{:S(2)}, u32[]{:S(2)}) collective-permute-start(bf16[960,256]{1,0:T(8,128)(2,1)S(1)} %add_convert_fusion.4), channel_id=1, source_target_pairs={{0,6},{1,7},{2,0},{3,1},{4,2},{5,3},{6,4},{7,5},{8,14},{9,15},{10,... | collective-permute-start | bytes 1474568 | tf_op jit(solution)/shard_map/ppermute | solution.py:365
  414.6 6.0 %collective-permute-done.70 = bf16[4,256,256]{2,1,0:T(8,128)(2,1)S(1)} collective-permute-done((bf16[4,256,256]{2,1,0:T(8,128)(2,1)S(1)}, bf16[4,256,256]{2,1,0:T(8,128)(2,1)S(1)}, u32[]{:S(2)}, u32[]{:S(2)}) %collective-permute-start.70) | collective-permute-done | bytes 524320 | tf_op jit(solution)/shard_map/ppermute | solution.py:361
  (516 shorter events, 218.5 us)
Async XLA Ops:
  24.2 31.6 %collective-permute-start.14 = (bf16[4,208,256]{2,1,0:T(8,128)(2,1)S(1)}, bf16[4,208,256]{2,1,0:T(8,128)(2,1)S(1)}, u32[]{:S(2)}, u32[]{:S(2)}) collective-permute-start(bf16[4,208,256]{2,1,0:T(8,128)(2,1)S(1)} %pad_maximum_fusion.refs_1_), channel_id=1, source_target_pairs={{0,1},{1,0},{2,3},{3,2},{4,5},{5,4},{6,7},{7,6},{8,9},{9,8},{10,11... | collective-permute-start | bytes 1277960 | tf_op jit(solution)/shard_map/ppermute | solution.py:357
  61.6 24.9 %collective-permute-start.25 = (bf16[1088,256]{1,0:T(8,128)(2,1)}, bf16[1088,256]{1,0:T(8,128)(2,1)S(1)}, u32[]{:S(2)}, u32[]{:S(2)}) collective-permute-start(bf16[1088,256]{1,0:T(8,128)(2,1)} %collective-permute-done.7.refs_4_.refs_9_), channel_id=1, source_target_pairs={{0,16},{8,24},{16,0},{24,8},{1,17},{9,25},{17,1},{25,9},{2,18},{10... | collective-permute-start | bytes 1671176 | tf_op jit(solution)/shard_map/ppermute | solution.py:361
  68.4 20.3 %collective-permute-start.20 = (bf16[1088,256]{1,0:T(8,128)(2,1)}, bf16[1088,256]{1,0:T(8,128)(2,1)S(1)}, u32[]{:S(2)}, u32[]{:S(2)}) collective-permute-start(bf16[1088,256]{1,0:T(8,128)(2,1)} %collective-permute-done.5.refs_2_.refs_7_), channel_id=1, source_target_pairs={{0,8},{8,0},{16,24},{24,16},{1,9},{9,1},{17,25},{25,17},{2,10},{10... | collective-permute-start | bytes 1671176 | tf_op jit(solution)/shard_map/ppermute | solution.py:361
  72.9 25.5 %collective-permute-start.24 = (bf16[1088,256]{1,0:T(8,128)(2,1)S(1)}, bf16[1088,256]{1,0:T(8,128)(2,1)S(1)}, u32[]{:S(2)}, u32[]{:S(2)}) collective-permute-start(bf16[1088,256]{1,0:T(8,128)(2,1)S(1)} %collective-permute-done.6.refs_3_.refs_8_), channel_id=1, source_target_pairs={{0,16},{8,24},{16,0},{24,8},{1,17},{9,25},{17,1},{25,9},{2,18},{10... | collective-permute-start | bytes 1671176 | tf_op jit(solution)/shard_map/ppermute | solution.py:361
  74.5 35.8 %collective-permute-start.23 = (bf16[1088,256]{1,0:T(8,128)(2,1)}, bf16[1088,256]{1,0:T(8,128)(2,1)S(1)}, u32[]{:S(2)}, u32[]{:S(2)}) collective-permute-start(bf16[1088,256]{1,0:T(8,128)(2,1)} %collective-permute-done.5.refs_2_.refs_7_), channel_id=1, source_target_pairs={{0,16},{8,24},{16,0},{24,8},{1,17},{9,25},{17,1},{25,9},{2,18},{10... | collective-permute-start | bytes 1671176 | tf_op jit(solution)/shard_map/ppermute | solution.py:361
  76.8 37.6 %collective-permute-start.21 = (bf16[1088,256]{1,0:T(8,128)(2,1)S(1)}, bf16[1088,256]{1,0:T(8,128)(2,1)S(1)}, u32[]{:S(2)}, u32[]{:S(2)}) collective-permute-start(bf16[1088,256]{1,0:T(8,128)(2,1)S(1)} %collective-permute-done.6.refs_3_.refs_8_), channel_id=1, source_target_pairs={{0,8},{8,0},{16,24},{24,16},{1,9},{9,1},{17,25},{25,17},{2,10},{10... | collective-permute-start | bytes 1671176 | tf_op jit(solution)/shard_map/ppermute | solution.py:361
  86.4 30.0 %collective-permute-start.26 = (bf16[1088,256]{1,0:T(8,128)(2,1)S(1)}, bf16[1088,256]{1,0:T(8,128)(2,1)S(1)}, u32[]{:S(2)}, u32[]{:S(2)}) collective-permute-start(bf16[1088,256]{1,0:T(8,128)(2,1)S(1)} %collective-permute-done.22.refs_9_.refs_14_), channel_id=1, source_target_pairs={{0,8},{8,0},{16,24},{24,16},{1,9},{9,1},{17,25},{25,17},{2,10},{10... | collective-permute-start | bytes 1671176 | tf_op jit(solution)/shard_map/ppermute | solution.py:361
  88.7 32.3 %collective-permute-start.27 = (bf16[1088,256]{1,0:T(8,128)(2,1)S(1)}, bf16[1088,256]{1,0:T(8,128)(2,1)S(1)}, u32[]{:S(2)}, u32[]{:S(2)}) collective-permute-start(bf16[1088,256]{1,0:T(8,128)(2,1)S(1)} %collective-permute-done.20.refs_6_.refs_11_), channel_id=1, source_target_pairs={{0,16},{8,24},{16,0},{24,8},{1,17},{9,25},{17,1},{25,9},{2,18},{10... | collective-permute-start | bytes 1671176 | tf_op jit(solution)/shard_map/ppermute | solution.py:361
  98.4 24.6 %collective-permute-start.28 = (bf16[1088,256]{1,0:T(8,128)(2,1)S(1)}, bf16[1088,256]{1,0:T(8,128)(2,1)S(1)}, u32[]{:S(2)}, u32[]{:S(2)}) collective-permute-start(bf16[1088,256]{1,0:T(8,128)(2,1)S(1)} %collective-permute-done.24.refs_11_.refs_16_), channel_id=1, source_target_pairs={{0,8},{8,0},{16,24},{24,16},{1,9},{9,1},{17,25},{25,17},{2,10},{10... | collective-permute-start | bytes 1671176 | tf_op jit(solution)/shard_map/ppermute | solution.py:361
  116.4 21.7 %collective-permute-start.30 = (bf16[320,640]{1,0:T(8,128)(2,1)}, bf16[320,640]{1,0:T(8,128)(2,1)}, u32[]{:S(2)}, u32[]{:S(2)}) collective-permute-start(bf16[320,640]{1,0:T(8,128)(2,1)} %get-tuple-element.124.refs_3_.refs_4_), channel_id=1, source_target_pairs={{0,2},{1,3},{2,4},{3,5},{4,6},{5,7},{8,10},{9,11},{10,12},{11,13},... | collective-permute-start | bytes 1228808 | tf_op jit(solution)/shard_map/ppermute | solution.py:369
  124.4 37.1 %collective-permute-start.29 = (bf16[4,128,1024]{2,1,0:T(8,128)(2,1)S(1)}, bf16[4,128,1024]{2,1,0:T(8,128)(2,1)}, u32[]{:S(2)}, u32[]{:S(2)}) collective-permute-start(bf16[4,128,1024]{2,1,0:T(8,128)(2,1)S(1)} %collect.1.own_ref), channel_id=1, source_target_pairs={{0,1},{1,0},{2,3},{3,2},{4,5},{5,4},{6,7},{7,6},{8,9},{9,8},{10,11... | collective-permute-start | bytes 3145736 | tf_op jit(solution)/shard_map/ppermute | solution.py:357
  138.4 26.7 %collective-permute-start.38 = (bf16[960,384]{1,0:T(8,128)(2,1)}, bf16[960,384]{1,0:T(8,128)(2,1)S(1)}, u32[]{:S(2)}, u32[]{:S(2)}) collective-permute-start(bf16[960,384]{1,0:T(8,128)(2,1)} %copy-done.23), channel_id=1, source_target_pairs={{0,1},{1,0},{2,3},{3,2},{4,5},{5,4},{6,7},{7,6},{8,9},{9,8},{10,11... | collective-permute-start | bytes 2211848 | tf_op jit(solution)/shard_map/ppermute | solution.py:357
  205.2 22.2 %collective-permute-start.43 = (bf16[960,256]{1,0:T(8,128)(2,1)S(1)}, bf16[960,256]{1,0:T(8,128)(2,1)S(1)}, u32[]{:S(2)}, u32[]{:S(2)}) collective-permute-start(bf16[960,256]{1,0:T(8,128)(2,1)S(1)} %get-tuple-element.140), channel_id=1, source_target_pairs={{0,8},{8,0},{16,24},{24,16},{1,9},{9,1},{17,25},{25,17},{2,10},{10... | collective-permute-start | bytes 1474568 | tf_op jit(solution)/shard_map/ppermute | solution.py:361
  206.7 21.3 %collective-permute-start.44 = (bf16[960,256]{1,0:T(8,128)(2,1)S(1)}, bf16[960,256]{1,0:T(8,128)(2,1)S(1)}, u32[]{:S(2)}, u32[]{:S(2)}) collective-permute-start(bf16[960,256]{1,0:T(8,128)(2,1)S(1)} %get-tuple-element.141), channel_id=1, source_target_pairs={{0,16},{8,24},{16,0},{24,8},{1,17},{9,25},{17,1},{25,9},{2,18},{10... | collective-permute-start | bytes 1474568 | tf_op jit(solution)/shard_map/ppermute | solution.py:361
  228.0 58.7 %collective-permute-start.40 = (bf16[960,256]{1,0:T(8,128)(2,1)S(1)}, bf16[960,256]{1,0:T(8,128)(2,1)S(1)}, u32[]{:S(2)}, u32[]{:S(2)}) collective-permute-start(bf16[960,256]{1,0:T(8,128)(2,1)S(1)} %get-tuple-element.137), channel_id=1, source_target_pairs={{0,16},{8,24},{16,0},{24,8},{1,17},{9,25},{17,1},{25,9},{2,18},{10... | collective-permute-start | bytes 1474568 | tf_op jit(solution)/shard_map/ppermute | solution.py:361
  229.0 67.6 %collective-permute-start.52 = (bf16[960,256]{1,0:T(8,128)(2,1)}, bf16[960,256]{1,0:T(8,128)(2,1)}, u32[]{:S(2)}, u32[]{:S(2)}) collective-permute-start(bf16[960,256]{1,0:T(8,128)(2,1)} %get-tuple-element.166), channel_id=1, source_target_pairs={{0,8},{8,0},{16,24},{24,16},{1,9},{9,1},{17,25},{25,17},{2,10},{10... | collective-permute-start | bytes 1474568 | tf_op jit(solution)/shard_map/ppermute | solution.py:361
  248.7 26.9 %collective-permute-start.55 = (bf16[160,640]{1,0:T(8,128)(2,1)S(1)}, bf16[160,640]{1,0:T(8,128)(2,1)S(1)}, u32[]{:S(2)}, u32[]{:S(2)}) collective-permute-start(bf16[160,640]{1,0:T(8,128)(2,1)S(1)} %add_convert_fusion.18), channel_id=1, source_target_pairs={{4,0},{5,1},{6,2},{7,3},{12,8},{13,9},{14,10},{15,11},{20,16},{21,... | collective-permute-start | bytes 614408 | tf_op jit(solution)/shard_map/ppermute | solution.py:373
  250.2 46.3 %collective-permute-start.64 = (bf16[960,256]{1,0:T(8,128)(2,1)}, bf16[960,256]{1,0:T(8,128)(2,1)}, u32[]{:S(2)}, u32[]{:S(2)}) collective-permute-start(bf16[960,256]{1,0:T(8,128)(2,1)} %get-tuple-element.178), channel_id=1, source_target_pairs={{0,8},{8,0},{16,24},{24,16},{1,9},{9,1},{17,25},{25,17},{2,10},{10... | collective-permute-start | bytes 1474568 | tf_op jit(solution)/shard_map/ppermute | solution.py:361
  265.0 31.6 %collective-permute-start.65 = (bf16[960,256]{1,0:T(8,128)(2,1)}, bf16[960,256]{1,0:T(8,128)(2,1)}, u32[]{:S(2)}, u32[]{:S(2)}) collective-permute-start(bf16[960,256]{1,0:T(8,128)(2,1)} %get-tuple-element.180), channel_id=1, source_target_pairs={{0,16},{8,24},{16,0},{24,8},{1,17},{9,25},{17,1},{25,9},{2,18},{10... | collective-permute-start | bytes 1474568 | tf_op jit(solution)/shard_map/ppermute | solution.py:361
  315.8 28.8 %collective-permute-start.51 = (bf16[960,256]{1,0:T(8,128)(2,1)S(1)}, bf16[960,256]{1,0:T(8,128)(2,1)S(1)}, u32[]{:S(2)}, u32[]{:S(2)}) collective-permute-start(bf16[960,256]{1,0:T(8,128)(2,1)S(1)} %add_convert_fusion.10), channel_id=1, source_target_pairs={{0,8},{8,0},{16,24},{24,16},{1,9},{9,1},{17,25},{25,17},{2,10},{10... | collective-permute-start | bytes 1474568 | tf_op jit(solution)/shard_map/ppermute | solution.py:361
  337.2 34.4 %collective-permute-start.86 = (bf16[960,256]{1,0:T(8,128)(2,1)}, bf16[960,256]{1,0:T(8,128)(2,1)}, u32[]{:S(2)}, u32[]{:S(2)}) collective-permute-start(bf16[960,256]{1,0:T(8,128)(2,1)} %add_convert_fusion.6), channel_id=1, source_target_pairs={{0,6},{1,7},{2,0},{3,1},{4,2},{5,3},{6,4},{7,5},{8,14},{9,15},{10,... | collective-permute-start | bytes 1474568 | tf_op jit(solution)/shard_map/ppermute | solution.py:365
  392.6 22.0 %collective-permute-start.68 = (bf16[4,256,256]{2,1,0:T(8,128)(2,1)S(1)}, bf16[4,256,256]{2,1,0:T(8,128)(2,1)S(1)}, u32[]{:S(2)}, u32[]{:S(2)}) collective-permute-start(bf16[4,256,256]{2,1,0:T(8,128)(2,1)S(1)} %add_convert_fusion.2), channel_id=1, source_target_pairs={{0,8},{8,0},{16,24},{24,16},{1,9},{9,1},{17,25},{25,17},{2,10},{10... | collective-permute-start | bytes 1572872 | tf_op jit(solution)/shard_map/ppermute | solution.py:361
  396.8 23.8 %collective-permute-start.70 = (bf16[4,256,256]{2,1,0:T(8,128)(2,1)S(1)}, bf16[4,256,256]{2,1,0:T(8,128)(2,1)S(1)}, u32[]{:S(2)}, u32[]{:S(2)}) collective-permute-start(bf16[4,256,256]{2,1,0:T(8,128)(2,1)S(1)} %add_convert_fusion.1), channel_id=1, source_target_pairs={{0,16},{8,24},{16,0},{24,8},{1,17},{9,25},{17,1},{25,9},{2,18},{10... | collective-permute-start | bytes 1572872 | tf_op jit(solution)/shard_map/ppermute | solution.py:361
  410.2 25.8 %collective-permute-start.88 = (bf16[960,256]{1,0:T(8,128)(2,1)S(1)}, bf16[960,256]{1,0:T(8,128)(2,1)S(1)}, u32[]{:S(2)}, u32[]{:S(2)}) collective-permute-start(bf16[960,256]{1,0:T(8,128)(2,1)S(1)} %add_convert_fusion.4), channel_id=1, source_target_pairs={{0,6},{1,7},{2,0},{3,1},{4,2},{5,3},{6,4},{7,5},{8,14},{9,15},{10,... | collective-permute-start | bytes 1474568 | tf_op jit(solution)/shard_map/ppermute | solution.py:365
  (199 other events, 2916.7 us)

commit v4 on v3

--- a/solution.py
+++ b/solution.py
@@ -614,8 +614,8 @@
     ids_ref, counts_ref, q_ref, do_ref = refs[:4]
     blocks = refs[4:12]
     lse_ref, cos_ref, sin_ref, dq_ref = refs[12:16]
-    targets = refs[16:24]
-    k_ref, v_ref, bias_ref, dk_ref, dv_ref = refs[24:]
+    targets = [ref.at[s] for ref in refs[16:18] for s in range(4)]
+    k_ref, v_ref, bias_ref, dk_ref, dv_ref = refs[18:]
     cap = q_ref.shape[2] // 2
     share = QUERY_HEADS // KEY_HEADS
     half = HEAD_WIDTH // 2
@@ -742,8 +742,12 @@
             ).astype(jnp.bfloat16)
 
 
+def targets_of(refs):
+    return list(refs[:4]) + [refs[4].at[pl.ds(4 * k, 4)] for k in range(4)]
+
+
 def out_grad_kernel(ids_ref, att_a_ref, att_b_ref, pieces_ref, *refs):
-    grads, att_rel = refs[:8], refs[8]
+    grads, att_rel = targets_of(refs[:5]), refs[5]
     depth = pieces_ref.shape[0] // 8
     wide = att_rel.shape[0] // 4
     fill_relative(ids_ref, att_rel, att_a_ref, att_b_ref)
@@ -758,9 +762,9 @@
 def finish_q_kernel(*refs):
     ids_ref, own, other = refs[0], refs[1:6], refs[6:11]
     n1_ref, dq_a_ref, dq_b_ref = refs[11:14]
-    out_grads = refs[14:22]
-    dn_ref, grads = refs[22], refs[23:31]
-    n1_rel, d_ref, dq_ref = refs[31:]
+    out_grads = targets_of(refs[14:19])
+    dn_ref, grads = refs[19], targets_of(refs[20:25])
+    n1_rel, d_ref, dq_ref = refs[25:]
     cap = dq_a_ref.shape[1]
     width = dq_a_ref.shape[0]
     q_cols = width // 8
@@ -787,18 +791,15 @@
                 target[s, depth:, :] = out_grads[core_rel * 4 + k][s]
 
 
-def finish_kv_kernel(*refs):
-    ids_ref, own, other = refs[0], refs[1:6], refs[6:11]
-    n1_ref, dkv_a_ref, dkv_b_ref, cos_ref, sin_ref, dn_ref, dh_ref, x_ref, gain_ref = refs[11:20]
-    tokens_ref, gain_grad_ref = refs[20:22]
-    grads = refs[22:30]
-    n1_rel, d_ref, dkv_ref = refs[30:]
-    width, rows = dh_ref.shape
-    cap = rows // 2
+def kv_grad_kernel(
+    ids_ref, n1_ref, dkv_a_ref, dkv_b_ref, cos_ref, sin_ref, dkv_ref, *refs
+):
+    grads = targets_of(refs[:5])
+    n1_rel, d_ref = refs[5:]
+    cap = dkv_a_ref.shape[0]
     kv_width = KEY_HEADS * HEAD_WIDTH
-    q_cols, k_cols = width // 8, kv_width // 8
+    k_cols = kv_width // 8
     half = HEAD_WIDTH // 2
-    block = n1_ref.shape[1]
     wide = n1_rel.shape[0] // 4
     cosine, sine = cos_ref[...], sin_ref[...]
     d_ref[:, :cap] = dkv_a_ref[...].T
@@ -821,22 +822,31 @@
                 0,
             ).astype(jnp.bfloat16)
     fill_relative(ids_ref, n1_rel, n1_ref)
-    low = q_cols + 8
-    weights = jnp.concatenate(
-        [wide_rows(w, s, low, low + 2 * k_cols) for w in (own, other) for s in range(4)], 0
-    )
-    dn = product_tn(weights, dkv_ref[...])
-    for k in range(4):
-        i = ids_ref[0] ^ k
-        tokens_ref[pl.ds(pl.multiple_of(i * block, 16), block), :] = (
-            dn[k * wide : k * wide + block] + dn_ref[i]
-        )
     for core_rel in range(2):
         for s in range(4):
             low = (core_rel * 4 + s) * 2 * k_cols
             got = product_nt(dkv_ref[low : low + 2 * k_cols, :], n1_rel[...]).astype(jnp.bfloat16)
             for k in range(4):
                 grads[core_rel * 4 + k][s] = got[:, k * wide : (k + 1) * wide]
+
+
+def finish_kernel(*refs):
+    ids_ref, own, other = refs[0], refs[1:6], refs[6:11]
+    dkv_ref, dn_ref, dh_ref, x_ref, gain_ref, tokens_ref, gain_grad_ref = refs[11:]
+    width = dh_ref.shape[0]
+    block = dn_ref.shape[1]
+    kv_rows = dkv_ref.shape[0] // 8
+    low = own[0].shape[1] - kv_rows
+    wide = own[0].shape[2]
+    weights = jnp.concatenate(
+        [wide_rows(w, s, low, low + kv_rows) for w in (own, other) for s in range(4)], 0
+    )
+    dn = product_tn(weights, dkv_ref[...])
+    for k in range(4):
+        i = ids_ref[0] ^ k
+        tokens_ref[pl.ds(pl.multiple_of(i * block, 16), block), :] = (
+            dn[k * wide : k * wide + block] + dn_ref[i]
+        )
     x = x_ref[...].astype(jnp.float32)
     rms = mean_square(x)
     dn = tokens_ref[...]
@@ -1016,7 +1026,6 @@
         0,
         16,
     )
-    dy_other = swap_core(dy)
 
     along = jnp.stack(chain, 0)
     extras = along[:, q_cols : q_cols + 2, :block]
@@ -1033,7 +1042,7 @@
     z_three = shift_z(z_two, 1)
     far_zero = swap_dp(after(x_zero, *first_own[3:]), 2)
     z_one_next = after(z_one, *first_own[3:])
-    x_one, y_one = swap_dp(z_one_next, 1), swap_dp(z_one_next, 2)
+    x_one = swap_dp(z_one_next, 1)
 
     by_core = jnp.where(
         core_id == 0, jnp.stack([extras, other_extras], 1), jnp.stack([other_extras, extras], 1)
@@ -1053,7 +1062,7 @@
     cosine, sine = cosine[:, 0, :].T, sine[:, 0, :].T
     x_wide = x.astype(jnp.float32)
     n1 = (x_wide * mean_square(x_wide) * gain_one).astype(jnp.bfloat16).reshape(4, block, rows)
-    n1_next = after(n1, z_one)
+    n1_next = after(n1, z_two)
 
     query, kv = run(
         project_kernel,
@@ -1070,15 +1079,23 @@
         2 * (width + 2 * kv_width) * width * rows,
         24,
     )
-    kv_next = after(kv, z_two)
-    kv_own = [kv] + [shift_z_up(kv_next, step) for step in (1, 2, 3)]
-    kv_other = [swap_core(piece) for piece in kv_own]
-    z_two_next, x_zero_next = after(z_two, kv), after(y_one, kv)
-    x_two, y_two = swap_dp(z_two_next, 1), swap_dp(z_two_next, 2)
-    far_one = swap_dp(x_zero_next, 1)
-    x_three, y_three = swap_dp(z_three, 1), swap_dp(z_three, 2)
-    far_two = swap_dp(x_two, 2)
-    far_three = swap_dp(y_three, 1)
+    kv_zero = after(kv, x_one, far_zero)
+    kv_one = shift_z_up(kv_zero, 1)
+    x_two = swap_dp(after(z_two, kv_zero), 1)
+    y_one = swap_dp(after(z_one, kv_zero), 2)
+    wave = (kv_one, x_two, y_one, z_three)
+    kv_two = shift_z_up(after(*wave), 1)
+    far_one = swap_dp(after(y_one, *wave), 1)
+    y_two = swap_dp(after(z_two, *wave), 2)
+    wave = (kv_two, far_one, y_two)
+    kv_three = shift_z_up(after(*wave), 1)
+    x_three = swap_dp(after(z_three, *wave), 1)
+    y_three = swap_dp(after(z_three, *wave), 2)
+    wave = (kv_three, x_three, y_three)
+    far_two = swap_dp(after(x_two, *wave), 2)
+    far_three = swap_dp(after(y_three, *wave), 1)
+    kv_own = [kv, kv_one, kv_two, kv_three]
+    kv_other = [swap_core(piece) for piece in (kv_zero, kv_one, kv_two, kv_three)]
     pieces = [mlp_piece, z_one, z_two, z_three]
     pieces += [x_zero, x_one, x_two, x_three]
     pieces += [y_zero, y_one, y_two, y_three]
@@ -1106,17 +1123,11 @@
             24,
         )
 
-    att_a, lse_a = attend(0, after(query, x_one, y_one, far_zero, x_two, y_two, z_three))
-    att_b, lse_b = attend(1, after(query, x_three, y_three, far_one, far_two, att_a))
-    att_a = att_a.reshape(4, block, cap)
-    att_b = att_b.reshape(4, block, cap)
-    lse = (lse_a, lse_b)
-    blocks = (4, block, rows)
-    wide_blocks = (4, block, padded)
+    att_a, lse_a = attend(0, after(query, x_three, y_three))
     (out_own,) = run(
         collect_kernel,
         "collect",
-        tuple(pieces),
+        tuple(pieces[:15]) + (after(far_three, att_a),),
         [ANY] * 16,
         [struct((4, q_rows, 4 * wide))],
         [VMEM],
@@ -1125,10 +1136,17 @@
         8,
     )
     out_other = swap_core(out_own)
+    dy_other = swap_core(after(dy, att_a))
+    att_b, lse_b = attend(1, after(query, out_own))
+    att_a = att_a.reshape(4, block, cap)
+    att_b = att_b.reshape(4, block, cap)
+    lse = (lse_a, lse_b)
+    blocks = (4, block, rows)
+    wide_blocks = (4, block, padded)
     h, n2 = run(
         hidden_kernel,
         "hidden",
-        (ids, out_own, out_other, att_a, att_b, x, gain_two),
+        (ids, out_own, out_other, att_a, att_b, after(x, dy_other), gain_two),
         [SMEM] + [VMEM] * 6,
         (struct((width, rows), jnp.float32), struct((width, padded))),
         [VMEM] * 2,
@@ -1166,27 +1184,11 @@
         18 * 16 * half * block * 2 * rows,
         44,
     )
-    keep, send, grads = results[0], results[1], results[2:]
+    keep, send = results[:2]
+    home, to_x, to_y, far = results[2:6], results[6:10], results[10:14], results[14:18]
     arrived = swap_core(send)
-    home, to_x, to_y, far = grads[:4], grads[4:8], grads[8:12], grads[12:]
-
-    def first_leg(group, *deps):
-        a, b = 2 * group, 2 * group + 1
-        return (
-            swap_dp(after(far[a], *deps), 2),
-            swap_dp(after(far[b], *deps), 1),
-            swap_dp(after(to_x[b], *deps), 1),
-            swap_dp(after(to_y[a], *deps), 2),
-        )
-
-    def second_leg(group, legs, *deps):
-        a, b = 2 * group, 2 * group + 1
-        via_y, via_x = after(legs[0], *deps), after(legs[1], *deps)
-        x_a = swap_dp(add_low(to_x[a], via_y), 1)
-        y_b = swap_dp(add_low(to_y[b], via_x), 2)
-        return x_a, y_b
-
-    legs_one = first_leg(1)
+    via_three, via_two = swap_dp(far[3], 1), swap_dp(far[2], 2)
+
     output, dh, mixed_gradient, gain_two_grad, da_pieces = run(
         turn_point_kernel,
         "turn_point",
@@ -1205,9 +1207,6 @@
         24,
     )
     output = output.T.reshape(batches, cap, width)
-    legs_zero = first_leg(0, mixed_gradient)
-    turned_one = second_leg(1, legs_one, mixed_gradient)
-
     def attend_back(mb, mixed):
         return run(
             functools.partial(attend_back_kernel, mb),
@@ -1224,8 +1223,8 @@
                 sine,
             ),
             [SMEM, SMEM] + [VMEM] * 13,
-            [struct((QUERY_HEADS, HEAD_WIDTH, cap))] + [struct((cap, 2 * kv_width))] * 8,
-            [VMEM] * 9,
+            [struct((QUERY_HEADS, HEAD_WIDTH, cap))] + [struct((4, cap, 2 * kv_width))] * 2,
+            [VMEM] * 3,
             head_scratch
             + [
                 pltpu.VMEM((KEY_HEADS, 8 * cap, HEAD_WIDTH), jnp.bfloat16),
@@ -1236,7 +1235,8 @@
         )
 
     def sum_cores(own, other):
-        return [add_low(own[s], swap_core(other[s])) for s in (3, 2, 1, 0)][::-1]
+        arrived = swap_core(other)
+        return [add_low(own[s], arrived[s]) for s in range(4)]
 
     def sum_z(summed):
         total = summed[0].astype(jnp.float32)
@@ -1244,33 +1244,115 @@
             total = total + shift_z_down(summed[s], s).astype(jnp.float32)
         return total
 
-    back_a = attend_back(0, after(mixed_gradient, *legs_one))
+    wave = (via_three, via_two, mixed_gradient)
+    x_three, y_two = swap_dp(after(to_x[3], *wave), 1), swap_dp(after(to_y[2], *wave), 2)
+    x_two = swap_dp(add_low(to_x[2], after(via_two, *wave)), 1)
+    y_three = swap_dp(add_low(to_y[3], after(via_three, *wave)), 2)
+    back_a = attend_back(0, after(mixed_gradient, *wave))
+    wave = (back_a[0], x_three, y_two, x_two, y_three)
+    via_one, via_zero = swap_dp(after(far[1], *wave), 1), swap_dp(after(far[0], *wave), 2)
+    hop = shift_z(add_low(after(home[3], back_a[0]), x_three, y_three), -1)
     out_grads = run(
         out_grad_kernel,
         "out_grad",
-        (ids, att_a, att_b, after(da_pieces, back_a[0])),
+        (ids, att_a, att_b, after(da_pieces, *wave)),
         [SMEM] + [VMEM] * 3,
-        [struct((4, q_rows, wide))] * 8,
-        [VMEM] * 8,
+        [struct((4, q_rows, wide))] * 4 + [struct((16, q_rows, wide))],
+        [VMEM] * 5,
         [pltpu.VMEM((4 * wide, rows), jnp.bfloat16)],
         2 * width * width * rows,
         16,
     )
-    summed_a = sum_cores(back_a[1:5], back_a[5:9])
-    dkv_a = sum_z(summed_a)
-    back_b = attend_back(1, after(mixed_gradient, *summed_a, *turned_one, out_grads[0]))
-    dkv_b = sum_z(sum_cores(back_b[1:5], back_b[5:9]))
-    turned_zero = second_leg(0, legs_zero, back_b[0])
-    summed_three = add_low(home[3], legs_one[2], after(turned_one[1], back_b[0]))
-    summed_two = add_low(home[2], after(turned_one[0], back_b[0]), legs_one[3])
-    hop = shift_z(summed_three, -1)
-    hop = shift_z(add_low(summed_two, hop), -1)
-    summed_one = add_low(home[1], legs_zero[2], turned_zero[1])
-    hop = shift_z(add_low(summed_one, hop), -1)
+    summed_a = sum_cores(*back_a[1:])
+    wave = (via_one, via_zero, hop, out_grads[0])
+    dkv_a = sum_z([after(piece, *wave) for piece in summed_a])
+    x_one, y_zero = swap_dp(after(to_x[1], *wave), 1), swap_dp(after(to_y[0], *wave), 2)
+    back_b = attend_back(1, after(mixed_gradient, *summed_a, *wave))
+    wave = (back_b[0], dkv_a, x_one, y_zero)
+    x_zero = swap_dp(add_low(to_x[0], after(via_zero, *wave)), 1)
+    y_one = swap_dp(add_low(to_y[1], after(via_one, *wave)), 2)
+    summed_b = sum_cores(back_b[1], after(back_b[2], dkv_a, x_one, y_zero))
+    parts_b = [shift_z_down(summed_b[s], s) for s in (1, 2, 3)]
+    def sum_pair(parts):
+        arrived = swap_core(parts[4])
+        return [add_low(parts[k], arrived[4 * k : 4 * k + 4]) for k in range(4)]
+
+    def reduce_all(mine):
+        summed = [mine[0]] + [swap_dp(mine[k], k) for k in (1, 2, 3)]
+        out = [add_low(*[piece[s] for piece in summed]) for s in range(4)]
+        total = out[0].astype(jnp.float32)
+        for s in (1, 2, 3):
+            total = total + shift_z(out[s], -s).astype(jnp.float32)
+        return total
+
+    q_results = run(
+        finish_q_kernel,
+        "finish_q",
+        (
+            ids,
+            *first_own,
+            *first_other,
+            after(n1, *wave, *summed_b),
+            back_a[0].reshape(width, cap),
+            back_b[0].reshape(width, cap),
+            *out_grads,
+        ),
+        [SMEM] + [VMEM] * 18,
+        [struct(blocks, jnp.float32)]
+        + [struct((4, 2 * q_rows, wide))] * 4
+        + [struct((16, 2 * q_rows, wide))],
+        [VMEM] * 6,
+        [
+            pltpu.VMEM((4 * wide, rows), jnp.bfloat16),
+            pltpu.VMEM((width, rows), jnp.float32),
+            pltpu.VMEM((8 * q_rows, rows), jnp.bfloat16),
+        ],
+        4 * width * width * rows,
+        24,
+    )
+    dn_q = q_results[0]
+    dkv_b = after(summed_b[0], dn_q).astype(jnp.float32)
+    for part in parts_b:
+        dkv_b = dkv_b + part.astype(jnp.float32)
+    hop = shift_z(add_low(home[2], x_two, y_two, after(hop, dkv_b)), -1)
+    q_out_mine = sum_pair(q_results[1:])
+    q_out_total = reduce_all(q_out_mine)
+    grad_query = q_out_total[:q_cols, :block].T
+    grad_out = q_out_total[q_rows : q_rows + q_cols, :block].T
+
+    dkv_pieces, *kv_grads = run(
+        kv_grad_kernel,
+        "kv_grad",
+        (ids, after(n1, x_zero, y_one, *q_out_mine), dkv_a, dkv_b, cosine, sine),
+        [SMEM] + [VMEM] * 5,
+        [struct((16 * k_cols, rows))]
+        + [struct((4, 2 * k_cols, wide))] * 4
+        + [struct((16, 2 * k_cols, wide))],
+        [VMEM] * 6,
+        [
+            pltpu.VMEM((4 * wide, rows), jnp.bfloat16),
+            pltpu.VMEM((2 * kv_width, rows), jnp.float32),
+        ],
+        4 * kv_width * width * rows,
+        20,
+    )
+    grad_tokens, gain_one_grad = run(
+        finish_kernel,
+        "finish",
+        (ids, *first_own, *first_other, dkv_pieces, dn_q, dh, x, gain_one),
+        [SMEM] + [VMEM] * 15,
+        [struct((width, rows), jnp.float32), struct((width, 1), jnp.float32)],
+        [VMEM] * 2,
+        [],
+        4 * kv_width * width * rows,
+        24,
+    )
+    grad_tokens = grad_tokens.T.reshape(batches, cap, width)
+    hop = shift_z(add_low(home[1], x_one, y_one, after(hop, dkv_pieces)), -1)
     mlp_total = (
         home[0].astype(jnp.float32)
-        + turned_zero[0].astype(jnp.float32)
-        + legs_zero[3].astype(jnp.float32)
+        + y_zero.astype(jnp.float32)
+        + x_zero.astype(jnp.float32)
         + hop.astype(jnp.float32)
     )
     grad_gate = mlp_total[:half, :block].T
@@ -1284,82 +1366,16 @@
         core_id == 0, jnp.concatenate([stay, taken], 0), jnp.concatenate([taken, stay], 0)
     )
 
-    def reduce_all(parts):
-        mine = [add_low(parts[k], swap_core(parts[4 + k])) for k in range(4)]
-        summed = [mine[0]] + [swap_dp(mine[k], k) for k in (1, 2, 3)]
-        out = [add_low(*[piece[s] for piece in summed]) for s in range(4)]
-        total = out[0].astype(jnp.float32)
-        for s in (1, 2, 3):
-            total = total + shift_z(out[s], -s).astype(jnp.float32)
-        return total
-
-    q_results = run(
-        finish_q_kernel,
-        "finish_q",
-        (
-            ids,
-            *first_own,
-            *first_other,
-            after(n1, dkv_a, *legs_zero),
-            back_a[0].reshape(width, cap),
-            back_b[0].reshape(width, cap),
-            *out_grads,
-        ),
-        [SMEM] + [VMEM] * 21,
-        [struct(blocks, jnp.float32)] + [struct((4, 2 * q_rows, wide))] * 8,
-        [VMEM] * 9,
-        [
-            pltpu.VMEM((4 * wide, rows), jnp.bfloat16),
-            pltpu.VMEM((width, rows), jnp.float32),
-            pltpu.VMEM((8 * q_rows, rows), jnp.bfloat16),
-        ],
-        4 * width * width * rows,
-        24,
-    )
-    dn_q = q_results[0]
-    q_out_total = reduce_all(q_results[1:])
-    grad_query = q_out_total[:q_cols, :block].T
-    grad_out = q_out_total[q_rows : q_rows + q_cols, :block].T
-
-    kv_results = run(
-        finish_kv_kernel,
-        "finish_kv",
-        (
-            ids,
-            *first_own,
-            *first_other,
-            after(n1, *turned_zero),
-            dkv_a,
-            dkv_b,
-            cosine,
-            sine,
-            dn_q,
-            dh,
-            x,
-            gain_one,
-        ),
-        [SMEM] + [VMEM] * 19,
-        [struct((width, rows), jnp.float32), struct((width, 1), jnp.float32)]
-        + [struct((4, 2 * k_cols, wide))] * 8,
-        [VMEM] * 10,
-        [
-            pltpu.VMEM((4 * wide, rows), jnp.bfloat16),
-            pltpu.VMEM((2 * kv_width, rows), jnp.float32),
-            pltpu.VMEM((16 * k_cols, rows), jnp.bfloat16),
-        ],
-        8 * kv_width * width * rows,
-        24,
-    )
-    grad_tokens = kv_results[0].T.reshape(batches, cap, width)
-    kv_total = reduce_all(kv_results[2:])
-    gain_total = jnp.concatenate([kv_results[1], gain_two_grad], 1).T
+    kv_mine = sum_pair(kv_grads)
+    kv_total = reduce_all(kv_mine)
+    gain_total = after(jnp.concatenate([gain_one_grad, gain_two_grad], 1).T, *kv_mine)
     gain_total = gain_total + swap_core(gain_total)
-    gain_total = (gain_total + swap_dp(gain_total, 1)) + (
-        swap_dp(gain_total, 2) + swap_dp(gain_total, 3)
-    )
-    gain_total = (gain_total + shift_z(gain_total, 2)) + (
-        shift_z(gain_total, 1) + shift_z(gain_total, -1)
-    )
+    gain_total = gain_total + swap_dp(gain_total, 1)
+    gain_total = gain_total + swap_dp(gain_total, 2)
+    for mask in (2, 4):
+        gain_total = gain_total + lax.ppermute(
+            gain_total, "fsdp", [(j, j ^ mask) for j in range(8)]
+        )
     gain_grad = lax.dynamic_slice_in_dim(gain_total, slot * q_cols, q_cols, 1)
     return (
         output,

time: 448 us -> 367 us (0.82)
  waiting for transfers between devices: 165 us -> 100 us
  other arithmetic: 19.8 us -> 11.6 us
  starting transfers between devices: 101 us -> 94.5 us
  local copies, waits for them, and re-layouts: 43.5 us -> 48.6 us
  Pallas kernels: 108 us -> 103 us
    ppermute x37 -> x36, waiting for transfers between devices: 80.7 us -> 41 us  [swap_dp(): return lax.ppermute(value, 'dp', [(j, j ^ mask) for j in range(4)])]
    ppermute x6, waiting for transfers between devices: 44.7 us -> 16.1 us  [shift_z_down(): lax.ppermute(value, 'fsdp', [(j, j - 2 * step) for j in range(8) if j - 2...]
    ppermute x18 -> x15, starting transfers between devices: 35.4 us -> 24.7 us  [shift_z(): lax.ppermute(value, 'fsdp', [(j, (j + 2 * step) % 8) for j in range(8)])]
    convert_element_type x21 -> x11, other arithmetic: 12.4 us -> 4.42 us  [add_low(): return total.astype(jnp.bfloat16)]
    ppermute x3, starting transfers between devices: 8.78 us -> 15.5 us  [shift_z_up(): lax.ppermute(value, 'fsdp', [(j, j + 2 * step) for j in range(8) if j + 2...]
    pallas_call x15 -> x16, Pallas kernels: 108 us -> 103 us  [run(): pl.pallas_call(body, out_shape=tuple(outs), in_specs=in_specs, out_specs=...]
    unnamed x261 -> x187, local copies, waits for them, and re-layouts: 32.8 us -> 37.9 us
    ppermute x18 -> x15, waiting for transfers between devices: 20.3 us -> 17.3 us  [shift_z(): lax.ppermute(value, 'fsdp', [(j, (j + 2 * step) % 8) for j in range(8)])]
  transfers between devices with their start and end apart: 97 -> 83, of which waited for: 44 -> 35; matrix products, arithmetic and copies ran while one was open for 7% -> 7% of each run, Pallas kernels for 14% -> 18%
where the time goes in v4:
time: 367 us; the launch traced here: 360 us
  Pallas kernels  103 us (28%)
  waiting for transfers between devices  100 us (27%)
  starting transfers between devices  94.5 us (26%)
  local copies, waits for them, and re-layouts  48.6 us (13%)
  other arithmetic  11.6 us (3%)
    pallas_call x16, Pallas kernels, run(): pl.pallas_call(body, out_shape=tuple(outs), in_specs=in_specs, out_specs=...  103 us
    ppermute x36, starting transfers between devices, swap_dp(): return lax.ppermute(value, 'dp', [(j, j ^ mask) for j in range(4)])  41.2 us
    ppermute x36, waiting for transfers between devices, swap_dp(): return lax.ppermute(value, 'dp', [(j, j ^ mask) for j in range(4)])  41 us
    unnamed x187, local copies, waits for them, and re-layouts  37.9 us
    ppermute x15, starting transfers between devices, shift_z(): lax.ppermute(value, 'fsdp', [(j, (j + 2 * step) % 8) for j in range(8)])  24.7 us
    ppermute x15, waiting for transfers between devices, shift_z(): lax.ppermute(value, 'fsdp', [(j, (j + 2 * step) % 8) for j in range(8)])  17.3 us
    ppermute x6, waiting for transfers between devices, shift_z_down(): lax.ppermute(value, 'fsdp', [(j, j - 2 * step) for j in range(8) if j - 2...  16.1 us
    ppermute x3, waiting for transfers between devices, shift_z_up(): lax.ppermute(value, 'fsdp', [(j, j + 2 * step) for j in range(8) if j + 2...  16 us
  transfers between devices with their start and end apart: 83, of which 35 were waited for; matrix products, arithmetic and copies ran while one was open for 7% of the time, Pallas kernels for 18%

profile of v4, /device:TPU:0, one launch (start us, length us, event | category | flops | bytes accessed | tf_op | source)
XLA Modules:
  0.0 360.2 jit_solution(5012313680438969647)
XLA Ops:
  5.4 5.1 %collective-permute-start.3 = (bf16[208,256]{1,0:T(8,128)(2,1)S(1)}, bf16[208,256]{1,0:T(8,128)(2,1)S(1)}, u32[]{:S(2)}, u32[]{:S(2)}) collective-permute-start(bf16[208,256]{1,0:T(8,128)(2,1)S(1)} %pack_first.1), channel_id=1, source_target_pairs={{0,6},{1,7},{2,0},{3,1},{4,2},{5,3},{6,4},{7,5},{8,14},{9,15},{10,... | collective-permute-start | bytes 319496 | tf_op jit(solution)/shard_map/ppermute | solution.py:365
  25.5 7.0 %collective-permute-done.8.refs_8_.refs_13_ = bf16[1088,256]{1,0:T(8,128)(2,1)S(1)} collective-permute-done((bf16[1088,256]{1,0:T(8,128)(2,1)S(1)}, bf16[1088,256]{1,0:T(8,128)(2,1)S(1)}, u32[]{:S(2)}, u32[]{:S(2)}) %collective-permute-start.8) | collective-permute-done | bytes 557088 | tf_op jit(solution)/shard_map/ppermute | solution.py:361
  40.1 4.8 %collective-permute-done.11.refs_3_ = bf16[4,208,256]{2,1,0:T(8,128)(2,1)S(1)} collective-permute-done((bf16[4,208,256]{2,1,0:T(8,128)(2,1)S(1)}, bf16[4,208,256]{2,1,0:T(8,128)(2,1)S(1)}, u32[]{:S(2)}, u32[]{:S(2)}) %collective-permute-start.11) | collective-permute-done | bytes 426016 | tf_op jit(solution)/shard_map/ppermute | solution.py:361
  71.2 5.1 %collective-permute-start.22 = (bf16[320,640]{1,0:T(8,128)(2,1)S(1)}, bf16[320,640]{1,0:T(8,128)(2,1)}, u32[]{:S(2)}, u32[]{:S(2)}) collective-permute-start(bf16[320,640]{1,0:T(8,128)(2,1)S(1)} %get-tuple-element.120.refs_3_.refs_4_), channel_id=1, source_target_pairs={{0,2},{1,3},{2,4},{3,5},{4,6},{5,7},{8,10},{9,11},{10,12},{11,13},... | collective-permute-start | bytes 1228808 | tf_op jit(solution)/shard_map/ppermute | solution.py:369
  76.3 6.7 %collective-permute-done.22.refs_4_.refs_5_ = bf16[320,640]{1,0:T(8,128)(2,1)} collective-permute-done((bf16[320,640]{1,0:T(8,128)(2,1)S(1)}, bf16[320,640]{1,0:T(8,128)(2,1)}, u32[]{:S(2)}, u32[]{:S(2)}) %collective-permute-start.22) | collective-permute-done | bytes 409632 | tf_op jit(solution)/shard_map/ppermute | solution.py:369
  87.0 5.1 %collective-permute-start.24 = (bf16[320,640]{1,0:T(8,128)(2,1)}, bf16[320,640]{1,0:T(8,128)(2,1)}, u32[]{:S(2)}, u32[]{:S(2)}) collective-permute-start(bf16[320,640]{1,0:T(8,128)(2,1)} %collective-permute-done.22.refs_4_.refs_5_), channel_id=1, source_target_pairs={{0,2},{1,3},{2,4},{3,5},{4,6},{5,7},{8,10},{9,11},{10,12},{11,13},... | collective-permute-start | bytes 1228808 | tf_op jit(solution)/shard_map/ppermute | solution.py:369
  92.1 5.8 %collective-permute-done.24.refs_5_.refs_6_ = bf16[320,640]{1,0:T(8,128)(2,1)} collective-permute-done((bf16[320,640]{1,0:T(8,128)(2,1)}, bf16[320,640]{1,0:T(8,128)(2,1)}, u32[]{:S(2)}, u32[]{:S(2)}) %collective-permute-start.24) | collective-permute-done | bytes 409632 | tf_op jit(solution)/shard_map/ppermute | solution.py:369
  101.8 5.3 %collective-permute-start.29 = (bf16[320,640]{1,0:T(8,128)(2,1)}, bf16[320,640]{1,0:T(8,128)(2,1)}, u32[]{:S(2)}, u32[]{:S(2)}) collective-permute-start(bf16[320,640]{1,0:T(8,128)(2,1)} %collective-permute-done.24.refs_5_.refs_6_), channel_id=1, source_target_pairs={{0,2},{1,3},{2,4},{3,5},{4,6},{5,7},{8,10},{9,11},{10,12},{11,13},... | collective-permute-start | bytes 1228808 | tf_op jit(solution)/shard_map/ppermute | solution.py:369
  108.4 3.5 collective-permute-done.29.refs_6_.refs_7_
  120.8 9.5 %attend.2 = (bf16[15,64,160]{2,1,0:T(8,128)(2,1)S(1)}, f32[5,1,480]{2,1,0:T(1,128)S(1)}) custom-call(s32[4]{0:T(128)S(1)} %pad_add_fusion.ids_ref.refs_0_, s32[16]{0:T(128)S(1)} %reshape.239.refs_1_, bf16[15,64,320]{2,1,0:T(8,128)(2,1)S(1)} %copy-done.70, bf16[320,640]{1,0:T(8,128)(2,1)S(1)} %copy-done.76, ...), custom_call_target="tpu_custom_call" | custom-call | flops 3145728000 | bytes 4208080 | tf_op jit(solution)/shard_map/attend/pallas_call | solution.py:409
  132.2 9.9 %attend.3 = (bf16[15,64,160]{2,1,0:T(8,128)(2,1)S(1)}, f32[5,1,480]{2,1,0:T(1,128)S(1)}) custom-call(s32[4]{0:T(128)S(1)} %pad_add_fusion.ids_ref.refs_0_, s32[16]{0:T(128)S(1)} %reshape.239.refs_1_, bf16[15,64,320]{2,1,0:T(8,128)(2,1)S(1)} %copy-done.70, bf16[320,640]{1,0:T(8,128)(2,1)S(1)} %copy-done.76, ...), custom_call_target="tpu_custom_call" | custom-call | flops 3145728000 | bytes 4208080 | tf_op jit(solution)/shard_map/attend/pallas_call | solution.py:409
  147.9 29.7 %mlp.1 = (f32[2,960,320]{2,1,0:T(8,128)}, bf16[2,960,384]{2,1,0:T(8,128)(2,1)}, bf16[960,256]{1,0:T(8,128)(2,1)S(1)}, bf16[960,256]{1,0:T(8,128)(2,1)S(1)}, bf16...) custom-call(s32[4]{0:T(128)S(1)} %pad_add_fusion.ids_ref.refs_0_, ...), custom_call_target="tpu_custom_call" | custom-call | flops 14155776000 | bytes 23658512 | tf_op jit(solution)/shard_map/mlp/pallas_call | solution.py:409
  186.2 5.2 %collective-permute-done.40 = bf16[960,256]{1,0:T(8,128)(2,1)S(1)} collective-permute-done((bf16[960,256]{1,0:T(8,128)(2,1)S(1)}, bf16[960,256]{1,0:T(8,128)(2,1)S(1)}, u32[]{:S(2)}, u32[]{:S(2)}) %collective-permute-start.40) | collective-permute-done | bytes 491552 | tf_op jit(solution)/shard_map/ppermute | solution.py:361
  196.3 14.5 %attend_back.2 = (bf16[15,64,160]{2,1,0:T(8,128)(2,1)S(1)}, bf16[4,160,640]{2,1,0:T(8,128)(2,1)S(1)}, bf16[4,160,640]{2,1,0:T(8,128)(2,1)S(1)}) custom-call(s32[4]{0:T(128)S(1)} %pad_add_fusion.ids_ref.refs_0_, s32[16]{0:T(128)S(1)} %reshape.239.refs_1_, bf16[15,64,320]{2,1,0:T(8,128)(2,1)S(1)} %copy-done.71, bf16[15,64,320]{2,1,0:T(8,128)(2,1)S(1)} %bitcast.106, ...), custom_call_target="tpu_custom_call" | custom-call | flops 7864320000 | bytes 6542800 | tf_op jit(solution)/shard_map/attend_back/pallas_call | solution.py:409
  210.9 3.8 %collective-permute-done.44 = bf16[960,256]{1,0:T(8,128)(2,1)S(1)} collective-permute-done((bf16[960,256]{1,0:T(8,128)(2,1)S(1)}, bf16[960,256]{1,0:T(8,128)(2,1)S(1)}, u32[]{:S(2)}, u32[]{:S(2)}) %collective-permute-start.44) | collective-permute-done | bytes 491552 | tf_op jit(solution)/shard_map/ppermute | solution.py:361
  223.6 3.3 collective-permute-done.46
  235.3 14.8 %attend_back.3 = (bf16[15,64,160]{2,1,0:T(8,128)(2,1)S(1)}, bf16[4,160,640]{2,1,0:T(8,128)(2,1)S(1)}, bf16[4,160,640]{2,1,0:T(8,128)(2,1)S(1)}) custom-call(s32[4]{0:T(128)S(1)} %pad_add_fusion.ids_ref.refs_0_, s32[16]{0:T(128)S(1)} %reshape.239.refs_1_, bf16[15,64,320]{2,1,0:T(8,128)(2,1)S(1)} %copy-done.71, bf16[15,64,320]{2,1,0:T(8,128)(2,1)S(1)} %bitcast.107, ...), custom_call_target="tpu_custom_call" | custom-call | flops 7864320000 | bytes 6542800 | tf_op jit(solution)/shard_map/attend_back/pallas_call | solution.py:409
  254.2 4.0 %finish_q.1 = (f32[4,240,320]{2,1,0:T(8,128)S(1)}, bf16[4,256,256]{2,1,0:T(8,128)(2,1)S(1)}, bf16[4,256,256]{2,1,0:T(8,128)(2,1)S(1)}, bf16[4,256,256]{2,1,0:T(8...) custom-call(s32[4]{0:T(128)S(1)} %pad_add_fusion.ids_ref.refs_0_, ...), custom_call_target="tpu_custom_call" | custom-call | flops 1179648000 | bytes 12156944 | tf_op jit(solution)/shard_map/finish_q/pallas_call | solution.py:409
  263.4 8.4 %collective-permute-done.61 = bf16[160,640]{1,0:T(8,128)(2,1)S(1)} collective-permute-done((bf16[160,640]{1,0:T(8,128)(2,1)S(1)}, bf16[160,640]{1,0:T(8,128)(2,1)S(1)}, u32[]{:S(2)}, u32[]{:S(2)}) %collective-permute-start.61) | collective-permute-done | bytes 204832 | tf_op jit(solution)/shard_map/ppermute | solution.py:373
  272.8 7.2 %collective-permute-done.60 = bf16[160,640]{1,0:T(8,128)(2,1)S(1)} collective-permute-done((bf16[160,640]{1,0:T(8,128)(2,1)S(1)}, bf16[160,640]{1,0:T(8,128)(2,1)S(1)}, u32[]{:S(2)}, u32[]{:S(2)}) %collective-permute-start.60) | collective-permute-done | bytes 204832 | tf_op jit(solution)/shard_map/ppermute | solution.py:373
  283.8 3.3 kv_grad.1
  287.2 8.3 %collective-permute-done.75 = bf16[960,256]{1,0:T(8,128)(2,1)S(1)} collective-permute-done((bf16[960,256]{1,0:T(8,128)(2,1)S(1)}, bf16[960,256]{1,0:T(8,128)(2,1)S(1)}, u32[]{:S(2)}, u32[]{:S(2)}) %collective-permute-start.75) | collective-permute-done | bytes 491552 | tf_op jit(solution)/shard_map/ppermute | solution.py:365
  350.0 3.4 collective-permute-start.72
  355.4 3.9 %collective-permute-done.74 = bf16[80,256]{1,0:T(8,128)(2,1)S(1)} collective-permute-done((bf16[80,256]{1,0:T(8,128)(2,1)S(1)}, bf16[80,256]{1,0:T(8,128)(2,1)S(1)}, u32[]{:S(2)}, u32[]{:S(2)}) %collective-permute-start.74) | collective-permute-done | bytes 40992 | tf_op jit(solution)/shard_map/ppermute | solution.py:365
  (407 shorter events, 180.2 us)
Async XLA Ops:
  5.4 15.1 %collective-permute-start.3 = (bf16[208,256]{1,0:T(8,128)(2,1)S(1)}, bf16[208,256]{1,0:T(8,128)(2,1)S(1)}, u32[]{:S(2)}, u32[]{:S(2)}) collective-permute-start(bf16[208,256]{1,0:T(8,128)(2,1)S(1)} %pack_first.1), channel_id=1, source_target_pairs={{0,6},{1,7},{2,0},{3,1},{4,2},{5,3},{6,4},{7,5},{8,14},{9,15},{10,... | collective-permute-start | bytes 319496 | tf_op jit(solution)/shard_map/ppermute | solution.py:365
  21.5 16.4 %collective-permute-start.4 = (bf16[1088,256]{1,0:T(8,128)(2,1)S(1)}, bf16[1088,256]{1,0:T(8,128)(2,1)}, u32[]{:S(2)}, u32[]{:S(2)}) collective-permute-start(bf16[1088,256]{1,0:T(8,128)(2,1)S(1)} %pack_mlp.1.refs_0_.refs_5_), channel_id=1, source_target_pairs={{0,2},{1,3},{2,4},{3,5},{4,6},{5,7},{6,0},{7,1},{8,10},{9,11},{10,... | collective-permute-start | bytes 1671176 | tf_op jit(solution)/shard_map/ppermute | solution.py:365
  24.1 29.3 %collective-permute-start.14 = (bf16[4,208,256]{2,1,0:T(8,128)(2,1)S(1)}, bf16[4,208,256]{2,1,0:T(8,128)(2,1)S(1)}, u32[]{:S(2)}, u32[]{:S(2)}) collective-permute-start(bf16[4,208,256]{2,1,0:T(8,128)(2,1)S(1)} %pad_maximum_fusion.refs_1_), channel_id=1, source_target_pairs={{0,1},{1,0},{2,3},{3,2},{4,5},{5,4},{6,7},{7,6},{8,9},{9,8},{10,11... | collective-permute-start | bytes 1277960 | tf_op jit(solution)/shard_map/ppermute | solution.py:357
  37.9 17.3 %collective-permute-start.5 = (bf16[1088,256]{1,0:T(8,128)(2,1)}, bf16[1088,256]{1,0:T(8,128)(2,1)}, u32[]{:S(2)}, u32[]{:S(2)}) collective-permute-start(bf16[1088,256]{1,0:T(8,128)(2,1)} %collective-permute-done.4.refs_1_.refs_6_), channel_id=1, source_target_pairs={{0,2},{1,3},{2,4},{3,5},{4,6},{5,7},{6,0},{7,1},{8,10},{9,11},{10,... | collective-permute-start | bytes 1671176 | tf_op jit(solution)/shard_map/ppermute | solution.py:365
  57.1 19.2 %collective-permute-start.6 = (bf16[1088,256]{1,0:T(8,128)(2,1)}, bf16[1088,256]{1,0:T(8,128)(2,1)S(1)}, u32[]{:S(2)}, u32[]{:S(2)}) collective-permute-start(bf16[1088,256]{1,0:T(8,128)(2,1)} %collective-permute-done.5.refs_2_.refs_7_), channel_id=1, source_target_pairs={{0,2},{1,3},{2,4},{3,5},{4,6},{5,7},{6,0},{7,1},{8,10},{9,11},{10,... | collective-permute-start | bytes 1671176 | tf_op jit(solution)/shard_map/ppermute | solution.py:365
  113.3 17.0 %collective-permute-start.31 = (bf16[1088,256]{1,0:T(8,128)(2,1)}, bf16[1088,256]{1,0:T(8,128)(2,1)}, u32[]{:S(2)}, u32[]{:S(2)}) collective-permute-start(bf16[1088,256]{1,0:T(8,128)(2,1)} %collective-permute-done.28.refs_11_.refs_16_), channel_id=1, source_target_pairs={{0,8},{8,0},{16,24},{24,16},{1,9},{9,1},{17,25},{25,17},{2,10},{10... | collective-permute-start | bytes 1671176 | tf_op jit(solution)/shard_map/ppermute | solution.py:361
  191.8 19.1 %collective-permute-start.42 = (bf16[960,256]{1,0:T(8,128)(2,1)S(1)}, bf16[960,256]{1,0:T(8,128)(2,1)S(1)}, u32[]{:S(2)}, u32[]{:S(2)}) collective-permute-start(bf16[960,256]{1,0:T(8,128)(2,1)S(1)} %get-tuple-element.153), channel_id=1, source_target_pairs={{0,8},{8,0},{16,24},{24,16},{1,9},{9,1},{17,25},{25,17},{2,10},{10... | collective-permute-start | bytes 1474568 | tf_op jit(solution)/shard_map/ppermute | solution.py:361
  193.1 17.8 %collective-permute-start.43 = (bf16[960,256]{1,0:T(8,128)(2,1)S(1)}, bf16[960,256]{1,0:T(8,128)(2,1)S(1)}, u32[]{:S(2)}, u32[]{:S(2)}) collective-permute-start(bf16[960,256]{1,0:T(8,128)(2,1)S(1)} %get-tuple-element.155), channel_id=1, source_target_pairs={{0,16},{8,24},{16,0},{24,8},{1,17},{9,25},{17,1},{25,9},{2,18},{10... | collective-permute-start | bytes 1474568 | tf_op jit(solution)/shard_map/ppermute | solution.py:361
  194.2 20.5 %collective-permute-start.44 = (bf16[960,256]{1,0:T(8,128)(2,1)S(1)}, bf16[960,256]{1,0:T(8,128)(2,1)S(1)}, u32[]{:S(2)}, u32[]{:S(2)}) collective-permute-start(bf16[960,256]{1,0:T(8,128)(2,1)S(1)} %add_convert_fusion.10), channel_id=1, source_target_pairs={{0,8},{8,0},{16,24},{24,16},{1,9},{9,1},{17,25},{25,17},{2,10},{10... | collective-permute-start | bytes 1474568 | tf_op jit(solution)/shard_map/ppermute | solution.py:361
  195.2 20.5 %collective-permute-start.45 = (bf16[960,256]{1,0:T(8,128)(2,1)S(1)}, bf16[960,256]{1,0:T(8,128)(2,1)S(1)}, u32[]{:S(2)}, u32[]{:S(2)}) collective-permute-start(bf16[960,256]{1,0:T(8,128)(2,1)S(1)} %add_convert_fusion.9), channel_id=1, source_target_pairs={{0,16},{8,24},{16,0},{24,8},{1,17},{9,25},{17,1},{25,9},{2,18},{10... | collective-permute-start | bytes 1474568 | tf_op jit(solution)/shard_map/ppermute | solution.py:361
  229.1 21.7 %collective-permute-start.53 = (bf16[960,256]{1,0:T(8,128)(2,1)S(1)}, bf16[960,256]{1,0:T(8,128)(2,1)S(1)}, u32[]{:S(2)}, u32[]{:S(2)}) collective-permute-start(bf16[960,256]{1,0:T(8,128)(2,1)S(1)} %get-tuple-element.178), channel_id=1, source_target_pairs={{0,8},{8,0},{16,24},{24,16},{1,9},{9,1},{17,25},{25,17},{2,10},{10... | collective-permute-start | bytes 1474568 | tf_op jit(solution)/shard_map/ppermute | solution.py:361
  230.4 20.5 %collective-permute-start.54 = (bf16[960,256]{1,0:T(8,128)(2,1)S(1)}, bf16[960,256]{1,0:T(8,128)(2,1)S(1)}, u32[]{:S(2)}, u32[]{:S(2)}) collective-permute-start(bf16[960,256]{1,0:T(8,128)(2,1)S(1)} %get-tuple-element.180), channel_id=1, source_target_pairs={{0,16},{8,24},{16,0},{24,8},{1,17},{9,25},{17,1},{25,9},{2,18},{10... | collective-permute-start | bytes 1474568 | tf_op jit(solution)/shard_map/ppermute | solution.py:361
  231.4 18.7 %collective-permute-start.52 = (bf16[160,640]{1,0:T(8,128)(2,1)S(1)}, bf16[160,640]{1,0:T(8,128)(2,1)S(1)}, u32[]{:S(2)}, u32[]{:S(2)}) collective-permute-start(bf16[160,640]{1,0:T(8,128)(2,1)S(1)} %get-tuple-element.176), channel_id=1, source_target_pairs={{2,0},{3,1},{4,2},{5,3},{6,4},{7,5},{10,8},{11,9},{12,10},{13,11},... | collective-permute-start | bytes 614408 | tf_op jit(solution)/shard_map/ppermute | solution.py:373
  232.7 17.9 %collective-permute-start.51 = (bf16[160,640]{1,0:T(8,128)(2,1)S(1)}, bf16[160,640]{1,0:T(8,128)(2,1)S(1)}, u32[]{:S(2)}, u32[]{:S(2)}) collective-permute-start(bf16[160,640]{1,0:T(8,128)(2,1)S(1)} %get-tuple-element.175), channel_id=1, source_target_pairs={{4,0},{5,1},{6,2},{7,3},{12,8},{13,9},{14,10},{15,11},{20,16},{21,... | collective-permute-start | bytes 614408 | tf_op jit(solution)/shard_map/ppermute | solution.py:373
  234.0 16.6 %collective-permute-start.50 = (bf16[160,640]{1,0:T(8,128)(2,1)S(1)}, bf16[160,640]{1,0:T(8,128)(2,1)S(1)}, u32[]{:S(2)}, u32[]{:S(2)}) collective-permute-start(bf16[160,640]{1,0:T(8,128)(2,1)S(1)} %get-tuple-element.174), channel_id=1, source_target_pairs={{6,0},{7,1},{14,8},{15,9},{22,16},{23,17},{30,24},{31,25}} | collective-permute-start | bytes 614408 | tf_op jit(solution)/shard_map/ppermute | solution.py:373
  258.2 22.2 %collective-permute-start.58 = (bf16[16,256,256]{2,1,0:T(8,128)(2,1)S(1)}, bf16[16,256,256]{2,1,0:T(8,128)(2,1)S(1)}, u32[]{:S(2)}, u32[]{:S(2)}) collective-permute-start(bf16[16,256,256]{2,1,0:T(8,128)(2,1)S(1)} %get-tuple-element.193), channel_id=1, source_target_pairs={{0,1},{1,0},{2,3},{3,2},{4,5},{5,4},{6,7},{7,6},{8,9},{9,8},{10,11... | collective-permute-start | bytes 6291464 | tf_op jit(solution)/shard_map/ppermute | solution.py:357
  258.5 23.7 %collective-permute-start.55 = (bf16[960,256]{1,0:T(8,128)(2,1)S(1)}, bf16[960,256]{1,0:T(8,128)(2,1)S(1)}, u32[]{:S(2)}, u32[]{:S(2)}) collective-permute-start(bf16[960,256]{1,0:T(8,128)(2,1)S(1)} %add_convert_fusion.7), channel_id=1, source_target_pairs={{0,8},{8,0},{16,24},{24,16},{1,9},{9,1},{17,25},{25,17},{2,10},{10... | collective-permute-start | bytes 1474568 | tf_op jit(solution)/shard_map/ppermute | solution.py:361
  260.6 19.3 %collective-permute-start.60 = (bf16[160,640]{1,0:T(8,128)(2,1)S(1)}, bf16[160,640]{1,0:T(8,128)(2,1)S(1)}, u32[]{:S(2)}, u32[]{:S(2)}) collective-permute-start(bf16[160,640]{1,0:T(8,128)(2,1)S(1)} %get-tuple-element.264), channel_id=1, source_target_pairs={{4,0},{5,1},{6,2},{7,3},{12,8},{13,9},{14,10},{15,11},{20,16},{21,... | collective-permute-start | bytes 614408 | tf_op jit(solution)/shard_map/ppermute | solution.py:373
  261.9 18.0 %collective-permute-start.59 = (bf16[160,640]{1,0:T(8,128)(2,1)S(1)}, bf16[160,640]{1,0:T(8,128)(2,1)S(1)}, u32[]{:S(2)}, u32[]{:S(2)}) collective-permute-start(bf16[160,640]{1,0:T(8,128)(2,1)S(1)} %get-tuple-element.265), channel_id=1, source_target_pairs={{2,0},{3,1},{4,2},{5,3},{6,4},{7,5},{10,8},{11,9},{12,10},{13,11},... | collective-permute-start | bytes 614408 | tf_op jit(solution)/shard_map/ppermute | solution.py:373
  280.3 15.2 %collective-permute-start.75 = (bf16[960,256]{1,0:T(8,128)(2,1)S(1)}, bf16[960,256]{1,0:T(8,128)(2,1)S(1)}, u32[]{:S(2)}, u32[]{:S(2)}) collective-permute-start(bf16[960,256]{1,0:T(8,128)(2,1)S(1)} %add_convert_fusion.5), channel_id=1, source_target_pairs={{0,6},{1,7},{2,0},{3,1},{4,2},{5,3},{6,4},{7,5},{8,14},{9,15},{10,... | collective-permute-start | bytes 1474568 | tf_op jit(solution)/shard_map/ppermute | solution.py:365
  296.6 22.9 %collective-permute-start.76 = (bf16[960,256]{1,0:T(8,128)(2,1)}, bf16[960,256]{1,0:T(8,128)(2,1)}, u32[]{:S(2)}, u32[]{:S(2)}) collective-permute-start(bf16[960,256]{1,0:T(8,128)(2,1)} %add_convert_fusion.4), channel_id=1, source_target_pairs={{0,6},{1,7},{2,0},{3,1},{4,2},{5,3},{6,4},{7,5},{8,14},{9,15},{10,... | collective-permute-start | bytes 1474568 | tf_op jit(solution)/shard_map/ppermute | solution.py:365
  300.4 22.0 %collective-permute-start.64 = (bf16[4,256,256]{2,1,0:T(8,128)(2,1)}, bf16[4,256,256]{2,1,0:T(8,128)(2,1)}, u32[]{:S(2)}, u32[]{:S(2)}) collective-permute-start(bf16[4,256,256]{2,1,0:T(8,128)(2,1)} %get-tuple-element.259), channel_id=1, source_target_pairs={{0,24},{8,16},{16,8},{24,0},{1,25},{9,17},{17,9},{25,1},{2,26},{10... | collective-permute-start | bytes 1572872 | tf_op jit(solution)/shard_map/ppermute | solution.py:361
  302.1 23.4 %collective-permute-start.63 = (bf16[4,256,256]{2,1,0:T(8,128)(2,1)}, bf16[4,256,256]{2,1,0:T(8,128)(2,1)}, u32[]{:S(2)}, u32[]{:S(2)}) collective-permute-start(bf16[4,256,256]{2,1,0:T(8,128)(2,1)} %get-tuple-element.260), channel_id=1, source_target_pairs={{0,16},{8,24},{16,0},{24,8},{1,17},{9,25},{17,1},{25,9},{2,18},{10... | collective-permute-start | bytes 1572872 | tf_op jit(solution)/shard_map/ppermute | solution.py:361
  303.2 22.4 %collective-permute-start.62 = (bf16[4,256,256]{2,1,0:T(8,128)(2,1)}, bf16[4,256,256]{2,1,0:T(8,128)(2,1)}, u32[]{:S(2)}, u32[]{:S(2)}) collective-permute-start(bf16[4,256,256]{2,1,0:T(8,128)(2,1)} %get-tuple-element.261), channel_id=1, source_target_pairs={{0,8},{8,0},{16,24},{24,16},{1,9},{9,1},{17,25},{25,17},{2,10},{10... | collective-permute-start | bytes 1572872 | tf_op jit(solution)/shard_map/ppermute | solution.py:361
  (148 other events, 1080.6 us)

commit v5 on v4

--- a/solution.py
+++ b/solution.py
@@ -450,8 +450,8 @@
         [
             wq_ref[...].astype(jnp.float32).T,
             extra,
-            wk_ref[...].astype(jnp.float32).T,
-            wv_ref[...].astype(jnp.float32).T,
+            wk_ref[...].astype(jnp.float32),
+            wv_ref[...].astype(jnp.float32),
         ],
         0,
     )
@@ -460,16 +460,17 @@
 
 
 def pack_mlp_kernel(ids_ref, wg_ref, wu_ref, wd_ref, other_ref, wo_ref, out_ref):
-    block, half = wg_ref.shape
+    half, block = wg_ref.shape
     core = ids_ref[2]
     out_ref[...] = jnp.zeros_like(out_ref)
-    out_ref[:half, :block] = wg_ref[...].astype(jnp.float32).T.astype(jnp.bfloat16)
-    out_ref[half : 2 * half, :block] = wu_ref[...].astype(jnp.float32).T.astype(jnp.bfloat16)
-    own = wd_ref[pl.ds(pl.multiple_of(core * half, 16), half), :]
-    other = other_ref[...]
+    out_ref[:half, :block] = wg_ref[...]
+    out_ref[half : 2 * half, :block] = wu_ref[...]
+    down = wd_ref[...].astype(jnp.float32)
+    own = jnp.where(core == 0, down[:, :half], down[:, half:])
+    other = other_ref[:, :half].astype(jnp.float32)
     low = jnp.where(core == 0, own, other)
     high = jnp.where(core == 0, other, own)
-    out_ref[2 * half : 3 * half, :block] = jnp.concatenate([low, high], 1)
+    out_ref[2 * half : 3 * half, :block] = jnp.concatenate([low, high], 0).T.astype(jnp.bfloat16)
     out_ref[3 * half :, :block] = jnp.concatenate(
         [wo_ref[...].astype(jnp.float32).T, jnp.zeros((8, block), jnp.float32)], 0
     ).astype(jnp.bfloat16)
@@ -991,7 +992,7 @@
     (first_piece,) = run(
         pack_first_kernel,
         "pack_first",
-        (counts, w_query, key_weight, value_weight, gains),
+        (counts, w_query, key_weight.T, value_weight.T, gains),
         [SMEM] + [VMEM] * 4,
         [struct((depth, wide))],
         [VMEM],
@@ -1000,14 +1001,13 @@
         16,
     )
     chain = [first_piece] + [shift_z(first_piece, step) for step in (1, 2, 3)]
-    down_halves = w_down.reshape(2, half, -1)
-    other_down = swap_core(
-        lax.dynamic_index_in_dim(down_halves, 1 - core_id, 0, keepdims=False)
-    )
+    down = w_down.T
+    give = jnp.where(core_id == 0, down[:, half:], down[:, :half])
+    other_down = swap_core(jnp.pad(give, ((0, 0), (0, -half % 128))))
     (mlp_piece,) = run(
         pack_mlp_kernel,
         "pack_mlp",
-        (ids, w_gate, w_up, w_down, other_down, w_out),
+        (ids, w_gate.T, w_up.T, down, other_down, w_out),
         [SMEM] + [VMEM] * 5,
         [struct((mlp_rows, wide))],
         [VMEM],
@@ -1030,19 +1030,16 @@
     along = jnp.stack(chain, 0)
     extras = along[:, q_cols : q_cols + 2, :block]
     other_extras = swap_core(extras)
-    x_zero, y_zero = swap_dp(mlp_piece, 1), swap_dp(mlp_piece, 2)
-    along_next = after(along, x_zero, y_zero)
-    from_x = swap_dp(along_next, 1)
-    from_y = swap_dp(along_next, 2)
+    from_x = swap_dp(along, 1)
+    from_y = swap_dp(along, 2)
     first_own = [along, from_x, from_y, swap_dp(from_x[:2], 2), swap_dp(from_y[2:], 1)]
     first_other = [swap_core(piece) for piece in first_own]
 
     z_one = shift_z(after(mlp_piece, along), 1)
     z_two = shift_z(z_one, 1)
     z_three = shift_z(z_two, 1)
-    far_zero = swap_dp(after(x_zero, *first_own[3:]), 2)
-    z_one_next = after(z_one, *first_own[3:])
-    x_one = swap_dp(z_one_next, 1)
+    mlp_next = after(mlp_piece, *first_own[3:])
+    x_zero, y_zero = swap_dp(mlp_next, 1), swap_dp(mlp_next, 2)
 
     by_core = jnp.where(
         core_id == 0, jnp.stack([extras, other_extras], 1), jnp.stack([other_extras, extras], 1)
@@ -1079,28 +1076,23 @@
         2 * (width + 2 * kv_width) * width * rows,
         24,
     )
-    kv_zero = after(kv, x_one, far_zero)
+    kv_zero = after(kv, x_zero, y_zero)
     kv_one = shift_z_up(kv_zero, 1)
-    x_two = swap_dp(after(z_two, kv_zero), 1)
-    y_one = swap_dp(after(z_one, kv_zero), 2)
-    wave = (kv_one, x_two, y_one, z_three)
+    x_one = swap_dp(after(z_one, kv_zero), 1)
+    far_zero = swap_dp(after(x_zero, kv_zero), 2)
+    wave = (kv_one, x_one, far_zero, z_three)
     kv_two = shift_z_up(after(*wave), 1)
+    x_two = swap_dp(after(z_two, *wave), 1)
+    y_one = swap_dp(after(z_one, *wave), 2)
+    wave = (kv_two, x_two, y_one)
+    kv_three = shift_z_up(after(*wave), 1)
     far_one = swap_dp(after(y_one, *wave), 1)
     y_two = swap_dp(after(z_two, *wave), 2)
-    wave = (kv_two, far_one, y_two)
-    kv_three = shift_z_up(after(*wave), 1)
+    wave = (kv_three, far_one, y_two)
     x_three = swap_dp(after(z_three, *wave), 1)
     y_three = swap_dp(after(z_three, *wave), 2)
-    wave = (kv_three, x_three, y_three)
-    far_two = swap_dp(after(x_two, *wave), 2)
-    far_three = swap_dp(after(y_three, *wave), 1)
     kv_own = [kv, kv_one, kv_two, kv_three]
     kv_other = [swap_core(piece) for piece in (kv_zero, kv_one, kv_two, kv_three)]
-    pieces = [mlp_piece, z_one, z_two, z_three]
-    pieces += [x_zero, x_one, x_two, x_three]
-    pieces += [y_zero, y_one, y_two, y_three]
-    pieces += [far_zero, far_one, far_two, far_three]
-
     pair_flops = 2 * QUERY_HEADS * HEAD_WIDTH * rows * 8 * cap
     head_scratch = [
         pltpu.VMEM((KEY_HEADS, 8 * cap, HEAD_WIDTH), jnp.bfloat16),
@@ -1123,11 +1115,20 @@
             24,
         )
 
-    att_a, lse_a = attend(0, after(query, x_three, y_three))
+    att_a, lse_a = attend(0, after(query, far_one, y_two))
+    wave = (att_a, x_three, y_three)
+    far_two = swap_dp(after(x_two, *wave), 2)
+    far_three = swap_dp(after(y_three, *wave), 1)
+    dy_other = swap_core(after(dy, att_a))
+    att_b, lse_b = attend(1, after(query, *wave))
+    pieces = [mlp_piece, z_one, z_two, z_three]
+    pieces += [x_zero, x_one, x_two, x_three]
+    pieces += [y_zero, y_one, y_two, y_three]
+    pieces += [far_zero, far_one, far_two, far_three]
     (out_own,) = run(
         collect_kernel,
         "collect",
-        tuple(pieces[:15]) + (after(far_three, att_a),),
+        tuple(pieces[:15]) + (after(far_three, att_b),),
         [ANY] * 16,
         [struct((4, q_rows, 4 * wide))],
         [VMEM],
@@ -1136,8 +1137,6 @@
         8,
     )
     out_other = swap_core(out_own)
-    dy_other = swap_core(after(dy, att_a))
-    att_b, lse_b = attend(1, after(query, out_own))
     att_a = att_a.reshape(4, block, cap)
     att_b = att_b.reshape(4, block, cap)
     lse = (lse_a, lse_b)
@@ -1187,7 +1186,6 @@
     keep, send = results[:2]
     home, to_x, to_y, far = results[2:6], results[6:10], results[10:14], results[14:18]
     arrived = swap_core(send)
-    via_three, via_two = swap_dp(far[3], 1), swap_dp(far[2], 2)
 
     output, dh, mixed_gradient, gain_two_grad, da_pieces = run(
         turn_point_kernel,
@@ -1244,14 +1242,15 @@
             total = total + shift_z_down(summed[s], s).astype(jnp.float32)
         return total
 
-    wave = (via_three, via_two, mixed_gradient)
-    x_three, y_two = swap_dp(after(to_x[3], *wave), 1), swap_dp(after(to_y[2], *wave), 2)
+    via_three = swap_dp(after(far[3], mixed_gradient), 1)
+    via_two = swap_dp(after(far[2], mixed_gradient), 2)
+    x_three = swap_dp(after(to_x[3], mixed_gradient), 1)
+    y_two = swap_dp(after(to_y[2], mixed_gradient), 2)
+    back_a = attend_back(0, mixed_gradient)
+    wave = (back_a[0], via_three, via_two, x_three, y_two)
     x_two = swap_dp(add_low(to_x[2], after(via_two, *wave)), 1)
     y_three = swap_dp(add_low(to_y[3], after(via_three, *wave)), 2)
-    back_a = attend_back(0, after(mixed_gradient, *wave))
-    wave = (back_a[0], x_three, y_two, x_two, y_three)
     via_one, via_zero = swap_dp(after(far[1], *wave), 1), swap_dp(after(far[0], *wave), 2)
-    hop = shift_z(add_low(after(home[3], back_a[0]), x_three, y_three), -1)
     out_grads = run(
         out_grad_kernel,
         "out_grad",
@@ -1264,21 +1263,22 @@
         16,
     )
     summed_a = sum_cores(*back_a[1:])
-    wave = (via_one, via_zero, hop, out_grads[0])
+    wave = (x_two, y_three, out_grads[0])
     dkv_a = sum_z([after(piece, *wave) for piece in summed_a])
+    back_b = attend_back(1, after(mixed_gradient, *summed_a, *wave))
+    wave = (back_b[0], dkv_a, via_one, via_zero)
     x_one, y_zero = swap_dp(after(to_x[1], *wave), 1), swap_dp(after(to_y[0], *wave), 2)
-    back_b = attend_back(1, after(mixed_gradient, *summed_a, *wave))
-    wave = (back_b[0], dkv_a, x_one, y_zero)
-    x_zero = swap_dp(add_low(to_x[0], after(via_zero, *wave)), 1)
-    y_one = swap_dp(add_low(to_y[1], after(via_one, *wave)), 2)
-    summed_b = sum_cores(back_b[1], after(back_b[2], dkv_a, x_one, y_zero))
+    summed_b = sum_cores(back_b[1], after(back_b[2], *wave))
     parts_b = [shift_z_down(summed_b[s], s) for s in (1, 2, 3)]
+
     def sum_pair(parts):
         arrived = swap_core(parts[4])
         return [add_low(parts[k], arrived[4 * k : 4 * k + 4]) for k in range(4)]
 
-    def reduce_all(mine):
-        summed = [mine[0]] + [swap_dp(mine[k], k) for k in (1, 2, 3)]
+    def share_square(mine):
+        return [mine[0]] + [swap_dp(mine[k], k) for k in (1, 2, 3)]
+
+    def reduce_all(summed):
         out = [add_low(*[piece[s] for piece in summed]) for s in range(4)]
         total = out[0].astype(jnp.float32)
         for s in (1, 2, 3):
@@ -1292,7 +1292,7 @@
             ids,
             *first_own,
             *first_other,
-            after(n1, *wave, *summed_b),
+            after(n1, *wave),
             back_a[0].reshape(width, cap),
             back_b[0].reshape(width, cap),
             *out_grads,
@@ -1311,19 +1311,22 @@
         24,
     )
     dn_q = q_results[0]
-    dkv_b = after(summed_b[0], dn_q).astype(jnp.float32)
+    dkv_b = summed_b[0].astype(jnp.float32)
     for part in parts_b:
         dkv_b = dkv_b + part.astype(jnp.float32)
-    hop = shift_z(add_low(home[2], x_two, y_two, after(hop, dkv_b)), -1)
+    x_zero = swap_dp(add_low(to_x[0], after(via_zero, dkv_b)), 1)
+    y_one = swap_dp(add_low(to_y[1], after(via_one, dkv_b)), 2)
+    hop = shift_z(add_low(after(home[3], dkv_b), x_three, y_three), -1)
     q_out_mine = sum_pair(q_results[1:])
-    q_out_total = reduce_all(q_out_mine)
+    q_out_shared = share_square(q_out_mine)
+    q_out_total = reduce_all(q_out_shared)
     grad_query = q_out_total[:q_cols, :block].T
     grad_out = q_out_total[q_rows : q_rows + q_cols, :block].T
 
     dkv_pieces, *kv_grads = run(
         kv_grad_kernel,
         "kv_grad",
-        (ids, after(n1, x_zero, y_one, *q_out_mine), dkv_a, dkv_b, cosine, sine),
+        (ids, after(n1, x_one, y_zero, *q_out_mine), dkv_a, dkv_b, cosine, sine),
         [SMEM] + [VMEM] * 5,
         [struct((16 * k_cols, rows))]
         + [struct((4, 2 * k_cols, wide))] * 4
@@ -1339,7 +1342,7 @@
     grad_tokens, gain_one_grad = run(
         finish_kernel,
         "finish",
-        (ids, *first_own, *first_other, dkv_pieces, dn_q, dh, x, gain_one),
+        (ids, *first_own, *first_other, dkv_pieces, dn_q, dh, after(x, x_zero, y_one), gain_one),
         [SMEM] + [VMEM] * 15,
         [struct((width, rows), jnp.float32), struct((width, 1), jnp.float32)],
         [VMEM] * 2,
@@ -1348,7 +1351,9 @@
         24,
     )
     grad_tokens = grad_tokens.T.reshape(batches, cap, width)
-    hop = shift_z(add_low(home[1], x_one, y_one, after(hop, dkv_pieces)), -1)
+    kv_mine = sum_pair(kv_grads)
+    hop = shift_z(add_low(home[2], x_two, y_two, after(hop, dkv_pieces)), -1)
+    hop = shift_z(add_low(home[1], x_one, y_one, after(hop, *kv_mine)), -1)
     mlp_total = (
         home[0].astype(jnp.float32)
         + y_zero.astype(jnp.float32)
@@ -1366,8 +1371,7 @@
         core_id == 0, jnp.concatenate([stay, taken], 0), jnp.concatenate([taken, stay], 0)
     )
 
-    kv_mine = sum_pair(kv_grads)
-    kv_total = reduce_all(kv_mine)
+    kv_total = reduce_all(share_square(kv_mine))
     gain_total = after(jnp.concatenate([gain_one_grad, gain_two_grad], 1).T, *kv_mine)
     gain_total = gain_total + swap_core(gain_total)
     gain_total = gain_total + swap_dp(gain_total, 1)

time: 367 us -> 389 us (1.060)
  local copies, waits for them, and re-layouts: 48.6 us -> 63.1 us
  starting transfers between devices: 94.5 us -> 86.1 us
  other arithmetic: 11.6 us -> 18.8 us
  waiting for transfers between devices: 100 us -> 107 us
    unnamed x187 -> x246, local copies, waits for them, and re-layouts: 37.9 us -> 46.9 us
    ppermute x15, starting transfers between devices: 24.7 us -> 16.5 us  [shift_z(): lax.ppermute(value, 'fsdp', [(j, (j + 2 * step) % 8) for j in range(8)])]
    ppermute x2, starting transfers between devices: 1.67 us -> 8.12 us  [fast(): lax.ppermute(gain_total, 'fsdp', [(j, j ^ mask) for j in range(8)])]
    convert_element_type x11, other arithmetic: 4.42 us -> 9.06 us  [add_low(): return total.astype(jnp.bfloat16)]
    ppermute x36, starting transfers between devices: 41.2 us -> 36.8 us  [swap_dp(): return lax.ppermute(value, 'dp', [(j, j ^ mask) for j in range(4)])]
  transfers between devices with their start and end apart: 83 -> 83, of which waited for: 35 -> 34; matrix products, arithmetic and copies ran while one was open for 7% -> 9% of each run, Pallas kernels for 18% -> 17%
where the time goes in v5:
time: 389 us; the launch traced here: 382 us
  waiting for transfers between devices  107 us (28%)
  Pallas kernels  104 us (27%)
  starting transfers between devices  86.1 us (22%)
  local copies, waits for them, and re-layouts  63.1 us (16%)
  other arithmetic  18.8 us (5%)
    pallas_call x16, Pallas kernels, run(): pl.pallas_call(body, out_shape=tuple(outs), in_specs=in_specs, out_specs=...  104 us
    unnamed x246, local copies, waits for them, and re-layouts  46.9 us
    ppermute x36, waiting for transfers between devices, swap_dp(): return lax.ppermute(value, 'dp', [(j, j ^ mask) for j in range(4)])  38.7 us
    ppermute x36, starting transfers between devices, swap_dp(): return lax.ppermute(value, 'dp', [(j, j ^ mask) for j in range(4)])  36.8 us
    ppermute x15, waiting for transfers between devices, shift_z(): lax.ppermute(value, 'fsdp', [(j, (j + 2 * step) % 8) for j in range(8)])  18.8 us
    ppermute x6, waiting for transfers between devices, shift_z_down(): lax.ppermute(value, 'fsdp', [(j, j - 2 * step) for j in range(8) if j - 2...  18.4 us
    ppermute x3, waiting for transfers between devices, shift_z_up(): lax.ppermute(value, 'fsdp', [(j, j + 2 * step) for j in range(8) if j + 2...  17.1 us
    ppermute x15, starting transfers between devices, shift_z(): lax.ppermute(value, 'fsdp', [(j, (j + 2 * step) % 8) for j in range(8)])  16.5 us
  transfers between devices with their start and end apart: 83, of which 34 were waited for; matrix products, arithmetic and copies ran while one was open for 9% of the time, Pallas kernels for 17%

profile of v5, /device:TPU:0, one launch (start us, length us, event | category | flops | bytes accessed | tf_op | source)
XLA Modules:
  0.0 381.5 jit_solution(15257937066843868383)
XLA Ops:
  5.0 5.1 %collective-permute-start.3 = (bf16[208,256]{1,0:T(8,128)(2,1)S(1)}, bf16[208,256]{1,0:T(8,128)(2,1)S(1)}, u32[]{:S(2)}, u32[]{:S(2)}) collective-permute-start(bf16[208,256]{1,0:T(8,128)(2,1)S(1)} %pack_first.1), channel_id=1, source_target_pairs={{0,6},{1,7},{2,0},{3,1},{4,2},{5,3},{6,4},{7,5},{8,14},{9,15},{10,... | collective-permute-start | bytes 319496 | tf_op jit(solution)/shard_map/ppermute | solution.py:365
  24.8 8.1 %collective-permute-done.9.refs_3_ = bf16[4,208,256]{2,1,0:T(8,128)(2,1)S(1)} collective-permute-done((bf16[4,208,256]{2,1,0:T(8,128)(2,1)S(1)}, bf16[4,208,256]{2,1,0:T(8,128)(2,1)S(1)}, u32[]{:S(2)}, u32[]{:S(2)}) %collective-permute-start.9) | collective-permute-done | bytes 426016 | tf_op jit(solution)/shard_map/ppermute | solution.py:361
  34.5 5.6 %collective-permute-done.4.refs_1_.refs_6_ = bf16[1088,256]{1,0:T(8,128)(2,1)} collective-permute-done((bf16[1088,256]{1,0:T(8,128)(2,1)S(1)}, bf16[1088,256]{1,0:T(8,128)(2,1)}, u32[]{:S(2)}, u32[]{:S(2)}) %collective-permute-start.4) | collective-permute-done | bytes 557088 | tf_op jit(solution)/shard_map/ppermute | solution.py:365
  50.6 4.7 %collective-permute-done.5.refs_2_.refs_7_ = bf16[1088,256]{1,0:T(8,128)(2,1)} collective-permute-done((bf16[1088,256]{1,0:T(8,128)(2,1)}, bf16[1088,256]{1,0:T(8,128)(2,1)}, u32[]{:S(2)}, u32[]{:S(2)}) %collective-permute-start.5) | collective-permute-done | bytes 557088 | tf_op jit(solution)/shard_map/ppermute | solution.py:365
  66.8 3.8 collective-permute-start.20
  70.6 7.1 %collective-permute-done.20.refs_4_.refs_5_ = bf16[320,640]{1,0:T(8,128)(2,1)} collective-permute-done((bf16[320,640]{1,0:T(8,128)(2,1)S(1)}, bf16[320,640]{1,0:T(8,128)(2,1)}, u32[]{:S(2)}, u32[]{:S(2)}) %collective-permute-start.20) | collective-permute-done | bytes 409632 | tf_op jit(solution)/shard_map/ppermute | solution.py:369
  82.2 5.2 %collective-permute-start.23 = (bf16[320,640]{1,0:T(8,128)(2,1)}, bf16[320,640]{1,0:T(8,128)(2,1)}, u32[]{:S(2)}, u32[]{:S(2)}) collective-permute-start(bf16[320,640]{1,0:T(8,128)(2,1)} %collective-permute-done.20.refs_4_.refs_5_), channel_id=1, source_target_pairs={{0,2},{1,3},{2,4},{3,5},{4,6},{5,7},{8,10},{9,11},{10,12},{11,13},... | collective-permute-start | bytes 1228808 | tf_op jit(solution)/shard_map/ppermute | solution.py:369
  87.4 6.2 %collective-permute-done.23.refs_5_.refs_6_ = bf16[320,640]{1,0:T(8,128)(2,1)} collective-permute-done((bf16[320,640]{1,0:T(8,128)(2,1)}, bf16[320,640]{1,0:T(8,128)(2,1)}, u32[]{:S(2)}, u32[]{:S(2)}) %collective-permute-start.23) | collective-permute-done | bytes 409632 | tf_op jit(solution)/shard_map/ppermute | solution.py:369
  97.3 4.5 %collective-permute-start.25 = (bf16[320,640]{1,0:T(8,128)(2,1)}, bf16[320,640]{1,0:T(8,128)(2,1)}, u32[]{:S(2)}, u32[]{:S(2)}) collective-permute-start(bf16[320,640]{1,0:T(8,128)(2,1)} %collective-permute-done.23.refs_5_.refs_6_), channel_id=1, source_target_pairs={{0,2},{1,3},{2,4},{3,5},{4,6},{5,7},{8,10},{9,11},{10,12},{11,13},... | collective-permute-start | bytes 1228808 | tf_op jit(solution)/shard_map/ppermute | solution.py:369
  103.1 3.8 %collective-permute-done.25.refs_6_.refs_7_ = bf16[320,640]{1,0:T(8,128)(2,1)} collective-permute-done((bf16[320,640]{1,0:T(8,128)(2,1)}, bf16[320,640]{1,0:T(8,128)(2,1)}, u32[]{:S(2)}, u32[]{:S(2)}) %collective-permute-start.25) | collective-permute-done | bytes 409632 | tf_op jit(solution)/shard_map/ppermute | solution.py:369
  121.2 9.5 %attend.2 = (bf16[15,64,160]{2,1,0:T(8,128)(2,1)S(1)}, f32[5,1,480]{2,1,0:T(1,128)S(1)}) custom-call(s32[4]{0:T(128)S(1)} %copy-done.80, s32[16]{0:T(128)S(1)} %copy-done.104, bf16[15,64,320]{2,1,0:T(8,128)(2,1)S(1)} %copy-done.87, bf16[320,640]{1,0:T(8,128)(2,1)S(1)} %copy-done.99, bf16[320,640]{1,0:T(8,128)(2,1)} %collective-permute-done.20.refs_4_.refs_5_, ...), custom_call_target="tpu_custom_call" | custom-call | flops 3145728000 | bytes 4208080 | tf_op jit(solution)/shard_map/attend/pallas_call | solution.py:409
  133.6 9.9 %attend.3 = (bf16[15,64,160]{2,1,0:T(8,128)(2,1)S(1)}, f32[5,1,480]{2,1,0:T(1,128)S(1)}) custom-call(s32[4]{0:T(128)S(1)} %copy-done.80, s32[16]{0:T(128)S(1)} %copy-done.104, bf16[15,64,320]{2,1,0:T(8,128)(2,1)S(1)} %copy-done.87, bf16[320,640]{1,0:T(8,128)(2,1)S(1)} %copy-done.99, bf16[320,640]{1,0:T(8,128)(2,1)} %collective-permute-done.20.refs_4_.refs_5_, ...), custom_call_target="tpu_custom_call" | custom-call | flops 3145728000 | bytes 4208080 | tf_op jit(solution)/shard_map/attend/pallas_call | solution.py:409
  157.2 30.0 %mlp.1 = (f32[2,960,320]{2,1,0:T(8,128)}, bf16[2,960,384]{2,1,0:T(8,128)(2,1)}, bf16[960,256]{1,0:T(8,128)(2,1)S(1)}, bf16[960,256]{1,0:T(8,128)(2,1)S(1)}, bf16...) custom-call(s32[4]{0:T(128)S(1)} %copy-done.81, ...), custom_call_target="tpu_custom_call" | custom-call | flops 14155776000 | bytes 23658512 | tf_op jit(solution)/shard_map/mlp/pallas_call | solution.py:409
  207.0 14.5 %attend_back.2 = (bf16[15,64,160]{2,1,0:T(8,128)(2,1)S(1)}, bf16[4,160,640]{2,1,0:T(8,128)(2,1)S(1)}, bf16[4,160,640]{2,1,0:T(8,128)(2,1)S(1)}) custom-call(s32[4]{0:T(128)S(1)} %copy-done.81, s32[16]{0:T(128)S(1)} %copy-done.105, bf16[15,64,320]{2,1,0:T(8,128)(2,1)S(1)} %copy-done.88, bf16[15,64,320]{2,1,0:T(8,128)(2,1)S(1)} %bitcast.116, ...), custom_call_target="tpu_custom_call" | custom-call | flops 7864320000 | bytes 6542800 | tf_op jit(solution)/shard_map/attend_back/pallas_call | solution.py:409
  221.7 5.3 %collective-permute-done.43 = bf16[960,256]{1,0:T(8,128)(2,1)S(1)} collective-permute-done((bf16[960,256]{1,0:T(8,128)(2,1)}, bf16[960,256]{1,0:T(8,128)(2,1)S(1)}, u32[]{:S(2)}, u32[]{:S(2)}) %collective-permute-start.43) | collective-permute-done | bytes 491552 | tf_op jit(solution)/shard_map/ppermute | solution.py:361
  234.5 6.9 %collective-permute-done.45 = bf16[960,256]{1,0:T(8,128)(2,1)S(1)} collective-permute-done((bf16[960,256]{1,0:T(8,128)(2,1)S(1)}, bf16[960,256]{1,0:T(8,128)(2,1)S(1)}, u32[]{:S(2)}, u32[]{:S(2)}) %collective-permute-start.45) | collective-permute-done | bytes 491552 | tf_op jit(solution)/shard_map/ppermute | solution.py:361
  246.9 14.8 %attend_back.3 = (bf16[15,64,160]{2,1,0:T(8,128)(2,1)S(1)}, bf16[4,160,640]{2,1,0:T(8,128)(2,1)S(1)}, bf16[4,160,640]{2,1,0:T(8,128)(2,1)S(1)}) custom-call(s32[4]{0:T(128)S(1)} %copy-done.81, s32[16]{0:T(128)S(1)} %copy-done.105, bf16[15,64,320]{2,1,0:T(8,128)(2,1)S(1)} %copy-done.88, bf16[15,64,320]{2,1,0:T(8,128)(2,1)S(1)} %bitcast.117, ...), custom_call_target="tpu_custom_call" | custom-call | flops 7864320000 | bytes 6542800 | tf_op jit(solution)/shard_map/attend_back/pallas_call | solution.py:409
  262.9 4.0 %finish_q.1 = (f32[4,240,320]{2,1,0:T(8,128)S(1)}, bf16[4,256,256]{2,1,0:T(8,128)(2,1)S(1)}, bf16[4,256,256]{2,1,0:T(8,128)(2,1)S(1)}, bf16[4,256,256]{2,1,0:T(8...) custom-call(s32[4]{0:T(128)S(1)} %copy-done.81, ...), custom_call_target="tpu_custom_call" | custom-call | flops 1179648000 | bytes 12156944 | tf_op jit(solution)/shard_map/finish_q/pallas_call | solution.py:409
  272.4 4.5 %collective-permute-done.56 = bf16[160,640]{1,0:T(8,128)(2,1)S(1)} collective-permute-done((bf16[160,640]{1,0:T(8,128)(2,1)S(1)}, bf16[160,640]{1,0:T(8,128)(2,1)S(1)}, u32[]{:S(2)}, u32[]{:S(2)}) %collective-permute-start.56) | collective-permute-done | bytes 204832 | tf_op jit(solution)/shard_map/ppermute | solution.py:373
  278.0 6.7 %collective-permute-done.58 = bf16[160,640]{1,0:T(8,128)(2,1)S(1)} collective-permute-done((bf16[160,640]{1,0:T(8,128)(2,1)S(1)}, bf16[160,640]{1,0:T(8,128)(2,1)S(1)}, u32[]{:S(2)}, u32[]{:S(2)}) %collective-permute-start.58) | collective-permute-done | bytes 204832 | tf_op jit(solution)/shard_map/ppermute | solution.py:373
  284.7 6.8 %collective-permute-done.57 = bf16[160,640]{1,0:T(8,128)(2,1)S(1)} collective-permute-done((bf16[160,640]{1,0:T(8,128)(2,1)S(1)}, bf16[160,640]{1,0:T(8,128)(2,1)S(1)}, u32[]{:S(2)}, u32[]{:S(2)}) %collective-permute-start.57) | collective-permute-done | bytes 204832 | tf_op jit(solution)/shard_map/ppermute | solution.py:373
  299.0 4.1 %kv_grad.1 = (bf16[640,320]{1,0:T(8,128)(2,1)S(1)}, bf16[4,80,256]{2,1,0:T(8,128)(2,1)S(1)}, bf16[4,80,256]{2,1,0:T(8,128)(2,1)S(1)}, bf16[4,80,256]{2,1,0:T(8,1...) custom-call(s32[4]{0:T(128)S(1)} %copy-done.81, bf16[4,240,320]{2,1,0:T(8,128)(2,1)S(1)} %bitcast.97, ...), custom_call_target="tpu_custom_call" | custom-call | flops 393216000 | bytes 3235856 | tf_op jit(solution)/shard_map/kv_grad/pallas_call | solution.py:409
  332.9 3.7 collective-permute-done.62
  357.0 6.9 %collective-permute-start.81 = (f32[2,960]{1,0:T(2,128)S(1)}, f32[2,960]{1,0:T(2,128)S(1)}, u32[]{:S(2)}, u32[]{:S(2)}) collective-permute-start(f32[2,960]{1,0:T(2,128)S(1)} %add.393), channel_id=1, source_target_pairs={{0,2},{1,3},{2,0},{3,1},{4,6},{5,7},{6,4},{7,5},{8,10},{9,11},{10,... | collective-permute-start | bytes 23048 | tf_op jit(solution)/shard_map/ppermute | solution.py:1380
  (467 shorter events, 197.5 us)
Async XLA Ops:
  20.6 27.3 %collective-permute-start.12 = (bf16[4,208,256]{2,1,0:T(8,128)(2,1)S(1)}, bf16[4,208,256]{2,1,0:T(8,128)(2,1)S(1)}, u32[]{:S(2)}, u32[]{:S(2)}) collective-permute-start(bf16[4,208,256]{2,1,0:T(8,128)(2,1)S(1)} %pad_maximum_fusion.refs_1_), channel_id=1, source_target_pairs={{0,1},{1,0},{2,3},{3,2},{4,5},{5,4},{6,7},{7,6},{8,9},{9,8},{10,11... | collective-permute-start | bytes 1277960 | tf_op jit(solution)/shard_map/ppermute | solution.py:357
  22.6 19.3 %collective-permute-start.7 = (bf16[4,208,256]{2,1,0:T(8,128)(2,1)S(1)}, bf16[4,208,256]{2,1,0:T(8,128)(2,1)S(1)}, u32[]{:S(2)}, u32[]{:S(2)}) collective-permute-start(bf16[4,208,256]{2,1,0:T(8,128)(2,1)S(1)} %pad_maximum_fusion.refs_1_), channel_id=1, source_target_pairs={{0,8},{8,0},{16,24},{24,16},{1,9},{9,1},{17,25},{25,17},{2,10},{10... | collective-permute-start | bytes 1277960 | tf_op jit(solution)/shard_map/ppermute | solution.py:361
  55.6 22.0 %collective-permute-start.6 = (bf16[1088,256]{1,0:T(8,128)(2,1)}, bf16[1088,256]{1,0:T(8,128)(2,1)}, u32[]{:S(2)}, u32[]{:S(2)}) collective-permute-start(bf16[1088,256]{1,0:T(8,128)(2,1)} %collective-permute-done.5.refs_2_.refs_7_), channel_id=1, source_target_pairs={{0,2},{1,3},{2,4},{3,5},{4,6},{5,7},{6,0},{7,1},{8,10},{9,11},{10,... | collective-permute-start | bytes 1671176 | tf_op jit(solution)/shard_map/ppermute | solution.py:365
  110.1 20.5 %collective-permute-start.29 = (bf16[1088,256]{1,0:T(8,128)(2,1)}, bf16[1088,256]{1,0:T(8,128)(2,1)}, u32[]{:S(2)}, u32[]{:S(2)}) collective-permute-start(bf16[1088,256]{1,0:T(8,128)(2,1)} %collective-permute-done.6.refs_3_.refs_8_), channel_id=1, source_target_pairs={{0,16},{8,24},{16,0},{24,8},{1,17},{9,25},{17,1},{25,9},{2,18},{10... | collective-permute-start | bytes 1671176 | tf_op jit(solution)/shard_map/ppermute | solution.py:361
  111.6 19.0 %collective-permute-start.28 = (bf16[1088,256]{1,0:T(8,128)(2,1)}, bf16[1088,256]{1,0:T(8,128)(2,1)}, u32[]{:S(2)}, u32[]{:S(2)}) collective-permute-start(bf16[1088,256]{1,0:T(8,128)(2,1)} %collective-permute-done.6.refs_3_.refs_8_), channel_id=1, source_target_pairs={{0,8},{8,0},{16,24},{24,16},{1,9},{9,1},{17,25},{25,17},{2,10},{10... | collective-permute-start | bytes 1671176 | tf_op jit(solution)/shard_map/ppermute | solution.py:361
  202.9 18.8 %collective-permute-start.41 = (bf16[960,256]{1,0:T(8,128)(2,1)S(1)}, bf16[960,256]{1,0:T(8,128)(2,1)S(1)}, u32[]{:S(2)}, u32[]{:S(2)}) collective-permute-start(bf16[960,256]{1,0:T(8,128)(2,1)S(1)} %get-tuple-element.152), channel_id=1, source_target_pairs={{0,16},{8,24},{16,0},{24,8},{1,17},{9,25},{17,1},{25,9},{2,18},{10... | collective-permute-start | bytes 1474568 | tf_op jit(solution)/shard_map/ppermute | solution.py:361
  203.4 18.3 %collective-permute-start.42 = (bf16[960,256]{1,0:T(8,128)(2,1)S(1)}, bf16[960,256]{1,0:T(8,128)(2,1)S(1)}, u32[]{:S(2)}, u32[]{:S(2)}) collective-permute-start(bf16[960,256]{1,0:T(8,128)(2,1)S(1)} %get-tuple-element.155), channel_id=1, source_target_pairs={{0,8},{8,0},{16,24},{24,16},{1,9},{9,1},{17,25},{25,17},{2,10},{10... | collective-permute-start | bytes 1474568 | tf_op jit(solution)/shard_map/ppermute | solution.py:361
  204.8 22.1 %collective-permute-start.43 = (bf16[960,256]{1,0:T(8,128)(2,1)}, bf16[960,256]{1,0:T(8,128)(2,1)S(1)}, u32[]{:S(2)}, u32[]{:S(2)}) collective-permute-start(bf16[960,256]{1,0:T(8,128)(2,1)} %get-tuple-element.157), channel_id=1, source_target_pairs={{0,8},{8,0},{16,24},{24,16},{1,9},{9,1},{17,25},{25,17},{2,10},{10... | collective-permute-start | bytes 1474568 | tf_op jit(solution)/shard_map/ppermute | solution.py:361
  205.5 21.5 %collective-permute-start.44 = (bf16[960,256]{1,0:T(8,128)(2,1)}, bf16[960,256]{1,0:T(8,128)(2,1)S(1)}, u32[]{:S(2)}, u32[]{:S(2)}) collective-permute-start(bf16[960,256]{1,0:T(8,128)(2,1)} %get-tuple-element.159), channel_id=1, source_target_pairs={{0,16},{8,24},{16,0},{24,8},{1,17},{9,25},{17,1},{25,9},{2,18},{10... | collective-permute-start | bytes 1474568 | tf_op jit(solution)/shard_map/ppermute | solution.py:361
  229.6 32.6 %collective-permute-start.50 = (bf16[960,256]{1,0:T(8,128)(2,1)S(1)}, bf16[960,256]{1,0:T(8,128)(2,1)S(1)}, u32[]{:S(2)}, u32[]{:S(2)}) collective-permute-start(bf16[960,256]{1,0:T(8,128)(2,1)S(1)} %copy-done.97), channel_id=1, source_target_pairs={{0,8},{8,0},{16,24},{24,16},{1,9},{9,1},{17,25},{25,17},{2,10},{10... | collective-permute-start | bytes 1474568 | tf_op jit(solution)/shard_map/ppermute | solution.py:361
  231.0 31.2 %collective-permute-start.51 = (bf16[960,256]{1,0:T(8,128)(2,1)S(1)}, bf16[960,256]{1,0:T(8,128)(2,1)S(1)}, u32[]{:S(2)}, u32[]{:S(2)}) collective-permute-start(bf16[960,256]{1,0:T(8,128)(2,1)S(1)} %copy-done.95), channel_id=1, source_target_pairs={{0,16},{8,24},{16,0},{24,8},{1,17},{9,25},{17,1},{25,9},{2,18},{10... | collective-permute-start | bytes 1474568 | tf_op jit(solution)/shard_map/ppermute | solution.py:361
  243.0 18.8 %collective-permute-start.49 = (bf16[160,640]{1,0:T(8,128)(2,1)S(1)}, bf16[160,640]{1,0:T(8,128)(2,1)S(1)}, u32[]{:S(2)}, u32[]{:S(2)}) collective-permute-start(bf16[160,640]{1,0:T(8,128)(2,1)S(1)} %get-tuple-element.172), channel_id=1, source_target_pairs={{2,0},{3,1},{4,2},{5,3},{6,4},{7,5},{10,8},{11,9},{12,10},{13,11},... | collective-permute-start | bytes 614408 | tf_op jit(solution)/shard_map/ppermute | solution.py:373
  244.3 17.8 %collective-permute-start.48 = (bf16[160,640]{1,0:T(8,128)(2,1)S(1)}, bf16[160,640]{1,0:T(8,128)(2,1)S(1)}, u32[]{:S(2)}, u32[]{:S(2)}) collective-permute-start(bf16[160,640]{1,0:T(8,128)(2,1)S(1)} %get-tuple-element.171), channel_id=1, source_target_pairs={{4,0},{5,1},{6,2},{7,3},{12,8},{13,9},{14,10},{15,11},{20,16},{21,... | collective-permute-start | bytes 614408 | tf_op jit(solution)/shard_map/ppermute | solution.py:373
  266.9 30.1 %collective-permute-start.54 = (bf16[16,256,256]{2,1,0:T(8,128)(2,1)S(1)}, bf16[16,256,256]{2,1,0:T(8,128)(2,1)S(1)}, u32[]{:S(2)}, u32[]{:S(2)}) collective-permute-start(bf16[16,256,256]{2,1,0:T(8,128)(2,1)S(1)} %get-tuple-element.186), channel_id=1, source_target_pairs={{0,1},{1,0},{2,3},{3,2},{4,5},{5,4},{6,7},{7,6},{8,9},{9,8},{10,11... | collective-permute-start | bytes 6291464 | tf_op jit(solution)/shard_map/ppermute | solution.py:357
  269.9 21.7 %collective-permute-start.57 = (bf16[160,640]{1,0:T(8,128)(2,1)S(1)}, bf16[160,640]{1,0:T(8,128)(2,1)S(1)}, u32[]{:S(2)}, u32[]{:S(2)}) collective-permute-start(bf16[160,640]{1,0:T(8,128)(2,1)S(1)} %get-tuple-element.267), channel_id=1, source_target_pairs={{4,0},{5,1},{6,2},{7,3},{12,8},{13,9},{14,10},{15,11},{20,16},{21,... | collective-permute-start | bytes 614408 | tf_op jit(solution)/shard_map/ppermute | solution.py:373
  271.2 27.8 %collective-permute-start.52 = (bf16[960,256]{1,0:T(8,128)(2,1)S(1)}, bf16[960,256]{1,0:T(8,128)(2,1)S(1)}, u32[]{:S(2)}, u32[]{:S(2)}) collective-permute-start(bf16[960,256]{1,0:T(8,128)(2,1)S(1)} %copy-done.93), channel_id=1, source_target_pairs={{0,8},{8,0},{16,24},{24,16},{1,9},{9,1},{17,25},{25,17},{2,10},{10... | collective-permute-start | bytes 1474568 | tf_op jit(solution)/shard_map/ppermute | solution.py:361
  276.9 22.0 %collective-permute-start.53 = (bf16[960,256]{1,0:T(8,128)(2,1)S(1)}, bf16[960,256]{1,0:T(8,128)(2,1)S(1)}, u32[]{:S(2)}, u32[]{:S(2)}) collective-permute-start(bf16[960,256]{1,0:T(8,128)(2,1)S(1)} %copy-done.91), channel_id=1, source_target_pairs={{0,16},{8,24},{16,0},{24,8},{1,17},{9,25},{17,1},{25,9},{2,18},{10... | collective-permute-start | bytes 1474568 | tf_op jit(solution)/shard_map/ppermute | solution.py:361
  292.6 17.4 %collective-permute-start.59 = (bf16[960,256]{1,0:T(8,128)(2,1)}, bf16[960,256]{1,0:T(8,128)(2,1)}, u32[]{:S(2)}, u32[]{:S(2)}) collective-permute-start(bf16[960,256]{1,0:T(8,128)(2,1)} %add_convert_fusion.8), channel_id=1, source_target_pairs={{0,8},{8,0},{16,24},{24,16},{1,9},{9,1},{17,25},{25,17},{2,10},{10... | collective-permute-start | bytes 1474568 | tf_op jit(solution)/shard_map/ppermute | solution.py:361
  297.0 31.8 %collective-permute-start.74 = (bf16[960,256]{1,0:T(8,128)(2,1)}, bf16[960,256]{1,0:T(8,128)(2,1)}, u32[]{:S(2)}, u32[]{:S(2)}) collective-permute-start(bf16[960,256]{1,0:T(8,128)(2,1)} %add_convert_fusion.6), channel_id=1, source_target_pairs={{0,6},{1,7},{2,0},{3,1},{4,2},{5,3},{6,4},{7,5},{8,14},{9,15},{10,... | collective-permute-start | bytes 1474568 | tf_op jit(solution)/shard_map/ppermute | solution.py:365
  306.5 24.9 %collective-permute-start.67 = (bf16[16,80,256]{2,1,0:T(8,128)(2,1)}, bf16[16,80,256]{2,1,0:T(8,128)(2,1)}, u32[]{:S(2)}, u32[]{:S(2)}) collective-permute-start(bf16[16,80,256]{2,1,0:T(8,128)(2,1)} %get-tuple-element.204), channel_id=1, source_target_pairs={{0,1},{1,0},{2,3},{3,2},{4,5},{5,4},{6,7},{7,6},{8,9},{9,8},{10,11... | collective-permute-start | bytes 1966088 | tf_op jit(solution)/shard_map/ppermute | solution.py:357
  310.0 22.9 %collective-permute-start.63 = (bf16[4,256,256]{2,1,0:T(8,128)(2,1)}, bf16[4,256,256]{2,1,0:T(8,128)(2,1)}, u32[]{:S(2)}, u32[]{:S(2)}) collective-permute-start(bf16[4,256,256]{2,1,0:T(8,128)(2,1)} %get-tuple-element.261), channel_id=1, source_target_pairs={{0,24},{8,16},{16,8},{24,0},{1,25},{9,17},{17,9},{25,1},{2,26},{10... | collective-permute-start | bytes 1572872 | tf_op jit(solution)/shard_map/ppermute | solution.py:361
  311.1 25.5 %collective-permute-start.62 = (bf16[4,256,256]{2,1,0:T(8,128)(2,1)}, bf16[4,256,256]{2,1,0:T(8,128)(2,1)}, u32[]{:S(2)}, u32[]{:S(2)}) collective-permute-start(bf16[4,256,256]{2,1,0:T(8,128)(2,1)} %get-tuple-element.262), channel_id=1, source_target_pairs={{0,16},{8,24},{16,0},{24,8},{1,17},{9,25},{17,1},{25,9},{2,18},{10... | collective-permute-start | bytes 1572872 | tf_op jit(solution)/shard_map/ppermute | solution.py:361
  312.2 24.4 %collective-permute-start.61 = (bf16[4,256,256]{2,1,0:T(8,128)(2,1)}, bf16[4,256,256]{2,1,0:T(8,128)(2,1)}, u32[]{:S(2)}, u32[]{:S(2)}) collective-permute-start(bf16[4,256,256]{2,1,0:T(8,128)(2,1)} %get-tuple-element.263), channel_id=1, source_target_pairs={{0,8},{8,0},{16,24},{24,16},{1,9},{9,1},{17,25},{25,17},{2,10},{10... | collective-permute-start | bytes 1572872 | tf_op jit(solution)/shard_map/ppermute | solution.py:361
  345.0 22.0 %collective-permute-start.70 = (bf16[4,80,256]{2,1,0:T(8,128)(2,1)S(1)}, bf16[4,80,256]{2,1,0:T(8,128)(2,1)S(1)}, u32[]{:S(2)}, u32[]{:S(2)}) collective-permute-start(bf16[4,80,256]{2,1,0:T(8,128)(2,1)S(1)} %get-tuple-element.278), channel_id=1, source_target_pairs={{0,24},{8,16},{16,8},{24,0},{1,25},{9,17},{17,9},{25,1},{2,26},{10... | collective-permute-start | bytes 491528 | tf_op jit(solution)/shard_map/ppermute | solution.py:361
  (180 other events, 1417.7 us)

commit v6 on v5

--- a/solution.py
+++ b/solution.py
@@ -400,7 +400,7 @@
 
 VMEM = pl.BlockSpec(memory_space=pltpu.VMEM)
 SMEM = pl.BlockSpec(memory_space=pltpu.SMEM)
-ANY = pl.BlockSpec(memory_space=pl.ANY)
+HBM = pl.BlockSpec(memory_space=pltpu.HBM)
 
 
 def run(body, name, ins, in_specs, outs, out_specs, scratch, flops, megabytes):
@@ -505,7 +505,7 @@
 
 def project_kernel(*refs):
     ids_ref, own, other = refs[0], refs[1:6], refs[6:11]
-    n1_ref, cos_ref, sin_ref, q_ref, kv_ref, proj_ref, turned_ref, rel_ref = refs[11:]
+    n1_ref, cos_ref, sin_ref, q_ref, kv_ref, all_ref, proj_ref, turned_ref, rel_ref = refs[11:]
     width = n1_ref.shape[0] * n1_ref.shape[1]
     kv_width = KEY_HEADS * HEAD_WIDTH
     q_cols, k_cols = width // 8, kv_width // 8
@@ -514,7 +514,8 @@
     for core_rel, weights in ((0, own), (1, other)):
         for s in range(4):
             f = column_index(ids_ref, core_rel, s)
-            total = product_nn(wide_rows(weights, s, 0, depth), rel_ref[...])
+            all_ref[core_rel * 4 + s] = wide_rows(weights, s, 0, depth)
+            total = product_nn(all_ref[core_rel * 4 + s], rel_ref[...])
             proj_ref[start_row(f, q_cols), :] = total[:q_cols]
             proj_ref[pl.ds(pl.multiple_of(width + f * k_cols, 8), k_cols), :] = total[
                 q_cols + 8 : q_cols + 8 + k_cols
@@ -612,16 +613,14 @@
 
 
 def attend_back_kernel(mb, *refs):
-    ids_ref, counts_ref, q_ref, do_ref = refs[:4]
-    blocks = refs[4:12]
-    lse_ref, cos_ref, sin_ref, dq_ref = refs[12:16]
-    targets = [ref.at[s] for ref in refs[16:18] for s in range(4)]
-    k_ref, v_ref, bias_ref, dk_ref, dv_ref = refs[18:]
+    ids_ref, counts_ref, q_ref, do_ref, k_ref, v_ref, lse_ref, cos_ref, sin_ref = refs[:9]
+    dq_ref = refs[9]
+    targets = [ref.at[s] for ref in refs[10:12] for s in range(4)]
+    bias_ref, dk_ref, dv_ref = refs[12:]
     cap = q_ref.shape[2] // 2
     share = QUERY_HEADS // KEY_HEADS
     half = HEAD_WIDTH // 2
     kv_width = KEY_HEADS * HEAD_WIDTH
-    stage_heads(mb, cap, blocks, k_ref, v_ref)
     stage_bias(ids_ref, counts_ref, mb, cap, share, bias_ref)
     cosine = jnp.concatenate([cos_ref[:, mb * cap : (mb + 1) * cap]] * share, 1)
     sine = jnp.concatenate([sin_ref[:, mb * cap : (mb + 1) * cap]] * share, 1)
@@ -761,11 +760,10 @@
 
 
 def finish_q_kernel(*refs):
-    ids_ref, own, other = refs[0], refs[1:6], refs[6:11]
-    n1_ref, dq_a_ref, dq_b_ref = refs[11:14]
-    out_grads = targets_of(refs[14:19])
-    dn_ref, grads = refs[19], targets_of(refs[20:25])
-    n1_rel, d_ref, dq_ref = refs[25:]
+    ids_ref, all_ref, n1_ref, dq_a_ref, dq_b_ref = refs[:5]
+    out_grads = targets_of(refs[5:10])
+    dn_ref, grads = refs[10], targets_of(refs[11:16])
+    n1_rel, d_ref, dq_ref = refs[16:]
     cap = dq_a_ref.shape[1]
     width = dq_a_ref.shape[0]
     q_cols = width // 8
@@ -776,9 +774,7 @@
     d_ref[:, cap:] = dq_b_ref[...].astype(jnp.float32)
     spread(ids_ref, d_ref, dq_ref, q_cols)
     fill_relative(ids_ref, n1_rel, n1_ref)
-    weights = jnp.concatenate(
-        [wide_rows(w, s, 0, depth) for w in (own, other) for s in range(4)], 0
-    )
+    weights = jnp.concatenate([all_ref[j, :depth, :] for j in range(8)], 0)
     dn = product_tn(weights, dq_ref[...])
     for k in range(4):
         dn_ref[ids_ref[0] ^ k] = dn[k * wide : k * wide + block]
@@ -832,16 +828,14 @@
 
 
 def finish_kernel(*refs):
-    ids_ref, own, other = refs[0], refs[1:6], refs[6:11]
-    dkv_ref, dn_ref, dh_ref, x_ref, gain_ref, tokens_ref, gain_grad_ref = refs[11:]
+    ids_ref, all_ref, dkv_ref, dn_ref, dh_ref, x_ref, gain_ref = refs[:7]
+    tokens_ref, gain_grad_ref = refs[7:]
     width = dh_ref.shape[0]
     block = dn_ref.shape[1]
     kv_rows = dkv_ref.shape[0] // 8
-    low = own[0].shape[1] - kv_rows
-    wide = own[0].shape[2]
-    weights = jnp.concatenate(
-        [wide_rows(w, s, low, low + kv_rows) for w in (own, other) for s in range(4)], 0
-    )
+    low = all_ref.shape[1] - kv_rows
+    wide = all_ref.shape[2] // 4
+    weights = jnp.concatenate([all_ref[j, low:, :] for j in range(8)], 0)
     dn = product_tn(weights, dkv_ref[...])
     for k in range(4):
         i = ids_ref[0] ^ k
@@ -1059,22 +1053,26 @@
     cosine, sine = cosine[:, 0, :].T, sine[:, 0, :].T
     x_wide = x.astype(jnp.float32)
     n1 = (x_wide * mean_square(x_wide) * gain_one).astype(jnp.bfloat16).reshape(4, block, rows)
-    n1_next = after(n1, z_two)
-
-    query, kv = run(
+    n1_next = after(n1, z_two, flat_counts, gain_one, gain_two)
+
+    query, kv, first_all = run(
         project_kernel,
         "project",
         (ids, *first_own, *first_other, n1_next, cosine, sine),
         [SMEM] + [VMEM] * 13,
-        (struct((QUERY_HEADS, HEAD_WIDTH, rows)), struct((rows, 2 * kv_width))),
-        [VMEM] * 2,
+        (
+            struct((QUERY_HEADS, HEAD_WIDTH, rows)),
+            struct((rows, 2 * kv_width)),
+            struct((8, depth, 4 * wide)),
+        ),
+        [VMEM] * 3,
         [
             pltpu.VMEM((width + 2 * kv_width, rows), jnp.float32),
             pltpu.VMEM((2 * kv_width, rows), jnp.float32),
             pltpu.VMEM((4 * wide, rows), jnp.bfloat16),
         ],
         2 * (width + 2 * kv_width) * width * rows,
-        24,
+        20,
     )
     kv_zero = after(kv, x_zero, y_zero)
     kv_one = shift_z_up(kv_zero, 1)
@@ -1094,11 +1092,7 @@
     kv_own = [kv, kv_one, kv_two, kv_three]
     kv_other = [swap_core(piece) for piece in (kv_zero, kv_one, kv_two, kv_three)]
     pair_flops = 2 * QUERY_HEADS * HEAD_WIDTH * rows * 8 * cap
-    head_scratch = [
-        pltpu.VMEM((KEY_HEADS, 8 * cap, HEAD_WIDTH), jnp.bfloat16),
-        pltpu.VMEM((KEY_HEADS, 8 * cap, HEAD_WIDTH), jnp.bfloat16),
-        pltpu.VMEM((8 * cap, share * cap), jnp.float32),
-    ]
+    bias_scratch = pltpu.VMEM((8 * cap, share * cap), jnp.float32)
     def attend(mb, queries):
         return run(
             functools.partial(attend_kernel, mb),
@@ -1108,19 +1102,21 @@
             (
                 struct((QUERY_HEADS, HEAD_WIDTH, cap)),
                 struct((KEY_HEADS, 1, share * cap), jnp.float32),
+                struct((KEY_HEADS, 8 * cap, HEAD_WIDTH)),
+                struct((KEY_HEADS, 8 * cap, HEAD_WIDTH)),
             ),
-            [VMEM] * 2,
-            head_scratch,
+            [VMEM] * 4,
+            [bias_scratch],
             4 * pair_flops,
-            24,
-        )
-
-    att_a, lse_a = attend(0, after(query, far_one, y_two))
+            20,
+        )
+
+    att_a, lse_a, *heads_a = attend(0, after(query, far_one, y_two))
     wave = (att_a, x_three, y_three)
     far_two = swap_dp(after(x_two, *wave), 2)
     far_three = swap_dp(after(y_three, *wave), 1)
     dy_other = swap_core(after(dy, att_a))
-    att_b, lse_b = attend(1, after(query, *wave))
+    att_b, lse_b, *heads_b = attend(1, after(query, *wave))
     pieces = [mlp_piece, z_one, z_two, z_three]
     pieces += [x_zero, x_one, x_two, x_three]
     pieces += [y_zero, y_one, y_two, y_three]
@@ -1129,7 +1125,7 @@
         collect_kernel,
         "collect",
         tuple(pieces[:15]) + (after(far_three, att_b),),
-        [ANY] * 16,
+        [HBM] * 16,
         [struct((4, q_rows, 4 * wide))],
         [VMEM],
         [pltpu.SemaphoreType.DMA((16,))],
@@ -1151,7 +1147,7 @@
         [VMEM] * 2,
         [pltpu.VMEM((4 * wide, rows), jnp.bfloat16)],
         2 * width * width * rows,
-        24,
+        16,
     )
     n2_other = swap_core(n2)
     results = run(
@@ -1165,10 +1161,10 @@
             dy_other.reshape(wide_blocks),
             *pieces,
         ),
-        [SMEM] + [VMEM] * 4 + [ANY] * 16,
+        [SMEM] + [VMEM] * 4 + [HBM] * 16,
         [struct((2, width, rows), jnp.float32), struct((2, width, padded))]
         + [struct((3 * half, wide))] * 16,
-        [VMEM] * 2 + [ANY] * 16,
+        [VMEM] * 2 + [HBM] * 16,
         [
             pltpu.VMEM((8 * half, 4 * wide), jnp.bfloat16),
             pltpu.VMEM((4 * half, 4 * wide), jnp.bfloat16),
@@ -1181,7 +1177,7 @@
             pltpu.SemaphoreType.DMA((2, 16)),
         ],
         18 * 16 * half * block * 2 * rows,
-        44,
+        40,
     )
     keep, send = results[:2]
     home, to_x, to_y, far = results[2:6], results[6:10], results[10:14], results[14:18]
@@ -1202,7 +1198,7 @@
         [VMEM] * 5,
         [pltpu.VMEM((width, rows), jnp.float32)],
         2 * width * width * rows,
-        24,
+        22,
     )
     output = output.T.reshape(batches, cap, width)
     def attend_back(mb, mixed):
@@ -1214,17 +1210,16 @@
                 flat_counts,
                 query,
                 mixed.reshape(QUERY_HEADS, HEAD_WIDTH, rows),
-                *kv_own,
-                *kv_other,
+                *(heads_a, heads_b)[mb],
                 lse[mb],
                 cosine,
                 sine,
             ),
-            [SMEM, SMEM] + [VMEM] * 13,
+            [SMEM, SMEM] + [VMEM] * 7,
             [struct((QUERY_HEADS, HEAD_WIDTH, cap))] + [struct((4, cap, 2 * kv_width))] * 2,
             [VMEM] * 3,
-            head_scratch
-            + [
+            [
+                bias_scratch,
                 pltpu.VMEM((KEY_HEADS, 8 * cap, HEAD_WIDTH), jnp.bfloat16),
                 pltpu.VMEM((KEY_HEADS, 8 * cap, HEAD_WIDTH), jnp.bfloat16),
             ],
@@ -1260,7 +1255,7 @@
         [VMEM] * 5,
         [pltpu.VMEM((4 * wide, rows), jnp.bfloat16)],
         2 * width * width * rows,
-        16,
+        14,
     )
     summed_a = sum_cores(*back_a[1:])
     wave = (x_two, y_three, out_grads[0])
@@ -1290,14 +1285,13 @@
         "finish_q",
         (
             ids,
-            *first_own,
-            *first_other,
+            first_all,
             after(n1, *wave),
             back_a[0].reshape(width, cap),
             back_b[0].reshape(width, cap),
             *out_grads,
         ),
-        [SMEM] + [VMEM] * 18,
+        [SMEM] + [VMEM] * 9,
         [struct(blocks, jnp.float32)]
         + [struct((4, 2 * q_rows, wide))] * 4
         + [struct((16, 2 * q_rows, wide))],
@@ -1308,7 +1302,7 @@
             pltpu.VMEM((8 * q_rows, rows), jnp.bfloat16),
         ],
         4 * width * width * rows,
-        24,
+        22,
     )
     dn_q = q_results[0]
     dkv_b = summed_b[0].astype(jnp.float32)
@@ -1337,18 +1331,18 @@
             pltpu.VMEM((2 * kv_width, rows), jnp.float32),
         ],
         4 * kv_width * width * rows,
-        20,
+        14,
     )
     grad_tokens, gain_one_grad = run(
         finish_kernel,
         "finish",
-        (ids, *first_own, *first_other, dkv_pieces, dn_q, dh, after(x, x_zero, y_one), gain_one),
-        [SMEM] + [VMEM] * 15,
+        (ids, first_all, dkv_pieces, dn_q, dh, after(x, x_zero, y_one), gain_one),
+        [SMEM] + [VMEM] * 6,
         [struct((width, rows), jnp.float32), struct((width, 1), jnp.float32)],
         [VMEM] * 2,
         [],
         4 * kv_width * width * rows,
-        24,
+        20,
     )
     grad_tokens = grad_tokens.T.reshape(batches, cap, width)
     kv_mine = sum_pair(kv_grads)

time: 389 us -> 377 us (0.969)
  waiting for transfers between devices: 107 us -> 119 us
  local copies, waits for them, and re-layouts: 63.1 us -> 54.8 us
  starting transfers between devices: 86.1 us -> 78.4 us
  Pallas kernels: 104 us -> 99.3 us
    ppermute x2, waiting for transfers between devices: 3.08 us -> 8.54 us  [fast(): lax.ppermute(gain_total, 'fsdp', [(j, j ^ mask) for j in range(8)])]
    ppermute x2, starting transfers between devices: 8.12 us -> 3.18 us  [fast(): lax.ppermute(gain_total, 'fsdp', [(j, j ^ mask) for j in range(8)])]
    pallas_call x16, Pallas kernels: 104 us -> 99.3 us  [run(): pl.pallas_call(body, out_shape=tuple(outs), in_specs=in_specs, out_specs=...]
    unnamed x246 -> x222, local copies, waits for them, and re-layouts: 46.9 us -> 42.2 us
    ppermute x3, waiting for transfers between devices: 17.1 us -> 21.5 us  [shift_z_up(): lax.ppermute(value, 'fsdp', [(j, j + 2 * step) for j in range(8) if j + 2...]
  transfers between devices with their start and end apart: 83 -> 83, of which waited for: 34 -> 36; matrix products, arithmetic and copies ran while one was open for 9% -> 8% of each run, Pallas kernels for 17% -> 17%
where the time goes in v6:
time: 377 us; the launch traced here: 370 us
  waiting for transfers between devices  119 us (32%)
  Pallas kernels  99.3 us (26%)
  starting transfers between devices  78.4 us (21%)
  local copies, waits for them, and re-layouts  54.8 us (15%)
  other arithmetic  16.7 us (4%)
    pallas_call x16, Pallas kernels, run(): pl.pallas_call(body, out_shape=tuple(outs), in_specs=in_specs, out_specs=...  99.3 us
    unnamed x222, local copies, waits for them, and re-layouts  42.2 us
    ppermute x36, waiting for transfers between devices, swap_dp(): return lax.ppermute(value, 'dp', [(j, j ^ mask) for j in range(4)])  40.8 us
    ppermute x36, starting transfers between devices, swap_dp(): return lax.ppermute(value, 'dp', [(j, j ^ mask) for j in range(4)])  37.2 us
    ppermute x3, waiting for transfers between devices, shift_z_up(): lax.ppermute(value, 'fsdp', [(j, j + 2 * step) for j in range(8) if j + 2...  21.5 us
    ppermute x15, waiting for transfers between devices, shift_z(): lax.ppermute(value, 'fsdp', [(j, (j + 2 * step) % 8) for j in range(8)])  18.6 us
    ppermute x6, waiting for transfers between devices, shift_z_down(): lax.ppermute(value, 'fsdp', [(j, j - 2 * step) for j in range(8) if j - 2...  18.5 us
    ppermute x15, starting transfers between devices, shift_z(): lax.ppermute(value, 'fsdp', [(j, (j + 2 * step) % 8) for j in range(8)])  15.5 us
  transfers between devices with their start and end apart: 83, of which 36 were waited for; matrix products, arithmetic and copies ran while one was open for 8% of the time, Pallas kernels for 17%

profile of v6, /device:TPU:0, one launch (start us, length us, event | category | flops | bytes accessed | tf_op | source)
XLA Modules:
  0.0 370.5 jit_solution(18408920117667102326)
XLA Ops:
  5.0 5.1 %collective-permute-start.3 = (bf16[208,256]{1,0:T(8,128)(2,1)S(1)}, bf16[208,256]{1,0:T(8,128)(2,1)S(1)}, u32[]{:S(2)}, u32[]{:S(2)}) collective-permute-start(bf16[208,256]{1,0:T(8,128)(2,1)S(1)} %pack_first.1), channel_id=1, source_target_pairs={{0,6},{1,7},{2,0},{3,1},{4,2},{5,3},{6,4},{7,5},{8,14},{9,15},{10,... | collective-permute-start | bytes 319496 | tf_op jit(solution)/shard_map/ppermute | solution.py:365
  16.1 3.3 collective-permute-done.2
  25.5 8.1 %collective-permute-done.9.refs_3_ = bf16[4,208,256]{2,1,0:T(8,128)(2,1)S(1)} collective-permute-done((bf16[4,208,256]{2,1,0:T(8,128)(2,1)S(1)}, bf16[4,208,256]{2,1,0:T(8,128)(2,1)S(1)}, u32[]{:S(2)}, u32[]{:S(2)}) %collective-permute-start.9) | collective-permute-done | bytes 426016 | tf_op jit(solution)/shard_map/ppermute | solution.py:361
  35.8 5.0 %collective-permute-done.4.refs_1_.refs_6_ = bf16[1088,256]{1,0:T(8,128)(2,1)S(1)} collective-permute-done((bf16[1088,256]{1,0:T(8,128)(2,1)}, bf16[1088,256]{1,0:T(8,128)(2,1)S(1)}, u32[]{:S(2)}, u32[]{:S(2)}) %collective-permute-start.4) | collective-permute-done | bytes 557088 | tf_op jit(solution)/shard_map/ppermute | solution.py:365
  49.7 6.1 %collective-permute-done.5.refs_2_.refs_7_ = bf16[1088,256]{1,0:T(8,128)(2,1)} collective-permute-done((bf16[1088,256]{1,0:T(8,128)(2,1)S(1)}, bf16[1088,256]{1,0:T(8,128)(2,1)}, u32[]{:S(2)}, u32[]{:S(2)}) %collective-permute-start.5) | collective-permute-done | bytes 557088 | tf_op jit(solution)/shard_map/ppermute | solution.py:365
  68.9 9.0 %collective-permute-done.20.refs_4_ = bf16[320,640]{1,0:T(8,128)(2,1)S(1)} collective-permute-done((bf16[320,640]{1,0:T(8,128)(2,1)S(1)}, bf16[320,640]{1,0:T(8,128)(2,1)S(1)}, u32[]{:S(2)}, u32[]{:S(2)}) %collective-permute-start.20) | collective-permute-done | bytes 409632 | tf_op jit(solution)/shard_map/ppermute | solution.py:369
  84.0 6.9 %collective-permute-done.23.refs_5_ = bf16[320,640]{1,0:T(8,128)(2,1)S(1)} collective-permute-done((bf16[320,640]{1,0:T(8,128)(2,1)S(1)}, bf16[320,640]{1,0:T(8,128)(2,1)S(1)}, u32[]{:S(2)}, u32[]{:S(2)}) %collective-permute-start.23) | collective-permute-done | bytes 409632 | tf_op jit(solution)/shard_map/ppermute | solution.py:369
  94.2 4.6 %collective-permute-start.25 = (bf16[320,640]{1,0:T(8,128)(2,1)S(1)}, bf16[320,640]{1,0:T(8,128)(2,1)S(1)}, u32[]{:S(2)}, u32[]{:S(2)}) collective-permute-start(bf16[320,640]{1,0:T(8,128)(2,1)S(1)} %collective-permute-done.23.refs_5_), channel_id=1, source_target_pairs={{0,2},{1,3},{2,4},{3,5},{4,6},{5,7},{8,10},{9,11},{10,12},{11,13},... | collective-permute-start | bytes 1228808 | tf_op jit(solution)/shard_map/ppermute | solution.py:369
  99.4 5.5 %collective-permute-done.25.refs_6_ = bf16[320,640]{1,0:T(8,128)(2,1)S(1)} collective-permute-done((bf16[320,640]{1,0:T(8,128)(2,1)S(1)}, bf16[320,640]{1,0:T(8,128)(2,1)S(1)}, u32[]{:S(2)}, u32[]{:S(2)}) %collective-permute-start.25) | collective-permute-done | bytes 409632 | tf_op jit(solution)/shard_map/ppermute | solution.py:369
  107.8 8.5 %attend.2 = (bf16[15,64,160]{2,1,0:T(8,128)(2,1)S(1)}, f32[5,1,480]{2,1,0:T(1,128)S(1)}, bf16[5,1280,64]{2,1,0:T(8,128)(2,1)S(1)}, bf16[5,1280,64]{2,1,0:T(8,128)(2,1)S(1)}) custom-call(s32[4]{0:T(128)S(1)} %pad_add_fusion.ids_ref.refs_0_, s32[16]{0:T(128)S(1)} %reshape.237.refs_1_, bf16[15,64,320]{2,1,0:T(8,128)(2,1)S(1)} %get-tuple-element.139.refs_2_, ...), custom_call_target="tpu_custom_call" | custom-call | flops 3145728000 | bytes 5846480 | tf_op jit(solution)/shard_map/attend/pallas_call | solution.py:409
  122.7 8.9 %attend.3 = (bf16[15,64,160]{2,1,0:T(8,128)(2,1)S(1)}, f32[5,1,480]{2,1,0:T(1,128)S(1)}, bf16[5,1280,64]{2,1,0:T(8,128)(2,1)S(1)}, bf16[5,1280,64]{2,1,0:T(8,128)(2,1)S(1)}) custom-call(s32[4]{0:T(128)S(1)} %pad_add_fusion.ids_ref.refs_0_, s32[16]{0:T(128)S(1)} %reshape.237.refs_1_, bf16[15,64,320]{2,1,0:T(8,128)(2,1)S(1)} %get-tuple-element.139.refs_2_, ...), custom_call_target="tpu_custom_call" | custom-call | flops 3145728000 | bytes 5846480 | tf_op jit(solution)/shard_map/attend/pallas_call | solution.py:409
  137.2 3.2 collective-permute-done.37
  147.3 29.5 %mlp.1 = (f32[2,960,320]{2,1,0:T(8,128)}, bf16[2,960,384]{2,1,0:T(8,128)(2,1)}, bf16[960,256]{1,0:T(8,128)(2,1)S(1)}, bf16[960,256]{1,0:T(8,128)(2,1)S(1)}, bf16...) custom-call(s32[4]{0:T(128)S(1)} %pad_add_fusion.ids_ref.refs_0_, ...), custom_call_target="tpu_custom_call" | custom-call | flops 14155776000 | bytes 23658512 | tf_op jit(solution)/shard_map/mlp/pallas_call | solution.py:409
  184.9 3.3 collective-permute-done.39.arrived_ref
  199.5 13.2 %attend_back.2 = (bf16[15,64,160]{2,1,0:T(8,128)(2,1)S(1)}, bf16[4,160,640]{2,1,0:T(8,128)(2,1)S(1)}, bf16[4,160,640]{2,1,0:T(8,128)(2,1)S(1)}) custom-call(s32[4]{0:T(128)S(1)} %pad_add_fusion.ids_ref.refs_0_, s32[16]{0:T(128)S(1)} %reshape.237.refs_1_, bf16[15,64,320]{2,1,0:T(8,128)(2,1)S(1)} %copy-done.78, bf16[15,64,320]{2,1,0:T(8,128)(2,1)S(1)} %bitcast.116, ...), custom_call_target="tpu_custom_call" | custom-call | flops 7864320000 | bytes 4904400 | tf_op jit(solution)/shard_map/attend_back/pallas_call | solution.py:409
  212.8 7.0 %collective-permute-done.43 = bf16[960,256]{1,0:T(8,128)(2,1)S(1)} collective-permute-done((bf16[960,256]{1,0:T(8,128)(2,1)S(1)}, bf16[960,256]{1,0:T(8,128)(2,1)S(1)}, u32[]{:S(2)}, u32[]{:S(2)}) %collective-permute-start.43) | collective-permute-done | bytes 491552 | tf_op jit(solution)/shard_map/ppermute | solution.py:361
  227.3 6.9 %collective-permute-done.45 = bf16[960,256]{1,0:T(8,128)(2,1)S(1)} collective-permute-done((bf16[960,256]{1,0:T(8,128)(2,1)S(1)}, bf16[960,256]{1,0:T(8,128)(2,1)S(1)}, u32[]{:S(2)}, u32[]{:S(2)}) %collective-permute-start.45) | collective-permute-done | bytes 491552 | tf_op jit(solution)/shard_map/ppermute | solution.py:361
  239.5 13.0 %attend_back.3 = (bf16[15,64,160]{2,1,0:T(8,128)(2,1)S(1)}, bf16[4,160,640]{2,1,0:T(8,128)(2,1)S(1)}, bf16[4,160,640]{2,1,0:T(8,128)(2,1)S(1)}) custom-call(s32[4]{0:T(128)S(1)} %pad_add_fusion.ids_ref.refs_0_, s32[16]{0:T(128)S(1)} %reshape.237.refs_1_, bf16[15,64,320]{2,1,0:T(8,128)(2,1)S(1)} %copy-done.78, bf16[15,64,320]{2,1,0:T(8,128)(2,1)S(1)} %bitcast.117, ...), custom_call_target="tpu_custom_call" | custom-call | flops 7864320000 | bytes 4904400 | tf_op jit(solution)/shard_map/attend_back/pallas_call | solution.py:409
  255.2 4.0 %finish_q.1 = (f32[4,240,320]{2,1,0:T(8,128)S(1)}, bf16[4,256,256]{2,1,0:T(8,128)(2,1)S(1)}, bf16[4,256,256]{2,1,0:T(8,128)(2,1)S(1)}, bf16[4,256,256]{2,1,0:T(8...) custom-call(s32[4]{0:T(128)S(1)} %pad_add_fusion.ids_ref.refs_0_, ...), custom_call_target="tpu_custom_call" | custom-call | flops 1179648000 | bytes 12156944 | tf_op jit(solution)/shard_map/finish_q/pallas_call | solution.py:409
  265.1 9.8 %collective-permute-done.56 = bf16[160,640]{1,0:T(8,128)(2,1)S(1)} collective-permute-done((bf16[160,640]{1,0:T(8,128)(2,1)S(1)}, bf16[160,640]{1,0:T(8,128)(2,1)S(1)}, u32[]{:S(2)}, u32[]{:S(2)}) %collective-permute-start.56) | collective-permute-done | bytes 204832 | tf_op jit(solution)/shard_map/ppermute | solution.py:373
  276.1 6.1 %collective-permute-done.57 = bf16[160,640]{1,0:T(8,128)(2,1)S(1)} collective-permute-done((bf16[160,640]{1,0:T(8,128)(2,1)S(1)}, bf16[160,640]{1,0:T(8,128)(2,1)S(1)}, u32[]{:S(2)}, u32[]{:S(2)}) %collective-permute-start.57) | collective-permute-done | bytes 204832 | tf_op jit(solution)/shard_map/ppermute | solution.py:373
  289.2 4.1 %kv_grad.1 = (bf16[640,320]{1,0:T(8,128)(2,1)S(1)}, bf16[4,80,256]{2,1,0:T(8,128)(2,1)S(1)}, bf16[4,80,256]{2,1,0:T(8,128)(2,1)S(1)}, bf16[4,80,256]{2,1,0:T(8,1...) custom-call(s32[4]{0:T(128)S(1)} %pad_add_fusion.ids_ref.refs_0_, ...), custom_call_target="tpu_custom_call" | custom-call | flops 393216000 | bytes 3235856 | tf_op jit(solution)/shard_map/kv_grad/pallas_call | solution.py:409
  321.4 5.7 %collective-permute-done.62 = bf16[4,256,256]{2,1,0:T(8,128)(2,1)} collective-permute-done((bf16[4,256,256]{2,1,0:T(8,128)(2,1)}, bf16[4,256,256]{2,1,0:T(8,128)(2,1)}, u32[]{:S(2)}, u32[]{:S(2)}) %collective-permute-start.62) | collective-permute-done | bytes 524320 | tf_op jit(solution)/shard_map/ppermute | solution.py:361
  354.6 8.5 %collective-permute-done.82 = f32[2,960]{1,0:T(2,128)S(1)} collective-permute-done((f32[2,960]{1,0:T(2,128)S(1)}, f32[2,960]{1,0:T(2,128)S(1)}, u32[]{:S(2)}, u32[]{:S(2)}) %collective-permute-start.82) | collective-permute-done | bytes 7712 | tf_op jit(solution)/shard_map/ppermute | solution.py:1374
  (443 shorter events, 182.6 us)
Async XLA Ops:
  21.3 27.0 %collective-permute-start.12 = (bf16[4,208,256]{2,1,0:T(8,128)(2,1)S(1)}, bf16[4,208,256]{2,1,0:T(8,128)(2,1)S(1)}, u32[]{:S(2)}, u32[]{:S(2)}) collective-permute-start(bf16[4,208,256]{2,1,0:T(8,128)(2,1)S(1)} %pad_maximum_fusion.refs_1_), channel_id=1, source_target_pairs={{0,1},{1,0},{2,3},{3,2},{4,5},{5,4},{6,7},{7,6},{8,9},{9,8},{10,11... | collective-permute-start | bytes 1277960 | tf_op jit(solution)/shard_map/ppermute | solution.py:357
  23.4 19.0 %collective-permute-start.7 = (bf16[4,208,256]{2,1,0:T(8,128)(2,1)S(1)}, bf16[4,208,256]{2,1,0:T(8,128)(2,1)S(1)}, u32[]{:S(2)}, u32[]{:S(2)}) collective-permute-start(bf16[4,208,256]{2,1,0:T(8,128)(2,1)S(1)} %pad_maximum_fusion.refs_1_), channel_id=1, source_target_pairs={{0,8},{8,0},{16,24},{24,16},{1,9},{9,1},{17,25},{25,17},{2,10},{10... | collective-permute-start | bytes 1277960 | tf_op jit(solution)/shard_map/ppermute | solution.py:361
  24.8 16.0 %collective-permute-start.4 = (bf16[1088,256]{1,0:T(8,128)(2,1)}, bf16[1088,256]{1,0:T(8,128)(2,1)S(1)}, u32[]{:S(2)}, u32[]{:S(2)}) collective-permute-start(bf16[1088,256]{1,0:T(8,128)(2,1)} %pack_mlp.1.refs_0_.refs_5_), channel_id=1, source_target_pairs={{0,2},{1,3},{2,4},{3,5},{4,6},{5,7},{6,0},{7,1},{8,10},{9,11},{10,... | collective-permute-start | bytes 1671176 | tf_op jit(solution)/shard_map/ppermute | solution.py:365
  56.1 21.9 %collective-permute-start.6 = (bf16[1088,256]{1,0:T(8,128)(2,1)}, bf16[1088,256]{1,0:T(8,128)(2,1)S(1)}, u32[]{:S(2)}, u32[]{:S(2)}) collective-permute-start(bf16[1088,256]{1,0:T(8,128)(2,1)} %collective-permute-done.5.refs_2_.refs_7_), channel_id=1, source_target_pairs={{0,2},{1,3},{2,4},{3,5},{4,6},{5,7},{6,0},{7,1},{8,10},{9,11},{10,... | collective-permute-start | bytes 1671176 | tf_op jit(solution)/shard_map/ppermute | solution.py:365
  195.5 17.3 %collective-permute-start.41 = (bf16[960,256]{1,0:T(8,128)(2,1)S(1)}, bf16[960,256]{1,0:T(8,128)(2,1)S(1)}, u32[]{:S(2)}, u32[]{:S(2)}) collective-permute-start(bf16[960,256]{1,0:T(8,128)(2,1)S(1)} %get-tuple-element.160), channel_id=1, source_target_pairs={{0,16},{8,24},{16,0},{24,8},{1,17},{9,25},{17,1},{25,9},{2,18},{10... | collective-permute-start | bytes 1474568 | tf_op jit(solution)/shard_map/ppermute | solution.py:361
  196.3 16.5 %collective-permute-start.42 = (bf16[960,256]{1,0:T(8,128)(2,1)S(1)}, bf16[960,256]{1,0:T(8,128)(2,1)S(1)}, u32[]{:S(2)}, u32[]{:S(2)}) collective-permute-start(bf16[960,256]{1,0:T(8,128)(2,1)S(1)} %get-tuple-element.163), channel_id=1, source_target_pairs={{0,8},{8,0},{16,24},{24,16},{1,9},{9,1},{17,25},{25,17},{2,10},{10... | collective-permute-start | bytes 1474568 | tf_op jit(solution)/shard_map/ppermute | solution.py:361
  197.5 22.3 %collective-permute-start.43 = (bf16[960,256]{1,0:T(8,128)(2,1)S(1)}, bf16[960,256]{1,0:T(8,128)(2,1)S(1)}, u32[]{:S(2)}, u32[]{:S(2)}) collective-permute-start(bf16[960,256]{1,0:T(8,128)(2,1)S(1)} %copy-done.89), channel_id=1, source_target_pairs={{0,8},{8,0},{16,24},{24,16},{1,9},{9,1},{17,25},{25,17},{2,10},{10... | collective-permute-start | bytes 1474568 | tf_op jit(solution)/shard_map/ppermute | solution.py:361
  198.3 21.5 %collective-permute-start.44 = (bf16[960,256]{1,0:T(8,128)(2,1)}, bf16[960,256]{1,0:T(8,128)(2,1)S(1)}, u32[]{:S(2)}, u32[]{:S(2)}) collective-permute-start(bf16[960,256]{1,0:T(8,128)(2,1)} %get-tuple-element.167), channel_id=1, source_target_pairs={{0,16},{8,24},{16,0},{24,8},{1,17},{9,25},{17,1},{25,9},{2,18},{10... | collective-permute-start | bytes 1474568 | tf_op jit(solution)/shard_map/ppermute | solution.py:361
  222.7 32.5 %collective-permute-start.50 = (bf16[960,256]{1,0:T(8,128)(2,1)S(1)}, bf16[960,256]{1,0:T(8,128)(2,1)S(1)}, u32[]{:S(2)}, u32[]{:S(2)}) collective-permute-start(bf16[960,256]{1,0:T(8,128)(2,1)S(1)} %copy-done.87), channel_id=1, source_target_pairs={{0,8},{8,0},{16,24},{24,16},{1,9},{9,1},{17,25},{25,17},{2,10},{10... | collective-permute-start | bytes 1474568 | tf_op jit(solution)/shard_map/ppermute | solution.py:361
  223.5 31.7 %collective-permute-start.51 = (bf16[960,256]{1,0:T(8,128)(2,1)S(1)}, bf16[960,256]{1,0:T(8,128)(2,1)S(1)}, u32[]{:S(2)}, u32[]{:S(2)}) collective-permute-start(bf16[960,256]{1,0:T(8,128)(2,1)S(1)} %copy-done.85), channel_id=1, source_target_pairs={{0,16},{8,24},{16,0},{24,8},{1,17},{9,25},{17,1},{25,9},{2,18},{10... | collective-permute-start | bytes 1474568 | tf_op jit(solution)/shard_map/ppermute | solution.py:361
  235.6 16.9 %collective-permute-start.49 = (bf16[160,640]{1,0:T(8,128)(2,1)S(1)}, bf16[160,640]{1,0:T(8,128)(2,1)S(1)}, u32[]{:S(2)}, u32[]{:S(2)}) collective-permute-start(bf16[160,640]{1,0:T(8,128)(2,1)S(1)} %get-tuple-element.182), channel_id=1, source_target_pairs={{2,0},{3,1},{4,2},{5,3},{6,4},{7,5},{10,8},{11,9},{12,10},{13,11},... | collective-permute-start | bytes 614408 | tf_op jit(solution)/shard_map/ppermute | solution.py:373
  236.9 18.1 %collective-permute-start.48 = (bf16[160,640]{1,0:T(8,128)(2,1)S(1)}, bf16[160,640]{1,0:T(8,128)(2,1)S(1)}, u32[]{:S(2)}, u32[]{:S(2)}) collective-permute-start(bf16[160,640]{1,0:T(8,128)(2,1)S(1)} %get-tuple-element.181), channel_id=1, source_target_pairs={{4,0},{5,1},{6,2},{7,3},{12,8},{13,9},{14,10},{15,11},{20,16},{21,... | collective-permute-start | bytes 614408 | tf_op jit(solution)/shard_map/ppermute | solution.py:373
  238.2 16.8 %collective-permute-start.47 = (bf16[160,640]{1,0:T(8,128)(2,1)S(1)}, bf16[160,640]{1,0:T(8,128)(2,1)S(1)}, u32[]{:S(2)}, u32[]{:S(2)}) collective-permute-start(bf16[160,640]{1,0:T(8,128)(2,1)S(1)} %get-tuple-element.180), channel_id=1, source_target_pairs={{6,0},{7,1},{14,8},{15,9},{22,16},{23,17},{30,24},{31,25}} | collective-permute-start | bytes 614408 | tf_op jit(solution)/shard_map/ppermute | solution.py:373
  259.3 28.1 %collective-permute-start.54 = (bf16[16,256,256]{2,1,0:T(8,128)(2,1)S(1)}, bf16[16,256,256]{2,1,0:T(8,128)(2,1)S(1)}, u32[]{:S(2)}, u32[]{:S(2)}) collective-permute-start(bf16[16,256,256]{2,1,0:T(8,128)(2,1)S(1)} %get-tuple-element.196), channel_id=1, source_target_pairs={{0,1},{1,0},{2,3},{3,2},{4,5},{5,4},{6,7},{7,6},{8,9},{9,8},{10,11... | collective-permute-start | bytes 6291464 | tf_op jit(solution)/shard_map/ppermute | solution.py:357
  262.9 19.4 %collective-permute-start.57 = (bf16[160,640]{1,0:T(8,128)(2,1)S(1)}, bf16[160,640]{1,0:T(8,128)(2,1)S(1)}, u32[]{:S(2)}, u32[]{:S(2)}) collective-permute-start(bf16[160,640]{1,0:T(8,128)(2,1)S(1)} %get-tuple-element.277), channel_id=1, source_target_pairs={{4,0},{5,1},{6,2},{7,3},{12,8},{13,9},{14,10},{15,11},{20,16},{21,... | collective-permute-start | bytes 614408 | tf_op jit(solution)/shard_map/ppermute | solution.py:373
  264.2 25.0 %collective-permute-start.52 = (bf16[960,256]{1,0:T(8,128)(2,1)S(1)}, bf16[960,256]{1,0:T(8,128)(2,1)S(1)}, u32[]{:S(2)}, u32[]{:S(2)}) collective-permute-start(bf16[960,256]{1,0:T(8,128)(2,1)S(1)} %copy-done.83), channel_id=1, source_target_pairs={{0,8},{8,0},{16,24},{24,16},{1,9},{9,1},{17,25},{25,17},{2,10},{10... | collective-permute-start | bytes 1474568 | tf_op jit(solution)/shard_map/ppermute | solution.py:361
  283.3 16.9 %collective-permute-start.59 = (bf16[960,256]{1,0:T(8,128)(2,1)}, bf16[960,256]{1,0:T(8,128)(2,1)}, u32[]{:S(2)}, u32[]{:S(2)}) collective-permute-start(bf16[960,256]{1,0:T(8,128)(2,1)} %add_convert_fusion.8), channel_id=1, source_target_pairs={{0,8},{8,0},{16,24},{24,16},{1,9},{9,1},{17,25},{25,17},{2,10},{10... | collective-permute-start | bytes 1474568 | tf_op jit(solution)/shard_map/ppermute | solution.py:361
  287.3 29.9 %collective-permute-start.74 = (bf16[960,256]{1,0:T(8,128)(2,1)}, bf16[960,256]{1,0:T(8,128)(2,1)}, u32[]{:S(2)}, u32[]{:S(2)}) collective-permute-start(bf16[960,256]{1,0:T(8,128)(2,1)} %add_convert_fusion.6), channel_id=1, source_target_pairs={{0,6},{1,7},{2,0},{3,1},{4,2},{5,3},{6,4},{7,5},{8,14},{9,15},{10,... | collective-permute-start | bytes 1474568 | tf_op jit(solution)/shard_map/ppermute | solution.py:365
  296.8 23.1 %collective-permute-start.67 = (bf16[16,80,256]{2,1,0:T(8,128)(2,1)}, bf16[16,80,256]{2,1,0:T(8,128)(2,1)}, u32[]{:S(2)}, u32[]{:S(2)}) collective-permute-start(bf16[16,80,256]{2,1,0:T(8,128)(2,1)} %get-tuple-element.214), channel_id=1, source_target_pairs={{0,1},{1,0},{2,3},{3,2},{4,5},{5,4},{6,7},{7,6},{8,9},{9,8},{10,11... | collective-permute-start | bytes 1966088 | tf_op jit(solution)/shard_map/ppermute | solution.py:357
  300.2 21.1 %collective-permute-start.63 = (bf16[4,256,256]{2,1,0:T(8,128)(2,1)}, bf16[4,256,256]{2,1,0:T(8,128)(2,1)}, u32[]{:S(2)}, u32[]{:S(2)}) collective-permute-start(bf16[4,256,256]{2,1,0:T(8,128)(2,1)} %get-tuple-element.271), channel_id=1, source_target_pairs={{0,24},{8,16},{16,8},{24,0},{1,25},{9,17},{17,9},{25,1},{2,26},{10... | collective-permute-start | bytes 1572872 | tf_op jit(solution)/shard_map/ppermute | solution.py:361
  301.7 25.4 %collective-permute-start.62 = (bf16[4,256,256]{2,1,0:T(8,128)(2,1)}, bf16[4,256,256]{2,1,0:T(8,128)(2,1)}, u32[]{:S(2)}, u32[]{:S(2)}) collective-permute-start(bf16[4,256,256]{2,1,0:T(8,128)(2,1)} %get-tuple-element.272), channel_id=1, source_target_pairs={{0,16},{8,24},{16,0},{24,8},{1,17},{9,25},{17,1},{25,9},{2,18},{10... | collective-permute-start | bytes 1572872 | tf_op jit(solution)/shard_map/ppermute | solution.py:361
  302.9 24.1 %collective-permute-start.61 = (bf16[4,256,256]{2,1,0:T(8,128)(2,1)}, bf16[4,256,256]{2,1,0:T(8,128)(2,1)}, u32[]{:S(2)}, u32[]{:S(2)}) collective-permute-start(bf16[4,256,256]{2,1,0:T(8,128)(2,1)} %get-tuple-element.273), channel_id=1, source_target_pairs={{0,8},{8,0},{16,24},{24,16},{1,9},{9,1},{17,25},{25,17},{2,10},{10... | collective-permute-start | bytes 1572872 | tf_op jit(solution)/shard_map/ppermute | solution.py:361
  332.3 18.4 %collective-permute-start.70 = (bf16[4,80,256]{2,1,0:T(8,128)(2,1)S(1)}, bf16[4,80,256]{2,1,0:T(8,128)(2,1)S(1)}, u32[]{:S(2)}, u32[]{:S(2)}) collective-permute-start(bf16[4,80,256]{2,1,0:T(8,128)(2,1)S(1)} %get-tuple-element.288), channel_id=1, source_target_pairs={{0,24},{8,16},{16,8},{24,0},{1,25},{9,17},{17,9},{25,1},{2,26},{10... | collective-permute-start | bytes 491528 | tf_op jit(solution)/shard_map/ppermute | solution.py:361
  349.0 16.6 %collective-permute-start.76 = (bf16[960,256]{1,0:T(8,128)(2,1)S(1)}, bf16[960,256]{1,0:T(8,128)(2,1)S(1)}, u32[]{:S(2)}, u32[]{:S(2)}) collective-permute-start(bf16[960,256]{1,0:T(8,128)(2,1)S(1)} %add_convert_fusion.4), channel_id=1, source_target_pairs={{0,6},{1,7},{2,0},{3,1},{4,2},{5,3},{6,4},{7,5},{8,14},{9,15},{10,... | collective-permute-start | bytes 1474568 | tf_op jit(solution)/shard_map/ppermute | solution.py:365
  (168 other events, 1550.8 us)

commit v7 on v6

--- a/solution.py
+++ b/solution.py
@@ -858,8 +858,11 @@
     ids_ref, n2_own, n2_other, dy_own, dy_other = refs[:5]
     pieces = refs[5:21]
     keep_ref, send_ref = refs[21:23]
-    grads = refs[23:39]
-    wgu, wdn, gu_ref, prod_ref, dgu_ref, n2_rel, dy_rel, sem_in, sem_out = refs[39:]
+    x_first, y_first = refs[35:37]
+    grads = list(refs[23:27]) + [refs[27], x_first.at[1], refs[28], refs[29]]
+    grads += [y_first.at[1], refs[30], refs[31], refs[32]]
+    grads += [y_first.at[0], x_first.at[0], refs[33], refs[34]]
+    wgu, wdn, gu_ref, prod_ref, dgu_ref, n2_rel, dy_rel, sem_in, sem_out = refs[37:]
     dp_id = ids_ref[0]
     z_id = ids_ref[1]
     block, rows = keep_ref.shape[1] // 4, keep_ref.shape[2]
@@ -1163,8 +1166,9 @@
         ),
         [SMEM] + [VMEM] * 4 + [HBM] * 16,
         [struct((2, width, rows), jnp.float32), struct((2, width, padded))]
-        + [struct((3 * half, wide))] * 16,
-        [VMEM] * 2 + [HBM] * 16,
+        + [struct((3 * half, wide))] * 12
+        + [struct((2, 3 * half, wide))] * 2,
+        [VMEM] * 2 + [HBM] * 14,
         [
             pltpu.VMEM((8 * half, 4 * wide), jnp.bfloat16),
             pltpu.VMEM((4 * half, 4 * wide), jnp.bfloat16),
@@ -1177,10 +1181,12 @@
             pltpu.SemaphoreType.DMA((2, 16)),
         ],
         18 * 16 * half * block * 2 * rows,
-        40,
+        52,
     )
     keep, send = results[:2]
-    home, to_x, to_y, far = results[2:6], results[6:10], results[10:14], results[14:18]
+    home = results[2:6]
+    to_x_zero, to_x_two, to_x_three, to_y_one, to_y_two, to_y_three = results[6:12]
+    far_two, far_three, x_first, y_first = results[12:]
     arrived = swap_core(send)
 
     output, dh, mixed_gradient, gain_two_grad, da_pieces = run(
@@ -1237,15 +1243,14 @@
             total = total + shift_z_down(summed[s], s).astype(jnp.float32)
         return total
 
-    via_three = swap_dp(after(far[3], mixed_gradient), 1)
-    via_two = swap_dp(after(far[2], mixed_gradient), 2)
-    x_three = swap_dp(after(to_x[3], mixed_gradient), 1)
-    y_two = swap_dp(after(to_y[2], mixed_gradient), 2)
+    via_three = swap_dp(after(far_three, mixed_gradient), 1)
+    via_two = swap_dp(after(far_two, mixed_gradient), 2)
+    x_three = swap_dp(after(to_x_three, mixed_gradient), 1)
+    y_two = swap_dp(after(to_y_two, mixed_gradient), 2)
     back_a = attend_back(0, mixed_gradient)
     wave = (back_a[0], via_three, via_two, x_three, y_two)
-    x_two = swap_dp(add_low(to_x[2], after(via_two, *wave)), 1)
-    y_three = swap_dp(add_low(to_y[3], after(via_three, *wave)), 2)
-    via_one, via_zero = swap_dp(after(far[1], *wave), 1), swap_dp(after(far[0], *wave), 2)
+    x_two = swap_dp(add_low(to_x_two, after(via_two, *wave)), 1)
+    y_three = swap_dp(add_low(to_y_three, after(via_three, *wave)), 2)
     out_grads = run(
         out_grad_kernel,
         "out_grad",
@@ -1260,9 +1265,11 @@
     summed_a = sum_cores(*back_a[1:])
     wave = (x_two, y_three, out_grads[0])
     dkv_a = sum_z([after(piece, *wave) for piece in summed_a])
+    x_first, y_first = swap_dp(after(x_first, *wave), 1), swap_dp(after(y_first, *wave), 2)
+    via_one, x_one = x_first[0], x_first[1]
+    via_zero, y_zero = y_first[0], y_first[1]
     back_b = attend_back(1, after(mixed_gradient, *summed_a, *wave))
-    wave = (back_b[0], dkv_a, via_one, via_zero)
-    x_one, y_zero = swap_dp(after(to_x[1], *wave), 1), swap_dp(after(to_y[0], *wave), 2)
+    wave = (back_b[0], dkv_a, x_first, y_first)
     summed_b = sum_cores(back_b[1], after(back_b[2], *wave))
     parts_b = [shift_z_down(summed_b[s], s) for s in (1, 2, 3)]
 
@@ -1308,8 +1315,8 @@
     dkv_b = summed_b[0].astype(jnp.float32)
     for part in parts_b:
         dkv_b = dkv_b + part.astype(jnp.float32)
-    x_zero = swap_dp(add_low(to_x[0], after(via_zero, dkv_b)), 1)
-    y_one = swap_dp(add_low(to_y[1], after(via_one, dkv_b)), 2)
+    x_zero = swap_dp(add_low(to_x_zero, via_zero), 1)
+    y_one = swap_dp(add_low(to_y_one, via_one), 2)
     hop = shift_z(add_low(after(home[3], dkv_b), x_three, y_three), -1)
     q_out_mine = sum_pair(q_results[1:])
     q_out_shared = share_square(q_out_mine)
@@ -1320,7 +1327,7 @@
     dkv_pieces, *kv_grads = run(
         kv_grad_kernel,
         "kv_grad",
-        (ids, after(n1, x_one, y_zero, *q_out_mine), dkv_a, dkv_b, cosine, sine),
+        (ids, after(n1, x_zero, y_one, *q_out_mine), dkv_a, dkv_b, cosine, sine),
         [SMEM] + [VMEM] * 5,
         [struct((16 * k_cols, rows))]
         + [struct((4, 2 * k_cols, wide))] * 4
@@ -1336,7 +1343,7 @@
     grad_tokens, gain_one_grad = run(
         finish_kernel,
         "finish",
-        (ids, first_all, dkv_pieces, dn_q, dh, after(x, x_zero, y_one), gain_one),
+        (ids, first_all, dkv_pieces, dn_q, dh, after(x, *q_out_shared), gain_one),
         [SMEM] + [VMEM] * 6,
         [struct((width, rows), jnp.float32), struct((width, 1), jnp.float32)],
         [VMEM] * 2,

time: 377 us -> 380 us (level)
  waiting for transfers between devices: 119 us -> 133 us
  local copies, waits for them, and re-layouts: 54.8 us -> 42.8 us
    unnamed x222 -> x212, local copies, waits for them, and re-layouts: 42.2 us -> 31.3 us
    ppermute x36 -> x34, waiting for transfers between devices: 40.8 us -> 48.8 us  [swap_dp(): return lax.ppermute(value, 'dp', [(j, j ^ mask) for j in range(4)])]
    ppermute x36 -> x34, starting transfers between devices: 37.2 us -> 35.2 us  [swap_dp(): return lax.ppermute(value, 'dp', [(j, j ^ mask) for j in range(4)])]
  transfers between devices with their start and end apart: 83 -> 81, of which waited for: 36 -> 39; matrix products, arithmetic and copies ran while one was open for 8% -> 8% of each run, Pallas kernels for 17% -> 15%
where the time goes in v7:
time: 380 us; the launch traced here: 373 us
  waiting for transfers between devices  133 us (35%)
  Pallas kernels  99.2 us (26%)
  starting transfers between devices  76.1 us (20%)
  local copies, waits for them, and re-layouts  42.8 us (11%)
  other arithmetic  19.6 us (5%)
    pallas_call x16, Pallas kernels, run(): pl.pallas_call(body, out_shape=tuple(outs), in_specs=in_specs, out_specs=...  99.2 us
    ppermute x34, waiting for transfers between devices, swap_dp(): return lax.ppermute(value, 'dp', [(j, j ^ mask) for j in range(4)])  48.8 us
    ppermute x34, starting transfers between devices, swap_dp(): return lax.ppermute(value, 'dp', [(j, j ^ mask) for j in range(4)])  35.2 us
    unnamed x212, local copies, waits for them, and re-layouts  31.3 us
    ppermute x6, waiting for transfers between devices, shift_z_down(): lax.ppermute(value, 'fsdp', [(j, j - 2 * step) for j in range(8) if j - 2...  21.8 us
    ppermute x3, waiting for transfers between devices, shift_z_up(): lax.ppermute(value, 'fsdp', [(j, j + 2 * step) for j in range(8) if j + 2...  21.5 us
    ppermute x15, waiting for transfers between devices, shift_z(): lax.ppermute(value, 'fsdp', [(j, (j + 2 * step) % 8) for j in range(8)])  19 us
    ppermute x15, starting transfers between devices, shift_z(): lax.ppermute(value, 'fsdp', [(j, (j + 2 * step) % 8) for j in range(8)])  15.5 us
  transfers between devices with their start and end apart: 81, of which 39 were waited for; matrix products, arithmetic and copies ran while one was open for 8% of the time, Pallas kernels for 15%

profile of v7, /device:TPU:0, one launch (start us, length us, event | category | flops | bytes accessed | tf_op | source)
XLA Modules:
  0.0 373.0 jit_solution(2527527312301368787)
XLA Ops:
  5.0 5.1 %collective-permute-start.3 = (bf16[208,256]{1,0:T(8,128)(2,1)S(1)}, bf16[208,256]{1,0:T(8,128)(2,1)S(1)}, u32[]{:S(2)}, u32[]{:S(2)}) collective-permute-start(bf16[208,256]{1,0:T(8,128)(2,1)S(1)} %pack_first.1), channel_id=1, source_target_pairs={{0,6},{1,7},{2,0},{3,1},{4,2},{5,3},{6,4},{7,5},{8,14},{9,15},{10,... | collective-permute-start | bytes 319496 | tf_op jit(solution)/shard_map/ppermute | solution.py:365
  25.5 8.1 %collective-permute-done.9.refs_3_ = bf16[4,208,256]{2,1,0:T(8,128)(2,1)S(1)} collective-permute-done((bf16[4,208,256]{2,1,0:T(8,128)(2,1)S(1)}, bf16[4,208,256]{2,1,0:T(8,128)(2,1)S(1)}, u32[]{:S(2)}, u32[]{:S(2)}) %collective-permute-start.9) | collective-permute-done | bytes 426016 | tf_op jit(solution)/shard_map/ppermute | solution.py:361
  35.1 5.7 %collective-permute-done.4.refs_1_.refs_6_ = bf16[1088,256]{1,0:T(8,128)(2,1)S(1)} collective-permute-done((bf16[1088,256]{1,0:T(8,128)(2,1)}, bf16[1088,256]{1,0:T(8,128)(2,1)S(1)}, u32[]{:S(2)}, u32[]{:S(2)}) %collective-permute-start.4) | collective-permute-done | bytes 557088 | tf_op jit(solution)/shard_map/ppermute | solution.py:365
  49.7 6.1 %collective-permute-done.5.refs_2_.refs_7_ = bf16[1088,256]{1,0:T(8,128)(2,1)} collective-permute-done((bf16[1088,256]{1,0:T(8,128)(2,1)S(1)}, bf16[1088,256]{1,0:T(8,128)(2,1)}, u32[]{:S(2)}, u32[]{:S(2)}) %collective-permute-start.5) | collective-permute-done | bytes 557088 | tf_op jit(solution)/shard_map/ppermute | solution.py:365
  68.9 9.0 %collective-permute-done.20.refs_4_ = bf16[320,640]{1,0:T(8,128)(2,1)S(1)} collective-permute-done((bf16[320,640]{1,0:T(8,128)(2,1)S(1)}, bf16[320,640]{1,0:T(8,128)(2,1)S(1)}, u32[]{:S(2)}, u32[]{:S(2)}) %collective-permute-start.20) | collective-permute-done | bytes 409632 | tf_op jit(solution)/shard_map/ppermute | solution.py:369
  84.0 6.9 %collective-permute-done.23.refs_5_ = bf16[320,640]{1,0:T(8,128)(2,1)S(1)} collective-permute-done((bf16[320,640]{1,0:T(8,128)(2,1)S(1)}, bf16[320,640]{1,0:T(8,128)(2,1)S(1)}, u32[]{:S(2)}, u32[]{:S(2)}) %collective-permute-start.23) | collective-permute-done | bytes 409632 | tf_op jit(solution)/shard_map/ppermute | solution.py:369
  94.2 4.6 %collective-permute-start.25 = (bf16[320,640]{1,0:T(8,128)(2,1)S(1)}, bf16[320,640]{1,0:T(8,128)(2,1)S(1)}, u32[]{:S(2)}, u32[]{:S(2)}) collective-permute-start(bf16[320,640]{1,0:T(8,128)(2,1)S(1)} %collective-permute-done.23.refs_5_), channel_id=1, source_target_pairs={{0,2},{1,3},{2,4},{3,5},{4,6},{5,7},{8,10},{9,11},{10,12},{11,13},... | collective-permute-start | bytes 1228808 | tf_op jit(solution)/shard_map/ppermute | solution.py:369
  99.3 5.6 %collective-permute-done.25.refs_6_ = bf16[320,640]{1,0:T(8,128)(2,1)S(1)} collective-permute-done((bf16[320,640]{1,0:T(8,128)(2,1)S(1)}, bf16[320,640]{1,0:T(8,128)(2,1)S(1)}, u32[]{:S(2)}, u32[]{:S(2)}) %collective-permute-start.25) | collective-permute-done | bytes 409632 | tf_op jit(solution)/shard_map/ppermute | solution.py:369
  107.8 8.4 %attend.2 = (bf16[15,64,160]{2,1,0:T(8,128)(2,1)S(1)}, f32[5,1,480]{2,1,0:T(1,128)S(1)}, bf16[5,1280,64]{2,1,0:T(8,128)(2,1)S(1)}, bf16[5,1280,64]{2,1,0:T(8,128)(2,1)S(1)}) custom-call(s32[4]{0:T(128)S(1)} %pad_add_fusion.ids_ref.refs_0_, s32[16]{0:T(128)S(1)} %reshape.245.refs_1_, bf16[15,64,320]{2,1,0:T(8,128)(2,1)S(1)} %get-tuple-element.133.refs_2_, ...), custom_call_target="tpu_custom_call" | custom-call | flops 3145728000 | bytes 5846480 | tf_op jit(solution)/shard_map/attend/pallas_call | solution.py:409
  122.7 8.8 %attend.3 = (bf16[15,64,160]{2,1,0:T(8,128)(2,1)S(1)}, f32[5,1,480]{2,1,0:T(1,128)S(1)}, bf16[5,1280,64]{2,1,0:T(8,128)(2,1)S(1)}, bf16[5,1280,64]{2,1,0:T(8,128)(2,1)S(1)}) custom-call(s32[4]{0:T(128)S(1)} %pad_add_fusion.ids_ref.refs_0_, s32[16]{0:T(128)S(1)} %reshape.245.refs_1_, bf16[15,64,320]{2,1,0:T(8,128)(2,1)S(1)} %get-tuple-element.133.refs_2_, ...), custom_call_target="tpu_custom_call" | custom-call | flops 3145728000 | bytes 5846480 | tf_op jit(solution)/shard_map/attend/pallas_call | solution.py:409
  146.2 30.1 %mlp.1 = (f32[2,960,320]{2,1,0:T(8,128)}, bf16[2,960,384]{2,1,0:T(8,128)(2,1)}, bf16[960,256]{1,0:T(8,128)(2,1)S(1)}, bf16[960,256]{1,0:T(8,128)(2,1)S(1)}, bf16...) custom-call(s32[4]{0:T(128)S(1)} %pad_add_fusion.ids_ref.refs_0_, ...), custom_call_target="tpu_custom_call" | custom-call | flops 14155776000 | bytes 23658512 | tf_op jit(solution)/shard_map/mlp/pallas_call | solution.py:409
  194.9 12.8 %attend_back.2 = (bf16[15,64,160]{2,1,0:T(8,128)(2,1)S(1)}, bf16[4,160,640]{2,1,0:T(8,128)(2,1)S(1)}, bf16[4,160,640]{2,1,0:T(8,128)(2,1)S(1)}) custom-call(s32[4]{0:T(128)S(1)} %pad_add_fusion.ids_ref.refs_0_, s32[16]{0:T(128)S(1)} %reshape.245.refs_1_, bf16[15,64,320]{2,1,0:T(8,128)(2,1)S(1)} %copy-done.70, bf16[15,64,320]{2,1,0:T(8,128)(2,1)S(1)} %bitcast.136, ...), custom_call_target="tpu_custom_call" | custom-call | flops 7864320000 | bytes 4904400 | tf_op jit(solution)/shard_map/attend_back/pallas_call | solution.py:409
  207.9 7.2 %collective-permute-done.42 = bf16[960,256]{1,0:T(8,128)(2,1)S(1)} collective-permute-done((bf16[960,256]{1,0:T(8,128)(2,1)S(1)}, bf16[960,256]{1,0:T(8,128)(2,1)S(1)}, u32[]{:S(2)}, u32[]{:S(2)}) %collective-permute-start.42) | collective-permute-done | bytes 491552 | tf_op jit(solution)/shard_map/ppermute | solution.py:361
  221.0 6.3 %collective-permute-done.44 = bf16[960,256]{1,0:T(8,128)(2,1)S(1)} collective-permute-done((bf16[960,256]{1,0:T(8,128)(2,1)S(1)}, bf16[960,256]{1,0:T(8,128)(2,1)S(1)}, u32[]{:S(2)}, u32[]{:S(2)}) %collective-permute-start.44) | collective-permute-done | bytes 491552 | tf_op jit(solution)/shard_map/ppermute | solution.py:361
  234.7 13.1 %attend_back.3 = (bf16[15,64,160]{2,1,0:T(8,128)(2,1)S(1)}, bf16[4,160,640]{2,1,0:T(8,128)(2,1)S(1)}, bf16[4,160,640]{2,1,0:T(8,128)(2,1)S(1)}) custom-call(s32[4]{0:T(128)S(1)} %pad_add_fusion.ids_ref.refs_0_, s32[16]{0:T(128)S(1)} %reshape.245.refs_1_, bf16[15,64,320]{2,1,0:T(8,128)(2,1)S(1)} %copy-done.70, bf16[15,64,320]{2,1,0:T(8,128)(2,1)S(1)} %bitcast.137, ...), custom_call_target="tpu_custom_call" | custom-call | flops 7864320000 | bytes 4904400 | tf_op jit(solution)/shard_map/attend_back/pallas_call | solution.py:409
  250.3 3.6 collective-permute-done.46
  255.0 4.0 %finish_q.1 = (f32[4,240,320]{2,1,0:T(8,128)S(1)}, bf16[4,256,256]{2,1,0:T(8,128)(2,1)S(1)}, bf16[4,256,256]{2,1,0:T(8,128)(2,1)S(1)}, bf16[4,256,256]{2,1,0:T(8...) custom-call(s32[4]{0:T(128)S(1)} %pad_add_fusion.ids_ref.refs_0_, ...), custom_call_target="tpu_custom_call" | custom-call | flops 1179648000 | bytes 12156944 | tf_op jit(solution)/shard_map/finish_q/pallas_call | solution.py:409
  260.6 3.8 %collective-permute-done.55 = bf16[4,160,640]{2,1,0:T(8,128)(2,1)S(1)} collective-permute-done((bf16[4,160,640]{2,1,0:T(8,128)(2,1)S(1)}, bf16[4,160,640]{2,1,0:T(8,128)(2,1)S(1)}, u32[]{:S(2)}, u32[]{:S(2)}) %collective-permute-start.55) | collective-permute-done | bytes 819232 | tf_op jit(solution)/shard_map/ppermute | solution.py:357
  268.7 5.7 %collective-permute-done.56 = bf16[160,640]{1,0:T(8,128)(2,1)S(1)} collective-permute-done((bf16[160,640]{1,0:T(8,128)(2,1)S(1)}, bf16[160,640]{1,0:T(8,128)(2,1)S(1)}, u32[]{:S(2)}, u32[]{:S(2)}) %collective-permute-start.56) | collective-permute-done | bytes 204832 | tf_op jit(solution)/shard_map/ppermute | solution.py:373
  275.1 7.0 %collective-permute-done.58 = bf16[160,640]{1,0:T(8,128)(2,1)S(1)} collective-permute-done((bf16[160,640]{1,0:T(8,128)(2,1)S(1)}, bf16[160,640]{1,0:T(8,128)(2,1)S(1)}, u32[]{:S(2)}, u32[]{:S(2)}) %collective-permute-start.58) | collective-permute-done | bytes 204832 | tf_op jit(solution)/shard_map/ppermute | solution.py:373
  282.1 6.7 %collective-permute-done.57 = bf16[160,640]{1,0:T(8,128)(2,1)S(1)} collective-permute-done((bf16[160,640]{1,0:T(8,128)(2,1)S(1)}, bf16[160,640]{1,0:T(8,128)(2,1)S(1)}, u32[]{:S(2)}, u32[]{:S(2)}) %collective-permute-start.57) | collective-permute-done | bytes 204832 | tf_op jit(solution)/shard_map/ppermute | solution.py:373
  295.9 4.1 %kv_grad.1 = (bf16[640,320]{1,0:T(8,128)(2,1)S(1)}, bf16[4,80,256]{2,1,0:T(8,128)(2,1)S(1)}, bf16[4,80,256]{2,1,0:T(8,128)(2,1)S(1)}, bf16[4,80,256]{2,1,0:T(8,1...) custom-call(s32[4]{0:T(128)S(1)} %pad_add_fusion.ids_ref.refs_0_, ...), custom_call_target="tpu_custom_call" | custom-call | flops 393216000 | bytes 3235856 | tf_op jit(solution)/shard_map/kv_grad/pallas_call | solution.py:409
  310.7 6.2 %collective-permute-done.60 = bf16[4,256,256]{2,1,0:T(8,128)(2,1)} collective-permute-done((bf16[4,256,256]{2,1,0:T(8,128)(2,1)}, bf16[4,256,256]{2,1,0:T(8,128)(2,1)}, u32[]{:S(2)}, u32[]{:S(2)}) %collective-permute-start.60) | collective-permute-done | bytes 524320 | tf_op jit(solution)/shard_map/ppermute | solution.py:361
  358.5 7.5 %collective-permute-done.80 = f32[2,960]{1,0:T(2,128)S(1)} collective-permute-done((f32[2,960]{1,0:T(2,128)S(1)}, f32[2,960]{1,0:T(2,128)S(1)}, u32[]{:S(2)}, u32[]{:S(2)}) %collective-permute-start.80) | collective-permute-done | bytes 7712 | tf_op jit(solution)/shard_map/ppermute | solution.py:1381
  (429 shorter events, 184.6 us)
Async XLA Ops:
  21.3 27.0 %collective-permute-start.12 = (bf16[4,208,256]{2,1,0:T(8,128)(2,1)S(1)}, bf16[4,208,256]{2,1,0:T(8,128)(2,1)S(1)}, u32[]{:S(2)}, u32[]{:S(2)}) collective-permute-start(bf16[4,208,256]{2,1,0:T(8,128)(2,1)S(1)} %pad_maximum_fusion.refs_1_), channel_id=1, source_target_pairs={{0,1},{1,0},{2,3},{3,2},{4,5},{5,4},{6,7},{7,6},{8,9},{9,8},{10,11... | collective-permute-start | bytes 1277960 | tf_op jit(solution)/shard_map/ppermute | solution.py:357
  23.4 19.0 %collective-permute-start.7 = (bf16[4,208,256]{2,1,0:T(8,128)(2,1)S(1)}, bf16[4,208,256]{2,1,0:T(8,128)(2,1)S(1)}, u32[]{:S(2)}, u32[]{:S(2)}) collective-permute-start(bf16[4,208,256]{2,1,0:T(8,128)(2,1)S(1)} %pad_maximum_fusion.refs_1_), channel_id=1, source_target_pairs={{0,8},{8,0},{16,24},{24,16},{1,9},{9,1},{17,25},{25,17},{2,10},{10... | collective-permute-start | bytes 1277960 | tf_op jit(solution)/shard_map/ppermute | solution.py:361
  56.1 21.9 %collective-permute-start.6 = (bf16[1088,256]{1,0:T(8,128)(2,1)}, bf16[1088,256]{1,0:T(8,128)(2,1)S(1)}, u32[]{:S(2)}, u32[]{:S(2)}) collective-permute-start(bf16[1088,256]{1,0:T(8,128)(2,1)} %collective-permute-done.5.refs_2_.refs_7_), channel_id=1, source_target_pairs={{0,2},{1,3},{2,4},{3,5},{4,6},{5,7},{6,0},{7,1},{8,10},{9,11},{10,... | collective-permute-start | bytes 1671176 | tf_op jit(solution)/shard_map/ppermute | solution.py:365
  190.8 17.0 %collective-permute-start.40 = (bf16[960,256]{1,0:T(8,128)(2,1)S(1)}, bf16[960,256]{1,0:T(8,128)(2,1)S(1)}, u32[]{:S(2)}, u32[]{:S(2)}) collective-permute-start(bf16[960,256]{1,0:T(8,128)(2,1)S(1)} %copy-done.103), channel_id=1, source_target_pairs={{0,16},{8,24},{16,0},{24,8},{1,17},{9,25},{17,1},{25,9},{2,18},{10... | collective-permute-start | bytes 1474568 | tf_op jit(solution)/shard_map/ppermute | solution.py:361
  191.5 16.4 %collective-permute-start.41 = (bf16[960,256]{1,0:T(8,128)(2,1)S(1)}, bf16[960,256]{1,0:T(8,128)(2,1)S(1)}, u32[]{:S(2)}, u32[]{:S(2)}) collective-permute-start(bf16[960,256]{1,0:T(8,128)(2,1)S(1)} %copy-done.102), channel_id=1, source_target_pairs={{0,8},{8,0},{16,24},{24,16},{1,9},{9,1},{17,25},{25,17},{2,10},{10... | collective-permute-start | bytes 1474568 | tf_op jit(solution)/shard_map/ppermute | solution.py:361
  192.7 22.3 %collective-permute-start.42 = (bf16[960,256]{1,0:T(8,128)(2,1)S(1)}, bf16[960,256]{1,0:T(8,128)(2,1)S(1)}, u32[]{:S(2)}, u32[]{:S(2)}) collective-permute-start(bf16[960,256]{1,0:T(8,128)(2,1)S(1)} %copy-done.101), channel_id=1, source_target_pairs={{0,8},{8,0},{16,24},{24,16},{1,9},{9,1},{17,25},{25,17},{2,10},{10... | collective-permute-start | bytes 1474568 | tf_op jit(solution)/shard_map/ppermute | solution.py:361
  193.5 21.5 %collective-permute-start.43 = (bf16[960,256]{1,0:T(8,128)(2,1)S(1)}, bf16[960,256]{1,0:T(8,128)(2,1)S(1)}, u32[]{:S(2)}, u32[]{:S(2)}) collective-permute-start(bf16[960,256]{1,0:T(8,128)(2,1)S(1)} %copy-done.100), channel_id=1, source_target_pairs={{0,16},{8,24},{16,0},{24,8},{1,17},{9,25},{17,1},{25,9},{2,18},{10... | collective-permute-start | bytes 1474568 | tf_op jit(solution)/shard_map/ppermute | solution.py:361
  228.5 19.2 %collective-permute-start.53 = (bf16[160,640]{1,0:T(8,128)(2,1)S(1)}, bf16[160,640]{1,0:T(8,128)(2,1)S(1)}, u32[]{:S(2)}, u32[]{:S(2)}) collective-permute-start(bf16[160,640]{1,0:T(8,128)(2,1)S(1)} %get-tuple-element.181), channel_id=1, source_target_pairs={{2,0},{3,1},{4,2},{5,3},{6,4},{7,5},{10,8},{11,9},{12,10},{13,11},... | collective-permute-start | bytes 614408 | tf_op jit(solution)/shard_map/ppermute | solution.py:373
  229.8 20.4 %collective-permute-start.52 = (bf16[160,640]{1,0:T(8,128)(2,1)S(1)}, bf16[160,640]{1,0:T(8,128)(2,1)S(1)}, u32[]{:S(2)}, u32[]{:S(2)}) collective-permute-start(bf16[160,640]{1,0:T(8,128)(2,1)S(1)} %get-tuple-element.180), channel_id=1, source_target_pairs={{4,0},{5,1},{6,2},{7,3},{12,8},{13,9},{14,10},{15,11},{20,16},{21,... | collective-permute-start | bytes 614408 | tf_op jit(solution)/shard_map/ppermute | solution.py:373
  231.1 19.1 %collective-permute-start.51 = (bf16[160,640]{1,0:T(8,128)(2,1)S(1)}, bf16[160,640]{1,0:T(8,128)(2,1)S(1)}, u32[]{:S(2)}, u32[]{:S(2)}) collective-permute-start(bf16[160,640]{1,0:T(8,128)(2,1)S(1)} %get-tuple-element.179), channel_id=1, source_target_pairs={{6,0},{7,1},{14,8},{15,9},{22,16},{23,17},{30,24},{31,25}} | collective-permute-start | bytes 614408 | tf_op jit(solution)/shard_map/ppermute | solution.py:373
  232.4 21.5 %collective-permute-start.46 = (bf16[2,960,256]{2,1,0:T(8,128)(2,1)S(1)}, bf16[2,960,256]{2,1,0:T(8,128)(2,1)S(1)}, u32[]{:S(2)}, u32[]{:S(2)}) collective-permute-start(bf16[2,960,256]{2,1,0:T(8,128)(2,1)S(1)} %copy-done.97), channel_id=1, source_target_pairs={{0,16},{8,24},{16,0},{24,8},{1,17},{9,25},{17,1},{25,9},{2,18},{10... | collective-permute-start | bytes 2949128 | tf_op jit(solution)/shard_map/ppermute | solution.py:361
  233.8 21.2 %collective-permute-start.48 = (bf16[2,960,256]{2,1,0:T(8,128)(2,1)S(1)}, bf16[2,960,256]{2,1,0:T(8,128)(2,1)S(1)}, u32[]{:S(2)}, u32[]{:S(2)}) collective-permute-start(bf16[2,960,256]{2,1,0:T(8,128)(2,1)S(1)} %copy-done.96), channel_id=1, source_target_pairs={{0,8},{8,0},{16,24},{24,16},{1,9},{9,1},{17,25},{25,17},{2,10},{10... | collective-permute-start | bytes 2949128 | tf_op jit(solution)/shard_map/ppermute | solution.py:361
  259.0 30.9 %collective-permute-start.54 = (bf16[16,256,256]{2,1,0:T(8,128)(2,1)S(1)}, bf16[16,256,256]{2,1,0:T(8,128)(2,1)S(1)}, u32[]{:S(2)}, u32[]{:S(2)}) collective-permute-start(bf16[16,256,256]{2,1,0:T(8,128)(2,1)S(1)} %get-tuple-element.188), channel_id=1, source_target_pairs={{0,1},{1,0},{2,3},{3,2},{4,5},{5,4},{6,7},{7,6},{8,9},{9,8},{10,11... | collective-permute-start | bytes 6291464 | tf_op jit(solution)/shard_map/ppermute | solution.py:357
  259.7 34.2 %collective-permute-start.47 = (bf16[960,256]{1,0:T(8,128)(2,1)S(1)}, bf16[960,256]{1,0:T(8,128)(2,1)S(1)}, u32[]{:S(2)}, u32[]{:S(2)}) collective-permute-start(bf16[960,256]{1,0:T(8,128)(2,1)S(1)} %fusion.9), channel_id=1, source_target_pairs={{0,8},{8,0},{16,24},{24,16},{1,9},{9,1},{17,25},{25,17},{2,10},{10... | collective-permute-start | bytes 1474568 | tf_op jit(solution)/shard_map/ppermute | solution.py:361
  267.3 21.5 %collective-permute-start.57 = (bf16[160,640]{1,0:T(8,128)(2,1)S(1)}, bf16[160,640]{1,0:T(8,128)(2,1)S(1)}, u32[]{:S(2)}, u32[]{:S(2)}) collective-permute-start(bf16[160,640]{1,0:T(8,128)(2,1)S(1)} %get-tuple-element.265), channel_id=1, source_target_pairs={{4,0},{5,1},{6,2},{7,3},{12,8},{13,9},{14,10},{15,11},{20,16},{21,... | collective-permute-start | bytes 614408 | tf_op jit(solution)/shard_map/ppermute | solution.py:373
  274.4 20.6 %collective-permute-start.49 = (bf16[960,256]{1,0:T(8,128)(2,1)S(1)}, bf16[960,256]{1,0:T(8,128)(2,1)S(1)}, u32[]{:S(2)}, u32[]{:S(2)}) collective-permute-start(bf16[960,256]{1,0:T(8,128)(2,1)S(1)} %fusion.8), channel_id=1, source_target_pairs={{0,16},{8,24},{16,0},{24,8},{1,17},{9,25},{17,1},{25,9},{2,18},{10... | collective-permute-start | bytes 1474568 | tf_op jit(solution)/shard_map/ppermute | solution.py:361
  289.9 17.0 %collective-permute-start.72 = (bf16[960,256]{1,0:T(8,128)(2,1)}, bf16[960,256]{1,0:T(8,128)(2,1)}, u32[]{:S(2)}, u32[]{:S(2)}) collective-permute-start(bf16[960,256]{1,0:T(8,128)(2,1)} %add_convert_fusion.5), channel_id=1, source_target_pairs={{0,6},{1,7},{2,0},{3,1},{4,2},{5,3},{6,4},{7,5},{8,14},{9,15},{10,... | collective-permute-start | bytes 1474568 | tf_op jit(solution)/shard_map/ppermute | solution.py:365
  291.6 19.2 %collective-permute-start.61 = (bf16[4,256,256]{2,1,0:T(8,128)(2,1)}, bf16[4,256,256]{2,1,0:T(8,128)(2,1)}, u32[]{:S(2)}, u32[]{:S(2)}) collective-permute-start(bf16[4,256,256]{2,1,0:T(8,128)(2,1)} %get-tuple-element.259), channel_id=1, source_target_pairs={{0,24},{8,16},{16,8},{24,0},{1,25},{9,17},{17,9},{25,1},{2,26},{10... | collective-permute-start | bytes 1572872 | tf_op jit(solution)/shard_map/ppermute | solution.py:361
  292.5 24.4 %collective-permute-start.60 = (bf16[4,256,256]{2,1,0:T(8,128)(2,1)}, bf16[4,256,256]{2,1,0:T(8,128)(2,1)}, u32[]{:S(2)}, u32[]{:S(2)}) collective-permute-start(bf16[4,256,256]{2,1,0:T(8,128)(2,1)} %get-tuple-element.260), channel_id=1, source_target_pairs={{0,16},{8,24},{16,0},{24,8},{1,17},{9,25},{17,1},{25,9},{2,18},{10... | collective-permute-start | bytes 1572872 | tf_op jit(solution)/shard_map/ppermute | solution.py:361
  293.9 23.0 %collective-permute-start.59 = (bf16[4,256,256]{2,1,0:T(8,128)(2,1)}, bf16[4,256,256]{2,1,0:T(8,128)(2,1)}, u32[]{:S(2)}, u32[]{:S(2)}) collective-permute-start(bf16[4,256,256]{2,1,0:T(8,128)(2,1)} %get-tuple-element.261), channel_id=1, source_target_pairs={{0,8},{8,0},{16,24},{24,16},{1,9},{9,1},{17,25},{25,17},{2,10},{10... | collective-permute-start | bytes 1572872 | tf_op jit(solution)/shard_map/ppermute | solution.py:361
  303.4 22.1 %collective-permute-start.65 = (bf16[16,80,256]{2,1,0:T(8,128)(2,1)}, bf16[16,80,256]{2,1,0:T(8,128)(2,1)}, u32[]{:S(2)}, u32[]{:S(2)}) collective-permute-start(bf16[16,80,256]{2,1,0:T(8,128)(2,1)} %get-tuple-element.202), channel_id=1, source_target_pairs={{0,1},{1,0},{2,3},{3,2},{4,5},{5,4},{6,7},{7,6},{8,9},{9,8},{10,11... | collective-permute-start | bytes 1966088 | tf_op jit(solution)/shard_map/ppermute | solution.py:357
  309.5 25.4 %collective-permute-start.73 = (bf16[960,256]{1,0:T(8,128)(2,1)}, bf16[960,256]{1,0:T(8,128)(2,1)}, u32[]{:S(2)}, u32[]{:S(2)}) collective-permute-start(bf16[960,256]{1,0:T(8,128)(2,1)} %add_convert_fusion.4), channel_id=1, source_target_pairs={{0,6},{1,7},{2,0},{3,1},{4,2},{5,3},{6,4},{7,5},{8,14},{9,15},{10,... | collective-permute-start | bytes 1474568 | tf_op jit(solution)/shard_map/ppermute | solution.py:365
  334.9 18.7 %collective-permute-start.68 = (bf16[4,80,256]{2,1,0:T(8,128)(2,1)}, bf16[4,80,256]{2,1,0:T(8,128)(2,1)}, u32[]{:S(2)}, u32[]{:S(2)}) collective-permute-start(bf16[4,80,256]{2,1,0:T(8,128)(2,1)} %get-tuple-element.276), channel_id=1, source_target_pairs={{0,24},{8,16},{16,8},{24,0},{1,25},{9,17},{17,9},{25,1},{2,26},{10... | collective-permute-start | bytes 491528 | tf_op jit(solution)/shard_map/ppermute | solution.py:361
  351.8 17.4 %collective-permute-start.74 = (bf16[960,256]{1,0:T(8,128)(2,1)S(1)}, bf16[960,256]{1,0:T(8,128)(2,1)S(1)}, u32[]{:S(2)}, u32[]{:S(2)}) collective-permute-start(bf16[960,256]{1,0:T(8,128)(2,1)S(1)} %copy-done.89), channel_id=1, source_target_pairs={{0,6},{1,7},{2,0},{3,1},{4,2},{5,3},{6,4},{7,5},{8,14},{9,15},{10,... | collective-permute-start | bytes 1474568 | tf_op jit(solution)/shard_map/ppermute | solution.py:365
  (161 other events, 1748.7 us)

commit v8 on v6

--- a/solution.py
+++ b/solution.py
@@ -1177,11 +1177,12 @@
             pltpu.SemaphoreType.DMA((2, 16)),
         ],
         18 * 16 * half * block * 2 * rows,
-        40,
+        56,
     )
     keep, send = results[:2]
     home, to_x, to_y, far = results[2:6], results[6:10], results[10:14], results[14:18]
     arrived = swap_core(send)
+    via_three, via_two = swap_dp(far[3], 1), swap_dp(far[2], 2)
 
     output, dh, mixed_gradient, gain_two_grad, da_pieces = run(
         turn_point_kernel,
@@ -1237,15 +1238,14 @@
             total = total + shift_z_down(summed[s], s).astype(jnp.float32)
         return total
 
-    via_three = swap_dp(after(far[3], mixed_gradient), 1)
-    via_two = swap_dp(after(far[2], mixed_gradient), 2)
-    x_three = swap_dp(after(to_x[3], mixed_gradient), 1)
-    y_two = swap_dp(after(to_y[2], mixed_gradient), 2)
-    back_a = attend_back(0, mixed_gradient)
-    wave = (back_a[0], via_three, via_two, x_three, y_two)
+    wave = (via_three, via_two, mixed_gradient)
+    x_three, y_two = swap_dp(after(to_x[3], *wave), 1), swap_dp(after(to_y[2], *wave), 2)
     x_two = swap_dp(add_low(to_x[2], after(via_two, *wave)), 1)
     y_three = swap_dp(add_low(to_y[3], after(via_three, *wave)), 2)
+    back_a = attend_back(0, after(mixed_gradient, *wave))
+    wave = (back_a[0], x_three, y_two, x_two, y_three)
     via_one, via_zero = swap_dp(after(far[1], *wave), 1), swap_dp(after(far[0], *wave), 2)
+    hop = shift_z(add_low(after(home[3], back_a[0]), x_three, y_three), -1)
     out_grads = run(
         out_grad_kernel,
         "out_grad",
@@ -1258,12 +1258,14 @@
         14,
     )
     summed_a = sum_cores(*back_a[1:])
-    wave = (x_two, y_three, out_grads[0])
+    wave = (via_one, via_zero, hop, out_grads[0])
     dkv_a = sum_z([after(piece, *wave) for piece in summed_a])
+    x_one, y_zero = swap_dp(after(to_x[1], *wave), 1), swap_dp(after(to_y[0], *wave), 2)
     back_b = attend_back(1, after(mixed_gradient, *summed_a, *wave))
-    wave = (back_b[0], dkv_a, via_one, via_zero)
-    x_one, y_zero = swap_dp(after(to_x[1], *wave), 1), swap_dp(after(to_y[0], *wave), 2)
-    summed_b = sum_cores(back_b[1], after(back_b[2], *wave))
+    wave = (back_b[0], dkv_a, x_one, y_zero)
+    x_zero = swap_dp(add_low(to_x[0], after(via_zero, *wave)), 1)
+    y_one = swap_dp(add_low(to_y[1], after(via_one, *wave)), 2)
+    summed_b = sum_cores(back_b[1], after(back_b[2], dkv_a, x_one, y_zero))
     parts_b = [shift_z_down(summed_b[s], s) for s in (1, 2, 3)]
 
     def sum_pair(parts):
@@ -1286,7 +1288,7 @@
         (
             ids,
             first_all,
-            after(n1, *wave),
+            after(n1, *wave, *summed_b),
             back_a[0].reshape(width, cap),
             back_b[0].reshape(width, cap),
             *out_grads,
@@ -1305,12 +1307,10 @@
         22,
     )
     dn_q = q_results[0]
-    dkv_b = summed_b[0].astype(jnp.float32)
+    dkv_b = after(summed_b[0], dn_q).astype(jnp.float32)
     for part in parts_b:
         dkv_b = dkv_b + part.astype(jnp.float32)
-    x_zero = swap_dp(add_low(to_x[0], after(via_zero, dkv_b)), 1)
-    y_one = swap_dp(add_low(to_y[1], after(via_one, dkv_b)), 2)
-    hop = shift_z(add_low(after(home[3], dkv_b), x_three, y_three), -1)
+    hop = shift_z(add_low(home[2], x_two, y_two, after(hop, dkv_b)), -1)
     q_out_mine = sum_pair(q_results[1:])
     q_out_shared = share_square(q_out_mine)
     q_out_total = reduce_all(q_out_shared)
@@ -1320,7 +1320,7 @@
     dkv_pieces, *kv_grads = run(
         kv_grad_kernel,
         "kv_grad",
-        (ids, after(n1, x_one, y_zero, *q_out_mine), dkv_a, dkv_b, cosine, sine),
+        (ids, after(n1, x_zero, y_one, *q_out_mine), dkv_a, dkv_b, cosine, sine),
         [SMEM] + [VMEM] * 5,
         [struct((16 * k_cols, rows))]
         + [struct((4, 2 * k_cols, wide))] * 4
@@ -1336,7 +1336,7 @@
     grad_tokens, gain_one_grad = run(
         finish_kernel,
         "finish",
-        (ids, first_all, dkv_pieces, dn_q, dh, after(x, x_zero, y_one), gain_one),
+        (ids, first_all, dkv_pieces, dn_q, dh, after(x, *q_out_shared), gain_one),
         [SMEM] + [VMEM] * 6,
         [struct((width, rows), jnp.float32), struct((width, 1), jnp.float32)],
         [VMEM] * 2,
@@ -1346,8 +1346,7 @@
     )
     grad_tokens = grad_tokens.T.reshape(batches, cap, width)
     kv_mine = sum_pair(kv_grads)
-    hop = shift_z(add_low(home[2], x_two, y_two, after(hop, dkv_pieces)), -1)
-    hop = shift_z(add_low(home[1], x_one, y_one, after(hop, *kv_mine)), -1)
+    hop = shift_z(add_low(home[1], x_one, y_one, after(hop, gain_one_grad)), -1)
     mlp_total = (
         home[0].astype(jnp.float32)
         + y_zero.astype(jnp.float32)

time: 377 us -> 375 us (level)
  starting transfers between devices: 78.4 us -> 91.9 us
  local copies, waits for them, and re-layouts: 54.8 us -> 42.7 us
  waiting for transfers between devices: 119 us -> 115 us
    unnamed x222 -> x212, local copies, waits for them, and re-layouts: 42.2 us -> 31.2 us
    ppermute x2, waiting for transfers between devices: 8.54 us -> 0.11 us  [fast(): lax.ppermute(gain_total, 'fsdp', [(j, j ^ mask) for j in range(8)])]
    ppermute x2, starting transfers between devices: 3.18 us -> 10.6 us  [fast(): lax.ppermute(gain_total, 'fsdp', [(j, j ^ mask) for j in range(8)])]
    ppermute x15, starting transfers between devices: 15.5 us -> 22.3 us  [shift_z(): lax.ppermute(value, 'fsdp', [(j, (j + 2 * step) % 8) for j in range(8)])]
    ppermute x15, waiting for transfers between devices: 18.6 us -> 22.8 us  [shift_z(): lax.ppermute(value, 'fsdp', [(j, (j + 2 * step) % 8) for j in range(8)])]
  transfers between devices with their start and end apart: 83 -> 83, of which waited for: 36 -> 41; matrix products, arithmetic and copies ran while one was open for 8% -> 8% of each run, Pallas kernels for 17% -> 16%
where the time goes in v8:
time: 375 us; the launch traced here: 368 us
  waiting for transfers between devices  115 us (31%)
  Pallas kernels  98.3 us (26%)
  starting transfers between devices  91.9 us (25%)
  local copies, waits for them, and re-layouts  42.7 us (11%)
  other arithmetic  17.8 us (5%)
    pallas_call x16, Pallas kernels, run(): pl.pallas_call(body, out_shape=tuple(outs), in_specs=in_specs, out_specs=...  98.3 us
    ppermute x36, waiting for transfers between devices, swap_dp(): return lax.ppermute(value, 'dp', [(j, j ^ mask) for j in range(4)])  42 us
    ppermute x36, starting transfers between devices, swap_dp(): return lax.ppermute(value, 'dp', [(j, j ^ mask) for j in range(4)])  37.1 us
    unnamed x212, local copies, waits for them, and re-layouts  31.2 us
    ppermute x15, waiting for transfers between devices, shift_z(): lax.ppermute(value, 'fsdp', [(j, (j + 2 * step) % 8) for j in range(8)])  22.8 us
    ppermute x15, starting transfers between devices, shift_z(): lax.ppermute(value, 'fsdp', [(j, (j + 2 * step) % 8) for j in range(8)])  22.3 us
    ppermute x3, waiting for transfers between devices, shift_z_up(): lax.ppermute(value, 'fsdp', [(j, j + 2 * step) for j in range(8) if j + 2...  21.4 us
    ppermute x6, waiting for transfers between devices, shift_z_down(): lax.ppermute(value, 'fsdp', [(j, j - 2 * step) for j in range(8) if j - 2...  17.2 us
  transfers between devices with their start and end apart: 83, of which 41 were waited for; matrix products, arithmetic and copies ran while one was open for 8% of the time, Pallas kernels for 16%

profile of v8, /device:TPU:0, one launch (start us, length us, event | category | flops | bytes accessed | tf_op | source)
XLA Modules:
  0.0 367.8 jit_solution(8560542034946788018)
XLA Ops:
  5.0 5.1 %collective-permute-start.3 = (bf16[208,256]{1,0:T(8,128)(2,1)S(1)}, bf16[208,256]{1,0:T(8,128)(2,1)S(1)}, u32[]{:S(2)}, u32[]{:S(2)}) collective-permute-start(bf16[208,256]{1,0:T(8,128)(2,1)S(1)} %pack_first.1), channel_id=1, source_target_pairs={{0,6},{1,7},{2,0},{3,1},{4,2},{5,3},{6,4},{7,5},{8,14},{9,15},{10,... | collective-permute-start | bytes 319496 | tf_op jit(solution)/shard_map/ppermute | solution.py:365
  16.2 3.3 collective-permute-done.2
  25.5 8.1 %collective-permute-done.9.refs_3_ = bf16[4,208,256]{2,1,0:T(8,128)(2,1)S(1)} collective-permute-done((bf16[4,208,256]{2,1,0:T(8,128)(2,1)S(1)}, bf16[4,208,256]{2,1,0:T(8,128)(2,1)S(1)}, u32[]{:S(2)}, u32[]{:S(2)}) %collective-permute-start.9) | collective-permute-done | bytes 426016 | tf_op jit(solution)/shard_map/ppermute | solution.py:361
  35.2 5.7 %collective-permute-done.4.refs_1_.refs_6_ = bf16[1088,256]{1,0:T(8,128)(2,1)S(1)} collective-permute-done((bf16[1088,256]{1,0:T(8,128)(2,1)}, bf16[1088,256]{1,0:T(8,128)(2,1)S(1)}, u32[]{:S(2)}, u32[]{:S(2)}) %collective-permute-start.4) | collective-permute-done | bytes 557088 | tf_op jit(solution)/shard_map/ppermute | solution.py:365
  49.7 6.1 %collective-permute-done.5.refs_2_.refs_7_ = bf16[1088,256]{1,0:T(8,128)(2,1)} collective-permute-done((bf16[1088,256]{1,0:T(8,128)(2,1)S(1)}, bf16[1088,256]{1,0:T(8,128)(2,1)}, u32[]{:S(2)}, u32[]{:S(2)}) %collective-permute-start.5) | collective-permute-done | bytes 557088 | tf_op jit(solution)/shard_map/ppermute | solution.py:365
  69.0 9.0 %collective-permute-done.20.refs_4_ = bf16[320,640]{1,0:T(8,128)(2,1)S(1)} collective-permute-done((bf16[320,640]{1,0:T(8,128)(2,1)S(1)}, bf16[320,640]{1,0:T(8,128)(2,1)S(1)}, u32[]{:S(2)}, u32[]{:S(2)}) %collective-permute-start.20) | collective-permute-done | bytes 409632 | tf_op jit(solution)/shard_map/ppermute | solution.py:369
  84.0 6.9 %collective-permute-done.23.refs_5_ = bf16[320,640]{1,0:T(8,128)(2,1)S(1)} collective-permute-done((bf16[320,640]{1,0:T(8,128)(2,1)S(1)}, bf16[320,640]{1,0:T(8,128)(2,1)S(1)}, u32[]{:S(2)}, u32[]{:S(2)}) %collective-permute-start.23) | collective-permute-done | bytes 409632 | tf_op jit(solution)/shard_map/ppermute | solution.py:369
  94.2 4.6 %collective-permute-start.25 = (bf16[320,640]{1,0:T(8,128)(2,1)S(1)}, bf16[320,640]{1,0:T(8,128)(2,1)S(1)}, u32[]{:S(2)}, u32[]{:S(2)}) collective-permute-start(bf16[320,640]{1,0:T(8,128)(2,1)S(1)} %collective-permute-done.23.refs_5_), channel_id=1, source_target_pairs={{0,2},{1,3},{2,4},{3,5},{4,6},{5,7},{8,10},{9,11},{10,12},{11,13},... | collective-permute-start | bytes 1228808 | tf_op jit(solution)/shard_map/ppermute | solution.py:369
  99.4 5.5 %collective-permute-done.25.refs_6_ = bf16[320,640]{1,0:T(8,128)(2,1)S(1)} collective-permute-done((bf16[320,640]{1,0:T(8,128)(2,1)S(1)}, bf16[320,640]{1,0:T(8,128)(2,1)S(1)}, u32[]{:S(2)}, u32[]{:S(2)}) %collective-permute-start.25) | collective-permute-done | bytes 409632 | tf_op jit(solution)/shard_map/ppermute | solution.py:369
  107.8 8.4 %attend.2 = (bf16[15,64,160]{2,1,0:T(8,128)(2,1)S(1)}, f32[5,1,480]{2,1,0:T(1,128)S(1)}, bf16[5,1280,64]{2,1,0:T(8,128)(2,1)S(1)}, bf16[5,1280,64]{2,1,0:T(8,128)(2,1)S(1)}) custom-call(s32[4]{0:T(128)S(1)} %pad_add_fusion.ids_ref.refs_0_, s32[16]{0:T(128)S(1)} %reshape.235.refs_1_, bf16[15,64,320]{2,1,0:T(8,128)(2,1)S(1)} %get-tuple-element.139.refs_2_, ...), custom_call_target="tpu_custom_call" | custom-call | flops 3145728000 | bytes 5846480 | tf_op jit(solution)/shard_map/attend/pallas_call | solution.py:409
  122.7 8.8 %attend.3 = (bf16[15,64,160]{2,1,0:T(8,128)(2,1)S(1)}, f32[5,1,480]{2,1,0:T(1,128)S(1)}, bf16[5,1280,64]{2,1,0:T(8,128)(2,1)S(1)}, bf16[5,1280,64]{2,1,0:T(8,128)(2,1)S(1)}) custom-call(s32[4]{0:T(128)S(1)} %pad_add_fusion.ids_ref.refs_0_, s32[16]{0:T(128)S(1)} %reshape.235.refs_1_, bf16[15,64,320]{2,1,0:T(8,128)(2,1)S(1)} %get-tuple-element.139.refs_2_, ...), custom_call_target="tpu_custom_call" | custom-call | flops 3145728000 | bytes 5846480 | tf_op jit(solution)/shard_map/attend/pallas_call | solution.py:409
  147.2 29.2 %mlp.1 = (f32[2,960,320]{2,1,0:T(8,128)}, bf16[2,960,384]{2,1,0:T(8,128)(2,1)}, bf16[960,256]{1,0:T(8,128)(2,1)}, bf16[960,256]{1,0:T(8,128)(2,1)}, bf16[960,256...) custom-call(s32[4]{0:T(128)} %copy-done.61, ...), custom_call_target="tpu_custom_call" | custom-call | flops 14155776000 | bytes 23658512 | tf_op jit(solution)/shard_map/mlp/pallas_call | solution.py:409
  186.3 4.1 %collective-permute-done.40 = bf16[960,256]{1,0:T(8,128)(2,1)S(1)} collective-permute-done((bf16[960,256]{1,0:T(8,128)(2,1)}, bf16[960,256]{1,0:T(8,128)(2,1)S(1)}, u32[]{:S(2)}, u32[]{:S(2)}) %collective-permute-start.40) | collective-permute-done | bytes 491552 | tf_op jit(solution)/shard_map/ppermute | solution.py:361
  195.8 13.0 %attend_back.2 = (bf16[15,64,160]{2,1,0:T(8,128)(2,1)S(1)}, bf16[4,160,640]{2,1,0:T(8,128)(2,1)S(1)}, bf16[4,160,640]{2,1,0:T(8,128)(2,1)S(1)}) custom-call(s32[4]{0:T(128)S(1)} %copy-done.62, s32[16]{0:T(128)S(1)} %reshape.235.refs_1_, bf16[15,64,320]{2,1,0:T(8,128)(2,1)S(1)} %copy-done.67, bf16[15,64,320]{2,1,0:T(8,128)(2,1)S(1)} %bitcast.113, ...), custom_call_target="tpu_custom_call" | custom-call | flops 7864320000 | bytes 4904400 | tf_op jit(solution)/shard_map/attend_back/pallas_call | solution.py:409
  208.9 5.2 %collective-permute-done.44 = bf16[960,256]{1,0:T(8,128)(2,1)S(1)} collective-permute-done((bf16[960,256]{1,0:T(8,128)(2,1)S(1)}, bf16[960,256]{1,0:T(8,128)(2,1)S(1)}, u32[]{:S(2)}, u32[]{:S(2)}) %collective-permute-start.44) | collective-permute-done | bytes 491552 | tf_op jit(solution)/shard_map/ppermute | solution.py:361
  234.3 12.8 %attend_back.3 = (bf16[15,64,160]{2,1,0:T(8,128)(2,1)S(1)}, bf16[4,160,640]{2,1,0:T(8,128)(2,1)S(1)}, bf16[4,160,640]{2,1,0:T(8,128)(2,1)S(1)}) custom-call(s32[4]{0:T(128)S(1)} %copy-done.62, s32[16]{0:T(128)S(1)} %reshape.235.refs_1_, bf16[15,64,320]{2,1,0:T(8,128)(2,1)S(1)} %copy-done.67, bf16[15,64,320]{2,1,0:T(8,128)(2,1)S(1)} %bitcast.114, ...), custom_call_target="tpu_custom_call" | custom-call | flops 7864320000 | bytes 4904400 | tf_op jit(solution)/shard_map/attend_back/pallas_call | solution.py:409
  252.4 4.0 %finish_q.1 = (f32[4,240,320]{2,1,0:T(8,128)S(1)}, bf16[4,256,256]{2,1,0:T(8,128)(2,1)S(1)}, bf16[4,256,256]{2,1,0:T(8,128)(2,1)S(1)}, bf16[4,256,256]{2,1,0:T(8...) custom-call(s32[4]{0:T(128)S(1)} %copy-done.62, ...), custom_call_target="tpu_custom_call" | custom-call | flops 1179648000 | bytes 12156944 | tf_op jit(solution)/shard_map/finish_q/pallas_call | solution.py:409
  262.0 7.7 %collective-permute-done.61 = bf16[160,640]{1,0:T(8,128)(2,1)S(1)} collective-permute-done((bf16[160,640]{1,0:T(8,128)(2,1)S(1)}, bf16[160,640]{1,0:T(8,128)(2,1)S(1)}, u32[]{:S(2)}, u32[]{:S(2)}) %collective-permute-start.61) | collective-permute-done | bytes 204832 | tf_op jit(solution)/shard_map/ppermute | solution.py:373
  270.5 7.0 %collective-permute-done.60 = bf16[160,640]{1,0:T(8,128)(2,1)S(1)} collective-permute-done((bf16[160,640]{1,0:T(8,128)(2,1)S(1)}, bf16[160,640]{1,0:T(8,128)(2,1)S(1)}, u32[]{:S(2)}, u32[]{:S(2)}) %collective-permute-start.60) | collective-permute-done | bytes 204832 | tf_op jit(solution)/shard_map/ppermute | solution.py:373
  283.7 4.1 %kv_grad.1 = (bf16[640,320]{1,0:T(8,128)(2,1)S(1)}, bf16[4,80,256]{2,1,0:T(8,128)(2,1)S(1)}, bf16[4,80,256]{2,1,0:T(8,128)(2,1)S(1)}, bf16[4,80,256]{2,1,0:T(8,1...) custom-call(s32[4]{0:T(128)S(1)} %copy-done.62, bf16[4,240,320]{2,1,0:T(8,128)(2,1)S(1)} %bitcast.94, ...), custom_call_target="tpu_custom_call" | custom-call | flops 393216000 | bytes 3235856 | tf_op jit(solution)/shard_map/kv_grad/pallas_call | solution.py:409
  297.7 7.9 %collective-permute-done.63 = bf16[4,256,256]{2,1,0:T(8,128)(2,1)} collective-permute-done((bf16[4,256,256]{2,1,0:T(8,128)(2,1)}, bf16[4,256,256]{2,1,0:T(8,128)(2,1)}, u32[]{:S(2)}, u32[]{:S(2)}) %collective-permute-start.63) | collective-permute-done | bytes 524320 | tf_op jit(solution)/shard_map/ppermute | solution.py:361
  318.9 5.0 %collective-permute-start.67 = (bf16[256,256]{1,0:T(8,128)(2,1)}, bf16[256,256]{1,0:T(8,128)(2,1)}, u32[]{:S(2)}, u32[]{:S(2)}) collective-permute-start(bf16[256,256]{1,0:T(8,128)(2,1)} %get-tuple-element.269), channel_id=1, source_target_pairs={{0,2},{1,3},{2,4},{3,5},{4,6},{5,7},{6,0},{7,1},{8,10},{9,11},{10,... | collective-permute-start | bytes 393224 | tf_op jit(solution)/shard_map/ppermute | solution.py:365
  342.0 7.1 %collective-permute-start.81 = (f32[2,960]{1,0:T(2,128)S(1)}, f32[2,960]{1,0:T(2,128)S(1)}, u32[]{:S(2)}, u32[]{:S(2)}) collective-permute-start(f32[2,960]{1,0:T(2,128)S(1)} %add.393), channel_id=1, source_target_pairs={{0,2},{1,3},{2,0},{3,1},{4,6},{5,7},{6,4},{7,5},{8,10},{9,11},{10,... | collective-permute-start | bytes 23048 | tf_op jit(solution)/shard_map/ppermute | solution.py:1373
  350.7 3.5 collective-permute-start.82
  (433 shorter events, 183.2 us)
Async XLA Ops:
  21.3 27.0 %collective-permute-start.12 = (bf16[4,208,256]{2,1,0:T(8,128)(2,1)S(1)}, bf16[4,208,256]{2,1,0:T(8,128)(2,1)S(1)}, u32[]{:S(2)}, u32[]{:S(2)}) collective-permute-start(bf16[4,208,256]{2,1,0:T(8,128)(2,1)S(1)} %pad_maximum_fusion.refs_1_), channel_id=1, source_target_pairs={{0,1},{1,0},{2,3},{3,2},{4,5},{5,4},{6,7},{7,6},{8,9},{9,8},{10,11... | collective-permute-start | bytes 1277960 | tf_op jit(solution)/shard_map/ppermute | solution.py:357
  23.4 19.1 %collective-permute-start.7 = (bf16[4,208,256]{2,1,0:T(8,128)(2,1)S(1)}, bf16[4,208,256]{2,1,0:T(8,128)(2,1)S(1)}, u32[]{:S(2)}, u32[]{:S(2)}) collective-permute-start(bf16[4,208,256]{2,1,0:T(8,128)(2,1)S(1)} %pad_maximum_fusion.refs_1_), channel_id=1, source_target_pairs={{0,8},{8,0},{16,24},{24,16},{1,9},{9,1},{17,25},{25,17},{2,10},{10... | collective-permute-start | bytes 1277960 | tf_op jit(solution)/shard_map/ppermute | solution.py:361
  56.1 21.9 %collective-permute-start.6 = (bf16[1088,256]{1,0:T(8,128)(2,1)}, bf16[1088,256]{1,0:T(8,128)(2,1)S(1)}, u32[]{:S(2)}, u32[]{:S(2)}) collective-permute-start(bf16[1088,256]{1,0:T(8,128)(2,1)} %collective-permute-done.5.refs_2_.refs_7_), channel_id=1, source_target_pairs={{0,2},{1,3},{2,4},{3,5},{4,6},{5,7},{6,0},{7,1},{8,10},{9,11},{10,... | collective-permute-start | bytes 1671176 | tf_op jit(solution)/shard_map/ppermute | solution.py:365
  191.3 17.6 %collective-permute-start.42 = (bf16[960,256]{1,0:T(8,128)(2,1)S(1)}, bf16[960,256]{1,0:T(8,128)(2,1)S(1)}, u32[]{:S(2)}, u32[]{:S(2)}) collective-permute-start(bf16[960,256]{1,0:T(8,128)(2,1)S(1)} %copy-done.103), channel_id=1, source_target_pairs={{0,8},{8,0},{16,24},{24,16},{1,9},{9,1},{17,25},{25,17},{2,10},{10... | collective-permute-start | bytes 1474568 | tf_op jit(solution)/shard_map/ppermute | solution.py:361
  192.1 16.8 %collective-permute-start.43 = (bf16[960,256]{1,0:T(8,128)(2,1)S(1)}, bf16[960,256]{1,0:T(8,128)(2,1)S(1)}, u32[]{:S(2)}, u32[]{:S(2)}) collective-permute-start(bf16[960,256]{1,0:T(8,128)(2,1)S(1)} %copy-done.102), channel_id=1, source_target_pairs={{0,16},{8,24},{16,0},{24,8},{1,17},{9,25},{17,1},{25,9},{2,18},{10... | collective-permute-start | bytes 1474568 | tf_op jit(solution)/shard_map/ppermute | solution.py:361
  193.1 21.1 %collective-permute-start.44 = (bf16[960,256]{1,0:T(8,128)(2,1)S(1)}, bf16[960,256]{1,0:T(8,128)(2,1)S(1)}, u32[]{:S(2)}, u32[]{:S(2)}) collective-permute-start(bf16[960,256]{1,0:T(8,128)(2,1)S(1)} %add_convert_fusion.10), channel_id=1, source_target_pairs={{0,8},{8,0},{16,24},{24,16},{1,9},{9,1},{17,25},{25,17},{2,10},{10... | collective-permute-start | bytes 1474568 | tf_op jit(solution)/shard_map/ppermute | solution.py:361
  194.5 20.3 %collective-permute-start.45 = (bf16[960,256]{1,0:T(8,128)(2,1)S(1)}, bf16[960,256]{1,0:T(8,128)(2,1)S(1)}, u32[]{:S(2)}, u32[]{:S(2)}) collective-permute-start(bf16[960,256]{1,0:T(8,128)(2,1)S(1)} %add_convert_fusion.9), channel_id=1, source_target_pairs={{0,16},{8,24},{16,0},{24,8},{1,17},{9,25},{17,1},{25,9},{2,18},{10... | collective-permute-start | bytes 1474568 | tf_op jit(solution)/shard_map/ppermute | solution.py:361
  228.3 21.4 %collective-permute-start.53 = (bf16[960,256]{1,0:T(8,128)(2,1)S(1)}, bf16[960,256]{1,0:T(8,128)(2,1)S(1)}, u32[]{:S(2)}, u32[]{:S(2)}) collective-permute-start(bf16[960,256]{1,0:T(8,128)(2,1)S(1)} %copy-done.99), channel_id=1, source_target_pairs={{0,8},{8,0},{16,24},{24,16},{1,9},{9,1},{17,25},{25,17},{2,10},{10... | collective-permute-start | bytes 1474568 | tf_op jit(solution)/shard_map/ppermute | solution.py:361
  229.2 20.5 %collective-permute-start.54 = (bf16[960,256]{1,0:T(8,128)(2,1)S(1)}, bf16[960,256]{1,0:T(8,128)(2,1)S(1)}, u32[]{:S(2)}, u32[]{:S(2)}) collective-permute-start(bf16[960,256]{1,0:T(8,128)(2,1)S(1)} %copy-done.98), channel_id=1, source_target_pairs={{0,16},{8,24},{16,0},{24,8},{1,17},{9,25},{17,1},{25,9},{2,18},{10... | collective-permute-start | bytes 1474568 | tf_op jit(solution)/shard_map/ppermute | solution.py:361
  230.4 16.8 %collective-permute-start.52 = (bf16[160,640]{1,0:T(8,128)(2,1)S(1)}, bf16[160,640]{1,0:T(8,128)(2,1)S(1)}, u32[]{:S(2)}, u32[]{:S(2)}) collective-permute-start(bf16[160,640]{1,0:T(8,128)(2,1)S(1)} %get-tuple-element.187), channel_id=1, source_target_pairs={{2,0},{3,1},{4,2},{5,3},{6,4},{7,5},{10,8},{11,9},{12,10},{13,11},... | collective-permute-start | bytes 614408 | tf_op jit(solution)/shard_map/ppermute | solution.py:373
  231.7 17.9 %collective-permute-start.51 = (bf16[160,640]{1,0:T(8,128)(2,1)S(1)}, bf16[160,640]{1,0:T(8,128)(2,1)S(1)}, u32[]{:S(2)}, u32[]{:S(2)}) collective-permute-start(bf16[160,640]{1,0:T(8,128)(2,1)S(1)} %get-tuple-element.186), channel_id=1, source_target_pairs={{4,0},{5,1},{6,2},{7,3},{12,8},{13,9},{14,10},{15,11},{20,16},{21,... | collective-permute-start | bytes 614408 | tf_op jit(solution)/shard_map/ppermute | solution.py:373
  256.4 21.3 %collective-permute-start.58 = (bf16[16,256,256]{2,1,0:T(8,128)(2,1)S(1)}, bf16[16,256,256]{2,1,0:T(8,128)(2,1)S(1)}, u32[]{:S(2)}, u32[]{:S(2)}) collective-permute-start(bf16[16,256,256]{2,1,0:T(8,128)(2,1)S(1)} %get-tuple-element.204), channel_id=1, source_target_pairs={{0,1},{1,0},{2,3},{3,2},{4,5},{5,4},{6,7},{7,6},{8,9},{9,8},{10,11... | collective-permute-start | bytes 6291464 | tf_op jit(solution)/shard_map/ppermute | solution.py:357
  256.7 26.2 %collective-permute-start.55 = (bf16[960,256]{1,0:T(8,128)(2,1)S(1)}, bf16[960,256]{1,0:T(8,128)(2,1)S(1)}, u32[]{:S(2)}, u32[]{:S(2)}) collective-permute-start(bf16[960,256]{1,0:T(8,128)(2,1)S(1)} %add_convert_fusion.7), channel_id=1, source_target_pairs={{0,8},{8,0},{16,24},{24,16},{1,9},{9,1},{17,25},{25,17},{2,10},{10... | collective-permute-start | bytes 1474568 | tf_op jit(solution)/shard_map/ppermute | solution.py:361
  259.2 18.4 %collective-permute-start.60 = (bf16[160,640]{1,0:T(8,128)(2,1)S(1)}, bf16[160,640]{1,0:T(8,128)(2,1)S(1)}, u32[]{:S(2)}, u32[]{:S(2)}) collective-permute-start(bf16[160,640]{1,0:T(8,128)(2,1)S(1)} %get-tuple-element.276), channel_id=1, source_target_pairs={{4,0},{5,1},{6,2},{7,3},{12,8},{13,9},{14,10},{15,11},{20,16},{21,... | collective-permute-start | bytes 614408 | tf_op jit(solution)/shard_map/ppermute | solution.py:373
  260.5 17.1 %collective-permute-start.59 = (bf16[160,640]{1,0:T(8,128)(2,1)S(1)}, bf16[160,640]{1,0:T(8,128)(2,1)S(1)}, u32[]{:S(2)}, u32[]{:S(2)}) collective-permute-start(bf16[160,640]{1,0:T(8,128)(2,1)S(1)} %get-tuple-element.277), channel_id=1, source_target_pairs={{2,0},{3,1},{4,2},{5,3},{6,4},{7,5},{10,8},{11,9},{12,10},{13,11},... | collective-permute-start | bytes 614408 | tf_op jit(solution)/shard_map/ppermute | solution.py:373
  279.4 18.2 %collective-permute-start.64 = (bf16[4,256,256]{2,1,0:T(8,128)(2,1)}, bf16[4,256,256]{2,1,0:T(8,128)(2,1)}, u32[]{:S(2)}, u32[]{:S(2)}) collective-permute-start(bf16[4,256,256]{2,1,0:T(8,128)(2,1)} %get-tuple-element.271), channel_id=1, source_target_pairs={{0,24},{8,16},{16,8},{24,0},{1,25},{9,17},{17,9},{25,1},{2,26},{10... | collective-permute-start | bytes 1572872 | tf_op jit(solution)/shard_map/ppermute | solution.py:361
  280.6 25.0 %collective-permute-start.63 = (bf16[4,256,256]{2,1,0:T(8,128)(2,1)}, bf16[4,256,256]{2,1,0:T(8,128)(2,1)}, u32[]{:S(2)}, u32[]{:S(2)}) collective-permute-start(bf16[4,256,256]{2,1,0:T(8,128)(2,1)} %get-tuple-element.272), channel_id=1, source_target_pairs={{0,16},{8,24},{16,0},{24,8},{1,17},{9,25},{17,1},{25,9},{2,18},{10... | collective-permute-start | bytes 1572872 | tf_op jit(solution)/shard_map/ppermute | solution.py:361
  281.8 23.8 %collective-permute-start.62 = (bf16[4,256,256]{2,1,0:T(8,128)(2,1)}, bf16[4,256,256]{2,1,0:T(8,128)(2,1)}, u32[]{:S(2)}, u32[]{:S(2)}) collective-permute-start(bf16[4,256,256]{2,1,0:T(8,128)(2,1)} %get-tuple-element.273), channel_id=1, source_target_pairs={{0,8},{8,0},{16,24},{24,16},{1,9},{9,1},{17,25},{25,17},{2,10},{10... | collective-permute-start | bytes 1572872 | tf_op jit(solution)/shard_map/ppermute | solution.py:361
  291.3 22.8 %collective-permute-start.68 = (bf16[16,80,256]{2,1,0:T(8,128)(2,1)}, bf16[16,80,256]{2,1,0:T(8,128)(2,1)}, u32[]{:S(2)}, u32[]{:S(2)}) collective-permute-start(bf16[16,80,256]{2,1,0:T(8,128)(2,1)} %get-tuple-element.216), channel_id=1, source_target_pairs={{0,1},{1,0},{2,3},{3,2},{4,5},{5,4},{6,7},{7,6},{8,9},{9,8},{10,11... | collective-permute-start | bytes 1966088 | tf_op jit(solution)/shard_map/ppermute | solution.py:357
  297.4 21.4 %collective-permute-start.75 = (bf16[960,256]{1,0:T(8,128)(2,1)}, bf16[960,256]{1,0:T(8,128)(2,1)}, u32[]{:S(2)}, u32[]{:S(2)}) collective-permute-start(bf16[960,256]{1,0:T(8,128)(2,1)} %add_convert_fusion.5), channel_id=1, source_target_pairs={{0,6},{1,7},{2,0},{3,1},{4,2},{5,3},{6,4},{7,5},{8,14},{9,15},{10,... | collective-permute-start | bytes 1474568 | tf_op jit(solution)/shard_map/ppermute | solution.py:365
  329.1 34.8 %collective-permute-start.76 = (bf16[960,256]{1,0:T(8,128)(2,1)S(1)}, bf16[960,256]{1,0:T(8,128)(2,1)S(1)}, u32[]{:S(2)}, u32[]{:S(2)}) collective-permute-start(bf16[960,256]{1,0:T(8,128)(2,1)S(1)} %add_convert_fusion.4), channel_id=1, source_target_pairs={{0,6},{1,7},{2,0},{3,1},{4,2},{5,3},{6,4},{7,5},{8,14},{9,15},{10,... | collective-permute-start | bytes 1474568 | tf_op jit(solution)/shard_map/ppermute | solution.py:365
  332.0 22.1 %collective-permute-start.71 = (bf16[4,80,256]{2,1,0:T(8,128)(2,1)}, bf16[4,80,256]{2,1,0:T(8,128)(2,1)S(1)}, u32[]{:S(2)}, u32[]{:S(2)}) collective-permute-start(bf16[4,80,256]{2,1,0:T(8,128)(2,1)} %get-tuple-element.289), channel_id=1, source_target_pairs={{0,24},{8,16},{16,8},{24,0},{1,25},{9,17},{17,9},{25,1},{2,26},{10... | collective-permute-start | bytes 491528 | tf_op jit(solution)/shard_map/ppermute | solution.py:361
  333.5 20.6 %collective-permute-start.70 = (bf16[4,80,256]{2,1,0:T(8,128)(2,1)}, bf16[4,80,256]{2,1,0:T(8,128)(2,1)S(1)}, u32[]{:S(2)}, u32[]{:S(2)}) collective-permute-start(bf16[4,80,256]{2,1,0:T(8,128)(2,1)} %get-tuple-element.290), channel_id=1, source_target_pairs={{0,16},{8,24},{16,0},{24,8},{1,17},{9,25},{17,1},{25,9},{2,18},{10... | collective-permute-start | bytes 491528 | tf_op jit(solution)/shard_map/ppermute | solution.py:361
  334.7 19.4 %collective-permute-start.69 = (bf16[4,80,256]{2,1,0:T(8,128)(2,1)}, bf16[4,80,256]{2,1,0:T(8,128)(2,1)}, u32[]{:S(2)}, u32[]{:S(2)}) collective-permute-start(bf16[4,80,256]{2,1,0:T(8,128)(2,1)} %get-tuple-element.291), channel_id=1, source_target_pairs={{0,8},{8,0},{16,24},{24,16},{1,9},{9,1},{17,25},{25,17},{2,10},{10... | collective-permute-start | bytes 491528 | tf_op jit(solution)/shard_map/ppermute | solution.py:361
  (163 other events, 1967.5 us)
